TPU v7x, 32 devices: a whole 2x2x4 slice. The times are simulated.
32 devices in a mesh: atoms: 8 (over z, core), kvec: 4 (over y, x).
Axes of the slice: x: 2, y: 2, z: 4, core: 2. Of those that a mesh axis runs over, the one named last changes fastest.
Arguments:
- positions: float32 [3, 16384], P(None, 'atoms'), may hold values from 0 to 1
- feats: float32 [64, 16384], P(None, 'atoms'), may hold values from -6 to 6
- species: int32 [16384], P('atoms'), may hold values from 0 to 15
- pad_count: int32 [64], P('atoms'), may hold values from 128 to 256
- k_lattice: int32 [3, 1024], P(None, 'kvec'), may hold values from -12 to 13, as said below
- filter_width: float32 [64], replicated, may hold values from 2e-05 to 0.002
- w_charge: float32 [64, 64], replicated, may hold values from -0.75 to 0.75
- species_embed: float32 [64, 16], replicated, may hold values from -3 to 3
- w_out: float32 [64, 64], replicated, may hold values from -0.75 to 0.75
- grad_out: float32 [64, 16384], P(None, ('atoms', 'kvec')), may hold values from -6 to 6
Outputs:
- message: float32 [64, 16384], P(None, ('atoms', 'kvec'))
- grad_positions: float32 [3, 16384], P(None, ('atoms', 'kvec'))
- grad_feats: float32 [64, 16384], P(None, ('atoms', 'kvec'))
Inputs may be any that keep to these rules, and one draw needn't show every extreme that they name: `k_lattice`: the 1024 columns are distinct nonzero integer vectors k with k[0] > 0, or k[0] = 0 and k[1] > 0, or k[0] = k[1] = 0 and k[2] > 0, and with squared length at most 169.
All inputs are finite; a program needn't handle non-finite values.
Results may differ from a plain program's by a relative error of at most 0.0003.
Values sent between devices are 32-bit elements; how exact they have to be, the bound alone decides.
No kernel may reach another device: no remote copies, remote signals or barrier semaphores. Data moves between devices by JAX's collectives and lax.ppermute only.
A program may use at most 64 MiB of HBM per device.

v0:
```python
import math

import jax
import jax.numpy as jnp
from jax import lax
from jax.sharding import PartitionSpec as P

exact = lax.Precision.HIGHEST
two_pi = 2.0 * math.pi


def filtered_sum(part_cos, part_sin, filter_gain):
    sum_cos, sum_sin = lax.psum((part_cos, part_sin), "atoms")
    return (filter_gain * sum_cos, filter_gain * sum_sin)


def on_device(
    positions,
    feats,
    species,
    pad_count,
    k_lattice,
    filter_width,
    w_charge,
    species_embed,
    w_out,
    grad_out,
):
    kvec_count = lax.axis_size("kvec")
    atom_total = feats.shape[1] * lax.axis_size("atoms")
    atom_rows = feats.shape[1]
    share_rows = atom_rows // kvec_count
    valid_mask = (jnp.arange(atom_rows) % 256 < jnp.repeat(pad_count, 256)).astype(jnp.float32)
    one_hot = (jnp.arange(species_embed.shape[1])[:, None] == species[None, :]).astype(jnp.float32)
    charges = valid_mask[None, :] * (
        jnp.dot(w_charge.T, feats, precision=exact)
        + jnp.dot(species_embed, one_hot, precision=exact)
    )
    wave_vec = two_pi * k_lattice.astype(jnp.float32)
    k_square = jnp.sum(wave_vec * wave_vec, axis=0)
    filter_gain = (
        jnp.exp(-k_square[:, None] * filter_width[None, :])
        * 40.0
        / (k_square[:, None] + 40.0)
        / math.sqrt(atom_total)
    )
    phase = jnp.dot(positions.T, wave_vec, precision=exact)
    cos_tile = jnp.cos(phase)
    sine_tile = jnp.sin(phase)
    part_cos = jnp.einsum("aj,ca->jc", cos_tile, charges, precision=exact)
    part_sin = jnp.einsum("aj,ca->jc", sine_tile, charges, precision=exact)
    h_cos, h_sin = filtered_sum(part_cos, part_sin, filter_gain)
    first_row = lax.axis_index("kvec") * share_rows
    mask_share = lax.dynamic_slice_in_dim(valid_mask, first_row, share_rows, 0)
    field_full = jnp.einsum("aj,jc->ca", cos_tile, h_cos, precision=exact) + jnp.einsum(
        "aj,jc->ca", sine_tile, h_sin, precision=exact
    )
    field_part = lax.psum_scatter(field_full, "kvec", scatter_dimension=1, tiled=True)
    field_out = mask_share[None, :] * field_part
    message = jnp.dot(w_out.T, field_out, precision=exact)
    cotangent = lax.all_gather(grad_out, "kvec", axis=1, tiled=True)
    adjoint = valid_mask[None, :] * jnp.dot(w_out, cotangent, precision=exact)
    e_cos = jnp.einsum("aj,ca->jc", cos_tile, adjoint, precision=exact)
    e_sin = jnp.einsum("aj,ca->jc", sine_tile, adjoint, precision=exact)
    b_cos, b_sin = filtered_sum(e_cos, e_sin, filter_gain)
    charge_grad = jnp.einsum("aj,jc->ca", cos_tile, b_cos, precision=exact) + jnp.einsum(
        "aj,jc->ca", sine_tile, b_sin, precision=exact
    )
    along_sin = jnp.einsum("ca,jc->aj", adjoint, h_sin, precision=exact) + jnp.einsum(
        "ca,jc->aj", charges, b_sin, precision=exact
    )
    along_cos = jnp.einsum("ca,jc->aj", adjoint, h_cos, precision=exact) + jnp.einsum(
        "ca,jc->aj", charges, b_cos, precision=exact
    )
    dphase = cos_tile * along_sin - sine_tile * along_cos
    force_part = jnp.einsum("xj,aj->xa", wave_vec, dphase, precision=exact)
    grad_share, force_share = (
        lax.psum_scatter(charge_grad, "kvec", scatter_dimension=1, tiled=True),
        lax.psum_scatter(force_part, "kvec", scatter_dimension=1, tiled=True),
    )
    grad_feats = jnp.dot(w_charge, mask_share[None, :] * grad_share, precision=exact)
    return (message, force_share, grad_feats)


def solution(mesh):
    placed = (
        P(None, "atoms"),
        P(None, "atoms"),
        P("atoms"),
        P("atoms"),
        P(None, "kvec"),
        P(),
        P(),
        P(),
        P(),
        P(None, ("atoms", "kvec")),
    )
    return jax.shard_map(
        on_device,
        mesh=mesh,
        in_specs=placed,
        out_specs=(
            P(None, ("atoms", "kvec")),
            P(None, ("atoms", "kvec")),
            P(None, ("atoms", "kvec")),
        ),
        check_vma=False,
    )
```

profile of v0, /device:TPU:0, one launch (start us, length us, event | category | flops | bytes accessed | tf_op | source)
XLA Modules:
  0.0 206.0 jit_solution(10983821932219730809)
XLA Ops:
  8.0 11.8 %all_gather.3 = f32[64,2048]{1,0:T(8,128)S(1)} all-gather(f32[64,512]{1,0:T(8,128)} %param.19), channel_id=1, replica_groups=mesh['atoms'=8,'kvec'=4] {'kvec'}, dimensions={1}, use_global_device_ids=true | all-gather | bytes 655360 | tf_op jit(solution)/shard_map/all_gather | solution.py:61
  19.9 1.1 convolution_bitcast_fusion.1
  21.0 9.7 %fusion.51 = (f32[256,2048]{1,0:T(8,128)S(1)}, f32[256,2048]{1,0:T(8,128)S(1)}) fusion(f32[3,2048]{1,0:T(4,128)} %param.10, s32[3,256]{1,0:T(4,128)} %param.14), kind=kOutput, calls=%fused_computation.61 | convolution fusion | flops 18875904 | bytes 4221952 | tf_op jit(solution)/shard_map/dot_general | solution.py:47
  31.3 2.6 %fusion.55 = f32[256,64]{0,1:T(8,128)} fusion(f32[256,2048]{1,0:T(8,128)S(1)} %get-tuple-element.7, f32[64,2048]{1,0:T(8,128)S(1)} %convolution_multiply_fusion), kind=kOutput, calls=%fused_computation.65 | convolution fusion | flops 402653184 | bytes 2686976 | tf_op jit(solution)/shard_map/aj,ca->jc/dot_general | solution.py:64
  34.0 0.8 fusion.3
  34.8 2.7 %fusion.54 = f32[256,64]{0,1:T(8,128)} fusion(f32[256,2048]{1,0:T(8,128)S(1)} %get-tuple-element.7, f32[64,2048]{1,0:T(8,128)S(1)} %fusion.3), kind=kOutput, calls=%fused_computation.64 | convolution fusion | flops 402653184 | bytes 2686976 | tf_op jit(solution)/shard_map/aj,ca->jc/dot_general | solution.py:51
  37.5 2.6 %fusion.56 = f32[256,64]{0,1:T(8,128)} fusion(f32[256,2048]{1,0:T(8,128)S(1)} %get-tuple-element.8, f32[64,2048]{1,0:T(8,128)S(1)} %convolution_multiply_fusion), kind=kOutput, calls=%fused_computation.66 | convolution fusion | flops 402653184 | bytes 2686976 | tf_op jit(solution)/shard_map/aj,ca->jc/dot_general | solution.py:63
  40.1 2.7 %fusion.53 = f32[256,64]{0,1:T(8,128)} fusion(f32[256,2048]{1,0:T(8,128)S(1)} %get-tuple-element.8, f32[64,2048]{1,0:T(8,128)S(1)} %fusion.3), kind=kOutput, calls=%fused_computation.63 | convolution fusion | flops 402653184 | bytes 2686976 | tf_op jit(solution)/shard_map/aj,ca->jc/dot_general | solution.py:50
  42.9 55.6 %all-reduce.3.cloned.1.call-done = (f32[256,64]{0,1:T(8,128)}, f32[256,64]{0,1:T(8,128)}, f32[256,64]{0,1:T(8,128)}, f32[256,64]{0,1:T(8,128)}) async-done(((f32[256,64]{0,1:T(8,128)}, f32[256,64]{0,1:T(8,128)}, f32[256,64]{0,1:T(8,128)}, f32[256,64]{0,1:T(8,128)}), (f32[256,64]{0,1:T(8,128)}, f32[256,64]{0,1:T(8,128)}, f32[256,64]{0,1:T(8,128)}, f32[256,64]{0,1:T(8,128)})) %all-reduce.3.cloned.1.call-update) | async-done | bytes 262160 | tf_op jit(solution)/shard_map/psum | solution.py:13
  98.5 3.9 %fusion.15 = f32[64,2048]{1,0:T(8,128)} fusion(f32[256,2048]{1,0:T(8,128)} %copy-done.1, f32[256,64]{0,1:T(8,128)} %get-tuple-element.3, f32[256]{0:T(256)S(1)} %get-tuple-element.10, f32[64]{0:T(128)S(1)} %copy-done.13, f32[256]{0:T(256)S(1)} %get-tuple-element.9), kind=kOutput, calls=%fused_computation.26 | convolution fusion | flops 402735104 | bytes 2689280 | tf_op jit(solution)/shard_map/aj,jc->ca/dot_general | solution.py:55
  102.4 1.9 fusion.13
  104.3 1.9 fusion.17
  106.3 2.2 %fusion.2 = f32[2048,256]{0,1:T(8,128)S(1)} fusion(f32[2048,256]{0,1:T(8,128)S(1)} %fusion.17, f32[64,2048]{1,0:T(8,128)S(1)} %fusion.3, f32[256,2048]{1,0:T(8,128)S(1)} %copy-done.2, f32[256,64]{0,1:T(8,128)S(1)} %copy-done.6, f32[256]{0:T(256)S(1)} %get-tuple-element.10, f32[64]{0:T(128)S(1)} %copy-done.13, f32[256]{0:T(256)S(1)} %get-tuple-element.9), kind=kOutput, calls=%fused_computation.4 | convolution fusion | flops 403783680 | bytes 6883584 | tf_op jit(solution)/shard_map/ca,jc->aj/dot_general | solution.py:69
  108.5 2.2 %fusion.1 = f32[2048,256]{0,1:T(8,128)S(1)} fusion(f32[2048,256]{0,1:T(8,128)S(1)} %fusion.2, f32[2048,256]{0,1:T(8,128)S(1)} %fusion.13, f32[64,2048]{1,0:T(8,128)S(1)} %fusion.3, f32[256,2048]{1,0:T(8,128)S(1)} %get-tuple-element.7, f32[256,64]{0,1:T(8,128)S(1)} %copy-done.7, f32[256]{0:T(256)S(1)} %get-tuple-element.10, f32[64]{0:T(128)S(1)} %copy-done.13, ...), kind=kOutput, calls=%fused_computation.2 | convolution fusion | flops 404307968 | bytes 8980736 | tf_op jit(solution)/shard_map/ca,jc->aj/dot_general | solution.py:72
  110.8 4.5 %convolution_bitcast_fusion = f32[2048,3]{1,0:T(8,128)} fusion(f32[2048,256]{0,1:T(8,128)S(1)} %fusion.1, s32[3,256]{1,0:T(4,128)S(1)} %copy-done.12), kind=kOutput, calls=%fused_computation.5 | convolution fusion | flops 18875904 | bytes 2124800
  115.6 2.2 %convolution_add_fusion.3 = f32[64,2048]{1,0:T(8,128)} fusion(f32[64,2048]{1,0:T(8,128)S(1)} %copy-done.5, f32[256,2048]{1,0:T(8,128)S(1)} %get-tuple-element.7, f32[256,64]{0,1:T(8,128)S(1)} %copy-done.8, f32[256]{0:T(256)S(1)} %get-tuple-element.10, f32[64]{0:T(128)S(1)} %copy-done.13, f32[256]{0:T(256)S(1)} %get-tuple-element.9), kind=kOutput, calls=%fused_computation.8 | convolution fusion | flops 402866176 | bytes 3213568 | tf_op jit(solution)/shard_map/aj,jc->ca/dot_general | solution.py:55
  117.9 3.0 %fusion.22 = f32[64,2048]{1,0:T(8,128)S(1)} fusion(f32[256,2048]{1,0:T(8,128)} %copy-done.1, f32[256,64]{0,1:T(8,128)S(1)} %copy-done.7, f32[256]{0:T(256)S(1)} %get-tuple-element.10, f32[64]{0:T(128)S(1)} %copy-done.13, f32[256]{0:T(256)S(1)} %get-tuple-element.9), kind=kOutput, calls=%fused_computation.28 | convolution fusion | flops 402735104 | bytes 2689280 | tf_op jit(solution)/shard_map/aj,jc->ca/dot_general | solution.py:66
  120.9 2.2 %convolution_add_fusion.2 = f32[64,2048]{1,0:T(8,128)} fusion(f32[64,2048]{1,0:T(8,128)S(1)} %fusion.22, f32[256,2048]{1,0:T(8,128)S(1)} %get-tuple-element.7, f32[256,64]{0,1:T(8,128)S(1)} %copy-done.6, f32[256]{0:T(256)S(1)} %get-tuple-element.10, f32[64]{0:T(128)S(1)} %copy-done.13, f32[256]{0:T(256)S(1)} %get-tuple-element.9), kind=kOutput, calls=%fused_computation.6 | convolution fusion | flops 402866176 | bytes 3213568 | tf_op jit(solution)/shard_map/aj,jc->ca/dot_general | solution.py:66
  123.2 19.0 %reduce-scatter.10.cloned.1.call-done = f32[512,3]{1,0:T(8,128)} async-done(((f32[2048,3]{1,0:T(8,128)}), f32[512,3]{1,0:T(8,128)}) %reduce-scatter.10.cloned.1.call-update) | async-done | bytes 6160
  142.2 1.7 copy.14
  143.9 26.0 %reduce-scatter.6.cloned.1.call-done = f32[64,512]{1,0:T(8,128)} async-done(((f32[64,2048]{1,0:T(8,128)}), f32[64,512]{1,0:T(8,128)}) %reduce-scatter.6.cloned.1.call-update) | async-done | bytes 131088 | tf_op jit(solution)/shard_map/reduce_scatter | solution.py:58
  169.9 1.9 convolution_bitcast_fusion.3
  171.7 25.9 %reduce-scatter.8.cloned.1.call-done = f32[64,512]{1,0:T(8,128)} async-done(((f32[64,2048]{1,0:T(8,128)}), f32[64,512]{1,0:T(8,128)}) %reduce-scatter.8.cloned.1.call-update) | async-done | bytes 131088 | tf_op jit(solution)/shard_map/reduce_scatter | solution.py:78
  197.6 1.8 convolution_bitcast_fusion.2
  (43 shorter events, 2.0 us)
Async XLA Ops:
  7.2 26.8 %copy-start = (f32[64,2048]{1,0:T(8,128)S(1)}, f32[64,2048]{1,0:T(8,128)}, u32[]{:S(2)}) copy-start(f32[64,2048]{1,0:T(8,128)} %param.11) | copy-start | bytes 1572868
  7.2 91.3 %all-reduce.3.cloned.1.call-start = ((), (), s32[]{:S(2)}) async-start(), calls=%async_computation.6 | async-start | bytes 524288 | tf_op jit(solution)/shard_map/psum | solution.py:13
  21.0 9.7 %copy-start.10 = (f32[64,64]{1,0:T(8,128)S(1)}, f32[64,64]{1,0:T(8,128)}, u32[]{:S(2)}) copy-start(f32[64,64]{1,0:T(8,128)} %param.18) | copy-start | bytes 49156
  30.7 9.4 %copy-start.1 = (f32[256,2048]{1,0:T(8,128)}, f32[256,2048]{1,0:T(8,128)S(1)}, u32[]{:S(2)}) copy-start(f32[256,2048]{1,0:T(8,128)S(1)} %get-tuple-element.8) | copy-start | bytes 6291460
  30.7 3.2 %copy-start.11 = (f32[64,64]{1,0:T(8,128)S(1)}, f32[64,64]{1,0:T(8,128)}, u32[]{:S(2)}) copy-start(f32[64,64]{1,0:T(8,128)} %param.16) | copy-start | bytes 49156
  31.3 6.1 %copy-start.3 = (f32[64,2048]{1,0:T(8,128)}, f32[64,2048]{1,0:T(8,128)S(1)}, u32[]{:S(2)}) copy-start(f32[64,2048]{1,0:T(8,128)S(1)} %convolution_multiply_fusion) | copy-start | bytes 1572868
  40.1 2.7 %copy-start.12 = (s32[3,256]{1,0:T(4,128)S(1)}, s32[3,256]{1,0:T(4,128)}, u32[]{:S(2)}) copy-start(s32[3,256]{1,0:T(4,128)} %param.14) | copy-start | bytes 9220
  40.1 58.4 %copy-start.13 = (f32[64]{0:T(128)S(1)}, f32[64]{0:T(128)}, u32[]{:S(2)}) copy-start(f32[64]{0:T(128)} %param.15) | copy-start | bytes 772
  42.8 99.4 %reduce-scatter.10.cloned.1.call-start = ((), (), s32[]{:S(2)}) async-start(), calls=%async_computation.5 | async-start | bytes 1310720
  98.5 3.9 %copy-start.4 = (f32[64,2048]{1,0:T(8,128)S(1)}, f32[64,2048]{1,0:T(8,128)}, u32[]{:S(2)}) copy-start(f32[64,2048]{1,0:T(8,128)} %copy-done.3) | copy-start | bytes 1572868
  98.5 3.9 %copy-start.9 = (f32[256,64]{0,1:T(8,128)S(1)}, f32[256,64]{0,1:T(8,128)}, u32[]{:S(2)}) copy-start(f32[256,64]{0,1:T(8,128)} %get-tuple-element.3) | copy-start | bytes 196612
  98.5 5.9 %copy-start.8 = (f32[256,64]{0,1:T(8,128)S(1)}, f32[256,64]{0,1:T(8,128)}, u32[]{:S(2)}) copy-start(f32[256,64]{0,1:T(8,128)} %get-tuple-element.4) | copy-start | bytes 196612
  102.4 3.9 %copy-start.2 = (f32[256,2048]{1,0:T(8,128)S(1)}, f32[256,2048]{1,0:T(8,128)}, u32[]{:S(2)}) copy-start(f32[256,2048]{1,0:T(8,128)} %copy-done.1) | copy-start | bytes 6291460
  102.4 3.9 %copy-start.6 = (f32[256,64]{0,1:T(8,128)S(1)}, f32[256,64]{0,1:T(8,128)}, u32[]{:S(2)}) copy-start(f32[256,64]{0,1:T(8,128)} %get-tuple-element.5) | copy-start | bytes 196612
  106.3 2.2 %copy-start.7 = (f32[256,64]{0,1:T(8,128)S(1)}, f32[256,64]{0,1:T(8,128)}, u32[]{:S(2)}) copy-start(f32[256,64]{0,1:T(8,128)} %get-tuple-element.6) | copy-start | bytes 196612
  110.8 4.8 %copy-start.5 = (f32[64,2048]{1,0:T(8,128)S(1)}, f32[64,2048]{1,0:T(8,128)}, u32[]{:S(2)}) copy-start(f32[64,2048]{1,0:T(8,128)} %fusion.15) | copy-start | bytes 1572868
  115.3 54.5 %reduce-scatter.6.cloned.1.call-start = ((), (), s32[]{:S(2)}) async-start(), calls=%async_computation.3 | async-start | bytes 655360 | tf_op jit(solution)/shard_map/reduce_scatter | solution.py:58
  117.9 79.8 %reduce-scatter.8.cloned.1.call-start = ((), (), s32[]{:S(2)}) async-start(), calls=%async_computation.4 | async-start | bytes 655360 | tf_op jit(solution)/shard_map/reduce_scatter | solution.py:78
Sparse Core Ops, SparseCore 0:
  42.9 55.5 all-reduce.2
  115.4 26.7 reduce-scatter.9
  145.1 24.7 reduce-scatter.5
  172.8 24.7 reduce-scatter.7
where the time goes:
time: 206 us
  waiting for transfers between devices  126 us (61%)
  matrix products  50.7 us (25%)
  between operations  14 us (7%)
  blocking collectives  11.8 us (6%)
  local copies, waits for them, and re-layouts  2.58 us (1%)
    psum x1, waiting for transfers between devices, filtered_sum(): sum_cos, sum_sin = lax.psum((part_cos, part_sin), 'atoms')  55.6 us
    reduce_scatter x1, waiting for transfers between devices, on_device(): lax.psum_scatter(field_full, 'kvec', scatter_dimension=1, tiled=True)  26 us
    reduce_scatter x1, waiting for transfers between devices, on_device(): lax.psum_scatter(charge_grad, 'kvec', scatter_dimension=1, tiled=True)  25.9 us
    unnamed x5, waiting for transfers between devices  19.1 us
    all_gather x1, blocking collectives, on_device(): cotangent = lax.all_gather(grad_out, 'kvec', axis=1, tiled=True)  11.8 us
    dot_general x1, matrix products, on_device(): phase = jnp.dot(positions.T, wave_vec, precision=exact)  9.71 us
    unnamed x1, matrix products  4.52 us
  transfers between devices with their start and end apart: 4, of which 4 were waited for; matrix products, arithmetic and copies ran while one was open for 5% of the time, Pallas kernels for 0%

commit v1 on v0

v1 whole, which is shorter than its diff:
```python
import functools
import math

import jax
import jax.numpy as jnp
from jax import lax
from jax.experimental import pallas as pl
from jax.experimental.pallas import tpu as pltpu
from jax.sharding import PartitionSpec as P

F32, BF16 = jnp.float32, jnp.bfloat16
HALF_SIN = (4.442867755889893, -7.307443618774414, 3.594788074493408, -0.7843740582466125)
HALF_COS = (1.4142135381698608, -6.978850841522217, 5.7394609451293945, -1.8835630416870117, 0.31069818139076233)
VMEM = pl.BlockSpec(memory_space=pltpu.VMEM)
SMEM = pl.BlockSpec(memory_space=pltpu.SMEM)
ANY = pl.BlockSpec(memory_space=pl.ANY)
PARAMS = pltpu.CompilerParams(vmem_limit_bytes=32 * 2**20)
NN, NT, TN = ((1,), (0,)), ((1,), (1,)), ((0,), (0,))


def halves(value):
    high = value.astype(BF16)
    return high, (value - high.astype(F32)).astype(BF16)


def dot16(left, right, dims):
    return lax.dot_general(left, right, (dims, ((), ())), preferred_element_type=F32)


def dot3(left, right, dims):
    left_high, left_low = halves(left)
    right_high, right_low = halves(right)
    return (
        dot16(left_high, right_high, dims)
        + dot16(left_low, right_high, dims)
        + dot16(left_high, right_low, dims)
    )


def horner(terms, square):
    total = terms[-1] * square + terms[-2]
    for term in terms[-3::-1]:
        total = total * square + term
    return total


def trig(columns, rows):
    turns = columns[0] * rows[0] + columns[1] * rows[1] + columns[2] * rows[2]
    turns = turns - jnp.round(turns)
    square = turns * turns
    half_sin = horner(HALF_SIN, square) * turns
    return 1.0 - half_sin * half_sin, half_sin * horner(HALF_COS, square)


def trig_blocks(k_ref, pos_ref, first, high_low, full=None):
    vectors, atoms = high_low[0].shape
    step = 32
    width = min(256, atoms)
    per_body = max(1, 2048 // atoms)
    per_body = min(per_body, vectors // step)

    def body(block, _):
        for inner in range(per_body):
            here = pl.ds(pl.multiple_of((block * per_body + inner) * step, step), step)
            columns = [k_ref[here, x : x + 1] for x in range(3)]
            for chunk in range(atoms // width):
                lanes = pl.ds(chunk * width, width)
                start = chunk * width if first is None else pl.multiple_of(first + chunk * width, 128)
                rows = [pos_ref[x : x + 1, pl.ds(start, width)] for x in range(3)]
                cos, sin = trig(columns, rows)
                high_low[0][here, lanes], high_low[1][here, lanes] = halves(cos)
                high_low[2][here, lanes], high_low[3][here, lanes] = halves(sin)
                if full is not None:
                    full[0][here, lanes], full[1][here, lanes] = cos, sin
        return 0

    lax.fori_loop(0, vectors // (step * per_body), body, 0)


def tile_kernel(pos_ref, k_ref, cos_high, cos_low, sin_high, sin_low, k_column):
    k_column[:, 0:3] = k_ref[...].astype(F32).T
    trig_blocks(k_column, pos_ref, None, (cos_high, cos_low, sin_high, sin_low))


def sums_kernel(
    here_ref, pad_ref, cos_high, cos_low, sin_high, sin_low, feats_ref, species_ref, w_charge_ref, embed_ref, w_out_ref,
    *rest, groups,
):
    cotangents = rest[:groups]
    keep_ref, send_ref, own_ref, mask_ref, both, total = rest[-6:]
    channels, atoms = feats_ref.shape
    share = cotangents[0].shape[1]
    place, group = here_ref[0], here_ref[1]
    embed_high, embed_low = halves(embed_ref[...])
    for block in range(atoms // 256):
        lanes = slice(block * 256, (block + 1) * 256)
        mask = (lax.broadcasted_iota(jnp.int32, (1, 256), 1) < pad_ref[block]).astype(F32)
        mask_ref[:, lanes] = mask
        species_at = lax.broadcasted_iota(jnp.int32, (embed_ref.shape[0], 256), 0)
        one_hot = (species_at == species_ref[:, lanes]).astype(BF16)
        both[0:channels, lanes] = mask * (
            dot3(w_charge_ref[...], feats_ref[:, lanes], TN)
            + dot16(embed_high, one_hot, TN)
            + dot16(embed_low, one_hot, TN)
        )
    for offset, cotangent in enumerate(cotangents):
        lanes = pl.ds(pl.multiple_of((group ^ offset) * share, share), share)
        adjoint = mask_ref[:, lanes] * dot3(w_out_ref[...], cotangent[...], NN)
        both[channels:, lanes] = adjoint
        if offset == 0:
            own_ref[0:channels, :] = adjoint
            own_ref[channels : 2 * channels, :] = both[0:channels, lanes]
            own_ref[2 * channels :, :] = jnp.broadcast_to(mask_ref[:, lanes], (8, share))
    high, low = halves(both[...])
    pair = jnp.concatenate([high, low], axis=0)
    for part, (tile_high, tile_low) in enumerate(((cos_high, cos_low), (sin_high, sin_low))):
        wide = dot16(tile_high[...], pair, NT)
        total[part] = (
            wide[:, : 2 * channels] + wide[:, 2 * channels :] + dot16(tile_low[...], high, NT)
        )
    rows = keep_ref.shape[1]
    core = place & 1
    for flip, out in enumerate((keep_ref, send_ref)):
        start = pl.multiple_of((core ^ flip) * rows, rows)
        for part in range(2):
            out[part] = total[part, pl.ds(start, rows), :]


def gain_kernel(here_ref, width_ref, k_ref, gain_ref, *, atom_total):
    rows = gain_ref.shape[0]
    start = pl.multiple_of((here_ref[0] & 1) * rows, rows)
    waves = [2.0 * math.pi * k_ref[pl.ds(start, rows), x : x + 1] for x in range(3)]
    square = waves[0] * waves[0] + waves[1] * waves[1] + waves[2] * waves[2]
    gain = jnp.exp(-square * width_ref[...]) * 40.0 / (square + 40.0) / math.sqrt(atom_total)
    gain_ref[...] = jnp.concatenate([gain, gain], axis=1)


def wave_kernel(here_ref, pos_ref, lattice_ref, after_ref, cos, sin, cos_high, cos_low, sin_high, sin_low, k_ref, k_column):
    rows = lattice_ref.shape[1] // 2
    k_column[:, 0:3] = lattice_ref[...].astype(F32).T
    for flip in range(2):
        start = pl.multiple_of(((here_ref[0] & 1) ^ flip) * rows, rows)
        k_ref[flip * rows : (flip + 1) * rows, :] = k_column[pl.ds(start, rows), :]
    first = here_ref[1] * cos.shape[1]
    trig_blocks(k_ref, pos_ref, first, (cos_high, cos_low, sin_high, sin_low), (cos, sin))


def coefficient_stack(near_ref, far_ref, part):
    high, low = halves(jnp.concatenate([near_ref[part], far_ref[part]], axis=0))
    return jnp.concatenate([high, low, high], axis=1)


def own_stack(own_ref, channels):
    high, low = halves(own_ref[0 : 2 * channels, :])
    return jnp.concatenate([high, high, low], axis=0)


def add_field(stack, tile_high, tile_low):
    width = stack.shape[1] // 3
    wide = dot16(stack[:, : 2 * width], tile_high, TN)
    return wide[:width] + wide[width:] + dot16(stack[:, :width], tile_low, TN)


def add_force(sums, rows, get):
    step = 16
    for block in range(rows // step):
        cos, sin, along_cos, along_sin, columns = get(block * step, step)
        slope = cos * along_sin - sin * along_cos
        for x in range(3):
            term = columns[:, x : x + 1] * slope
            sums[x] = sums[x] + (term[0:8] + term[8:16])
    return sums


def own_field_kernel(
    here_ref, cos_high, cos_low, sin_high, sin_low, k_ref, own_ref, near_ref, far_ref,
    field_ref, sums_ref, k_column, along, *tiles,
):
    share = own_ref.shape[1]
    rows = near_ref.shape[1]
    channels = near_ref.shape[2] // 2
    lanes = pl.ds(pl.multiple_of(here_ref[1] * share, share), share)
    for flip in range(2):
        here = pl.ds(pl.multiple_of(((here_ref[0] & 1) ^ flip) * rows, rows), rows)
        to = slice(flip * rows, (flip + 1) * rows)
        k_column[to, :] = k_ref[here, :]
        for tile, source in zip(tiles, (cos_high, cos_low, sin_high, sin_low)):
            tile[to, :] = source[here, lanes]
    other = own_stack(own_ref, channels)
    stacks = [coefficient_stack(near_ref, far_ref, part) for part in range(2)]
    for part in range(2):
        along[part] = dot16(stacks[part], other, NN)
    field_ref[...] = add_field(stacks[0], tiles[0][...], tiles[1][...]) + add_field(
        stacks[1], tiles[2][...], tiles[3][...]
    )

    def get(first, step):
        at = slice(first, first + step)
        cos = tiles[0][at, :].astype(F32) + tiles[1][at, :].astype(F32)
        sin = tiles[2][at, :].astype(F32) + tiles[3][at, :].astype(F32)
        return cos, sin, along[0, at, :], along[1, at, :], k_column[at, 0:3]

    sums = add_force([jnp.zeros((8, share), F32)] * 3, 2 * rows, get)
    for x in range(3):
        sums_ref[8 * x : 8 * x + 8, :] = sums[x]


def field_kernel(own_ref, w_out_ref, w_charge_ref, field_ref, sums_ref, *rest, groups):
    *waves, message_ref, force_ref, grad_ref, along = rest
    waves, coefs = waves[: 7 * groups], waves[7 * groups :]
    channels = w_out_ref.shape[0]
    share = own_ref.shape[1]
    rows = 2 * coefs[0].shape[1]
    other = own_stack(own_ref, channels)
    parts = [[coefficient_stack(coefs[2 * g], coefs[2 * g + 1], part) for g in range(groups)] for part in range(2)]
    for part in range(2):
        along[part] = dot16(jnp.concatenate(parts[part], axis=0), other, NN)
    field = field_ref[...]
    sums = [sums_ref[8 * x : 8 * x + 8, :] for x in range(3)]
    for g in range(groups):
        cos, sin, cos_high, cos_low, sin_high, sin_low, k_ref = waves[7 * g : 7 * g + 7]
        field += add_field(parts[0][g], cos_high[...], cos_low[...])
        field += add_field(parts[1][g], sin_high[...], sin_low[...])
    field = own_ref[2 * channels : 2 * channels + 1, :] * field
    message_ref[...] = dot3(w_out_ref[...], field[:channels], TN)
    grad_ref[...] = dot3(w_charge_ref[...], field[channels:], NN)
    for g in range(groups):
        cos, sin, _, _, _, _, k_ref = waves[7 * g : 7 * g + 7]

        def get(first, step):
            at = slice(first, first + step)
            there = slice(g * rows + first, g * rows + first + step)
            return cos[at, :], sin[at, :], along[0, there, :], along[1, there, :], k_ref[at, 0:3]

        sums = add_force(sums, rows, get)
    for x in range(3):
        force_ref[x : x + 1, :] = 2.0 * math.pi * jnp.sum(sums[x], axis=0, keepdims=True)


def swap(value, axis, offset):
    size = lax.axis_size(axis)
    return lax.ppermute(value, axis, [(place, place ^ offset) for place in range(size)])


def cost(work):
    return pl.CostEstimate(flops=work, bytes_accessed=0, transcendentals=0)


def on_device(
    positions, feats, species, pad_count, k_lattice, filter_width, w_charge, species_embed, w_out, grad_out,
):
    atom_count, group_count = lax.axis_size("atoms"), lax.axis_size("kvec")
    channels, atoms = feats.shape
    share = grad_out.shape[1]
    vectors = k_lattice.shape[1]
    half = vectors // 2
    both = 2 * channels
    here = jnp.stack([lax.axis_index("atoms"), lax.axis_index("kvec")]).astype(jnp.int32)
    f32 = lambda *shape: jax.ShapeDtypeStruct(shape, F32)
    bf16 = lambda *shape: jax.ShapeDtypeStruct(shape, BF16)

    cotangents = [grad_out] + [swap(grad_out, "kvec", m) for m in range(1, group_count)]
    lattices = [k_lattice] + [swap(k_lattice, "kvec", m) for m in range(1, group_count)]

    *tiles, k_column = pl.pallas_call(
        tile_kernel,
        out_shape=[bf16(vectors, atoms)] * 4 + [f32(vectors, 128)],
        in_specs=[VMEM] * 2,
        out_specs=[VMEM] * 5,
        compiler_params=PARAMS,
        cost_estimate=cost(9000 * vectors * atoms),
        name="waves_of_own_vectors",
    )(positions, k_lattice)

    keep, send, own = pl.pallas_call(
        functools.partial(sums_kernel, groups=group_count),
        out_shape=[f32(2, half, both), f32(2, half, both), f32(both + 8, share)],
        in_specs=[SMEM, SMEM] + [VMEM] * (9 + group_count) + [ANY] * (group_count - 1),
        out_specs=[VMEM] * 3,
        scratch_shapes=[
            pltpu.VMEM((1, atoms), F32), pltpu.VMEM((both, atoms), F32), pltpu.VMEM((2, vectors, both), F32),
        ],
        compiler_params=PARAMS,
        cost_estimate=cost(100 * vectors * atoms * channels),
        name="structure_sums",
    )(
        here, pad_count, *tiles, feats, species.reshape(1, atoms), w_charge, species_embed.T, w_out,
        *cotangents, *lattices[1:],
    )

    gain = pl.pallas_call(
        functools.partial(gain_kernel, atom_total=atoms * atom_count),
        out_shape=f32(half, both),
        in_specs=[SMEM, VMEM, VMEM],
        out_specs=VMEM,
        compiler_params=PARAMS,
        cost_estimate=cost(9000 * half * both),
        name="filter_gain",
    )(here, filter_width.reshape(1, channels), k_column)

    def waves_of(lattice, after):
        return pl.pallas_call(
            wave_kernel,
            out_shape=[f32(vectors, share)] * 2 + [bf16(vectors, share)] * 4 + [f32(vectors, 128)],
            in_specs=[SMEM, VMEM, VMEM, ANY],
            out_specs=[VMEM] * 7,
            scratch_shapes=[pltpu.VMEM((vectors, 128), F32)],
            compiler_params=PARAMS,
            cost_estimate=cost(9000 * vectors * share),
            name="waves_of_own_atoms",
        )(here, positions, lattice, after)

    total = keep + swap(send, "atoms", 1)
    waves = []
    offset, made = 2, 1
    while offset < atom_count:
        arrived = swap(total, "atoms", offset)
        last = offset * 2 >= atom_count
        count = group_count - made if last else 1
        beside = [waves_of(lattices[m], total) for m in range(made, min(made + count, group_count))]
        made += len(beside)
        arrived, beside = lax.optimization_barrier((arrived, beside))
        for tiles_made in beside:
            waves += tiles_made
        total = total + arrived
        offset *= 2
    near = gain[None] * total
    plane = [swap(near, "kvec", m) for m in range(1, group_count)]
    field, sums = pl.pallas_call(
        own_field_kernel,
        out_shape=[f32(both, share), f32(24, share)],
        in_specs=[SMEM] + [VMEM] * 8,
        out_specs=[VMEM] * 2,
        scratch_shapes=[pltpu.VMEM((vectors, 128), F32), pltpu.VMEM((2, vectors, share), F32)]
        + [pltpu.VMEM((vectors, share), BF16)] * 4,
        compiler_params=PARAMS,
        cost_estimate=cost(120 * vectors * share * channels),
        name="fields_of_own_vectors",
    )(here, *tiles, k_column, own, near, swap(near, "atoms", 1))
    plane, field = lax.optimization_barrier((plane, field))
    coefs = []
    for part in plane:
        coefs += [part, swap(part, "atoms", 1)]

    return tuple(
        pl.pallas_call(
            functools.partial(field_kernel, groups=group_count - 1),
            out_shape=[f32(channels, share), f32(3, share), f32(channels, share)],
            in_specs=[VMEM] * (5 + 9 * (group_count - 1)),
            out_specs=[VMEM] * 3,
            scratch_shapes=[pltpu.VMEM((2, (group_count - 1) * vectors, share), F32)],
            compiler_params=PARAMS,
            cost_estimate=cost(300 * vectors * share * channels),
            name="fields_and_forces",
        )(own, w_out, w_charge, field, sums, *waves, *coefs)
    )


def solution(mesh):
    shared = P(None, ("atoms", "kvec"))
    placed = (
        P(None, "atoms"), P(None, "atoms"), P("atoms"), P("atoms"), P(None, "kvec"),
        P(), P(), P(), P(), shared,
    )
    return jax.shard_map(
        on_device, mesh=mesh, in_specs=placed, out_specs=(shared, shared, shared), check_vma=False
    )
```

time: 206 us -> 56.5 us (0.27)
  waiting for transfers between devices: 126 us -> 14.9 us
  matrix products: 50.7 us -> 0 us
  starting transfers between devices: 0.38 us -> 16.6 us
  Pallas kernels: 0 us -> 15.4 us
  between operations: 14 us -> 0.8 us
  blocking collectives: 11.8 us -> 0 us
  local copies, waits for them, and re-layouts: 2.58 us -> 8.17 us
    psum x1 -> x0, waiting for transfers between devices: 55.6 us -> none  [filtered_sum(): sum_cos, sum_sin = lax.psum((part_cos, part_sin), 'atoms')]
    reduce_scatter x2 -> x0, waiting for transfers between devices: 51.8 us -> none  [the longest x1 26 us: on_device(): lax.psum_scatter(field_full, 'kvec', scatter_dimension=1, tiled=True)]
    dot_general x18 -> x0, matrix products: 46.2 us -> none  [the longest x1 9.71 us: on_device(): phase = jnp.dot(positions.T, wave_vec, precision=exact)]
    unnamed x5 -> x0, waiting for transfers between devices: 19.1 us -> none
    ppermute x0 -> x16, starting transfers between devices: none -> 16.6 us  [swap(): lax.ppermute(value, axis, [(place, place ^ offset) for place in range(siz...]
    pallas_call x0 -> x8, Pallas kernels: none -> 15.4 us  [the longest x3 4.25 us: waves_of(): pl.pallas_call(wave_kernel, out_shape=[f32(vectors, share)] * 2 + [bf16(v...]
    ppermute x0 -> x16, waiting for transfers between devices: none -> 14.9 us  [swap(): lax.ppermute(value, axis, [(place, place ^ offset) for place in range(siz...]
    all_gather x1 -> x0, blocking collectives: 11.8 us -> none  [on_device(): cotangent = lax.all_gather(grad_out, 'kvec', axis=1, tiled=True)]
  transfers between devices with their start and end apart: 4 -> 16, of which waited for: 4 -> 9; matrix products, arithmetic and copies ran while one was open for 5% -> 0% of each run, Pallas kernels for 0% -> 17%
where the time goes in v1:
time: 56.5 us; the launch traced here: 56 us
  starting transfers between devices  16.6 us (29%)
  Pallas kernels  15.4 us (27%)
  waiting for transfers between devices  14.9 us (26%)
  local copies, waits for them, and re-layouts  8.17 us (14%)
  between operations  0.8 us (1%)
    ppermute x16, starting transfers between devices, swap(): lax.ppermute(value, axis, [(place, place ^ offset) for place in range(siz...  16.6 us
    ppermute x16, waiting for transfers between devices, swap(): lax.ppermute(value, axis, [(place, place ^ offset) for place in range(siz...  14.9 us
    unnamed x34, local copies, waits for them, and re-layouts  8.17 us
    pallas_call x3, Pallas kernels, waves_of(): pl.pallas_call(wave_kernel, out_shape=[f32(vectors, share)] * 2 + [bf16(v...  4.25 us
    pallas_call x1, Pallas kernels, on_device(): pl.pallas_call(functools.partial(sums_kernel, groups=group_count), out_sh...  3.07 us
    pallas_call x1, Pallas kernels, on_device(): pl.pallas_call(tile_kernel, out_shape=[bf16(vectors, atoms)] * 4 + [f32(v...  3.05 us
    pallas_call x1, Pallas kernels, on_device(): pl.pallas_call(functools.partial(field_kernel, groups=group_count - 1), o...  2.88 us
    pallas_call x1, Pallas kernels, on_device(): pl.pallas_call(own_field_kernel, out_shape=[f32(both, share), f32(24, sha...  1.3 us
  transfers between devices with their start and end apart: 16, of which 9 were waited for; matrix products, arithmetic and copies ran while one was open for 0% of the time, Pallas kernels for 17%

profile of v1, /device:TPU:0, one launch (start us, length us, event | category | flops | bytes accessed | tf_op | source)
XLA Modules:
  0.0 56.0 jit_solution(13364128761185149201)
XLA Ops:
  0.6 3.0 %collective-permute-start.3 = (s32[3,256]{1,0:T(4,128)}, s32[3,256]{1,0:T(4,128)S(1)}, u32[]{:S(2)}, u32[]{:S(2)}) collective-permute-start(s32[3,256]{1,0:T(4,128)} %k_ref.1), channel_id=1, source_target_pairs={{0,1},{1,0},{2,3},{3,2},{4,5},{5,4},{6,7},{7,6},{8,9},{9,8},{10,11... | collective-permute-start | bytes 9224 | tf_op jit(solution)/shard_map/ppermute | solution.py:242
  3.6 1.5 %collective-permute-start.5 = (s32[3,256]{1,0:T(4,128)}, s32[3,256]{1,0:T(4,128)S(1)}, u32[]{:S(2)}, u32[]{:S(2)}) collective-permute-start(s32[3,256]{1,0:T(4,128)} %k_ref.1), channel_id=1, source_target_pairs={{0,3},{1,2},{2,1},{3,0},{4,7},{5,6},{6,5},{7,4},{8,11},{9,10},{10,... | collective-permute-start | bytes 9224 | tf_op jit(solution)/shard_map/ppermute | solution.py:242
  5.2 1.9 %collective-permute-start = (f32[64,512]{1,0:T(8,128)}, f32[64,512]{1,0:T(8,128)}, u32[]{:S(2)}, u32[]{:S(2)}) collective-permute-start(f32[64,512]{1,0:T(8,128)} %rest_0_.1), channel_id=1, source_target_pairs={{0,1},{1,0},{2,3},{3,2},{4,5},{5,4},{6,7},{7,6},{8,9},{9,8},{10,11... | collective-permute-start | bytes 393224 | tf_op jit(solution)/shard_map/ppermute | solution.py:242
  7.1 1.5 %collective-permute-start.2 = (f32[64,512]{1,0:T(8,128)}, f32[64,512]{1,0:T(8,128)}, u32[]{:S(2)}, u32[]{:S(2)}) collective-permute-start(f32[64,512]{1,0:T(8,128)} %rest_0_.1), channel_id=1, source_target_pairs={{0,3},{1,2},{2,1},{3,0},{4,7},{5,6},{6,5},{7,4},{8,11},{9,10},{10,... | collective-permute-start | bytes 393224 | tf_op jit(solution)/shard_map/ppermute | solution.py:242
  10.1 3.0 %waves_of_own_vectors.1 = (bf16[256,2048]{1,0:T(8,128)(2,1)S(1)}, bf16[256,2048]{1,0:T(8,128)(2,1)S(1)}, bf16[256,2048]{1,0:T(8,128)(2,1)S(1)}, bf16[256,2048]{1,0:T(8,128)(2,1)S(1)}, f32[256,128]{1,0:T(8,128)S(1)}) custom-call(f32[3,2048]{1,0:T(4,128)S(1)} %copy-done.5, s32[3,256]{1,0:T(4,128)S(1)} %copy-done.13), custom_call_target="tpu_custom_call" | custom-call | flops 4718592000 | tf_op jit(solution)/shard_map/waves_of_own_vectors/pallas_call | solution.py:265
  13.1 1.0 %copy-done = bf16[256,2048]{1,0:T(8,128)(2,1)} copy-done((bf16[256,2048]{1,0:T(8,128)(2,1)}, bf16[256,2048]{1,0:T(8,128)(2,1)S(1)}, u32[]{:S(2)}) %copy-start) | copy-done | bytes 1048600
  14.9 3.5 %collective-permute-done.4.rest_5_.lattice_ref = s32[3,256]{1,0:T(4,128)S(1)} collective-permute-done((s32[3,256]{1,0:T(4,128)S(1)}, s32[3,256]{1,0:T(4,128)S(1)}, u32[]{:S(2)}, u32[]{:S(2)}) %collective-permute-start.4) | collective-permute-done | bytes 3104 | tf_op jit(solution)/shard_map/ppermute | solution.py:242
  19.1 1.2 %copy-done.1 = bf16[256,2048]{1,0:T(8,128)(2,1)S(1)} copy-done((bf16[256,2048]{1,0:T(8,128)(2,1)S(1)}, bf16[256,2048]{1,0:T(8,128)(2,1)}, u32[]{:S(2)}) %copy-start.1) | copy-done | bytes 1048600
  20.3 1.0 %copy-done.3 = f32[64,2048]{1,0:T(8,128)S(1)} copy-done((f32[64,2048]{1,0:T(8,128)S(1)}, f32[64,2048]{1,0:T(8,128)}, u32[]{:S(2)}) %copy-start.3) | copy-done | bytes 524312
  22.8 3.1 %structure_sums.1 = (f32[2,128,128]{2,1,0:T(8,128)S(1)}, f32[2,128,128]{2,1,0:T(8,128)S(1)}, f32[136,512]{1,0:T(8,128)S(1)}) custom-call(s32[2]{0:T(128)S(1)} %pad_add_fusion.here_ref, s32[8]{0:T(128)S(1)} %copy-done.15, bf16[256,2048]{1,0:T(8,128)(2,1)S(1)} %get-tuple-element.61.cos_high, bf16[256,2048]{1,0:T(8,128)(2,1)S(1)} %get-tuple-element.62.cos_low, ...), custom_call_target="tpu_custom_call" | custom-call | flops 3355443200 | tf_op jit(solution)/shard_map/structure_sums/pallas_call | solution.py:275
  26.0 1.3 %collective-permute-done.6 = f32[2,128,128]{2,1,0:T(8,128)S(1)} collective-permute-done((f32[2,128,128]{2,1,0:T(8,128)S(1)}, f32[2,128,128]{2,1,0:T(8,128)S(1)}, u32[]{:S(2)}, u32[]{:S(2)}) %collective-permute-start.6) | collective-permute-done | bytes 131104 | tf_op jit(solution)/shard_map/ppermute | solution.py:242
  27.4 1.6 %collective-permute-start.7 = (f32[2,128,128]{2,1,0:T(8,128)S(1)}, f32[2,128,128]{2,1,0:T(8,128)S(1)}, u32[]{:S(2)}, u32[]{:S(2)}) collective-permute-start(f32[2,128,128]{2,1,0:T(8,128)S(1)} %add.9.after_ref), channel_id=1, source_target_pairs={{0,8},{4,12},{8,0},{12,4},{16,24},{20,28},{24,16},{28,20},{1,9},{5... | collective-permute-start | bytes 393224 | tf_op jit(solution)/shard_map/ppermute | solution.py:242
  30.5 1.4 %waves_of_own_atoms.3 = (f32[256,512]{1,0:T(8,128)S(1)}, f32[256,512]{1,0:T(8,128)S(1)}, bf16[256,512]{1,0:T(8,128)(2,1)S(1)}, bf16[256,512]{1,0:T(8,128)(2,1)S(...) custom-call(s32[2]{0:T(128)S(1)} %pad_add_fusion.here_ref, ...), custom_call_target="tpu_custom_call" | custom-call | flops 1179648000 | tf_op jit(solution)/shard_map/waves_of_own_atoms/pallas_call | solution.py:302
  31.9 1.1 %collective-permute-done.7 = f32[2,128,128]{2,1,0:T(8,128)S(1)} collective-permute-done((f32[2,128,128]{2,1,0:T(8,128)S(1)}, f32[2,128,128]{2,1,0:T(8,128)S(1)}, u32[]{:S(2)}, u32[]{:S(2)}) %collective-permute-start.7) | collective-permute-done | bytes 131104 | tf_op jit(solution)/shard_map/ppermute | solution.py:242
  33.0 2.6 %collective-permute-start.8 = (f32[2,128,128]{2,1,0:T(8,128)S(1)}, f32[2,128,128]{2,1,0:T(8,128)S(1)}, u32[]{:S(2)}, u32[]{:S(2)}) collective-permute-start(f32[2,128,128]{2,1,0:T(8,128)S(1)} %add.10.after_ref), channel_id=1, source_target_pairs={{0,16},{4,20},{8,24},{12,28},{16,0},{20,4},{24,8},{28,12},{1,17},{... | collective-permute-start | bytes 393224 | tf_op jit(solution)/shard_map/ppermute | solution.py:242
  35.6 1.4 %waves_of_own_atoms.5 = (f32[256,512]{1,0:T(8,128)S(1)}, f32[256,512]{1,0:T(8,128)S(1)}, bf16[256,512]{1,0:T(8,128)(2,1)S(1)}, bf16[256,512]{1,0:T(8,128)(2,1)S(...) custom-call(s32[2]{0:T(128)S(1)} %pad_add_fusion.here_ref, ...), custom_call_target="tpu_custom_call" | custom-call | flops 1179648000 | tf_op jit(solution)/shard_map/waves_of_own_atoms/pallas_call | solution.py:302
  37.1 1.4 %waves_of_own_atoms.4 = (f32[256,512]{1,0:T(8,128)S(1)}, f32[256,512]{1,0:T(8,128)S(1)}, bf16[256,512]{1,0:T(8,128)(2,1)S(1)}, bf16[256,512]{1,0:T(8,128)(2,1)S(...) custom-call(s32[2]{0:T(128)S(1)} %pad_add_fusion.here_ref, ...), custom_call_target="tpu_custom_call" | custom-call | flops 1179648000 | tf_op jit(solution)/shard_map/waves_of_own_atoms/pallas_call | solution.py:302
  38.5 3.0 %collective-permute-done.8 = f32[2,128,128]{2,1,0:T(8,128)S(1)} collective-permute-done((f32[2,128,128]{2,1,0:T(8,128)S(1)}, f32[2,128,128]{2,1,0:T(8,128)S(1)}, u32[]{:S(2)}, u32[]{:S(2)}) %collective-permute-start.8) | collective-permute-done | bytes 131104 | tf_op jit(solution)/shard_map/ppermute | solution.py:242
  41.6 1.5 %collective-permute-start.11 = (f32[2,128,128]{2,1,0:T(8,128)S(1)}, f32[2,128,128]{2,1,0:T(8,128)S(1)}, u32[]{:S(2)}, u32[]{:S(2)}) collective-permute-start(f32[2,128,128]{2,1,0:T(8,128)S(1)} %add_multiply_fusion.near_ref), channel_id=1, source_target_pairs={{0,3},{1,2},{2,1},{3,0},{4,7},{5,6},{6,5},{7,4},{8,11},{9,10},{10,... | collective-permute-start | bytes 393224 | tf_op jit(solution)/shard_map/ppermute | solution.py:242
  43.1 1.5 %collective-permute-start.10 = (f32[2,128,128]{2,1,0:T(8,128)S(1)}, f32[2,128,128]{2,1,0:T(8,128)S(1)}, u32[]{:S(2)}, u32[]{:S(2)}) collective-permute-start(f32[2,128,128]{2,1,0:T(8,128)S(1)} %add_multiply_fusion.near_ref), channel_id=1, source_target_pairs={{0,2},{1,3},{2,0},{3,1},{4,6},{5,7},{6,4},{7,5},{8,10},{9,11},{10,... | collective-permute-start | bytes 393224 | tf_op jit(solution)/shard_map/ppermute | solution.py:242
  45.2 1.3 %fields_of_own_vectors.1 = (f32[128,512]{1,0:T(8,128)S(1)}, f32[24,512]{1,0:T(8,128)S(1)}) custom-call(s32[2]{0:T(128)S(1)} %pad_add_fusion.here_ref, bf16[256,2048]{1,0:T(8,128)(2,1)S(1)} %get-tuple-element.61.cos_high, bf16[256,2048]{1,0:T(8,128)(2,1)S(1)} %get-tuple-element.62.cos_low, bf16[256,2048]{1,0:T(8,128)(2,1)S(1)} %get-tuple-element.63.sin_high, ...), custom_call_target="tpu_custom_call" | custom-call | flops 1006632960 | tf_op jit(solution)/shard_map/fields_of_own_vectors/pallas_call | solution.py:329
  46.5 2.4 %collective-permute-done.11.rest_25_ = f32[2,128,128]{2,1,0:T(8,128)S(1)} collective-permute-done((f32[2,128,128]{2,1,0:T(8,128)S(1)}, f32[2,128,128]{2,1,0:T(8,128)S(1)}, u32[]{:S(2)}, u32[]{:S(2)}) %collective-permute-start.11) | collective-permute-done | bytes 131104 | tf_op jit(solution)/shard_map/ppermute | solution.py:242
  48.9 2.3 %collective-permute-done.10.rest_23_ = f32[2,128,128]{2,1,0:T(8,128)S(1)} collective-permute-done((f32[2,128,128]{2,1,0:T(8,128)S(1)}, f32[2,128,128]{2,1,0:T(8,128)S(1)}, u32[]{:S(2)}, u32[]{:S(2)}) %collective-permute-start.10) | collective-permute-done | bytes 131104 | tf_op jit(solution)/shard_map/ppermute | solution.py:242
  53.1 2.9 %fields_and_forces.1 = (f32[64,512]{1,0:T(8,128)}, f32[3,512]{1,0:T(4,128)}, f32[64,512]{1,0:T(8,128)}) custom-call(f32[136,512]{1,0:T(8,128)S(1)} %get-tuple-element.65.own_ref, f32[64,64]{1,0:T(8,128)S(1)} %copy-done.10, f32[64,64]{1,0:T(8,128)S(1)} %copy-done.8, f32[128,512]{1,0:T(8,128)S(1)} %get-tuple-element.93.field_ref, ...), custom_call_target="tpu_custom_call" | custom-call | flops 2516582400 | tf_op jit(solution)/shard_map/fields_and_forces/pallas_call | solution.py:346
  (54 shorter events, 8.6 us)
Async XLA Ops:
  0.6 17.8 %copy-start.4 = (f32[64,512]{1,0:T(8,128)S(1)}, f32[64,512]{1,0:T(8,128)}, u32[]{:S(2)}) copy-start(f32[64,512]{1,0:T(8,128)} %rest_0_.1) | copy-start | bytes 393220
  0.6 13.5 %collective-permute-start.3 = (s32[3,256]{1,0:T(4,128)}, s32[3,256]{1,0:T(4,128)S(1)}, u32[]{:S(2)}, u32[]{:S(2)}) collective-permute-start(s32[3,256]{1,0:T(4,128)} %k_ref.1), channel_id=1, source_target_pairs={{0,1},{1,0},{2,3},{3,2},{4,5},{5,4},{6,7},{7,6},{8,9},{9,8},{10,11... | collective-permute-start | bytes 9224 | tf_op jit(solution)/shard_map/ppermute | solution.py:242
  3.6 11.3 %collective-permute-start.5 = (s32[3,256]{1,0:T(4,128)}, s32[3,256]{1,0:T(4,128)S(1)}, u32[]{:S(2)}, u32[]{:S(2)}) collective-permute-start(s32[3,256]{1,0:T(4,128)} %k_ref.1), channel_id=1, source_target_pairs={{0,3},{1,2},{2,1},{3,0},{4,7},{5,6},{6,5},{7,4},{8,11},{9,10},{10,... | collective-permute-start | bytes 9224 | tf_op jit(solution)/shard_map/ppermute | solution.py:242
  5.1 13.3 %collective-permute-start.1 = (f32[64,512]{1,0:T(8,128)}, f32[64,512]{1,0:T(8,128)S(1)}, u32[]{:S(2)}, u32[]{:S(2)}) collective-permute-start(f32[64,512]{1,0:T(8,128)} %rest_0_.1), channel_id=1, source_target_pairs={{0,2},{1,3},{2,0},{3,1},{4,6},{5,7},{6,4},{7,5},{8,10},{9,11},{10,... | collective-permute-start | bytes 393224 | tf_op jit(solution)/shard_map/ppermute | solution.py:242
  5.2 13.2 %collective-permute-start = (f32[64,512]{1,0:T(8,128)}, f32[64,512]{1,0:T(8,128)}, u32[]{:S(2)}, u32[]{:S(2)}) collective-permute-start(f32[64,512]{1,0:T(8,128)} %rest_0_.1), channel_id=1, source_target_pairs={{0,1},{1,0},{2,3},{3,2},{4,5},{5,4},{6,7},{7,6},{8,9},{9,8},{10,11... | collective-permute-start | bytes 393224 | tf_op jit(solution)/shard_map/ppermute | solution.py:242
  7.1 11.3 %collective-permute-start.2 = (f32[64,512]{1,0:T(8,128)}, f32[64,512]{1,0:T(8,128)}, u32[]{:S(2)}, u32[]{:S(2)}) collective-permute-start(f32[64,512]{1,0:T(8,128)} %rest_0_.1), channel_id=1, source_target_pairs={{0,3},{1,2},{2,1},{3,0},{4,7},{5,6},{6,5},{7,4},{8,11},{9,10},{10,... | collective-permute-start | bytes 393224 | tf_op jit(solution)/shard_map/ppermute | solution.py:242
  14.8 3.6 %collective-permute-start.4 = (s32[3,256]{1,0:T(4,128)S(1)}, s32[3,256]{1,0:T(4,128)S(1)}, u32[]{:S(2)}, u32[]{:S(2)}) collective-permute-start(s32[3,256]{1,0:T(4,128)S(1)} %copy-done.14), channel_id=1, source_target_pairs={{0,2},{1,3},{2,0},{3,1},{4,6},{5,7},{6,4},{7,5},{8,10},{9,11},{10,... | collective-permute-start | bytes 9224 | tf_op jit(solution)/shard_map/ppermute | solution.py:242
  14.8 3.6 %copy-start.12 = (f32[64,16]{0,1:T(8,128)S(1)}, f32[64,16]{0,1:T(8,128)}, u32[]{:S(2)}) copy-start(f32[64,16]{0,1:T(8,128)} %param.17) | copy-start | bytes 12292
  14.8 3.6 %copy-start.11 = (s32[2048]{0:T(1024)S(1)}, s32[2048]{0:T(1024)}, u32[]{:S(2)}) copy-start(s32[2048]{0:T(1024)} %param.12) | copy-start | bytes 24580
  19.1 1.2 %copy-start.1 = (bf16[256,2048]{1,0:T(8,128)(2,1)S(1)}, bf16[256,2048]{1,0:T(8,128)(2,1)}, u32[]{:S(2)}) copy-start(bf16[256,2048]{1,0:T(8,128)(2,1)} %copy-done) | copy-start | bytes 3145732
  20.3 1.0 %copy-start.3 = (f32[64,2048]{1,0:T(8,128)S(1)}, f32[64,2048]{1,0:T(8,128)}, u32[]{:S(2)}) copy-start(f32[64,2048]{1,0:T(8,128)} %feats_ref.1) | copy-start | bytes 1572868
  25.9 1.4 %collective-permute-start.6 = (f32[2,128,128]{2,1,0:T(8,128)S(1)}, f32[2,128,128]{2,1,0:T(8,128)S(1)}, u32[]{:S(2)}, u32[]{:S(2)}) collective-permute-start(f32[2,128,128]{2,1,0:T(8,128)S(1)} %get-tuple-element.68), channel_id=1, source_target_pairs={{0,4},{4,0},{8,12},{12,8},{16,20},{20,16},{24,28},{28,24},{1,5},{5... | collective-permute-start | bytes 393224 | tf_op jit(solution)/shard_map/ppermute | solution.py:242
  27.4 5.6 %collective-permute-start.7 = (f32[2,128,128]{2,1,0:T(8,128)S(1)}, f32[2,128,128]{2,1,0:T(8,128)S(1)}, u32[]{:S(2)}, u32[]{:S(2)}) collective-permute-start(f32[2,128,128]{2,1,0:T(8,128)S(1)} %add.9.after_ref), channel_id=1, source_target_pairs={{0,8},{4,12},{8,0},{12,4},{16,24},{20,28},{24,16},{28,20},{1,9},{5... | collective-permute-start | bytes 393224 | tf_op jit(solution)/shard_map/ppermute | solution.py:242
  33.0 8.5 %collective-permute-start.8 = (f32[2,128,128]{2,1,0:T(8,128)S(1)}, f32[2,128,128]{2,1,0:T(8,128)S(1)}, u32[]{:S(2)}, u32[]{:S(2)}) collective-permute-start(f32[2,128,128]{2,1,0:T(8,128)S(1)} %add.10.after_ref), channel_id=1, source_target_pairs={{0,16},{4,20},{8,24},{12,28},{16,0},{20,4},{24,8},{28,12},{1,17},{... | collective-permute-start | bytes 393224 | tf_op jit(solution)/shard_map/ppermute | solution.py:242
  37.1 8.1 %copy-start.2 = (bf16[256,2048]{1,0:T(8,128)(2,1)S(1)}, bf16[256,2048]{1,0:T(8,128)(2,1)}, u32[]{:S(2)}) copy-start(bf16[256,2048]{1,0:T(8,128)(2,1)} %copy-done) | copy-start | bytes 3145732
  41.5 3.6 %collective-permute-start.12 = (f32[2,128,128]{2,1,0:T(8,128)S(1)}, f32[2,128,128]{2,1,0:T(8,128)S(1)}, u32[]{:S(2)}, u32[]{:S(2)}) collective-permute-start(f32[2,128,128]{2,1,0:T(8,128)S(1)} %add_multiply_fusion.near_ref), channel_id=1, source_target_pairs={{0,4},{4,0},{8,12},{12,8},{16,20},{20,16},{24,28},{28,24},{1,5},{5... | collective-permute-start | bytes 393224 | tf_op jit(solution)/shard_map/ppermute | solution.py:242
  41.6 7.3 %collective-permute-start.11 = (f32[2,128,128]{2,1,0:T(8,128)S(1)}, f32[2,128,128]{2,1,0:T(8,128)S(1)}, u32[]{:S(2)}, u32[]{:S(2)}) collective-permute-start(f32[2,128,128]{2,1,0:T(8,128)S(1)} %add_multiply_fusion.near_ref), channel_id=1, source_target_pairs={{0,3},{1,2},{2,1},{3,0},{4,7},{5,6},{6,5},{7,4},{8,11},{9,10},{10,... | collective-permute-start | bytes 393224 | tf_op jit(solution)/shard_map/ppermute | solution.py:242
  43.1 8.1 %collective-permute-start.10 = (f32[2,128,128]{2,1,0:T(8,128)S(1)}, f32[2,128,128]{2,1,0:T(8,128)S(1)}, u32[]{:S(2)}, u32[]{:S(2)}) collective-permute-start(f32[2,128,128]{2,1,0:T(8,128)S(1)} %add_multiply_fusion.near_ref), channel_id=1, source_target_pairs={{0,2},{1,3},{2,0},{3,1},{4,6},{5,7},{6,4},{7,5},{8,10},{9,11},{10,... | collective-permute-start | bytes 393224 | tf_op jit(solution)/shard_map/ppermute | solution.py:242
  44.6 6.6 %collective-permute-start.9 = (f32[2,128,128]{2,1,0:T(8,128)S(1)}, f32[2,128,128]{2,1,0:T(8,128)S(1)}, u32[]{:S(2)}, u32[]{:S(2)}) collective-permute-start(f32[2,128,128]{2,1,0:T(8,128)S(1)} %add_multiply_fusion.near_ref), channel_id=1, source_target_pairs={{0,1},{1,0},{2,3},{3,2},{4,5},{5,4},{6,7},{7,6},{8,9},{9,8},{10,11... | collective-permute-start | bytes 393224 | tf_op jit(solution)/shard_map/ppermute | solution.py:242
  45.2 7.9 %copy-start.8 = (f32[64,64]{1,0:T(8,128)S(1)}, f32[64,64]{1,0:T(8,128)}, u32[]{:S(2)}) copy-start(f32[64,64]{1,0:T(8,128)} %w_charge_ref.3) | copy-start | bytes 49156
  45.2 7.9 %copy-start.10 = (f32[64,64]{1,0:T(8,128)S(1)}, f32[64,64]{1,0:T(8,128)}, u32[]{:S(2)}) copy-start(f32[64,64]{1,0:T(8,128)} %w_out_ref.3) | copy-start | bytes 49156
  51.2 1.3 %collective-permute-start.13 = (f32[2,128,128]{2,1,0:T(8,128)S(1)}, f32[2,128,128]{2,1,0:T(8,128)S(1)}, u32[]{:S(2)}, u32[]{:S(2)}) collective-permute-start(f32[2,128,128]{2,1,0:T(8,128)S(1)} %collective-permute-done.9.rest_21_), channel_id=1, source_target_pairs={{0,4},{4,0},{8,12},{12,8},{16,20},{20,16},{24,28},{28,24},{1,5},{5... | collective-permute-start | bytes 393224 | tf_op jit(solution)/shard_map/ppermute | solution.py:242
  51.3 1.5 %collective-permute-start.14 = (f32[2,128,128]{2,1,0:T(8,128)S(1)}, f32[2,128,128]{2,1,0:T(8,128)S(1)}, u32[]{:S(2)}, u32[]{:S(2)}) collective-permute-start(f32[2,128,128]{2,1,0:T(8,128)S(1)} %collective-permute-done.10.rest_23_), channel_id=1, source_target_pairs={{0,4},{4,0},{8,12},{12,8},{16,20},{20,16},{24,28},{28,24},{1,5},{5... | collective-permute-start | bytes 393224 | tf_op jit(solution)/shard_map/ppermute | solution.py:242
  51.7 1.3 %collective-permute-start.15 = (f32[2,128,128]{2,1,0:T(8,128)S(1)}, f32[2,128,128]{2,1,0:T(8,128)S(1)}, u32[]{:S(2)}, u32[]{:S(2)}) collective-permute-start(f32[2,128,128]{2,1,0:T(8,128)S(1)} %collective-permute-done.11.rest_25_), channel_id=1, source_target_pairs={{0,4},{4,0},{8,12},{12,8},{16,20},{20,16},{24,28},{28,24},{1,5},{5... | collective-permute-start | bytes 393224 | tf_op jit(solution)/shard_map/ppermute | solution.py:242
  (9 other events, 6.7 us)

commit v2 on v1

v2 whole, which is shorter than its diff:
```python
import functools
import math

import jax
import jax.numpy as jnp
from jax import lax
from jax.experimental import pallas as pl
from jax.experimental.pallas import tpu as pltpu
from jax.sharding import PartitionSpec as P

F32, BF16 = jnp.float32, jnp.bfloat16
HALF_SIN = (4.442867755889893, -7.307443618774414, 3.594788074493408, -0.7843740582466125)
HALF_COS = (1.4142135381698608, -6.978850841522217, 5.7394609451293945, -1.8835630416870117, 0.31069818139076233)
VMEM = pl.BlockSpec(memory_space=pltpu.VMEM)
SMEM = pl.BlockSpec(memory_space=pltpu.SMEM)
ANY = pl.BlockSpec(memory_space=pl.ANY)
PARAMS = pltpu.CompilerParams(vmem_limit_bytes=32 * 2**20)
NN, NT, TN = ((1,), (0,)), ((1,), (1,)), ((0,), (0,))


def halves(value):
    high = value.astype(BF16)
    return high, (value - high.astype(F32)).astype(BF16)


def dot16(left, right, dims):
    return lax.dot_general(left, right, (dims, ((), ())), preferred_element_type=F32)


def dot3(left, right, dims):
    left_high, left_low = halves(left)
    right_high, right_low = halves(right)
    return (
        dot16(left_high, right_high, dims)
        + dot16(left_low, right_high, dims)
        + dot16(left_high, right_low, dims)
    )


def horner(terms, square):
    total = terms[-1] * square + terms[-2]
    for term in terms[-3::-1]:
        total = total * square + term
    return total


def trig(columns, rows):
    turns = columns[0] * rows[0] + columns[1] * rows[1] + columns[2] * rows[2]
    turns = turns - jnp.round(turns)
    square = turns * turns
    half_sin = horner(HALF_SIN, square) * turns
    return 1.0 - half_sin * half_sin, half_sin * horner(HALF_COS, square)


def trig_blocks(k_ref, pos_ref, first, high_low, full=None):
    vectors, atoms = high_low[0].shape
    step = 32
    width = min(256, atoms)
    per_body = max(1, 2048 // atoms)
    per_body = min(per_body, vectors // step)

    def body(block, _):
        for inner in range(per_body):
            here = pl.ds(pl.multiple_of((block * per_body + inner) * step, step), step)
            columns = [k_ref[here, x : x + 1] for x in range(3)]
            for chunk in range(atoms // width):
                lanes = pl.ds(chunk * width, width)
                start = chunk * width if first is None else pl.multiple_of(first + chunk * width, 128)
                rows = [pos_ref[x : x + 1, pl.ds(start, width)] for x in range(3)]
                cos, sin = trig(columns, rows)
                high_low[0][here, lanes], high_low[1][here, lanes] = halves(cos)
                high_low[2][here, lanes], high_low[3][here, lanes] = halves(sin)
                if full is not None:
                    full[0][here, lanes], full[1][here, lanes] = cos, sin
        return 0

    lax.fori_loop(0, vectors // (step * per_body), body, 0)


def lattice_rows(packed, channels, vectors):
    share = packed.shape[1]
    width = min(share, vectors)
    chunks = [packed[channels + 3 * n : channels + 3 * n + 3, 0:width] for n in range(-(-vectors // share))]
    return jnp.concatenate(chunks, axis=1)


def tile_kernel(pos_ref, k_ref, cos_high, cos_low, sin_high, sin_low, k_column):
    k_column[:, 0:3] = k_ref[...].T
    trig_blocks(k_column, pos_ref, None, (cos_high, cos_low, sin_high, sin_low))


def sums_kernel(
    here_ref, pad_ref, cos_high, cos_low, sin_high, sin_low, feats_ref, species_ref, w_charge_ref, embed_ref, w_out_ref,
    *rest, groups,
):
    cotangents = rest[:groups]
    keep_ref, send_ref, own_ref, mask_ref, both, total = rest[-6:]
    channels, atoms = feats_ref.shape
    share = cotangents[0].shape[1]
    place, group = here_ref[0], here_ref[1]
    embed_high, embed_low = halves(embed_ref[...])
    for block in range(atoms // 256):
        lanes = slice(block * 256, (block + 1) * 256)
        mask = (lax.broadcasted_iota(jnp.int32, (1, 256), 1) < pad_ref[block]).astype(F32)
        mask_ref[:, lanes] = mask
        species_at = lax.broadcasted_iota(jnp.int32, (embed_ref.shape[0], 256), 0)
        one_hot = (species_at == species_ref[:, lanes]).astype(BF16)
        both[0:channels, lanes] = mask * (
            dot3(w_charge_ref[...], feats_ref[:, lanes], TN)
            + dot16(embed_high, one_hot, TN)
            + dot16(embed_low, one_hot, TN)
        )
    for offset, cotangent in enumerate(cotangents):
        lanes = pl.ds(pl.multiple_of((group ^ offset) * share, share), share)
        adjoint = mask_ref[:, lanes] * dot3(w_out_ref[...], cotangent[0:channels, :], NN)
        both[channels:, lanes] = adjoint
        if offset == 0:
            own_ref[0:channels, :] = adjoint
            own_ref[channels : 2 * channels, :] = both[0:channels, lanes]
            own_ref[2 * channels :, :] = jnp.broadcast_to(mask_ref[:, lanes], (8, share))
    high, low = halves(both[...])
    pair = jnp.concatenate([high, low], axis=0)
    for part, (tile_high, tile_low) in enumerate(((cos_high, cos_low), (sin_high, sin_low))):
        wide = dot16(tile_high[...], pair, NT)
        total[part] = (
            wide[:, : 2 * channels] + wide[:, 2 * channels :] + dot16(tile_low[...], high, NT)
        )
    rows = keep_ref.shape[2]
    for offset in range(keep_ref.shape[0]):
        for flip, out in enumerate((keep_ref, send_ref)):
            start = pl.multiple_of((place ^ (2 * offset + flip)) * rows, rows)
            for part in range(2):
                out[offset, part] = total[part, pl.ds(start, rows), :]


def wave_kernel(here_ref, pos_ref, packed_ref, width_ref, after_ref, *rest, atom_total, rows):
    *gain_ref, cos, sin, cos_high, cos_low, sin_high, sin_low, k_ref, k_column = rest
    vectors = cos.shape[0]
    k_column[:, 0:3] = lattice_rows(packed_ref, width_ref.shape[1], vectors).T
    count = vectors // rows
    for piece in range(count):
        start = pl.multiple_of((here_ref[0] ^ piece) * rows, rows)
        to = ((piece % 2) * (count // 2) + piece // 2) * rows
        k_ref[to : to + rows, :] = k_column[pl.ds(start, rows), :]
    if gain_ref:
        waves = [2.0 * math.pi * k_ref[0:rows, x : x + 1] for x in range(3)]
        square = waves[0] * waves[0] + waves[1] * waves[1] + waves[2] * waves[2]
        gain = jnp.exp(-square * width_ref[...]) * 40.0 / (square + 40.0) / math.sqrt(atom_total)
        gain_ref[0][...] = jnp.concatenate([gain, gain], axis=1)
    first = here_ref[1] * cos.shape[1]
    trig_blocks(k_ref, pos_ref, first, (cos_high, cos_low, sin_high, sin_low), (cos, sin))


def coefficient_stack(near_ref, far_ref, part):
    flat = (near_ref.shape[0] * near_ref.shape[2], near_ref.shape[3])
    high, low = halves(jnp.concatenate([near_ref[:, part].reshape(flat), far_ref[:, part].reshape(flat)], axis=0))
    return jnp.concatenate([high, low, high], axis=1)


def own_stack(own_ref, channels):
    high, low = halves(own_ref[0 : 2 * channels, :])
    return jnp.concatenate([high, high, low], axis=0)


def add_field(stack, tile_high, tile_low):
    width = stack.shape[1] // 3
    wide = dot16(stack[:, : 2 * width], tile_high, TN)
    return wide[:width] + wide[width:] + dot16(stack[:, :width], tile_low, TN)


def add_force(sums, wave, along, first):
    step = 16
    cos, sin, _, _, _, _, k_ref = wave
    for start in range(0, cos.shape[0], step):
        here = slice(start, start + step)
        there = slice(first + start, first + start + step)
        slope = cos[here, :] * along[1, there, :] - sin[here, :] * along[0, there, :]
        for x in range(3):
            term = k_ref[here, x : x + 1] * slope
            sums[x] = sums[x] + (term[0:8] + term[8:16])
    return sums


def fields(own_ref, waves, coefs, channels, along, field, sums):
    other = own_stack(own_ref, channels)
    parts = [
        [coefficient_stack(near, far, part) for near, far in zip(coefs[::2], coefs[1::2])] for part in range(2)
    ]
    for part in range(2):
        along[part] = dot16(jnp.concatenate(parts[part], axis=0), other, NN)
    waves = [waves[at : at + 7] for at in range(0, len(waves), 7)]
    for group, wave in enumerate(waves):
        _, _, cos_high, cos_low, sin_high, sin_low, _ = wave
        for part, high, low in ((parts[0], cos_high, cos_low), (parts[1], sin_high, sin_low)):
            added = add_field(part[group], high[...], low[...])
            field = added if field is None else field + added
    for group, wave in enumerate(waves):
        sums = add_force(sums, wave, along, group * wave[0].shape[0])
    return field, sums


def own_field_kernel(own_ref, *rest):
    *waves, near_ref, far_ref, field_ref, sums_ref, along = rest
    share = own_ref.shape[1]
    field, sums = fields(
        own_ref, waves, [near_ref, far_ref], near_ref.shape[3] // 2, along, None, [jnp.zeros((8, share), F32)] * 3
    )
    field_ref[...] = field
    for x in range(3):
        sums_ref[8 * x : 8 * x + 8, :] = sums[x]


def field_kernel(own_ref, w_out_ref, w_charge_ref, field_ref, sums_ref, *rest, groups):
    *waves, message_ref, force_ref, grad_ref, along = rest
    waves, coefs = waves[: 7 * groups], waves[7 * groups :]
    channels = w_out_ref.shape[0]
    sums = [sums_ref[8 * x : 8 * x + 8, :] for x in range(3)]
    field, sums = fields(own_ref, waves, coefs, channels, along, field_ref[...], sums)
    field = own_ref[2 * channels : 2 * channels + 1, :] * field
    message_ref[...] = dot3(w_out_ref[...], field[:channels], TN)
    grad_ref[...] = dot3(w_charge_ref[...], field[channels:], NN)
    for x in range(3):
        force_ref[x : x + 1, :] = 2.0 * math.pi * jnp.sum(sums[x], axis=0, keepdims=True)


def swap(value, axis, offset):
    size = lax.axis_size(axis)
    return lax.ppermute(value, axis, [(place, place ^ offset) for place in range(size)])


def cost(work):
    return pl.CostEstimate(flops=work, bytes_accessed=0, transcendentals=0)


def on_device(
    positions, feats, species, pad_count, k_lattice, filter_width, w_charge, species_embed, w_out, grad_out,
):
    atom_count, group_count = lax.axis_size("atoms"), lax.axis_size("kvec")
    channels, atoms = feats.shape
    share = grad_out.shape[1]
    vectors = k_lattice.shape[1]
    rows = vectors // atom_count
    depth = atom_count // 2
    both = 2 * channels
    here = jnp.stack([lax.axis_index("atoms"), lax.axis_index("kvec")]).astype(jnp.int32)
    f32 = lambda *shape: jax.ShapeDtypeStruct(shape, F32)
    bf16 = lambda *shape: jax.ShapeDtypeStruct(shape, BF16)

    chunks = -(-vectors // share)
    below = -(-3 * chunks // 8) * 8
    packed = jnp.pad(grad_out, ((0, below), (0, 0)))
    lattice = k_lattice.astype(F32)
    for n in range(chunks):
        chunk = lattice[:, n * share : (n + 1) * share]
        first = channels + 3 * n
        packed += jnp.pad(chunk, ((first, channels + below - first - 3), (0, share - chunk.shape[1])))
    packed = [packed] + [swap(packed, "kvec", m) for m in range(1, group_count)]

    *tiles, _ = pl.pallas_call(
        tile_kernel,
        out_shape=[bf16(vectors, atoms)] * 4 + [f32(vectors, 128)],
        in_specs=[VMEM] * 2,
        out_specs=[VMEM] * 5,
        compiler_params=PARAMS,
        cost_estimate=cost(9000 * vectors * atoms),
        name="waves_of_own_vectors",
    )(positions, lattice)

    piece = f32(depth, 2, rows, both)
    keep, send, own = pl.pallas_call(
        functools.partial(sums_kernel, groups=group_count),
        out_shape=[piece, piece, f32(both + 8, share)],
        in_specs=[SMEM, SMEM] + [VMEM] * (9 + group_count),
        out_specs=[VMEM] * 3,
        scratch_shapes=[
            pltpu.VMEM((1, atoms), F32), pltpu.VMEM((both, atoms), F32), pltpu.VMEM((2, vectors, both), F32),
        ],
        compiler_params=PARAMS,
        cost_estimate=cost(100 * vectors * atoms * channels),
        name="structure_sums",
    )(here, pad_count, *tiles, feats, species.reshape(1, atoms), w_charge, species_embed.T, w_out, *packed)

    wave_shapes = [f32(vectors, share)] * 2 + [bf16(vectors, share)] * 4 + [f32(vectors, 128)]

    def waves_of(group, after):
        shapes = ([f32(rows, both)] if group == 0 else []) + wave_shapes
        return pl.pallas_call(
            functools.partial(wave_kernel, atom_total=atoms * atom_count, rows=rows),
            out_shape=shapes,
            in_specs=[SMEM, VMEM, VMEM, VMEM, ANY],
            out_specs=[VMEM] * len(shapes),
            scratch_shapes=[pltpu.VMEM((vectors, 128), F32)],
            compiler_params=PARAMS,
            cost_estimate=cost(9000 * vectors * share),
            name="waves_of_own_atoms",
        )(here, positions, packed[group], filter_width.reshape(1, channels), after)

    arrived = swap(send, "atoms", 1)
    gain, *own_waves = waves_of(0, send)
    arrived, gain = lax.optimization_barrier((arrived, gain))
    half = keep + arrived

    arrived = [swap(half[offset], "atoms", 2 * offset) for offset in range(1, depth)]
    waves = waves_of(1, half)
    arrived, waves = lax.optimization_barrier((arrived, waves))
    total = half[0]
    for part in arrived:
        total = total + part
    total = gain[None] * total

    arrived = [swap(total, "atoms", 2 * offset) for offset in range(1, depth)]
    more = waves_of(2, total)
    arrived, more = lax.optimization_barrier((arrived, more))
    waves = waves + more
    near = jnp.stack([total] + arrived)

    plane = [swap(near, "kvec", m) for m in range(1, group_count)]
    field, sums = pl.pallas_call(
        own_field_kernel,
        out_shape=[f32(both, share), f32(24, share)],
        in_specs=[VMEM] * 10,
        out_specs=[VMEM] * 2,
        scratch_shapes=[pltpu.VMEM((2, vectors, share), F32)],
        compiler_params=PARAMS,
        cost_estimate=cost(120 * vectors * share * channels),
        name="fields_of_own_vectors",
    )(own, *own_waves, near, swap(near, "atoms", 1))
    for group in range(3, group_count):
        waves = waves + waves_of(group, near)
    coefs = []
    for part in plane:
        part, field, waves = lax.optimization_barrier((part, field, waves))
        coefs += [part, swap(part, "atoms", 1)]

    return tuple(
        pl.pallas_call(
            functools.partial(field_kernel, groups=group_count - 1),
            out_shape=[f32(channels, share), f32(3, share), f32(channels, share)],
            in_specs=[VMEM] * (5 + 9 * (group_count - 1)),
            out_specs=[VMEM] * 3,
            scratch_shapes=[pltpu.VMEM((2, (group_count - 1) * vectors, share), F32)],
            compiler_params=PARAMS,
            cost_estimate=cost(300 * vectors * share * channels),
            name="fields_and_forces",
        )(own, w_out, w_charge, field, sums, *waves, *coefs)
    )


def solution(mesh):
    shared = P(None, ("atoms", "kvec"))
    placed = (
        P(None, "atoms"), P(None, "atoms"), P("atoms"), P("atoms"), P(None, "kvec"),
        P(), P(), P(), P(), shared,
    )
    return jax.shard_map(
        on_device, mesh=mesh, in_specs=placed, out_specs=(shared, shared, shared), check_vma=False
    )
```

time: 56.5 us -> 51.9 us (0.919)
  waiting for transfers between devices: 14.9 us -> 9.9 us
  local copies, waits for them, and re-layouts: 8.17 us -> 5.61 us
  other arithmetic: 0.14 us -> 1.73 us
  starting transfers between devices: 16.6 us -> 17.7 us
    ppermute x16 -> x17, waiting for transfers between devices: 14.9 us -> 9.9 us  [swap(): lax.ppermute(value, axis, [(place, place ^ offset) for place in range(siz...]
    unnamed x34 -> x24, local copies, waits for them, and re-layouts: 8.17 us -> 5.6 us
    ppermute x16 -> x17, starting transfers between devices: 16.6 us -> 17.7 us  [swap(): lax.ppermute(value, axis, [(place, place ^ offset) for place in range(siz...]
    add x2, other arithmetic: 0.04 us -> 0.94 us  [the longest x1 0.92 us: on_device(): packed += jnp.pad(chunk, ((first, channels + below - first - 3), (0, shar...]
    pallas_call x4, Pallas kernels: 5.05 us -> 5.85 us  [waves_of(): pl.pallas_call(functools.partial(wave_kernel, atom_total=atoms * atom_cou...]
    pallas_call x1, Pallas kernels: 3.05 us -> 3.75 us  [on_device(): pl.pallas_call(tile_kernel, out_shape=[bf16(vectors, atoms)] * 4 + [f32(v...]
    convert_element_type x0 -> x1, other arithmetic: none -> 0.69 us  [on_device(): lattice = k_lattice.astype(F32)]
  transfers between devices with their start and end apart: 16 -> 17, of which waited for: 9 -> 10; matrix products, arithmetic and copies ran while one was open for 0% -> 0% of each run, Pallas kernels for 17% -> 20%
where the time goes in v2:
time: 51.9 us; the launch traced here: 51.6 us
  starting transfers between devices  17.7 us (34%)
  Pallas kernels  15.8 us (30%)
  waiting for transfers between devices  9.9 us (19%)
  local copies, waits for them, and re-layouts  5.61 us (11%)
  other arithmetic  1.73 us (3%)
  between operations  0.82 us (2%)
    ppermute x17, starting transfers between devices, swap(): lax.ppermute(value, axis, [(place, place ^ offset) for place in range(siz...  17.7 us
    ppermute x17, waiting for transfers between devices, swap(): lax.ppermute(value, axis, [(place, place ^ offset) for place in range(siz...  9.9 us
    pallas_call x4, Pallas kernels, waves_of(): pl.pallas_call(functools.partial(wave_kernel, atom_total=atoms * atom_cou...  5.85 us
    unnamed x24, local copies, waits for them, and re-layouts  5.6 us
    pallas_call x1, Pallas kernels, on_device(): pl.pallas_call(tile_kernel, out_shape=[bf16(vectors, atoms)] * 4 + [f32(v...  3.75 us
    pallas_call x1, Pallas kernels, on_device(): pl.pallas_call(functools.partial(field_kernel, groups=group_count - 1), o...  2.86 us
    pallas_call x1, Pallas kernels, on_device(): pl.pallas_call(functools.partial(sums_kernel, groups=group_count), out_sh...  2.62 us
  transfers between devices with their start and end apart: 17, of which 10 were waited for; matrix products, arithmetic and copies ran while one was open for 0% of the time, Pallas kernels for 20%

profile of v2, /device:TPU:0, one launch (start us, length us, event | category | flops | bytes accessed | tf_op | source)
XLA Modules:
  0.0 51.6 jit_solution(15527744471108902388)
XLA Ops:
  1.3 0.9 %pad_add_fusion.rest_0_.packed_ref = f32[72,512]{1,0:T(8,128)S(1)} fusion(f32[3,256]{1,0:T(4,128)S(1)} %convert_element_type.7.k_ref, f32[64,512]{1,0:T(8,128)} %param.19), kind=kLoop, calls=%fused_computation | loop fusion | flops 36864 | bytes 281600 | tf_op jit(solution)/shard_map/add | solution.py:256
  2.3 4.0 %collective-permute-start.2 = (f32[72,512]{1,0:T(8,128)S(1)}, f32[72,512]{1,0:T(8,128)S(1)}, u32[]{:S(2)}, u32[]{:S(2)}) collective-permute-start(f32[72,512]{1,0:T(8,128)S(1)} %pad_add_fusion.rest_0_.packed_ref), channel_id=1, source_target_pairs={{0,3},{1,2},{2,1},{3,0},{4,7},{5,6},{6,5},{7,4},{8,11},{9,10},{10,... | collective-permute-start | bytes 442376 | tf_op jit(solution)/shard_map/ppermute | solution.py:228
  6.9 3.7 %waves_of_own_vectors.1 = (bf16[256,2048]{1,0:T(8,128)(2,1)S(1)}, bf16[256,2048]{1,0:T(8,128)(2,1)S(1)}, bf16[256,2048]{1,0:T(8,128)(2,1)S(1)}, bf16[256,2048]{1,0:T(8,128)(2,1)S(1)}, f32[256,128]{1,0:T(8,128)}) custom-call(f32[3,2048]{1,0:T(4,128)S(1)} %copy-done.1, f32[3,256]{1,0:T(4,128)S(1)} %convert_element_type.7.k_ref), custom_call_target="tpu_custom_call" | custom-call | flops 4718592000 | tf_op jit(solution)/shard_map/waves_of_own_vectors/pallas_call | solution.py:259
  10.6 1.0 %copy-done.8 = bf16[256,2048]{1,0:T(8,128)(2,1)} copy-done((bf16[256,2048]{1,0:T(8,128)(2,1)}, bf16[256,2048]{1,0:T(8,128)(2,1)S(1)}, u32[]{:S(2)}) %copy-start.8) | copy-done | bytes 1048600
  11.6 1.0 %copy-done.10 = bf16[256,2048]{1,0:T(8,128)(2,1)} copy-done((bf16[256,2048]{1,0:T(8,128)(2,1)}, bf16[256,2048]{1,0:T(8,128)(2,1)S(1)}, u32[]{:S(2)}) %copy-start.10) | copy-done | bytes 1048600
  14.2 1.2 %copy-done.9 = bf16[256,2048]{1,0:T(8,128)(2,1)S(1)} copy-done((bf16[256,2048]{1,0:T(8,128)(2,1)S(1)}, bf16[256,2048]{1,0:T(8,128)(2,1)}, u32[]{:S(2)}) %copy-start.9) | copy-done | bytes 1048600
  15.4 1.2 %copy-done.11 = bf16[256,2048]{1,0:T(8,128)(2,1)S(1)} copy-done((bf16[256,2048]{1,0:T(8,128)(2,1)S(1)}, bf16[256,2048]{1,0:T(8,128)(2,1)}, u32[]{:S(2)}) %copy-start.11) | copy-done | bytes 1048600
  16.6 2.6 %structure_sums.1 = (f32[4,2,32,128]{3,2,1,0:T(8,128)S(1)}, f32[4,2,32,128]{3,2,1,0:T(8,128)S(1)}, f32[136,512]{1,0:T(8,128)S(1)}) custom-call(s32[2]{0:T(128)S(1)} %pad_add_fusion.1.here_ref, s32[8]{0:T(128)S(1)} %copy-done.6, bf16[256,2048]{1,0:T(8,128)(2,1)S(1)} %get-tuple-element.132.cos_high, bf16[256,2048]{1,0:T(8,128)(2,1)S(1)} %get-tuple-element.133.cos_low, ...), custom_call_target="tpu_custom_call" | custom-call | flops 3355443200 | tf_op jit(solution)/shard_map/structure_sums/pallas_call | solution.py:270
  19.9 1.6 %waves_of_own_atoms.4 = (f32[32,128]{1,0:T(8,128)S(1)}, f32[256,512]{1,0:T(8,128)S(1)}, f32[256,512]{1,0:T(8,128)S(1)}, bf16[256,512]{1,0:T(8,128)(2,1)S(1)}, bf...) custom-call(s32[2]{0:T(128)S(1)} %pad_add_fusion.1.here_ref, ...), custom_call_target="tpu_custom_call" | custom-call | flops 1179648000 | tf_op jit(solution)/shard_map/waves_of_own_atoms/pallas_call | solution.py:287
  21.6 3.7 %collective-permute-start.6 = (f32[2,32,128]{2,1,0:T(8,128)S(1)}, f32[2,32,128]{2,1,0:T(8,128)S(1)}, u32[]{:S(2)}, u32[]{:S(2)}) collective-permute-start(f32[2,32,128]{2,1,0:T(8,128)S(1)} %get-tuple-element.261), channel_id=1, source_target_pairs={{0,24},{4,28},{8,16},{12,20},{16,8},{20,12},{24,0},{28,4},{1,25},{... | collective-permute-start | bytes 98312 | tf_op jit(solution)/shard_map/ppermute | solution.py:228
  25.3 0.8 %collective-permute-start.4 = (f32[2,32,128]{2,1,0:T(8,128)S(1)}, f32[2,32,128]{2,1,0:T(8,128)S(1)}, u32[]{:S(2)}, u32[]{:S(2)}) collective-permute-start(f32[2,32,128]{2,1,0:T(8,128)S(1)} %get-tuple-element.263), channel_id=1, source_target_pairs={{0,8},{4,12},{8,0},{12,4},{16,24},{20,28},{24,16},{28,20},{1,9},{5... | collective-permute-start | bytes 98312 | tf_op jit(solution)/shard_map/ppermute | solution.py:228
  26.1 1.4 %waves_of_own_atoms.5 = (f32[256,512]{1,0:T(8,128)S(1)}, f32[256,512]{1,0:T(8,128)S(1)}, bf16[256,512]{1,0:T(8,128)(2,1)S(1)}, bf16[256,512]{1,0:T(8,128)(2,1)S(...) custom-call(s32[2]{0:T(128)S(1)} %pad_add_fusion.1.here_ref, ...), custom_call_target="tpu_custom_call" | custom-call | flops 1179648000 | tf_op jit(solution)/shard_map/waves_of_own_atoms/pallas_call | solution.py:287
  27.5 2.6 %collective-permute-done.5 = f32[2,32,128]{2,1,0:T(8,128)S(1)} collective-permute-done((f32[2,32,128]{2,1,0:T(8,128)S(1)}, f32[2,32,128]{2,1,0:T(8,128)S(1)}, u32[]{:S(2)}, u32[]{:S(2)}) %collective-permute-start.5) | collective-permute-done | bytes 32800 | tf_op jit(solution)/shard_map/ppermute | solution.py:228
  30.1 1.5 %collective-permute-start.9 = (f32[2,32,128]{2,1,0:T(8,128)S(1)}, f32[2,32,128]{2,1,0:T(8,128)S(1)}, u32[]{:S(2)}, u32[]{:S(2)}) collective-permute-start(f32[2,32,128]{2,1,0:T(8,128)S(1)} %fusion.3.after_ref), channel_id=1, source_target_pairs={{0,24},{4,28},{8,16},{12,20},{16,8},{20,12},{24,0},{28,4},{1,25},{... | collective-permute-start | bytes 98312 | tf_op jit(solution)/shard_map/ppermute | solution.py:228
  32.3 2.3 %collective-permute-start.7 = (f32[2,32,128]{2,1,0:T(8,128)S(1)}, f32[2,32,128]{2,1,0:T(8,128)S(1)}, u32[]{:S(2)}, u32[]{:S(2)}) collective-permute-start(f32[2,32,128]{2,1,0:T(8,128)S(1)} %fusion.3.after_ref), channel_id=1, source_target_pairs={{0,8},{4,12},{8,0},{12,4},{16,24},{20,28},{24,16},{28,20},{1,9},{5... | collective-permute-start | bytes 98312 | tf_op jit(solution)/shard_map/ppermute | solution.py:228
  34.6 1.4 %waves_of_own_atoms.6 = (f32[256,512]{1,0:T(8,128)S(1)}, f32[256,512]{1,0:T(8,128)S(1)}, bf16[256,512]{1,0:T(8,128)(2,1)S(1)}, bf16[256,512]{1,0:T(8,128)(2,1)S(...) custom-call(s32[2]{0:T(128)S(1)} %pad_add_fusion.1.here_ref, ...), custom_call_target="tpu_custom_call" | custom-call | flops 1179648000 | tf_op jit(solution)/shard_map/waves_of_own_atoms/pallas_call | solution.py:287
  36.9 1.6 %collective-permute-start.12 = (f32[4,2,32,128]{3,2,1,0:T(8,128)S(1)}, f32[4,2,32,128]{3,2,1,0:T(8,128)S(1)}, u32[]{:S(2)}, u32[]{:S(2)}) collective-permute-start(f32[4,2,32,128]{3,2,1,0:T(8,128)S(1)} %pad_maximum_fusion.rest_7_.after_ref), channel_id=1, source_target_pairs={{0,1},{1,0},{2,3},{3,2},{4,5},{5,4},{6,7},{7,6},{8,9},{9,8},{10,11... | collective-permute-start | bytes 393224 | tf_op jit(solution)/shard_map/ppermute | solution.py:228
  38.5 1.0 %collective-permute-start.11 = (f32[4,2,32,128]{3,2,1,0:T(8,128)S(1)}, f32[4,2,32,128]{3,2,1,0:T(8,128)S(1)}, u32[]{:S(2)}, u32[]{:S(2)}) collective-permute-start(f32[4,2,32,128]{3,2,1,0:T(8,128)S(1)} %pad_maximum_fusion.rest_7_.after_ref), channel_id=1, source_target_pairs={{0,2},{1,3},{2,0},{3,1},{4,6},{5,7},{6,4},{7,5},{8,10},{9,11},{10,... | collective-permute-start | bytes 393224 | tf_op jit(solution)/shard_map/ppermute | solution.py:228
  39.5 0.9 %collective-permute-start.10 = (f32[4,2,32,128]{3,2,1,0:T(8,128)S(1)}, f32[4,2,32,128]{3,2,1,0:T(8,128)S(1)}, u32[]{:S(2)}, u32[]{:S(2)}) collective-permute-start(f32[4,2,32,128]{3,2,1,0:T(8,128)S(1)} %pad_maximum_fusion.rest_7_.after_ref), channel_id=1, source_target_pairs={{0,3},{1,2},{2,1},{3,0},{4,7},{5,6},{6,5},{7,4},{8,11},{9,10},{10,... | collective-permute-start | bytes 393224 | tf_op jit(solution)/shard_map/ppermute | solution.py:228
  40.5 1.4 %waves_of_own_atoms.7 = (f32[256,512]{1,0:T(8,128)S(1)}, f32[256,512]{1,0:T(8,128)S(1)}, bf16[256,512]{1,0:T(8,128)(2,1)S(1)}, bf16[256,512]{1,0:T(8,128)(2,1)S(...) custom-call(s32[2]{0:T(128)S(1)} %pad_add_fusion.1.here_ref, ...), custom_call_target="tpu_custom_call" | custom-call | flops 1179648000 | tf_op jit(solution)/shard_map/waves_of_own_atoms/pallas_call | solution.py:287
  41.9 0.7 %fields_of_own_vectors.1 = (f32[128,512]{1,0:T(8,128)S(1)}, f32[24,512]{1,0:T(8,128)S(1)}) custom-call(f32[136,512]{1,0:T(8,128)S(1)} %get-tuple-element.136.own_ref, f32[256,512]{1,0:T(8,128)S(1)} %get-tuple-element.162.rest_0_, f32[256,512]{1,0:T(8,128)S(1)} %get-tuple-element.163.rest_1_, bf16[256,512]{1,0:T(8,128)(2,1)S(1)} %get-tuple-element.164.rest_2_, ...), custom_call_target="tpu_custom_call" | custom-call | flops 1006632960 | tf_op jit(solution)/shard_map/fields_of_own_vectors/pallas_call | solution.py:318
  43.2 3.7 %collective-permute-done.11.rest_23_ = f32[4,2,32,128]{3,2,1,0:T(8,128)S(1)} collective-permute-done((f32[4,2,32,128]{3,2,1,0:T(8,128)S(1)}, f32[4,2,32,128]{3,2,1,0:T(8,128)S(1)}, u32[]{:S(2)}, u32[]{:S(2)}) %collective-permute-start.11) | collective-permute-done | bytes 131104 | tf_op jit(solution)/shard_map/ppermute | solution.py:228
  47.4 0.8 %collective-permute-done.16.rest_26_ = f32[4,2,32,128]{3,2,1,0:T(8,128)S(1)} collective-permute-done((f32[4,2,32,128]{3,2,1,0:T(8,128)S(1)}, f32[4,2,32,128]{3,2,1,0:T(8,128)S(1)}, u32[]{:S(2)}, u32[]{:S(2)}) %collective-permute-start.16) | collective-permute-done | bytes 131104 | tf_op jit(solution)/shard_map/ppermute | solution.py:228
  48.7 2.9 %fields_and_forces.1 = (f32[64,512]{1,0:T(8,128)}, f32[3,512]{1,0:T(4,128)}, f32[64,512]{1,0:T(8,128)}) custom-call(f32[136,512]{1,0:T(8,128)S(1)} %get-tuple-element.136.own_ref, f32[64,64]{1,0:T(8,128)S(1)} %copy-done.3, f32[64,64]{1,0:T(8,128)S(1)} %copy-done.2, f32[128,512]{1,0:T(8,128)S(1)} %get-tuple-element.235.field_ref, ...), custom_call_target="tpu_custom_call" | custom-call | flops 2516582400 | tf_op jit(solution)/shard_map/fields_and_forces/pallas_call | solution.py:336
  (49 shorter events, 6.7 us)
Async XLA Ops:
  1.3 5.6 %copy-start.1 = (f32[3,2048]{1,0:T(4,128)S(1)}, f32[3,2048]{1,0:T(4,128)}, u32[]{:S(2)}) copy-start(f32[3,2048]{1,0:T(4,128)} %pos_ref.9) | copy-start | bytes 73732
  2.2 11.3 %copy-start = (f32[64,2048]{1,0:T(8,128)S(1)}, f32[64,2048]{1,0:T(8,128)}, u32[]{:S(2)}) copy-start(f32[64,2048]{1,0:T(8,128)} %feats_ref.1) | copy-start | bytes 1572868
  2.3 11.3 %copy-start.2 = (f32[64,64]{1,0:T(8,128)S(1)}, f32[64,64]{1,0:T(8,128)}, u32[]{:S(2)}) copy-start(f32[64,64]{1,0:T(8,128)} %w_charge_ref.3) | copy-start | bytes 49156
  2.3 11.3 %copy-start.3 = (f32[64,64]{1,0:T(8,128)S(1)}, f32[64,64]{1,0:T(8,128)}, u32[]{:S(2)}) copy-start(f32[64,64]{1,0:T(8,128)} %w_out_ref.3) | copy-start | bytes 49156
  2.3 10.4 %collective-permute-start.2 = (f32[72,512]{1,0:T(8,128)S(1)}, f32[72,512]{1,0:T(8,128)S(1)}, u32[]{:S(2)}, u32[]{:S(2)}) collective-permute-start(f32[72,512]{1,0:T(8,128)S(1)} %pad_add_fusion.rest_0_.packed_ref), channel_id=1, source_target_pairs={{0,3},{1,2},{2,1},{3,0},{4,7},{5,6},{6,5},{7,4},{8,11},{9,10},{10,... | collective-permute-start | bytes 442376 | tf_op jit(solution)/shard_map/ppermute | solution.py:228
  6.2 7.0 %collective-permute-start.1 = (f32[72,512]{1,0:T(8,128)S(1)}, f32[72,512]{1,0:T(8,128)S(1)}, u32[]{:S(2)}, u32[]{:S(2)}) collective-permute-start(f32[72,512]{1,0:T(8,128)S(1)} %pad_add_fusion.rest_0_.packed_ref), channel_id=1, source_target_pairs={{0,2},{1,3},{2,0},{3,1},{4,6},{5,7},{6,4},{7,5},{8,10},{9,11},{10,... | collective-permute-start | bytes 442376 | tf_op jit(solution)/shard_map/ppermute | solution.py:228
  6.7 6.8 %collective-permute-start = (f32[72,512]{1,0:T(8,128)S(1)}, f32[72,512]{1,0:T(8,128)S(1)}, u32[]{:S(2)}, u32[]{:S(2)}) collective-permute-start(f32[72,512]{1,0:T(8,128)S(1)} %pad_add_fusion.rest_0_.packed_ref), channel_id=1, source_target_pairs={{0,1},{1,0},{2,3},{3,2},{4,5},{5,4},{6,7},{7,6},{8,9},{9,8},{10,11... | collective-permute-start | bytes 442376 | tf_op jit(solution)/shard_map/ppermute | solution.py:228
  12.6 1.0 %copy-start.4 = (s32[2048]{0:T(1024)S(1)}, s32[2048]{0:T(1024)}, u32[]{:S(2)}) copy-start(s32[2048]{0:T(1024)} %param.12) | copy-start | bytes 24580
  14.2 1.2 %copy-start.9 = (bf16[256,2048]{1,0:T(8,128)(2,1)S(1)}, bf16[256,2048]{1,0:T(8,128)(2,1)}, u32[]{:S(2)}) copy-start(bf16[256,2048]{1,0:T(8,128)(2,1)} %copy-done.8) | copy-start | bytes 3145732
  15.4 1.2 %copy-start.11 = (bf16[256,2048]{1,0:T(8,128)(2,1)S(1)}, bf16[256,2048]{1,0:T(8,128)(2,1)}, u32[]{:S(2)}) copy-start(bf16[256,2048]{1,0:T(8,128)(2,1)} %copy-done.10) | copy-start | bytes 3145732
  19.3 2.3 %collective-permute-start.3 = (f32[4,2,32,128]{3,2,1,0:T(8,128)S(1)}, f32[4,2,32,128]{3,2,1,0:T(8,128)S(1)}, u32[]{:S(2)}, u32[]{:S(2)}) collective-permute-start(f32[4,2,32,128]{3,2,1,0:T(8,128)S(1)} %get-tuple-element.137.after_ref), channel_id=1, source_target_pairs={{0,4},{4,0},{8,12},{12,8},{16,20},{20,16},{24,28},{28,24},{1,5},{5... | collective-permute-start | bytes 393224 | tf_op jit(solution)/shard_map/ppermute | solution.py:228
  21.6 5.9 %collective-permute-start.6 = (f32[2,32,128]{2,1,0:T(8,128)S(1)}, f32[2,32,128]{2,1,0:T(8,128)S(1)}, u32[]{:S(2)}, u32[]{:S(2)}) collective-permute-start(f32[2,32,128]{2,1,0:T(8,128)S(1)} %get-tuple-element.261), channel_id=1, source_target_pairs={{0,24},{4,28},{8,16},{12,20},{16,8},{20,12},{24,0},{28,4},{1,25},{... | collective-permute-start | bytes 98312 | tf_op jit(solution)/shard_map/ppermute | solution.py:228
  25.3 4.8 %collective-permute-start.5 = (f32[2,32,128]{2,1,0:T(8,128)S(1)}, f32[2,32,128]{2,1,0:T(8,128)S(1)}, u32[]{:S(2)}, u32[]{:S(2)}) collective-permute-start(f32[2,32,128]{2,1,0:T(8,128)S(1)} %get-tuple-element.262), channel_id=1, source_target_pairs={{0,16},{4,20},{8,24},{12,28},{16,0},{20,4},{24,8},{28,12},{1,17},{... | collective-permute-start | bytes 98312 | tf_op jit(solution)/shard_map/ppermute | solution.py:228
  25.3 4.8 %collective-permute-start.4 = (f32[2,32,128]{2,1,0:T(8,128)S(1)}, f32[2,32,128]{2,1,0:T(8,128)S(1)}, u32[]{:S(2)}, u32[]{:S(2)}) collective-permute-start(f32[2,32,128]{2,1,0:T(8,128)S(1)} %get-tuple-element.263), channel_id=1, source_target_pairs={{0,8},{4,12},{8,0},{12,4},{16,24},{20,28},{24,16},{28,20},{1,9},{5... | collective-permute-start | bytes 98312 | tf_op jit(solution)/shard_map/ppermute | solution.py:228
  30.1 5.9 %collective-permute-start.9 = (f32[2,32,128]{2,1,0:T(8,128)S(1)}, f32[2,32,128]{2,1,0:T(8,128)S(1)}, u32[]{:S(2)}, u32[]{:S(2)}) collective-permute-start(f32[2,32,128]{2,1,0:T(8,128)S(1)} %fusion.3.after_ref), channel_id=1, source_target_pairs={{0,24},{4,28},{8,16},{12,20},{16,8},{20,12},{24,0},{28,4},{1,25},{... | collective-permute-start | bytes 98312 | tf_op jit(solution)/shard_map/ppermute | solution.py:228
  31.7 4.8 %collective-permute-start.8 = (f32[2,32,128]{2,1,0:T(8,128)S(1)}, f32[2,32,128]{2,1,0:T(8,128)S(1)}, u32[]{:S(2)}, u32[]{:S(2)}) collective-permute-start(f32[2,32,128]{2,1,0:T(8,128)S(1)} %fusion.3.after_ref), channel_id=1, source_target_pairs={{0,16},{4,20},{8,24},{12,28},{16,0},{20,4},{24,8},{28,12},{1,17},{... | collective-permute-start | bytes 98312 | tf_op jit(solution)/shard_map/ppermute | solution.py:228
  32.3 4.5 %collective-permute-start.7 = (f32[2,32,128]{2,1,0:T(8,128)S(1)}, f32[2,32,128]{2,1,0:T(8,128)S(1)}, u32[]{:S(2)}, u32[]{:S(2)}) collective-permute-start(f32[2,32,128]{2,1,0:T(8,128)S(1)} %fusion.3.after_ref), channel_id=1, source_target_pairs={{0,8},{4,12},{8,0},{12,4},{16,24},{20,28},{24,16},{28,20},{1,9},{5... | collective-permute-start | bytes 98312 | tf_op jit(solution)/shard_map/ppermute | solution.py:228
  36.8 5.0 %collective-permute-start.13 = (f32[4,2,32,128]{3,2,1,0:T(8,128)S(1)}, f32[4,2,32,128]{3,2,1,0:T(8,128)S(1)}, u32[]{:S(2)}, u32[]{:S(2)}) collective-permute-start(f32[4,2,32,128]{3,2,1,0:T(8,128)S(1)} %pad_maximum_fusion.rest_7_.after_ref), channel_id=1, source_target_pairs={{0,4},{4,0},{8,12},{12,8},{16,20},{20,16},{24,28},{28,24},{1,5},{5... | collective-permute-start | bytes 393224 | tf_op jit(solution)/shard_map/ppermute | solution.py:228
  36.9 6.2 %collective-permute-start.12 = (f32[4,2,32,128]{3,2,1,0:T(8,128)S(1)}, f32[4,2,32,128]{3,2,1,0:T(8,128)S(1)}, u32[]{:S(2)}, u32[]{:S(2)}) collective-permute-start(f32[4,2,32,128]{3,2,1,0:T(8,128)S(1)} %pad_maximum_fusion.rest_7_.after_ref), channel_id=1, source_target_pairs={{0,1},{1,0},{2,3},{3,2},{4,5},{5,4},{6,7},{7,6},{8,9},{9,8},{10,11... | collective-permute-start | bytes 393224 | tf_op jit(solution)/shard_map/ppermute | solution.py:228
  38.5 8.4 %collective-permute-start.11 = (f32[4,2,32,128]{3,2,1,0:T(8,128)S(1)}, f32[4,2,32,128]{3,2,1,0:T(8,128)S(1)}, u32[]{:S(2)}, u32[]{:S(2)}) collective-permute-start(f32[4,2,32,128]{3,2,1,0:T(8,128)S(1)} %pad_maximum_fusion.rest_7_.after_ref), channel_id=1, source_target_pairs={{0,2},{1,3},{2,0},{3,1},{4,6},{5,7},{6,4},{7,5},{8,10},{9,11},{10,... | collective-permute-start | bytes 393224 | tf_op jit(solution)/shard_map/ppermute | solution.py:228
  39.5 7.3 %collective-permute-start.10 = (f32[4,2,32,128]{3,2,1,0:T(8,128)S(1)}, f32[4,2,32,128]{3,2,1,0:T(8,128)S(1)}, u32[]{:S(2)}, u32[]{:S(2)}) collective-permute-start(f32[4,2,32,128]{3,2,1,0:T(8,128)S(1)} %pad_maximum_fusion.rest_7_.after_ref), channel_id=1, source_target_pairs={{0,3},{1,2},{2,1},{3,0},{4,7},{5,6},{6,5},{7,4},{8,11},{9,10},{10,... | collective-permute-start | bytes 393224 | tf_op jit(solution)/shard_map/ppermute | solution.py:228
  46.9 1.3 %collective-permute-start.16 = (f32[4,2,32,128]{3,2,1,0:T(8,128)S(1)}, f32[4,2,32,128]{3,2,1,0:T(8,128)S(1)}, u32[]{:S(2)}, u32[]{:S(2)}) collective-permute-start(f32[4,2,32,128]{3,2,1,0:T(8,128)S(1)} %collective-permute-done.10.rest_25_), channel_id=1, source_target_pairs={{0,4},{4,0},{8,12},{12,8},{16,20},{20,16},{24,28},{28,24},{1,5},{5... | collective-permute-start | bytes 393224 | tf_op jit(solution)/shard_map/ppermute | solution.py:228
  46.9 1.5 %collective-permute-start.15 = (f32[4,2,32,128]{3,2,1,0:T(8,128)S(1)}, f32[4,2,32,128]{3,2,1,0:T(8,128)S(1)}, u32[]{:S(2)}, u32[]{:S(2)}) collective-permute-start(f32[4,2,32,128]{3,2,1,0:T(8,128)S(1)} %collective-permute-done.11.rest_23_), channel_id=1, source_target_pairs={{0,4},{4,0},{8,12},{12,8},{16,20},{20,16},{24,28},{28,24},{1,5},{5... | collective-permute-start | bytes 393224 | tf_op jit(solution)/shard_map/ppermute | solution.py:228
  47.4 1.3 %collective-permute-start.14 = (f32[4,2,32,128]{3,2,1,0:T(8,128)S(1)}, f32[4,2,32,128]{3,2,1,0:T(8,128)S(1)}, u32[]{:S(2)}, u32[]{:S(2)}) collective-permute-start(f32[4,2,32,128]{3,2,1,0:T(8,128)S(1)} %collective-permute-done.12.rest_21_), channel_id=1, source_target_pairs={{0,4},{4,0},{8,12},{12,8},{16,20},{20,16},{24,28},{28,24},{1,5},{5... | collective-permute-start | bytes 393224 | tf_op jit(solution)/shard_map/ppermute | solution.py:228
  (5 other events, 4.2 us)

commit v3 on v2

v3 whole, which is shorter than its diff:
```python
import functools
import math

import jax
import jax.numpy as jnp
from jax import lax
from jax.experimental import pallas as pl
from jax.experimental.pallas import tpu as pltpu
from jax.sharding import PartitionSpec as P

F32, BF16 = jnp.float32, jnp.bfloat16
HALF_SIN = (4.442867755889893, -7.307443618774414, 3.594788074493408, -0.7843740582466125)
HALF_COS = (1.4142135381698608, -6.978850841522217, 5.7394609451293945, -1.8835630416870117, 0.31069818139076233)
VMEM = pl.BlockSpec(memory_space=pltpu.VMEM)
ANY = pl.BlockSpec(memory_space=pl.ANY)
PARAMS = pltpu.CompilerParams(vmem_limit_bytes=32 * 2**20)
NN, NT, TN = ((1,), (0,)), ((1,), (1,)), ((0,), (0,))


def halves(value):
    high = value.astype(BF16)
    return high, (value - high.astype(F32)).astype(BF16)


def dot16(left, right, dims):
    return lax.dot_general(left, right, (dims, ((), ())), preferred_element_type=F32)


def dot3(left, right, dims):
    left_high, left_low = halves(left)
    right_high, right_low = halves(right)
    return (
        dot16(left_high, right_high, dims)
        + dot16(left_low, right_high, dims)
        + dot16(left_high, right_low, dims)
    )


def horner(terms, square):
    total = terms[-1] * square + terms[-2]
    for term in terms[-3::-1]:
        total = total * square + term
    return total


def trig(columns, rows):
    turns = columns[0] * rows[0] + columns[1] * rows[1] + columns[2] * rows[2]
    turns = turns - jnp.round(turns)
    square = turns * turns
    half_sin = horner(HALF_SIN, square) * turns
    return 1.0 - half_sin * half_sin, half_sin * horner(HALF_COS, square)


def trig_blocks(k_ref, pos_ref, first, high_low, full=None):
    vectors, atoms = high_low[0].shape
    step = 32
    width = min(256, atoms)
    per_body = max(1, 2048 // atoms)
    per_body = min(per_body, vectors // step)

    def body(block, _):
        for inner in range(per_body):
            here = pl.ds(pl.multiple_of((block * per_body + inner) * step, step), step)
            columns = [k_ref[here, x : x + 1] for x in range(3)]
            for chunk in range(atoms // width):
                lanes = pl.ds(chunk * width, width)
                start = chunk * width if first is None else pl.multiple_of(first + chunk * width, 128)
                rows = [pos_ref[x : x + 1, pl.ds(start, width)] for x in range(3)]
                cos, sin = trig(columns, rows)
                high_low[0][here, lanes], high_low[1][here, lanes] = halves(cos)
                high_low[2][here, lanes], high_low[3][here, lanes] = halves(sin)
                if full is not None:
                    full[0][here, lanes], full[1][here, lanes] = cos, sin
        return 0

    lax.fori_loop(0, vectors // (step * per_body), body, 0)


def lattice_rows(packed, channels, vectors):
    share = packed.shape[1]
    width = min(share, vectors)
    chunks = [packed[channels + 3 * n : channels + 3 * n + 3, 0:width] for n in range(-(-vectors // share))]
    return jnp.concatenate(chunks, axis=1)


def tile_kernel(pos_ref, packed_ref, cos_high, cos_low, sin_high, sin_low, k_column, *, channels, vectors, first):
    rows = cos_high.shape[0]
    k_column[:, 0:3] = lattice_rows(packed_ref, channels, vectors)[:, first : first + rows].T
    trig_blocks(k_column, pos_ref, None, (cos_high, cos_low, sin_high, sin_low))


def group_offset(label, groups):
    if groups != 4 or label in (0, 3):
        return label
    return jnp.where(lax.axis_index("atoms") % 2 == 0, label, 3 - label)


def sums_kernel(pad_ref, feats_ref, species_ref, w_charge_ref, embed_ref, w_out_ref, *rest, groups):
    tiles, packed = rest[:8], rest[8 : 8 + groups]
    keep_ref, send_ref, own_ref, mask_ref, both, total = rest[8 + groups :]
    channels, atoms = feats_ref.shape
    share = packed[0].shape[1]
    group = lax.axis_index("kvec")
    embed_high, embed_low = halves(embed_ref[...])
    for block in range(atoms // 256):
        lanes = slice(block * 256, (block + 1) * 256)
        used = pad_ref[0:1, block : block + 1]
        mask = (lax.broadcasted_iota(jnp.int32, (1, 256), 1) < used).astype(F32)
        mask_ref[:, lanes] = mask
        species_at = lax.broadcasted_iota(jnp.int32, (embed_ref.shape[0], 256), 0)
        one_hot = (species_at == species_ref[:, lanes]).astype(BF16)
        both[0:channels, lanes] = mask * (
            dot3(w_charge_ref[...], feats_ref[:, lanes], TN)
            + dot16(embed_high, one_hot, TN)
            + dot16(embed_low, one_hot, TN)
        )
    for label, cotangent in enumerate(packed):
        lanes = pl.ds(pl.multiple_of((group ^ group_offset(label, groups)) * share, share), share)
        adjoint = mask_ref[:, lanes] * dot3(w_out_ref[...], cotangent[0:channels, :], NN)
        both[channels:, lanes] = adjoint
        if label == 0:
            own_ref[0:channels, :] = adjoint
            own_ref[channels : 2 * channels, :] = both[0:channels, lanes]
            own_ref[2 * channels :, :] = jnp.broadcast_to(mask_ref[:, lanes], (8, share))
    high, low = halves(both[...])
    pair = jnp.concatenate([high, low], axis=0)
    tiles_high = jnp.concatenate([tiles[n][...] for n in (0, 4, 2, 6)], axis=0)
    tiles_low = jnp.concatenate([tiles[n][...] for n in (1, 5, 3, 7)], axis=0)
    wide = dot16(tiles_high, pair, NT)
    total[...] = wide[:, : 2 * channels] + wide[:, 2 * channels :] + dot16(tiles_low, high, NT)
    rows = keep_ref.shape[1]
    core = lax.axis_index("atoms") % 2
    for flip, out in enumerate((keep_ref, send_ref)):
        for part in range(2):
            start = pl.multiple_of(2 * rows * part + (core ^ flip) * rows, rows)
            out[part] = total[pl.ds(start, rows), :]


def wave_kernel(pos_ref, packed_ref, width_ref, after_ref, *rest, atom_total):
    *gain_ref, cos, sin, cos_high, cos_low, sin_high, sin_low, k_ref, k_column = rest
    vectors = cos.shape[0]
    rows = vectors // 2
    core = lax.axis_index("atoms") % 2
    k_column[:, 0:3] = lattice_rows(packed_ref, width_ref.shape[1], vectors).T
    for flip in range(2):
        start = pl.multiple_of((core ^ flip) * rows, rows)
        k_ref[flip * rows : (flip + 1) * rows, :] = k_column[pl.ds(start, rows), :]
    if gain_ref:
        waves = [2.0 * math.pi * k_ref[0:rows, x : x + 1] for x in range(3)]
        square = waves[0] * waves[0] + waves[1] * waves[1] + waves[2] * waves[2]
        gain = jnp.exp(-square * width_ref[...]) * 40.0 / (square + 40.0) / math.sqrt(atom_total)
        gain_ref[0][...] = jnp.concatenate([gain, gain], axis=1)
    first = lax.axis_index("kvec") * cos.shape[1]
    trig_blocks(k_ref, pos_ref, first, (cos_high, cos_low, sin_high, sin_low), (cos, sin))


def coefficient_stack(near_ref, far_ref, part):
    high, low = halves(jnp.concatenate([near_ref[part], far_ref[part]], axis=0))
    return jnp.concatenate([high, low, high], axis=1)


def own_stack(own_ref, channels):
    high, low = halves(own_ref[0 : 2 * channels, :])
    return jnp.concatenate([high, high, low], axis=0)


def add_field(stack, tile_high, tile_low):
    width = stack.shape[1] // 3
    wide = dot16(stack[:, : 2 * width], tile_high, TN)
    return wide[:width] + wide[width:] + dot16(stack[:, :width], tile_low, TN)


def add_force(sums, wave, along, first):
    step = 16
    cos, sin, _, _, _, _, k_ref = wave
    for start in range(0, cos.shape[0], step):
        here = slice(start, start + step)
        there = slice(first + start, first + start + step)
        slope = cos[here, :] * along[1, there, :] - sin[here, :] * along[0, there, :]
        for x in range(3):
            term = k_ref[here, x : x + 1] * slope
            sums[x] = sums[x] + (term[0:8] + term[8:16])
    return sums


def fields(own_ref, waves, coefs, channels, along, field, sums):
    other = own_stack(own_ref, channels)
    parts = [
        [coefficient_stack(near, far, part) for near, far in zip(coefs[::2], coefs[1::2])] for part in range(2)
    ]
    for part in range(2):
        along[part] = dot16(jnp.concatenate(parts[part], axis=0), other, NN)
    waves = [waves[at : at + 7] for at in range(0, len(waves), 7)]
    for group, wave in enumerate(waves):
        _, _, cos_high, cos_low, sin_high, sin_low, _ = wave
        for part, high, low in ((parts[0], cos_high, cos_low), (parts[1], sin_high, sin_low)):
            added = add_field(part[group], high[...], low[...])
            field = added if field is None else field + added
    for group, wave in enumerate(waves):
        sums = add_force(sums, wave, along, group * wave[0].shape[0])
    return field, sums


def partial_field_kernel(own_ref, *rest, groups, first):
    waves, coefs, before = rest[: 7 * groups], rest[7 * groups : 9 * groups], rest[9 * groups : -3]
    field_ref, sums_ref, along = rest[-3:]
    share = own_ref.shape[1]
    if first:
        field, sums = None, [jnp.zeros((8, share), F32)] * 3
    else:
        field, sums = before[0][...], [before[1][8 * x : 8 * x + 8, :] for x in range(3)]
    field, sums = fields(own_ref, waves, coefs, coefs[0].shape[2] // 2, along, field, sums)
    field_ref[...] = field
    for x in range(3):
        sums_ref[8 * x : 8 * x + 8, :] = sums[x]


def field_kernel(own_ref, w_out_ref, w_charge_ref, *rest):
    *waves, near_ref, far_ref, field_ref, sums_ref, message_ref, force_ref, grad_ref, along = rest
    channels = w_out_ref.shape[0]
    sums = [sums_ref[8 * x : 8 * x + 8, :] for x in range(3)]
    field, sums = fields(own_ref, waves, [near_ref, far_ref], channels, along, field_ref[...], sums)
    field = own_ref[2 * channels : 2 * channels + 1, :] * field
    message_ref[...] = dot3(w_out_ref[...], field[:channels], TN)
    grad_ref[...] = dot3(w_charge_ref[...], field[channels:], NN)
    for x in range(3):
        force_ref[x : x + 1, :] = 2.0 * math.pi * jnp.sum(sums[x], axis=0, keepdims=True)


def swap(value, axis, offset):
    size = lax.axis_size(axis)
    return lax.ppermute(value, axis, [(place, place ^ offset) for place in range(size)])


def swap_by_core(value, even, odd):
    groups = lax.axis_size("kvec")
    pairs = []
    for place in range(lax.axis_size("atoms")):
        for group in range(groups):
            other = group ^ (odd if place % 2 else even)
            pairs.append((place * groups + group, place * groups + other))
    return lax.ppermute(value, ("atoms", "kvec"), pairs)


def cost(work):
    return pl.CostEstimate(flops=work, bytes_accessed=0, transcendentals=0)


def on_device(
    positions, feats, species, pad_count, k_lattice, filter_width, w_charge, species_embed, w_out, grad_out,
):
    atom_count, group_count = lax.axis_size("atoms"), lax.axis_size("kvec")
    channels, atoms = feats.shape
    share = grad_out.shape[1]
    vectors = k_lattice.shape[1]
    half = vectors // 2
    both = 2 * channels
    four = group_count == 4
    f32 = lambda *shape: jax.ShapeDtypeStruct(shape, F32)
    bf16 = lambda *shape: jax.ShapeDtypeStruct(shape, BF16)

    def first_planes(value):
        if four:
            return [swap_by_core(value, 1, 2), swap_by_core(value, 2, 1)]
        return [swap(value, "kvec", m) for m in range(1, group_count)]

    chunks = -(-vectors // share)
    below = -(-3 * chunks // 8) * 8
    packed = jnp.pad(grad_out, ((0, below), (0, 0)))
    for n in range(chunks):
        chunk = k_lattice[:, n * share : (n + 1) * share]
        first = channels + 3 * n
        packed += jnp.pad(chunk, ((first, channels + below - first - 3), (0, share - chunk.shape[1]))).astype(F32)

    def tiles_of(part):
        made = pl.pallas_call(
            functools.partial(tile_kernel, channels=channels, vectors=vectors, first=part * half),
            out_shape=[bf16(half, atoms)] * 4,
            in_specs=[VMEM] * 2,
            out_specs=[VMEM] * 4,
            scratch_shapes=[pltpu.VMEM((half, 128), F32)],
            compiler_params=PARAMS,
            cost_estimate=cost(9000 * half * atoms),
            name="waves_of_own_vectors",
        )(positions, packed)
        return list(made)

    arrived = first_planes(packed)
    tiles = tiles_of(0)
    arrived[0], tiles = lax.optimization_barrier((arrived[0], tiles))
    if four:
        arrived.append(swap_by_core(arrived[0], 2, 1))
    tiles = tiles + tiles_of(1)
    packed = [packed] + arrived

    keep, send, own = pl.pallas_call(
        functools.partial(sums_kernel, groups=group_count),
        out_shape=[f32(2, half, both), f32(2, half, both), f32(both + 8, share)],
        in_specs=[VMEM] * (14 + group_count),
        out_specs=[VMEM] * 3,
        scratch_shapes=[
            pltpu.VMEM((1, atoms), F32), pltpu.VMEM((both, atoms), F32), pltpu.VMEM((2 * vectors, both), F32),
        ],
        compiler_params=PARAMS,
        cost_estimate=cost(100 * vectors * atoms * channels),
        name="structure_sums",
    )(
        pad_count.reshape(1, -1), feats, species.reshape(1, atoms), w_charge, species_embed.T, w_out,
        *tiles, *packed,
    )

    wave_shapes = [f32(vectors, share)] * 2 + [bf16(vectors, share)] * 4 + [f32(vectors, 128)]

    def waves_of(group, after):
        shapes = ([f32(half, both)] if group == 0 else []) + wave_shapes
        made = pl.pallas_call(
            functools.partial(wave_kernel, atom_total=atoms * atom_count),
            out_shape=shapes,
            in_specs=[VMEM, VMEM, VMEM, ANY],
            out_specs=[VMEM] * len(shapes),
            scratch_shapes=[pltpu.VMEM((vectors, 128), F32)],
            compiler_params=PARAMS,
            cost_estimate=cost(9000 * vectors * share),
            name="waves_of_own_atoms",
        )(positions, packed[group], filter_width.reshape(1, channels), after)
        return list(made)

    arrived = swap(send, "atoms", 1)
    gain, *own_waves = waves_of(0, send)
    arrived, gain = lax.optimization_barrier((arrived, gain))
    total = keep + arrived
    waves, made = [], 1
    steps = [2 << n for n in range((atom_count // 2).bit_length() - 1)]
    for near_step, far_step in zip(steps, steps[::-1]):
        pairs = [(place, place ^ (far_step if place % 2 else near_step)) for place in range(atom_count)]
        arrived = lax.ppermute(total, "atoms", pairs)
        count = group_count - made if near_step == steps[-1] else 1
        beside = []
        for group in range(made, min(made + count, group_count)):
            beside = beside + waves_of(group, total)
            made += 1
        arrived, beside = lax.optimization_barrier((arrived, beside))
        waves += beside
        total = total + arrived
    near = gain[None] * total

    def partial_fields(group_waves, coefs, before):
        groups = len(coefs) // 2
        return pl.pallas_call(
            functools.partial(partial_field_kernel, groups=groups, first=not before),
            out_shape=[f32(both, share), f32(24, share)],
            in_specs=[VMEM] * (1 + 9 * groups + len(before)),
            out_specs=[VMEM] * 2,
            scratch_shapes=[pltpu.VMEM((2, groups * vectors, share), F32)],
            compiler_params=PARAMS,
            cost_estimate=cost(120 * groups * vectors * share * channels),
            name="fields_of_some_groups",
        )(own, *group_waves, *coefs, *before)

    plane = first_planes(near)
    fields_so_far = partial_fields(own_waves, [near, swap(near, "atoms", 1)], [])
    plane[0], fields_so_far = lax.optimization_barrier((plane[0], fields_so_far))
    if four:
        last = swap_by_core(plane[0], 2, 1)
        plane = lax.optimization_barrier(plane)
        far = [swap(plane[1], "atoms", 1), swap(plane[0], "atoms", 1)]
    else:
        last = plane.pop()
        far = [swap(part, "atoms", 1) for part in plane]
    coefs = [part for pair in zip(plane, far) for part in pair]
    fields_so_far = partial_fields(waves[:-7], coefs, fields_so_far)
    last, fields_so_far = lax.optimization_barrier((last, fields_so_far))

    return tuple(
        pl.pallas_call(
            field_kernel,
            out_shape=[f32(channels, share), f32(3, share), f32(channels, share)],
            in_specs=[VMEM] * 14,
            out_specs=[VMEM] * 3,
            scratch_shapes=[pltpu.VMEM((2, vectors, share), F32)],
            compiler_params=PARAMS,
            cost_estimate=cost(120 * vectors * share * channels),
            name="fields_and_forces",
        )(own, w_out, w_charge, *waves[-7:], last, swap(last, "atoms", 1), *fields_so_far)
    )


def solution(mesh):
    shared = P(None, ("atoms", "kvec"))
    placed = (
        P(None, "atoms"), P(None, "atoms"), P("atoms"), P("atoms"), P(None, "kvec"),
        P(), P(), P(), P(), shared,
    )
    return jax.shard_map(
        on_device, mesh=mesh, in_specs=placed, out_specs=(shared, shared, shared), check_vma=False
    )
```

time: 51.9 us -> 47.2 us (0.909)
  waiting for transfers between devices: 9.9 us -> 15.7 us
  local copies, waits for them, and re-layouts: 5.61 us -> 1.22 us
  Pallas kernels: 15.8 us -> 12.9 us
  starting transfers between devices: 17.7 us -> 15.5 us
  other arithmetic: 1.73 us -> 0.99 us
    ppermute x17 -> x5, starting transfers between devices: 17.7 us -> 0.65 us  [swap(): lax.ppermute(value, axis, [(place, place ^ offset) for place in range(siz...]
    ppermute x0 -> x8, starting transfers between devices: none -> 14.8 us  [the longest x6 9.86 us: swap_by_core(): return lax.ppermute(value, ('atoms', 'kvec'), pairs)]
    ppermute x0 -> x8, waiting for transfers between devices: none -> 14 us  [the longest x6 9.02 us: swap_by_core(): return lax.ppermute(value, ('atoms', 'kvec'), pairs)]
    ppermute x17 -> x5, waiting for transfers between devices: 9.9 us -> 1.63 us  [swap(): lax.ppermute(value, axis, [(place, place ^ offset) for place in range(siz...]
    unnamed x24 -> x16, local copies, waits for them, and re-layouts: 5.6 us -> 1.22 us
    pallas_call x4, Pallas kernels: 5.85 us -> 3.76 us  [waves_of(): pl.pallas_call(functools.partial(wave_kernel, atom_total=atoms * atom_cou...]
    convert_element_type x1 -> x0, other arithmetic: 0.69 us -> none  [on_device(): lattice = k_lattice.astype(F32)]
    pallas_call x3 -> x5, Pallas kernels: 7.35 us -> 6.93 us  [the longest x2 3.16 us: tiles_of(): pl.pallas_call(functools.partial(tile_kernel, channels=channels, vectors=...]
  transfers between devices with their start and end apart: 17 -> 13, of which waited for: 10 -> 10; matrix products, arithmetic and copies ran while one was open for 0% -> 0% of each run, Pallas kernels for 20% -> 19%
where the time goes in v3:
time: 47.2 us; the launch traced here: 47 us
  waiting for transfers between devices  15.7 us (33%)
  starting transfers between devices  15.5 us (33%)
  Pallas kernels  12.9 us (27%)
  local copies, waits for them, and re-layouts  1.22 us (3%)
  other arithmetic  0.99 us (2%)
  between operations  0.81 us (2%)
    ppermute x6, starting transfers between devices, swap_by_core(): return lax.ppermute(value, ('atoms', 'kvec'), pairs)  9.86 us
    ppermute x6, waiting for transfers between devices, swap_by_core(): return lax.ppermute(value, ('atoms', 'kvec'), pairs)  9.02 us
    ppermute x2, waiting for transfers between devices, on_device(): arrived = lax.ppermute(total, 'atoms', pairs)  5.01 us
    ppermute x2, starting transfers between devices, on_device(): arrived = lax.ppermute(total, 'atoms', pairs)  4.96 us
    pallas_call x4, Pallas kernels, waves_of(): pl.pallas_call(functools.partial(wave_kernel, atom_total=atoms * atom_cou...  3.76 us
    pallas_call x2, Pallas kernels, tiles_of(): pl.pallas_call(functools.partial(tile_kernel, channels=channels, vectors=...  3.16 us
    pallas_call x1, Pallas kernels, on_device(): pl.pallas_call(functools.partial(sums_kernel, groups=group_count), out_sh...  2.19 us
    pallas_call x2, Pallas kernels, partial_fields(): pl.pallas_call(functools.partial(partial_field_kernel, groups=groups, fir...  2.12 us
  transfers between devices with their start and end apart: 13, of which 10 were waited for; matrix products, arithmetic and copies ran while one was open for 0% of the time, Pallas kernels for 19%

profile of v3, /device:TPU:0, one launch (start us, length us, event | category | flops | bytes accessed | tf_op | source)
XLA Modules:
  0.0 47.0 jit_solution(16746194518690281083)
XLA Ops:
  0.6 0.9 %convert_add_fusion.packed_ref.rest_8_ = f32[72,512]{1,0:T(8,128)S(1)} fusion(s32[3,256]{1,0:T(4,128)} %param.14, f32[64,512]{1,0:T(8,128)} %param.19), kind=kLoop, calls=%fused_computation | loop fusion | flops 73728 | bytes 281600 | tf_op jit(solution)/shard_map/add | solution.py:273
  1.6 3.0 %collective-permute-start = (f32[72,512]{1,0:T(8,128)S(1)}, f32[72,512]{1,0:T(8,128)S(1)}, u32[]{:S(2)}, u32[]{:S(2)}) collective-permute-start(f32[72,512]{1,0:T(8,128)S(1)} %convert_add_fusion.packed_ref.rest_8_), channel_id=1, source_target_pairs={{0,1},{1,0},{2,3},{3,2},{4,6},{5,7},{6,4},{7,5},{8,9},{9,8},{10,11... | collective-permute-start | bytes 442376 | tf_op jit(solution)/shard_map/ppermute | solution.py:242
  4.6 1.5 %collective-permute-start.1 = (f32[72,512]{1,0:T(8,128)S(1)}, f32[72,512]{1,0:T(8,128)S(1)}, u32[]{:S(2)}, u32[]{:S(2)}) collective-permute-start(f32[72,512]{1,0:T(8,128)S(1)} %convert_add_fusion.packed_ref.rest_8_), channel_id=1, source_target_pairs={{0,2},{1,3},{2,0},{3,1},{4,5},{5,4},{6,7},{7,6},{8,10},{9,11},{10,... | collective-permute-start | bytes 442376 | tf_op jit(solution)/shard_map/ppermute | solution.py:242
  6.1 1.6 %waves_of_own_vectors.2 = (bf16[128,2048]{1,0:T(8,128)(2,1)S(1)}, bf16[128,2048]{1,0:T(8,128)(2,1)S(1)}, bf16[128,2048]{1,0:T(8,128)(2,1)S(1)}, bf16[128,2048]{1,0:T(8,128)(2,1)S(1)}) custom-call(f32[3,2048]{1,0:T(4,128)S(1)} %copy-done.1, f32[72,512]{1,0:T(8,128)S(1)} %convert_add_fusion.packed_ref.rest_8_), custom_call_target="tpu_custom_call" | custom-call | flops 2359296000 | tf_op jit(solution)/shard_map/waves_of_own_vectors/pallas_call | solution.py:276
  7.7 1.0 %collective-permute-done.rest_9_.packed_ref = f32[72,512]{1,0:T(8,128)S(1)} collective-permute-done((f32[72,512]{1,0:T(8,128)S(1)}, f32[72,512]{1,0:T(8,128)S(1)}, u32[]{:S(2)}, u32[]{:S(2)}) %collective-permute-start) | collective-permute-done | bytes 147488 | tf_op jit(solution)/shard_map/ppermute | solution.py:242
  8.7 1.6 %collective-permute-start.2 = (f32[72,512]{1,0:T(8,128)S(1)}, f32[72,512]{1,0:T(8,128)S(1)}, u32[]{:S(2)}, u32[]{:S(2)}) collective-permute-start(f32[72,512]{1,0:T(8,128)S(1)} %collective-permute-done.rest_9_.packed_ref), channel_id=1, source_target_pairs={{0,2},{1,3},{2,0},{3,1},{4,5},{5,4},{6,7},{7,6},{8,10},{9,11},{10,... | collective-permute-start | bytes 442376 | tf_op jit(solution)/shard_map/ppermute | solution.py:242
  10.3 1.6 %waves_of_own_vectors.3 = (bf16[128,2048]{1,0:T(8,128)(2,1)S(1)}, bf16[128,2048]{1,0:T(8,128)(2,1)S(1)}, bf16[128,2048]{1,0:T(8,128)(2,1)S(1)}, bf16[128,2048]{1,0:T(8,128)(2,1)S(1)}) custom-call(f32[3,2048]{1,0:T(4,128)S(1)} %copy-done.1, f32[72,512]{1,0:T(8,128)S(1)} %convert_add_fusion.packed_ref.rest_8_), custom_call_target="tpu_custom_call" | custom-call | flops 2359296000 | tf_op jit(solution)/shard_map/waves_of_own_vectors/pallas_call | solution.py:276
  11.9 2.0 %collective-permute-done.2.rest_11_.packed_ref = f32[72,512]{1,0:T(8,128)S(1)} collective-permute-done((f32[72,512]{1,0:T(8,128)S(1)}, f32[72,512]{1,0:T(8,128)S(1)}, u32[]{:S(2)}, u32[]{:S(2)}) %collective-permute-start.2) | collective-permute-done | bytes 147488 | tf_op jit(solution)/shard_map/ppermute | solution.py:242
  14.5 2.2 %structure_sums.1 = (f32[2,128,128]{2,1,0:T(8,128)S(1)}, f32[2,128,128]{2,1,0:T(8,128)S(1)}, f32[136,512]{1,0:T(8,128)S(1)}) custom-call(s32[1,8]{1,0:T(1,128)S(1)} %bitcast.6, f32[64,2048]{1,0:T(8,128)S(1)} %copy-done, s32[1,2048]{1,0:T(1,128)S(1)} %bitcast.4, f32[64,64]{1,0:T(8,128)S(1)} %copy-done.2, f32[16,64]{1,0:T(8,128)S(1)} %bitcast.5, ...), custom_call_target="tpu_custom_call" | custom-call | flops 3355443200 | tf_op jit(solution)/shard_map/structure_sums/pallas_call | solution.py:296
  17.4 1.1 %waves_of_own_atoms.4 = (f32[128,128]{1,0:T(8,128)S(1)}, f32[256,512]{1,0:T(8,128)S(1)}, f32[256,512]{1,0:T(8,128)S(1)}, bf16[256,512]{1,0:T(8,128)(2,1)S(1)}, b...) custom-call(f32[3,2048]{1,0:T(4,128)S(1)} %copy-done.1, ...), custom_call_target="tpu_custom_call" | custom-call | flops 1179648000 | tf_op jit(solution)/shard_map/waves_of_own_atoms/pallas_call | solution.py:316
  18.6 2.6 %collective-permute-start.4 = (f32[2,128,128]{2,1,0:T(8,128)S(1)}, f32[2,128,128]{2,1,0:T(8,128)S(1)}, u32[]{:S(2)}, u32[]{:S(2)}) collective-permute-start(f32[2,128,128]{2,1,0:T(8,128)S(1)} %add.17.after_ref), channel_id=1, source_target_pairs={{0,8},{4,20},{8,0},{12,28},{16,24},{20,4},{24,16},{28,12},{1,9},{5... | collective-permute-start | bytes 393224 | tf_op jit(solution)/shard_map/ppermute | solution.py:336
  21.2 0.9 %waves_of_own_atoms.5 = (f32[256,512]{1,0:T(8,128)S(1)}, f32[256,512]{1,0:T(8,128)S(1)}, bf16[256,512]{1,0:T(8,128)(2,1)S(1)}, bf16[256,512]{1,0:T(8,128)(2,1)S(...) custom-call(f32[3,2048]{1,0:T(4,128)S(1)} %copy-done.1, ...), custom_call_target="tpu_custom_call" | custom-call | flops 1179648000 | tf_op jit(solution)/shard_map/waves_of_own_atoms/pallas_call | solution.py:316
  22.1 3.2 %collective-permute-done.4 = f32[2,128,128]{2,1,0:T(8,128)S(1)} collective-permute-done((f32[2,128,128]{2,1,0:T(8,128)S(1)}, f32[2,128,128]{2,1,0:T(8,128)S(1)}, u32[]{:S(2)}, u32[]{:S(2)}) %collective-permute-start.4) | collective-permute-done | bytes 131104 | tf_op jit(solution)/shard_map/ppermute | solution.py:336
  25.3 2.3 %collective-permute-start.5 = (f32[2,128,128]{2,1,0:T(8,128)S(1)}, f32[2,128,128]{2,1,0:T(8,128)S(1)}, u32[]{:S(2)}, u32[]{:S(2)}) collective-permute-start(f32[2,128,128]{2,1,0:T(8,128)S(1)} %add.18.after_ref), channel_id=1, source_target_pairs={{0,16},{4,12},{8,24},{12,4},{16,0},{20,28},{24,8},{28,20},{1,17},{... | collective-permute-start | bytes 393224 | tf_op jit(solution)/shard_map/ppermute | solution.py:336
  27.6 0.9 %waves_of_own_atoms.7 = (f32[256,512]{1,0:T(8,128)S(1)}, f32[256,512]{1,0:T(8,128)S(1)}, bf16[256,512]{1,0:T(8,128)(2,1)S(1)}, bf16[256,512]{1,0:T(8,128)(2,1)S(...) custom-call(f32[3,2048]{1,0:T(4,128)S(1)} %copy-done.1, ...), custom_call_target="tpu_custom_call" | custom-call | flops 1179648000 | tf_op jit(solution)/shard_map/waves_of_own_atoms/pallas_call | solution.py:316
  28.5 0.9 %waves_of_own_atoms.6 = (f32[256,512]{1,0:T(8,128)S(1)}, f32[256,512]{1,0:T(8,128)S(1)}, bf16[256,512]{1,0:T(8,128)(2,1)S(1)}, bf16[256,512]{1,0:T(8,128)(2,1)S(...) custom-call(f32[3,2048]{1,0:T(4,128)S(1)} %copy-done.1, ...), custom_call_target="tpu_custom_call" | custom-call | flops 1179648000 | tf_op jit(solution)/shard_map/waves_of_own_atoms/pallas_call | solution.py:316
  29.4 1.8 %collective-permute-done.5 = f32[2,128,128]{2,1,0:T(8,128)S(1)} collective-permute-done((f32[2,128,128]{2,1,0:T(8,128)S(1)}, f32[2,128,128]{2,1,0:T(8,128)S(1)}, u32[]{:S(2)}, u32[]{:S(2)}) %collective-permute-start.5) | collective-permute-done | bytes 131104 | tf_op jit(solution)/shard_map/ppermute | solution.py:336
  31.3 2.3 %collective-permute-start.6 = (f32[2,128,128]{2,1,0:T(8,128)S(1)}, f32[2,128,128]{2,1,0:T(8,128)S(1)}, u32[]{:S(2)}, u32[]{:S(2)}) collective-permute-start(f32[2,128,128]{2,1,0:T(8,128)S(1)} %add_multiply_fusion.rest_7_), channel_id=1, source_target_pairs={{0,1},{1,0},{2,3},{3,2},{4,6},{5,7},{6,4},{7,5},{8,9},{9,8},{10,11... | collective-permute-start | bytes 393224 | tf_op jit(solution)/shard_map/ppermute | solution.py:242
  35.0 2.5 %collective-permute-done.6.rest_14_ = f32[2,128,128]{2,1,0:T(8,128)S(1)} collective-permute-done((f32[2,128,128]{2,1,0:T(8,128)S(1)}, f32[2,128,128]{2,1,0:T(8,128)S(1)}, u32[]{:S(2)}, u32[]{:S(2)}) %collective-permute-start.6) | collective-permute-done | bytes 131104 | tf_op jit(solution)/shard_map/ppermute | solution.py:242
  37.5 1.0 %collective-permute-done.9.rest_16_ = f32[2,128,128]{2,1,0:T(8,128)S(1)} collective-permute-done((f32[2,128,128]{2,1,0:T(8,128)S(1)}, f32[2,128,128]{2,1,0:T(8,128)S(1)}, u32[]{:S(2)}, u32[]{:S(2)}) %collective-permute-start.9) | collective-permute-done | bytes 131104 | tf_op jit(solution)/shard_map/ppermute | solution.py:242
  40.1 1.4 %fields_of_some_groups.3 = (f32[128,512]{1,0:T(8,128)S(1)}, f32[24,512]{1,0:T(8,128)S(1)}) custom-call(f32[136,512]{1,0:T(8,128)S(1)} %get-tuple-element.98.own_ref, f32[256,512]{1,0:T(8,128)S(1)} %get-tuple-element.144.rest_0_, f32[256,512]{1,0:T(8,128)S(1)} %get-tuple-element.145.rest_1_, bf16[256,512]{1,0:T(8,128)(2,1)S(1)} %get-tuple-element.146.rest_2_, ...), custom_call_target="tpu_custom_call" | custom-call | flops 2013265920 | tf_op jit(solution)/shard_map/fields_of_some_groups/pallas_call | solution.py:349
  41.5 2.5 %collective-permute-done.8.rest_7_ = f32[2,128,128]{2,1,0:T(8,128)S(1)} collective-permute-done((f32[2,128,128]{2,1,0:T(8,128)S(1)}, f32[2,128,128]{2,1,0:T(8,128)S(1)}, u32[]{:S(2)}, u32[]{:S(2)}) %collective-permute-start.8) | collective-permute-done | bytes 131104 | tf_op jit(solution)/shard_map/ppermute | solution.py:242
  44.0 1.3 %collective-permute-done.12.rest_8_ = f32[2,128,128]{2,1,0:T(8,128)S(1)} collective-permute-done((f32[2,128,128]{2,1,0:T(8,128)S(1)}, f32[2,128,128]{2,1,0:T(8,128)S(1)}, u32[]{:S(2)}, u32[]{:S(2)}) %collective-permute-start.12) | collective-permute-done | bytes 131104 | tf_op jit(solution)/shard_map/ppermute | solution.py:232
  45.4 1.7 %fields_and_forces.1 = (f32[64,512]{1,0:T(8,128)}, f32[3,512]{1,0:T(4,128)}, f32[64,512]{1,0:T(8,128)}) custom-call(f32[136,512]{1,0:T(8,128)S(1)} %get-tuple-element.98.own_ref, f32[64,64]{1,0:T(8,128)S(1)} %copy-done.3, f32[64,64]{1,0:T(8,128)S(1)} %copy-done.2, f32[256,512]{1,0:T(8,128)S(1)} %get-tuple-element.125.rest_0_, ...), custom_call_target="tpu_custom_call" | custom-call | flops 1006632960 | tf_op jit(solution)/shard_map/fields_and_forces/pallas_call | solution.py:375
  (32 shorter events, 4.4 us)
Async XLA Ops:
  0.6 5.5 %copy-start.1 = (f32[3,2048]{1,0:T(4,128)S(1)}, f32[3,2048]{1,0:T(4,128)}, u32[]{:S(2)}) copy-start(f32[3,2048]{1,0:T(4,128)} %pos_ref.11) | copy-start | bytes 73732
  1.6 7.1 %collective-permute-start = (f32[72,512]{1,0:T(8,128)S(1)}, f32[72,512]{1,0:T(8,128)S(1)}, u32[]{:S(2)}, u32[]{:S(2)}) collective-permute-start(f32[72,512]{1,0:T(8,128)S(1)} %convert_add_fusion.packed_ref.rest_8_), channel_id=1, source_target_pairs={{0,1},{1,0},{2,3},{3,2},{4,6},{5,7},{6,4},{7,5},{8,9},{9,8},{10,11... | collective-permute-start | bytes 442376 | tf_op jit(solution)/shard_map/ppermute | solution.py:242
  4.6 7.3 %collective-permute-start.1 = (f32[72,512]{1,0:T(8,128)S(1)}, f32[72,512]{1,0:T(8,128)S(1)}, u32[]{:S(2)}, u32[]{:S(2)}) collective-permute-start(f32[72,512]{1,0:T(8,128)S(1)} %convert_add_fusion.packed_ref.rest_8_), channel_id=1, source_target_pairs={{0,2},{1,3},{2,0},{3,1},{4,5},{5,4},{6,7},{7,6},{8,10},{9,11},{10,... | collective-permute-start | bytes 442376 | tf_op jit(solution)/shard_map/ppermute | solution.py:242
  8.7 5.2 %copy-start = (f32[64,2048]{1,0:T(8,128)S(1)}, f32[64,2048]{1,0:T(8,128)}, u32[]{:S(2)}) copy-start(f32[64,2048]{1,0:T(8,128)} %feats_ref.1) | copy-start | bytes 1572868
  8.7 5.2 %copy-start.2 = (f32[64,64]{1,0:T(8,128)S(1)}, f32[64,64]{1,0:T(8,128)}, u32[]{:S(2)}) copy-start(f32[64,64]{1,0:T(8,128)} %w_charge_ref.3) | copy-start | bytes 49156
  8.7 5.2 %copy-start.3 = (f32[64,64]{1,0:T(8,128)S(1)}, f32[64,64]{1,0:T(8,128)}, u32[]{:S(2)}) copy-start(f32[64,64]{1,0:T(8,128)} %w_out_ref.3) | copy-start | bytes 49156
  8.7 5.1 %collective-permute-start.2 = (f32[72,512]{1,0:T(8,128)S(1)}, f32[72,512]{1,0:T(8,128)S(1)}, u32[]{:S(2)}, u32[]{:S(2)}) collective-permute-start(f32[72,512]{1,0:T(8,128)S(1)} %collective-permute-done.rest_9_.packed_ref), channel_id=1, source_target_pairs={{0,2},{1,3},{2,0},{3,1},{4,5},{5,4},{6,7},{7,6},{8,10},{9,11},{10,... | collective-permute-start | bytes 442376 | tf_op jit(solution)/shard_map/ppermute | solution.py:242
  10.3 3.6 %copy-start.5 = (f32[64,16]{0,1:T(8,128)S(1)}, f32[64,16]{0,1:T(8,128)}, u32[]{:S(2)}) copy-start(f32[64,16]{0,1:T(8,128)} %param.17) | copy-start | bytes 12292
  11.9 2.0 %copy-start.4 = (s32[2048]{0:T(1024)S(1)}, s32[2048]{0:T(1024)}, u32[]{:S(2)}) copy-start(s32[2048]{0:T(1024)} %param.12) | copy-start | bytes 24580
  13.9 0.7 %copy-start.6 = (s32[8]{0:T(128)S(1)}, s32[8]{0:T(128)}, u32[]{:S(2)}) copy-start(s32[8]{0:T(128)} %param.13) | copy-start | bytes 100
  16.7 0.7 %copy-start.7 = (f32[64]{0:T(128)S(1)}, f32[64]{0:T(128)}, u32[]{:S(2)}) copy-start(f32[64]{0:T(128)} %param.15) | copy-start | bytes 772
  16.7 1.8 %collective-permute-start.3 = (f32[2,128,128]{2,1,0:T(8,128)S(1)}, f32[2,128,128]{2,1,0:T(8,128)S(1)}, u32[]{:S(2)}, u32[]{:S(2)}) collective-permute-start(f32[2,128,128]{2,1,0:T(8,128)S(1)} %get-tuple-element.100.after_ref), channel_id=1, source_target_pairs={{0,4},{4,0},{8,12},{12,8},{16,20},{20,16},{24,28},{28,24},{1,5},{5... | collective-permute-start | bytes 393224 | tf_op jit(solution)/shard_map/ppermute | solution.py:232
  18.6 6.7 %collective-permute-start.4 = (f32[2,128,128]{2,1,0:T(8,128)S(1)}, f32[2,128,128]{2,1,0:T(8,128)S(1)}, u32[]{:S(2)}, u32[]{:S(2)}) collective-permute-start(f32[2,128,128]{2,1,0:T(8,128)S(1)} %add.17.after_ref), channel_id=1, source_target_pairs={{0,8},{4,20},{8,0},{12,28},{16,24},{20,4},{24,16},{28,12},{1,9},{5... | collective-permute-start | bytes 393224 | tf_op jit(solution)/shard_map/ppermute | solution.py:336
  25.3 5.9 %collective-permute-start.5 = (f32[2,128,128]{2,1,0:T(8,128)S(1)}, f32[2,128,128]{2,1,0:T(8,128)S(1)}, u32[]{:S(2)}, u32[]{:S(2)}) collective-permute-start(f32[2,128,128]{2,1,0:T(8,128)S(1)} %add.18.after_ref), channel_id=1, source_target_pairs={{0,16},{4,12},{8,24},{12,4},{16,0},{20,28},{24,8},{28,20},{1,17},{... | collective-permute-start | bytes 393224 | tf_op jit(solution)/shard_map/ppermute | solution.py:336
  31.2 3.1 %collective-permute-start.7 = (f32[2,128,128]{2,1,0:T(8,128)S(1)}, f32[2,128,128]{2,1,0:T(8,128)S(1)}, u32[]{:S(2)}, u32[]{:S(2)}) collective-permute-start(f32[2,128,128]{2,1,0:T(8,128)S(1)} %add_multiply_fusion.rest_7_), channel_id=1, source_target_pairs={{0,4},{4,0},{8,12},{12,8},{16,20},{20,16},{24,28},{28,24},{1,5},{5... | collective-permute-start | bytes 393224 | tf_op jit(solution)/shard_map/ppermute | solution.py:232
  31.3 6.3 %collective-permute-start.6 = (f32[2,128,128]{2,1,0:T(8,128)S(1)}, f32[2,128,128]{2,1,0:T(8,128)S(1)}, u32[]{:S(2)}, u32[]{:S(2)}) collective-permute-start(f32[2,128,128]{2,1,0:T(8,128)S(1)} %add_multiply_fusion.rest_7_), channel_id=1, source_target_pairs={{0,1},{1,0},{2,3},{3,2},{4,6},{5,7},{6,4},{7,5},{8,9},{9,8},{10,11... | collective-permute-start | bytes 393224 | tf_op jit(solution)/shard_map/ppermute | solution.py:242
  33.6 5.0 %collective-permute-start.9 = (f32[2,128,128]{2,1,0:T(8,128)S(1)}, f32[2,128,128]{2,1,0:T(8,128)S(1)}, u32[]{:S(2)}, u32[]{:S(2)}) collective-permute-start(f32[2,128,128]{2,1,0:T(8,128)S(1)} %add_multiply_fusion.rest_7_), channel_id=1, source_target_pairs={{0,2},{1,3},{2,0},{3,1},{4,5},{5,4},{6,7},{7,6},{8,10},{9,11},{10,... | collective-permute-start | bytes 393224 | tf_op jit(solution)/shard_map/ppermute | solution.py:242
  38.5 1.3 %collective-permute-start.10 = (f32[2,128,128]{2,1,0:T(8,128)S(1)}, f32[2,128,128]{2,1,0:T(8,128)S(1)}, u32[]{:S(2)}, u32[]{:S(2)}) collective-permute-start(f32[2,128,128]{2,1,0:T(8,128)S(1)} %collective-permute-done.9.rest_16_), channel_id=1, source_target_pairs={{0,4},{4,0},{8,12},{12,8},{16,20},{20,16},{24,28},{28,24},{1,5},{5... | collective-permute-start | bytes 393224 | tf_op jit(solution)/shard_map/ppermute | solution.py:232
  38.5 1.5 %collective-permute-start.11 = (f32[2,128,128]{2,1,0:T(8,128)S(1)}, f32[2,128,128]{2,1,0:T(8,128)S(1)}, u32[]{:S(2)}, u32[]{:S(2)}) collective-permute-start(f32[2,128,128]{2,1,0:T(8,128)S(1)} %collective-permute-done.6.rest_14_), channel_id=1, source_target_pairs={{0,4},{4,0},{8,12},{12,8},{16,20},{20,16},{24,28},{28,24},{1,5},{5... | collective-permute-start | bytes 393224 | tf_op jit(solution)/shard_map/ppermute | solution.py:232
  39.1 5.0 %collective-permute-start.8 = (f32[2,128,128]{2,1,0:T(8,128)S(1)}, f32[2,128,128]{2,1,0:T(8,128)S(1)}, u32[]{:S(2)}, u32[]{:S(2)}) collective-permute-start(f32[2,128,128]{2,1,0:T(8,128)S(1)} %collective-permute-done.6.rest_14_), channel_id=1, source_target_pairs={{0,2},{1,3},{2,0},{3,1},{4,5},{5,4},{6,7},{7,6},{8,10},{9,11},{10,... | collective-permute-start | bytes 393224 | tf_op jit(solution)/shard_map/ppermute | solution.py:242
  44.0 1.3 %collective-permute-start.12 = (f32[2,128,128]{2,1,0:T(8,128)S(1)}, f32[2,128,128]{2,1,0:T(8,128)S(1)}, u32[]{:S(2)}, u32[]{:S(2)}) collective-permute-start(f32[2,128,128]{2,1,0:T(8,128)S(1)} %collective-permute-done.8.rest_7_), channel_id=1, source_target_pairs={{0,4},{4,0},{8,12},{12,8},{16,20},{20,16},{24,28},{28,24},{1,5},{5... | collective-permute-start | bytes 393224 | tf_op jit(solution)/shard_map/ppermute | solution.py:232

commit v4 on v3

v4 whole, which is shorter than its diff:
```python
import functools
import math

import jax
import jax.numpy as jnp
from jax import lax
from jax.experimental import pallas as pl
from jax.experimental.pallas import tpu as pltpu
from jax.sharding import PartitionSpec as P

F32, BF16 = jnp.float32, jnp.bfloat16
HALF_SIN = (4.442867755889893, -7.307443618774414, 3.594788074493408, -0.7843740582466125)
HALF_COS = (1.4142135381698608, -6.978850841522217, 5.7394609451293945, -1.8835630416870117, 0.31069818139076233)
VMEM = pl.BlockSpec(memory_space=pltpu.VMEM)
ANY = pl.BlockSpec(memory_space=pl.ANY)
PARAMS = pltpu.CompilerParams(vmem_limit_bytes=32 * 2**20)
NN, NT, TN = ((1,), (0,)), ((1,), (1,)), ((0,), (0,))


def halves(value):
    high = value.astype(BF16)
    return high, (value - high.astype(F32)).astype(BF16)


def dot16(left, right, dims):
    return lax.dot_general(left, right, (dims, ((), ())), preferred_element_type=F32)


def dot3(left, right, dims):
    left_high, left_low = halves(left)
    right_high, right_low = halves(right)
    return (
        dot16(left_high, right_high, dims)
        + dot16(left_low, right_high, dims)
        + dot16(left_high, right_low, dims)
    )


def horner(terms, square):
    total = terms[-1] * square + terms[-2]
    for term in terms[-3::-1]:
        total = total * square + term
    return total


def trig(columns, rows):
    turns = columns[0] * rows[0] + columns[1] * rows[1] + columns[2] * rows[2]
    turns = turns - jnp.round(turns)
    square = turns * turns
    half_sin = horner(HALF_SIN, square) * turns
    return 1.0 - half_sin * half_sin, half_sin * horner(HALF_COS, square)


def trig_blocks(k_ref, pos_ref, first, high_low, full=None):
    vectors, atoms = high_low[0].shape
    step = 32
    width = min(256, atoms)
    per_body = max(1, 2048 // atoms)
    per_body = min(per_body, vectors // step)

    def body(block, _):
        for inner in range(per_body):
            here = pl.ds(pl.multiple_of((block * per_body + inner) * step, step), step)
            columns = [k_ref[here, x : x + 1] for x in range(3)]
            for chunk in range(atoms // width):
                lanes = pl.ds(chunk * width, width)
                start = chunk * width if first is None else pl.multiple_of(first + chunk * width, 128)
                rows = [pos_ref[x : x + 1, pl.ds(start, width)] for x in range(3)]
                cos, sin = trig(columns, rows)
                high_low[0][here, lanes], high_low[1][here, lanes] = halves(cos)
                high_low[2][here, lanes], high_low[3][here, lanes] = halves(sin)
                if full is not None:
                    full[0][here, lanes], full[1][here, lanes] = cos, sin
        return 0

    lax.fori_loop(0, vectors // (step * per_body), body, 0)


def tile_kernel(pos_ref, lattice_ref, high_ref, low_ref, k_column, *, first):
    rows = k_column.shape[0]
    k_column[:, 0:3] = lattice_ref[:, first : first + rows].astype(F32).T
    cos, sin = pl.ds(0, rows), pl.ds(rows, rows)
    trig_blocks(k_column, pos_ref, None, (high_ref.at[cos], low_ref.at[cos], high_ref.at[sin], low_ref.at[sin]))


def sum_over_atoms(tiles, lanes, value):
    count = value.shape[0]
    high, low = halves(value)
    tiles_high = jnp.concatenate([tile[:, lanes] for tile in tiles[::2]], axis=0)
    tiles_low = jnp.concatenate([tile[:, lanes] for tile in tiles[1::2]], axis=0)
    wide = dot16(tiles_high, jnp.concatenate([high, low], axis=0), NT)
    return wide[:, :count] + wide[:, count:] + dot16(tiles_low, high, NT)


def arranged(sums):
    rows = sums.shape[0] // 4
    parts = [sums[n * rows : (n + 1) * rows] for n in range(4)]
    return jnp.concatenate([jnp.concatenate(parts[:2], axis=1), jnp.concatenate(parts[2:], axis=1)], axis=0)


def split_by_core(total, keep_ref, send_ref):
    rows = keep_ref.shape[0]
    core = lax.axis_index("atoms") % 2
    for flip, out in enumerate((keep_ref, send_ref)):
        out[...] = total[pl.ds(pl.multiple_of((core ^ flip) * rows, rows), rows), :]


def halves_of_atoms(groups, atoms):
    side = lax.axis_index("kvec") // (groups // 2)
    span = atoms // 2
    return [pl.ds(pl.multiple_of(at * span, span), span) for at in (side, 1 - side)]


def adjoint_of(cotangent_ref, offset, mask_ref, w_out_ref):
    share = cotangent_ref.shape[1]
    lanes = pl.ds(pl.multiple_of((lax.axis_index("kvec") ^ offset) * share, share), share)
    return lanes, mask_ref[:, lanes] * dot3(w_out_ref[...], cotangent_ref[...], NN)


def charge_kernel(pad_ref, feats_ref, species_ref, w_charge_ref, embed_ref, w_out_ref, *rest, groups):
    tiles, cotangents = rest[:4], rest[4 : 4 + groups // 2]
    keep_ref, send_ref, own_ref, mask_ref, part_ref, both, total = rest[4 + groups // 2 :]
    channels, atoms = feats_ref.shape
    embed_high, embed_low = halves(embed_ref[...])
    for block in range(atoms // 256):
        lanes = slice(block * 256, (block + 1) * 256)
        used = pad_ref[0:1, block : block + 1]
        mask = (lax.broadcasted_iota(jnp.int32, (1, 256), 1) < used).astype(F32)
        mask_ref[:, lanes] = mask
        species_at = lax.broadcasted_iota(jnp.int32, (embed_ref.shape[0], 256), 0)
        one_hot = (species_at == species_ref[:, lanes]).astype(BF16)
        both[0:channels, lanes] = mask * (
            dot3(w_charge_ref[...], feats_ref[:, lanes], TN)
            + dot16(embed_high, one_hot, TN)
            + dot16(embed_low, one_hot, TN)
        )
    for offset, cotangent in enumerate(cotangents):
        lanes, adjoint = adjoint_of(cotangent, offset, mask_ref, w_out_ref)
        both[channels:, lanes] = adjoint
        if offset == 0:
            own_ref[0:channels, :] = adjoint
            own_ref[channels : 2 * channels, :] = both[0:channels, lanes]
            own_ref[2 * channels :, :] = jnp.broadcast_to(mask_ref[:, lanes], (8, adjoint.shape[1]))
    near, far = halves_of_atoms(groups, atoms)
    sums = sum_over_atoms(tiles, near, both[:, near])
    total[...] = arranged(sums[:, :channels] + sum_over_atoms(tiles, far, both[0:channels, far]))
    split_by_core(total, keep_ref, send_ref)
    part_ref[...] = arranged(sums[:, channels:])


def adjoint_kernel(mask_ref, w_out_ref, part_ref, *rest, groups):
    tiles, cotangents = rest[:4], rest[4 : 4 + groups // 2]
    keep_ref, send_ref, adjoint_ref, total = rest[4 + groups // 2 :]
    for offset, cotangent in enumerate(cotangents):
        lanes, adjoint = adjoint_of(cotangent, groups // 2 + offset, mask_ref, w_out_ref)
        adjoint_ref[:, lanes] = adjoint
    _, far = halves_of_atoms(groups, adjoint_ref.shape[1])
    total[...] = part_ref[...] + arranged(sum_over_atoms(tiles, far, adjoint_ref[:, far]))
    split_by_core(total, keep_ref, send_ref)


def wave_kernel(pos_ref, lattice_ref, width_ref, after_ref, *rest, atom_total):
    *gain_ref, cos, sin, cos_high, cos_low, sin_high, sin_low, k_ref, k_column = rest
    vectors = cos.shape[0]
    rows = vectors // 2
    core = lax.axis_index("atoms") % 2
    k_column[:, 0:3] = lattice_ref[...].astype(F32).T
    for flip in range(2):
        start = pl.multiple_of((core ^ flip) * rows, rows)
        k_ref[flip * rows : (flip + 1) * rows, :] = k_column[pl.ds(start, rows), :]
    if gain_ref:
        waves = [2.0 * math.pi * k_ref[0:rows, x : x + 1] for x in range(3)]
        square = waves[0] * waves[0] + waves[1] * waves[1] + waves[2] * waves[2]
        gain = jnp.exp(-square * width_ref[...]) * 40.0 / (square + 40.0) / math.sqrt(atom_total)
        gain_ref[0][...] = jnp.concatenate([gain, gain], axis=1)
    first = lax.axis_index("kvec") * cos.shape[1]
    trig_blocks(k_ref, pos_ref, first, (cos_high, cos_low, sin_high, sin_low), (cos, sin))


def coefficient_stack(near_ref, far_ref, part):
    channels = near_ref.shape[2] // 2
    lanes = slice(part * channels, (part + 1) * channels)
    sides = [jnp.concatenate([side[0, :, lanes], side[1, :, lanes]], axis=1) for side in (near_ref, far_ref)]
    high, low = halves(jnp.concatenate(sides, axis=0))
    return jnp.concatenate([high, low, high], axis=1)


def own_stack(own_ref, channels):
    high, low = halves(own_ref[0 : 2 * channels, :])
    return jnp.concatenate([high, high, low], axis=0)


def add_field(stack, tile_high, tile_low):
    width = stack.shape[1] // 3
    wide = dot16(stack[:, : 2 * width], tile_high, TN)
    return wide[:width] + wide[width:] + dot16(stack[:, :width], tile_low, TN)


def add_force(sums, wave, along, first):
    step = 16
    cos, sin, _, _, _, _, k_ref = wave
    for start in range(0, cos.shape[0], step):
        here = slice(start, start + step)
        there = slice(first + start, first + start + step)
        slope = cos[here, :] * along[1, there, :] - sin[here, :] * along[0, there, :]
        for x in range(3):
            term = k_ref[here, x : x + 1] * slope
            sums[x] = sums[x] + (term[0:8] + term[8:16])
    return sums


def fields(own_ref, waves, coefs, channels, along, field, sums):
    other = own_stack(own_ref, channels)
    coefs = [coefs[at : at + 2] for at in range(0, len(coefs), 2)]
    parts = [[coefficient_stack(*pair, part) for pair in coefs] for part in range(2)]
    for part in range(2):
        along[part] = dot16(jnp.concatenate(parts[part], axis=0), other, NN)
    waves = [waves[at : at + 7] for at in range(0, len(waves), 7)]
    for group, wave in enumerate(waves):
        _, _, cos_high, cos_low, sin_high, sin_low, _ = wave
        for part, high, low in ((parts[0], cos_high, cos_low), (parts[1], sin_high, sin_low)):
            added = add_field(part[group], high[...], low[...])
            field = added if field is None else field + added
    for group, wave in enumerate(waves):
        sums = add_force(sums, wave, along, group * wave[0].shape[0])
    return field, sums


def partial_field_kernel(own_ref, *rest, groups, first):
    waves, coefs, before = rest[: 7 * groups], rest[7 * groups : 9 * groups], rest[9 * groups : -3]
    field_ref, sums_ref, along = rest[-3:]
    share = own_ref.shape[1]
    if first:
        field, sums = None, [jnp.zeros((8, share), F32)] * 3
    else:
        field, sums = before[0][...], [before[1][8 * x : 8 * x + 8, :] for x in range(3)]
    field, sums = fields(own_ref, waves, coefs, coefs[0].shape[2] // 2, along, field, sums)
    field_ref[...] = field
    for x in range(3):
        sums_ref[8 * x : 8 * x + 8, :] = sums[x]


def field_kernel(own_ref, w_out_ref, w_charge_ref, *rest, groups):
    waves, coefs = rest[: 7 * groups], rest[7 * groups : 9 * groups]
    field_ref, sums_ref, message_ref, force_ref, grad_ref, along = rest[9 * groups :]
    channels = w_out_ref.shape[0]
    sums = [sums_ref[8 * x : 8 * x + 8, :] for x in range(3)]
    field, sums = fields(own_ref, waves, coefs, channels, along, field_ref[...], sums)
    field = own_ref[2 * channels : 2 * channels + 1, :] * field
    message_ref[...] = dot3(w_out_ref[...], field[:channels], TN)
    grad_ref[...] = dot3(w_charge_ref[...], field[channels:], NN)
    for x in range(3):
        force_ref[x : x + 1, :] = 2.0 * math.pi * jnp.sum(sums[x], axis=0, keepdims=True)


def swap(value, axis, offset):
    size = lax.axis_size(axis)
    return lax.ppermute(value, axis, [(place, place ^ offset) for place in range(size)])


def swap_along_z(value, even, odd):
    pairs = [(place, place ^ (odd if place % 2 else even)) for place in range(lax.axis_size("atoms"))]
    return lax.ppermute(value, "atoms", pairs)


def cost(work):
    return pl.CostEstimate(flops=work, bytes_accessed=0, transcendentals=0)


def on_device(
    positions, feats, species, pad_count, k_lattice, filter_width, w_charge, species_embed, w_out, grad_out,
):
    atom_count, group_count = lax.axis_size("atoms"), lax.axis_size("kvec")
    channels, atoms = feats.shape
    share = grad_out.shape[1]
    vectors = k_lattice.shape[1]
    half = vectors // 2
    both = 2 * channels
    f32 = lambda *shape: jax.ShapeDtypeStruct(shape, F32)
    bf16 = lambda *shape: jax.ShapeDtypeStruct(shape, BF16)

    def planes(value):
        return [swap(value, "kvec", m) for m in range(group_count - 1, 0, -1)][::-1]

    cotangents = [grad_out] + planes(grad_out)

    tiles = []
    for part in range(2):
        tiles += pl.pallas_call(
            functools.partial(tile_kernel, first=part * half),
            out_shape=[bf16(vectors, atoms)] * 2,
            in_specs=[VMEM] * 2,
            out_specs=[VMEM] * 2,
            scratch_shapes=[pltpu.VMEM((half, 128), F32)],
            compiler_params=PARAMS,
            cost_estimate=cost(9000 * half * atoms),
            name="waves_of_own_vectors",
        )(positions, k_lattice)

    middle = group_count // 2
    keep_h, send_h, own, mask, part = pl.pallas_call(
        functools.partial(charge_kernel, groups=group_count),
        out_shape=[f32(half, both)] * 2 + [f32(both + 8, share), f32(1, atoms), f32(vectors, both)],
        in_specs=[VMEM] * (10 + middle),
        out_specs=[VMEM] * 5,
        scratch_shapes=[pltpu.VMEM((both, atoms), F32), pltpu.VMEM((vectors, both), F32)],
        compiler_params=PARAMS,
        cost_estimate=cost(60 * vectors * atoms * channels),
        name="charge_sums",
    )(
        pad_count.reshape(1, -1), feats, species.reshape(1, atoms), w_charge, species_embed.T, w_out,
        *tiles, *cotangents[:middle],
    )

    wave_shapes = [f32(vectors, share)] * 2 + [bf16(vectors, share)] * 4 + [f32(vectors, 128)]

    def waves_of(group, after):
        shapes = ([f32(half, both)] if group == 0 else []) + wave_shapes
        made = pl.pallas_call(
            functools.partial(wave_kernel, atom_total=atoms * atom_count),
            out_shape=shapes,
            in_specs=[VMEM, VMEM, VMEM, ANY],
            out_specs=[VMEM] * len(shapes),
            scratch_shapes=[pltpu.VMEM((vectors, 128), F32)],
            compiler_params=PARAMS,
            cost_estimate=cost(20 * vectors * share),
            name="waves_of_own_atoms",
        )(positions, lattices[group], filter_width.reshape(1, channels), after)
        return list(made)

    arrived_h = swap(send_h, "atoms", 1)
    keep_b, send_b = pl.pallas_call(
        functools.partial(adjoint_kernel, groups=group_count),
        out_shape=[f32(half, both)] * 2,
        in_specs=[VMEM] * (7 + middle),
        out_specs=[VMEM] * 2,
        scratch_shapes=[pltpu.VMEM((channels, atoms), F32), pltpu.VMEM((vectors, both), F32)],
        compiler_params=PARAMS,
        cost_estimate=cost(60 * vectors * atoms * channels),
        name="adjoint_sums",
    )(mask, w_out, part, *tiles, *cotangents[middle:])

    arrived_h, send_b = lax.optimization_barrier((arrived_h, send_b))
    arrived_b = swap(send_b, "atoms", 1)
    sum_h = keep_h + arrived_h
    steps = [2 << n for n in range((atom_count // 2).bit_length() - 1)]
    next_h = swap_along_z(sum_h, steps[0], steps[-1])
    arrived_b, sum_h = lax.optimization_barrier((arrived_b, sum_h))
    sum_b = keep_b + arrived_b
    next_b = swap_along_z(sum_b, steps[0], steps[-1])

    next_h, next_b = lax.optimization_barrier((next_h, next_b))
    total = jnp.stack([sum_h + next_h, sum_b + next_b])
    lattices, waves = [k_lattice], []
    for step in zip(steps[1:], steps[-2::-1]):
        arrived = swap_along_z(total, *step)
        if not waves:
            gain, *made = waves_of(0, total)
            held, made = lax.optimization_barrier((k_lattice, made))
            lattices += planes(held)
            waves = [made, waves_of(1, total)]
            arrived, gain, waves, lattices = lax.optimization_barrier((arrived, gain, waves, lattices))
        total = total + arrived
    near = gain[None] * total
    plane = {0: near}
    for group in range(group_count - 1, 0, -1):
        plane[group] = swap(near, "kvec", group)
    waves += [waves_of(group, near) for group in range(2, group_count)]
    far = {0: swap(near, "atoms", 1)}

    def partial_fields(groups, before):
        count = len(groups)
        coefs = [part[g] for g in groups for part in (plane, far)]
        group_waves = [wave for g in groups for wave in waves[g]]
        return pl.pallas_call(
            functools.partial(partial_field_kernel, groups=count, first=not before),
            out_shape=[f32(both, share), f32(24, share)],
            in_specs=[VMEM] * (1 + 9 * count + len(before)),
            out_specs=[VMEM] * 2,
            scratch_shapes=[pltpu.VMEM((2, count * vectors, share), F32)],
            compiler_params=PARAMS,
            cost_estimate=cost(count * vectors * share),
            name="fields_of_some_groups",
        )(own, *group_waves, *coefs, *before)

    fields_so_far = partial_fields([0], [])
    waves, fields_so_far = lax.optimization_barrier((waves, fields_so_far))
    for group in range(group_count - 1, 0, -1):
        plane[group], fields_so_far = lax.optimization_barrier((plane[group], fields_so_far))
        far[group] = swap(plane[group], "atoms", 1)
    late = [2, 1] if group_count > 3 else [1]
    fields_so_far = partial_fields(list(range(group_count - 1, len(late), -1)), fields_so_far)
    late_operands = [wave for g in late for wave in waves[g]] + [part[g] for g in late for part in (plane, far)]

    return tuple(
        pl.pallas_call(
            functools.partial(field_kernel, groups=len(late)),
            out_shape=[f32(channels, share), f32(3, share), f32(channels, share)],
            in_specs=[VMEM] * (5 + 9 * len(late)),
            out_specs=[VMEM] * 3,
            scratch_shapes=[pltpu.VMEM((2, len(late) * vectors, share), F32)],
            compiler_params=PARAMS,
            cost_estimate=cost(vectors * share),
            name="fields_and_forces",
        )(
            own, w_out, w_charge, *late_operands, *fields_so_far
        )
    )


def solution(mesh):
    shared = P(None, ("atoms", "kvec"))
    placed = (
        P(None, "atoms"), P(None, "atoms"), P("atoms"), P("atoms"), P(None, "kvec"),
        P(), P(), P(), P(), shared,
    )
    return jax.shard_map(
        on_device, mesh=mesh, in_specs=placed, out_specs=(shared, shared, shared), check_vma=False
    )
```

time: 47.2 us -> 45.7 us (0.968)
  waiting for transfers between devices: 15.7 us -> 9.57 us
  starting transfers between devices: 15.5 us -> 18.8 us
  Pallas kernels: 12.9 us -> 14 us
  other arithmetic: 0.99 us -> 0.07 us
  local copies, waits for them, and re-layouts: 1.22 us -> 2.12 us
    ppermute x5 -> x15, starting transfers between devices: 0.65 us -> 12.8 us  [swap(): lax.ppermute(value, axis, [(place, place ^ offset) for place in range(siz...]
    ppermute x8 -> x3, waiting for transfers between devices: 14 us -> 3.45 us  [swap_along_z(): return lax.ppermute(value, 'atoms', pairs)]
    ppermute x8 -> x3, starting transfers between devices: 14.8 us -> 6.02 us  [swap_along_z(): return lax.ppermute(value, 'atoms', pairs)]
    ppermute x5 -> x15, waiting for transfers between devices: 1.63 us -> 6.12 us  [swap(): lax.ppermute(value, axis, [(place, place ^ offset) for place in range(siz...]
    pallas_call x6 -> x7, Pallas kernels: 9.12 us -> 10.2 us  [the longest x2 3.15 us: on_device(): pl.pallas_call(functools.partial(tile_kernel, first=part * half), out_sha...]
    add x3 -> x2, other arithmetic: 0.97 us -> 0.02 us  [the longest x1 0.01 us: on_device(): sum_h = keep_h + arrived_h]
    unnamed x16 -> x24, local copies, waits for them, and re-layouts: 1.22 us -> 2.12 us
  transfers between devices with their start and end apart: 13 -> 18, of which waited for: 10 -> 10; matrix products, arithmetic and copies ran while one was open for 0% -> 0% of each run, Pallas kernels for 19% -> 26%
where the time goes in v4:
time: 45.7 us; the launch traced here: 45.4 us
  starting transfers between devices  18.8 us (41%)
  Pallas kernels  14 us (31%)
  waiting for transfers between devices  9.57 us (21%)
  local copies, waits for them, and re-layouts  2.12 us (5%)
  between operations  0.91 us (2%)
    ppermute x15, starting transfers between devices, swap(): lax.ppermute(value, axis, [(place, place ^ offset) for place in range(siz...  12.8 us
    ppermute x15, waiting for transfers between devices, swap(): lax.ppermute(value, axis, [(place, place ^ offset) for place in range(siz...  6.12 us
    ppermute x3, starting transfers between devices, swap_along_z(): return lax.ppermute(value, 'atoms', pairs)  6.02 us
    pallas_call x4, Pallas kernels, waves_of(): pl.pallas_call(functools.partial(wave_kernel, atom_total=atoms * atom_cou...  3.77 us
    ppermute x3, waiting for transfers between devices, swap_along_z(): return lax.ppermute(value, 'atoms', pairs)  3.45 us
    pallas_call x2, Pallas kernels, on_device(): pl.pallas_call(functools.partial(tile_kernel, first=part * half), out_sha...  3.15 us
    pallas_call x1, Pallas kernels, on_device(): pl.pallas_call(functools.partial(field_kernel, groups=len(late)), out_sha...  2.33 us
    unnamed x24, local copies, waits for them, and re-layouts  2.12 us
  transfers between devices with their start and end apart: 18, of which 10 were waited for; matrix products, arithmetic and copies ran while one was open for 0% of the time, Pallas kernels for 26%

profile of v4, /device:TPU:0, one launch (start us, length us, event | category | flops | bytes accessed | tf_op | source)
XLA Modules:
  0.0 45.4 jit_solution(3152876659100525313)
XLA Ops:
  0.6 3.0 %collective-permute-start = (f32[64,512]{1,0:T(8,128)}, f32[64,512]{1,0:T(8,128)S(1)}, u32[]{:S(2)}, u32[]{:S(2)}) collective-permute-start(f32[64,512]{1,0:T(8,128)} %rest_4_.1), channel_id=1, source_target_pairs={{0,1},{1,0},{2,3},{3,2},{4,5},{5,4},{6,7},{7,6},{8,9},{9,8},{10,11... | collective-permute-start | bytes 393224 | tf_op jit(solution)/shard_map/ppermute | solution.py:258
  3.6 1.5 %collective-permute-start.2 = (f32[64,512]{1,0:T(8,128)}, f32[64,512]{1,0:T(8,128)S(1)}, u32[]{:S(2)}, u32[]{:S(2)}) collective-permute-start(f32[64,512]{1,0:T(8,128)} %rest_4_.1), channel_id=1, source_target_pairs={{0,2},{1,3},{2,0},{3,1},{4,6},{5,7},{6,4},{7,5},{8,10},{9,11},{10,... | collective-permute-start | bytes 393224 | tf_op jit(solution)/shard_map/ppermute | solution.py:258
  5.2 0.8 %copy-done = f32[3,2048]{1,0:T(4,128)S(1)} copy-done((f32[3,2048]{1,0:T(4,128)S(1)}, f32[3,2048]{1,0:T(4,128)}, u32[]{:S(2)}) %copy-start) | copy-done | bytes 24600
  6.6 1.6 %waves_of_own_vectors.2 = (bf16[256,2048]{1,0:T(8,128)(2,1)S(1)}, bf16[256,2048]{1,0:T(8,128)(2,1)S(1)}) custom-call(f32[3,2048]{1,0:T(4,128)S(1)} %copy-done, s32[3,256]{1,0:T(4,128)S(1)} %copy-done.5), custom_call_target="tpu_custom_call" | custom-call | flops 2359296000 | tf_op jit(solution)/shard_map/waves_of_own_vectors/pallas_call | solution.py:289
  8.3 1.6 %waves_of_own_vectors.3 = (bf16[256,2048]{1,0:T(8,128)(2,1)S(1)}, bf16[256,2048]{1,0:T(8,128)(2,1)S(1)}) custom-call(f32[3,2048]{1,0:T(4,128)S(1)} %copy-done, s32[3,256]{1,0:T(4,128)S(1)} %copy-done.5), custom_call_target="tpu_custom_call" | custom-call | flops 2359296000 | tf_op jit(solution)/shard_map/waves_of_own_vectors/pallas_call | solution.py:289
  10.6 2.1 %charge_sums.1 = (f32[128,128]{1,0:T(8,128)S(1)}, f32[128,128]{1,0:T(8,128)S(1)}, f32[136,512]{1,0:T(8,128)S(1)}, f32[1,2048]{1,0:T(1,128)S(1)}, f32[256,128]{1,0:T(8,128)S(1)}) custom-call(s32[1,8]{1,0:T(1,128)S(1)} %bitcast.14, f32[64,2048]{1,0:T(8,128)S(1)} %copy-done.7, s32[1,2048]{1,0:T(1,128)S(1)} %bitcast.12, f32[64,64]{1,0:T(8,128)S(1)} %copy-done.2, ...), custom_call_target="tpu_custom_call" | custom-call | flops 2013265920 | tf_op jit(solution)/shard_map/charge_sums/pallas_call | solution.py:301
  12.8 1.1 %adjoint_sums.1 = (f32[128,128]{1,0:T(8,128)S(1)}, f32[128,128]{1,0:T(8,128)S(1)}) custom-call(f32[1,2048]{1,0:T(1,128)S(1)} %get-tuple-element.117.mask_ref, f32[64,64]{1,0:T(8,128)S(1)} %copy-done.3, f32[256,128]{1,0:T(8,128)S(1)} %get-tuple-element.118.part_ref, bf16[256,2048]{1,0:T(8,128)(2,1)S(1)} %get-tuple-element.111.rest_0_, ...), custom_call_target="tpu_custom_call" | custom-call | flops 2013265920 | tf_op jit(solution)/shard_map/adjoint_sums/pallas_call | solution.py:332
  14.5 2.1 %collective-permute-start.5 = (f32[128,128]{1,0:T(8,128)S(1)}, f32[128,128]{1,0:T(8,128)S(1)}, u32[]{:S(2)}, u32[]{:S(2)}) collective-permute-start(f32[128,128]{1,0:T(8,128)S(1)} %add.15), channel_id=1, source_target_pairs={{0,8},{4,20},{8,0},{12,28},{16,24},{20,4},{24,16},{28,12},{1,9},{5... | collective-permute-start | bytes 196616 | tf_op jit(solution)/shard_map/ppermute | solution.py:263
  16.6 0.9 %collective-permute-start.6 = (f32[128,128]{1,0:T(8,128)S(1)}, f32[128,128]{1,0:T(8,128)S(1)}, u32[]{:S(2)}, u32[]{:S(2)}) collective-permute-start(f32[128,128]{1,0:T(8,128)S(1)} %add.16), channel_id=1, source_target_pairs={{0,8},{4,20},{8,0},{12,28},{16,24},{20,4},{24,16},{28,12},{1,9},{5... | collective-permute-start | bytes 196616 | tf_op jit(solution)/shard_map/ppermute | solution.py:263
  17.5 2.0 %collective-permute-done.5 = f32[128,128]{1,0:T(8,128)S(1)} collective-permute-done((f32[128,128]{1,0:T(8,128)S(1)}, f32[128,128]{1,0:T(8,128)S(1)}, u32[]{:S(2)}, u32[]{:S(2)}) %collective-permute-start.5) | collective-permute-done | bytes 65568 | tf_op jit(solution)/shard_map/ppermute | solution.py:263
  19.5 1.4 %collective-permute-done.6 = f32[128,128]{1,0:T(8,128)S(1)} collective-permute-done((f32[128,128]{1,0:T(8,128)S(1)}, f32[128,128]{1,0:T(8,128)S(1)}, u32[]{:S(2)}, u32[]{:S(2)}) %collective-permute-start.6) | collective-permute-done | bytes 65568 | tf_op jit(solution)/shard_map/ppermute | solution.py:263
  21.0 3.1 %collective-permute-start.7 = (f32[2,128,128]{2,1,0:T(8,128)S(1)}, f32[2,128,128]{2,1,0:T(8,128)S(1)}, u32[]{:S(2)}, u32[]{:S(2)}) collective-permute-start(f32[2,128,128]{2,1,0:T(8,128)S(1)} %pad_maximum_fusion.after_ref), channel_id=1, source_target_pairs={{0,16},{4,12},{8,24},{12,4},{16,0},{20,28},{24,8},{28,20},{1,17},{... | collective-permute-start | bytes 393224 | tf_op jit(solution)/shard_map/ppermute | solution.py:263
  24.0 1.1 %waves_of_own_atoms.4 = (f32[128,128]{1,0:T(8,128)S(1)}, f32[256,512]{1,0:T(8,128)S(1)}, f32[256,512]{1,0:T(8,128)S(1)}, bf16[256,512]{1,0:T(8,128)(2,1)S(1)}, b...) custom-call(f32[3,2048]{1,0:T(4,128)S(1)} %copy-done.1, ...), custom_call_target="tpu_custom_call" | custom-call | flops 2621440 | tf_op jit(solution)/shard_map/waves_of_own_atoms/pallas_call | solution.py:319
  25.2 1.5 %collective-permute-start.8 = (s32[3,256]{1,0:T(4,128)S(1)}, s32[3,256]{1,0:T(4,128)S(1)}, u32[]{:S(2)}, u32[]{:S(2)}) collective-permute-start(s32[3,256]{1,0:T(4,128)S(1)} %copy-done.6), channel_id=1, source_target_pairs={{0,1},{1,0},{2,3},{3,2},{4,5},{5,4},{6,7},{7,6},{8,9},{9,8},{10,11... | collective-permute-start | bytes 9224 | tf_op jit(solution)/shard_map/ppermute | solution.py:258
  26.7 1.5 %collective-permute-start.10 = (s32[3,256]{1,0:T(4,128)S(1)}, s32[3,256]{1,0:T(4,128)S(1)}, u32[]{:S(2)}, u32[]{:S(2)}) collective-permute-start(s32[3,256]{1,0:T(4,128)S(1)} %copy-done.6), channel_id=1, source_target_pairs={{0,3},{1,2},{2,1},{3,0},{4,7},{5,6},{6,5},{7,4},{8,11},{9,10},{10,... | collective-permute-start | bytes 9224 | tf_op jit(solution)/shard_map/ppermute | solution.py:258
  28.9 0.9 %waves_of_own_atoms.5 = (f32[256,512]{1,0:T(8,128)S(1)}, f32[256,512]{1,0:T(8,128)S(1)}, bf16[256,512]{1,0:T(8,128)(2,1)S(1)}, bf16[256,512]{1,0:T(8,128)(2,1)S(...) custom-call(f32[3,2048]{1,0:T(4,128)S(1)} %copy-done.1, ...), custom_call_target="tpu_custom_call" | custom-call | flops 2621440 | tf_op jit(solution)/shard_map/waves_of_own_atoms/pallas_call | solution.py:319
  29.7 1.5 %collective-permute-done.10.lattice_ref = s32[3,256]{1,0:T(4,128)S(1)} collective-permute-done((s32[3,256]{1,0:T(4,128)S(1)}, s32[3,256]{1,0:T(4,128)S(1)}, u32[]{:S(2)}, u32[]{:S(2)}) %collective-permute-start.10) | collective-permute-done | bytes 3104 | tf_op jit(solution)/shard_map/ppermute | solution.py:258
  31.9 1.5 %collective-permute-start.13 = (f32[2,128,128]{2,1,0:T(8,128)S(1)}, f32[2,128,128]{2,1,0:T(8,128)S(1)}, u32[]{:S(2)}, u32[]{:S(2)}) collective-permute-start(f32[2,128,128]{2,1,0:T(8,128)S(1)} %add_multiply_fusion.after_ref.rest_7_), channel_id=1, source_target_pairs={{0,3},{1,2},{2,1},{3,0},{4,7},{5,6},{6,5},{7,4},{8,11},{9,10},{10,... | collective-permute-start | bytes 393224 | tf_op jit(solution)/shard_map/ppermute | solution.py:258
  33.4 1.5 %collective-permute-start.12 = (f32[2,128,128]{2,1,0:T(8,128)S(1)}, f32[2,128,128]{2,1,0:T(8,128)S(1)}, u32[]{:S(2)}, u32[]{:S(2)}) collective-permute-start(f32[2,128,128]{2,1,0:T(8,128)S(1)} %add_multiply_fusion.after_ref.rest_7_), channel_id=1, source_target_pairs={{0,2},{1,3},{2,0},{3,1},{4,6},{5,7},{6,4},{7,5},{8,10},{9,11},{10,... | collective-permute-start | bytes 393224 | tf_op jit(solution)/shard_map/ppermute | solution.py:258
  35.5 0.9 %waves_of_own_atoms.7 = (f32[256,512]{1,0:T(8,128)S(1)}, f32[256,512]{1,0:T(8,128)S(1)}, bf16[256,512]{1,0:T(8,128)(2,1)S(1)}, bf16[256,512]{1,0:T(8,128)(2,1)S(...) custom-call(f32[3,2048]{1,0:T(4,128)S(1)} %copy-done.1, ...), custom_call_target="tpu_custom_call" | custom-call | flops 2621440 | tf_op jit(solution)/shard_map/waves_of_own_atoms/pallas_call | solution.py:319
  36.4 0.9 %waves_of_own_atoms.6 = (f32[256,512]{1,0:T(8,128)S(1)}, f32[256,512]{1,0:T(8,128)S(1)}, bf16[256,512]{1,0:T(8,128)(2,1)S(1)}, bf16[256,512]{1,0:T(8,128)(2,1)S(...) custom-call(f32[3,2048]{1,0:T(4,128)S(1)} %copy-done.1, ...), custom_call_target="tpu_custom_call" | custom-call | flops 2621440 | tf_op jit(solution)/shard_map/waves_of_own_atoms/pallas_call | solution.py:319
  38.0 1.2 %collective-permute-done.13.rest_7_ = f32[2,128,128]{2,1,0:T(8,128)S(1)} collective-permute-done((f32[2,128,128]{2,1,0:T(8,128)S(1)}, f32[2,128,128]{2,1,0:T(8,128)S(1)}, u32[]{:S(2)}, u32[]{:S(2)}) %collective-permute-start.13) | collective-permute-done | bytes 131104 | tf_op jit(solution)/shard_map/ppermute | solution.py:258
  39.3 2.3 %collective-permute-done.12.rest_14_ = f32[2,128,128]{2,1,0:T(8,128)S(1)} collective-permute-done((f32[2,128,128]{2,1,0:T(8,128)S(1)}, f32[2,128,128]{2,1,0:T(8,128)S(1)}, u32[]{:S(2)}, u32[]{:S(2)}) %collective-permute-start.12) | collective-permute-done | bytes 131104 | tf_op jit(solution)/shard_map/ppermute | solution.py:258
  43.1 2.3 %fields_and_forces.1 = (f32[64,512]{1,0:T(8,128)}, f32[3,512]{1,0:T(4,128)}, f32[64,512]{1,0:T(8,128)}) custom-call(f32[136,512]{1,0:T(8,128)S(1)} %get-tuple-element.115.own_ref, f32[64,64]{1,0:T(8,128)S(1)} %copy-done.3, f32[64,64]{1,0:T(8,128)S(1)} %copy-done.2, f32[256,512]{1,0:T(8,128)S(1)} %get-tuple-element.185.rest_0_, ...), custom_call_target="tpu_custom_call" | custom-call | flops 131072 | tf_op jit(solution)/shard_map/fields_and_forces/pallas_call | solution.py:396
  (52 shorter events, 6.2 us)
Async XLA Ops:
  0.6 9.2 %collective-permute-start = (f32[64,512]{1,0:T(8,128)}, f32[64,512]{1,0:T(8,128)S(1)}, u32[]{:S(2)}, u32[]{:S(2)}) collective-permute-start(f32[64,512]{1,0:T(8,128)} %rest_4_.1), channel_id=1, source_target_pairs={{0,1},{1,0},{2,3},{3,2},{4,5},{5,4},{6,7},{7,6},{8,9},{9,8},{10,11... | collective-permute-start | bytes 393224 | tf_op jit(solution)/shard_map/ppermute | solution.py:258
  3.6 9.1 %collective-permute-start.2 = (f32[64,512]{1,0:T(8,128)}, f32[64,512]{1,0:T(8,128)S(1)}, u32[]{:S(2)}, u32[]{:S(2)}) collective-permute-start(f32[64,512]{1,0:T(8,128)} %rest_4_.1), channel_id=1, source_target_pairs={{0,2},{1,3},{2,0},{3,1},{4,6},{5,7},{6,4},{7,5},{8,10},{9,11},{10,... | collective-permute-start | bytes 393224 | tf_op jit(solution)/shard_map/ppermute | solution.py:258
  5.2 7.6 %collective-permute-start.3 = (f32[64,512]{1,0:T(8,128)}, f32[64,512]{1,0:T(8,128)S(1)}, u32[]{:S(2)}, u32[]{:S(2)}) collective-permute-start(f32[64,512]{1,0:T(8,128)} %rest_4_.1), channel_id=1, source_target_pairs={{0,3},{1,2},{2,1},{3,0},{4,7},{5,6},{6,5},{7,4},{8,11},{9,10},{10,... | collective-permute-start | bytes 393224 | tf_op jit(solution)/shard_map/ppermute | solution.py:258
  8.2 1.7 %copy-start.2 = (f32[64,64]{1,0:T(8,128)S(1)}, f32[64,64]{1,0:T(8,128)}, u32[]{:S(2)}) copy-start(f32[64,64]{1,0:T(8,128)} %w_charge_ref.3) | copy-start | bytes 49156
  8.2 1.7 %copy-start.3 = (f32[64,64]{1,0:T(8,128)S(1)}, f32[64,64]{1,0:T(8,128)}, u32[]{:S(2)}) copy-start(f32[64,64]{1,0:T(8,128)} %w_out_ref.5) | copy-start | bytes 49156
  8.2 1.7 %copy-start.7 = (f32[64,2048]{1,0:T(8,128)S(1)}, f32[64,2048]{1,0:T(8,128)}, u32[]{:S(2)}) copy-start(f32[64,2048]{1,0:T(8,128)} %feats_ref.1) | copy-start | bytes 1572868
  12.7 1.3 %collective-permute-start.1 = (f32[128,128]{1,0:T(8,128)S(1)}, f32[128,128]{1,0:T(8,128)S(1)}, u32[]{:S(2)}, u32[]{:S(2)}) collective-permute-start(f32[128,128]{1,0:T(8,128)S(1)} %get-tuple-element.116), channel_id=1, source_target_pairs={{0,4},{4,0},{8,12},{12,8},{16,20},{20,16},{24,28},{28,24},{1,5},{5... | collective-permute-start | bytes 196616 | tf_op jit(solution)/shard_map/ppermute | solution.py:258
  14.0 2.6 %collective-permute-start.4 = (f32[128,128]{1,0:T(8,128)S(1)}, f32[128,128]{1,0:T(8,128)S(1)}, u32[]{:S(2)}, u32[]{:S(2)}) collective-permute-start(f32[128,128]{1,0:T(8,128)S(1)} %get-tuple-element.120), channel_id=1, source_target_pairs={{0,4},{4,0},{8,12},{12,8},{16,20},{20,16},{24,28},{28,24},{1,5},{5... | collective-permute-start | bytes 196616 | tf_op jit(solution)/shard_map/ppermute | solution.py:258
  14.5 5.0 %collective-permute-start.5 = (f32[128,128]{1,0:T(8,128)S(1)}, f32[128,128]{1,0:T(8,128)S(1)}, u32[]{:S(2)}, u32[]{:S(2)}) collective-permute-start(f32[128,128]{1,0:T(8,128)S(1)} %add.15), channel_id=1, source_target_pairs={{0,8},{4,20},{8,0},{12,28},{16,24},{20,4},{24,16},{28,12},{1,9},{5... | collective-permute-start | bytes 196616 | tf_op jit(solution)/shard_map/ppermute | solution.py:263
  16.6 4.3 %collective-permute-start.6 = (f32[128,128]{1,0:T(8,128)S(1)}, f32[128,128]{1,0:T(8,128)S(1)}, u32[]{:S(2)}, u32[]{:S(2)}) collective-permute-start(f32[128,128]{1,0:T(8,128)S(1)} %add.16), channel_id=1, source_target_pairs={{0,8},{4,20},{8,0},{12,28},{16,24},{20,4},{24,16},{28,12},{1,9},{5... | collective-permute-start | bytes 196616 | tf_op jit(solution)/shard_map/ppermute | solution.py:263
  20.9 3.1 %copy-start.1 = (f32[3,2048]{1,0:T(4,128)S(1)}, f32[3,2048]{1,0:T(4,128)}, u32[]{:S(2)}) copy-start(f32[3,2048]{1,0:T(4,128)} %pos_ref.11) | copy-start | bytes 73732
  20.9 3.1 %copy-start.6 = (s32[3,256]{1,0:T(4,128)S(1)}, s32[3,256]{1,0:T(4,128)}, u32[]{:S(2)}) copy-start(s32[3,256]{1,0:T(4,128)} %lattice_ref.5) | copy-start | bytes 9220
  21.0 3.1 %copy-start.4 = (f32[64]{0:T(128)S(1)}, f32[64]{0:T(128)}, u32[]{:S(2)}) copy-start(f32[64]{0:T(128)} %param.15) | copy-start | bytes 772
  21.0 10.9 %collective-permute-start.7 = (f32[2,128,128]{2,1,0:T(8,128)S(1)}, f32[2,128,128]{2,1,0:T(8,128)S(1)}, u32[]{:S(2)}, u32[]{:S(2)}) collective-permute-start(f32[2,128,128]{2,1,0:T(8,128)S(1)} %pad_maximum_fusion.after_ref), channel_id=1, source_target_pairs={{0,16},{4,12},{8,24},{12,4},{16,0},{20,28},{24,8},{28,20},{1,17},{... | collective-permute-start | bytes 393224 | tf_op jit(solution)/shard_map/ppermute | solution.py:263
  25.2 3.7 %collective-permute-start.8 = (s32[3,256]{1,0:T(4,128)S(1)}, s32[3,256]{1,0:T(4,128)S(1)}, u32[]{:S(2)}, u32[]{:S(2)}) collective-permute-start(s32[3,256]{1,0:T(4,128)S(1)} %copy-done.6), channel_id=1, source_target_pairs={{0,1},{1,0},{2,3},{3,2},{4,5},{5,4},{6,7},{7,6},{8,9},{9,8},{10,11... | collective-permute-start | bytes 9224 | tf_op jit(solution)/shard_map/ppermute | solution.py:258
  26.7 4.5 %collective-permute-start.10 = (s32[3,256]{1,0:T(4,128)S(1)}, s32[3,256]{1,0:T(4,128)S(1)}, u32[]{:S(2)}, u32[]{:S(2)}) collective-permute-start(s32[3,256]{1,0:T(4,128)S(1)} %copy-done.6), channel_id=1, source_target_pairs={{0,3},{1,2},{2,1},{3,0},{4,7},{5,6},{6,5},{7,4},{8,11},{9,10},{10,... | collective-permute-start | bytes 9224 | tf_op jit(solution)/shard_map/ppermute | solution.py:258
  28.2 3.6 %collective-permute-start.9 = (s32[3,256]{1,0:T(4,128)S(1)}, s32[3,256]{1,0:T(4,128)S(1)}, u32[]{:S(2)}, u32[]{:S(2)}) collective-permute-start(s32[3,256]{1,0:T(4,128)S(1)} %copy-done.6), channel_id=1, source_target_pairs={{0,2},{1,3},{2,0},{3,1},{4,6},{5,7},{6,4},{7,5},{8,10},{9,11},{10,... | collective-permute-start | bytes 9224 | tf_op jit(solution)/shard_map/ppermute | solution.py:258
  31.9 5.4 %collective-permute-start.11 = (f32[2,128,128]{2,1,0:T(8,128)S(1)}, f32[2,128,128]{2,1,0:T(8,128)S(1)}, u32[]{:S(2)}, u32[]{:S(2)}) collective-permute-start(f32[2,128,128]{2,1,0:T(8,128)S(1)} %add_multiply_fusion.after_ref.rest_7_), channel_id=1, source_target_pairs={{0,4},{4,0},{8,12},{12,8},{16,20},{20,16},{24,28},{28,24},{1,5},{5... | collective-permute-start | bytes 393224 | tf_op jit(solution)/shard_map/ppermute | solution.py:258
  31.9 7.3 %collective-permute-start.13 = (f32[2,128,128]{2,1,0:T(8,128)S(1)}, f32[2,128,128]{2,1,0:T(8,128)S(1)}, u32[]{:S(2)}, u32[]{:S(2)}) collective-permute-start(f32[2,128,128]{2,1,0:T(8,128)S(1)} %add_multiply_fusion.after_ref.rest_7_), channel_id=1, source_target_pairs={{0,3},{1,2},{2,1},{3,0},{4,7},{5,6},{6,5},{7,4},{8,11},{9,10},{10,... | collective-permute-start | bytes 393224 | tf_op jit(solution)/shard_map/ppermute | solution.py:258
  33.4 8.1 %collective-permute-start.12 = (f32[2,128,128]{2,1,0:T(8,128)S(1)}, f32[2,128,128]{2,1,0:T(8,128)S(1)}, u32[]{:S(2)}, u32[]{:S(2)}) collective-permute-start(f32[2,128,128]{2,1,0:T(8,128)S(1)} %add_multiply_fusion.after_ref.rest_7_), channel_id=1, source_target_pairs={{0,2},{1,3},{2,0},{3,1},{4,6},{5,7},{6,4},{7,5},{8,10},{9,11},{10,... | collective-permute-start | bytes 393224 | tf_op jit(solution)/shard_map/ppermute | solution.py:258
  35.0 6.6 %collective-permute-start.15 = (f32[2,128,128]{2,1,0:T(8,128)S(1)}, f32[2,128,128]{2,1,0:T(8,128)S(1)}, u32[]{:S(2)}, u32[]{:S(2)}) collective-permute-start(f32[2,128,128]{2,1,0:T(8,128)S(1)} %add_multiply_fusion.after_ref.rest_7_), channel_id=1, source_target_pairs={{0,1},{1,0},{2,3},{3,2},{4,5},{5,4},{6,7},{7,6},{8,9},{9,8},{10,11... | collective-permute-start | bytes 393224 | tf_op jit(solution)/shard_map/ppermute | solution.py:258
  39.3 2.8 %collective-permute-start.17 = (f32[2,128,128]{2,1,0:T(8,128)S(1)}, f32[2,128,128]{2,1,0:T(8,128)S(1)}, u32[]{:S(2)}, u32[]{:S(2)}) collective-permute-start(f32[2,128,128]{2,1,0:T(8,128)S(1)} %collective-permute-done.13.rest_7_), channel_id=1, source_target_pairs={{0,4},{4,0},{8,12},{12,8},{16,20},{20,16},{24,28},{28,24},{1,5},{5... | collective-permute-start | bytes 393224 | tf_op jit(solution)/shard_map/ppermute | solution.py:258
  41.6 1.3 %collective-permute-start.16 = (f32[2,128,128]{2,1,0:T(8,128)S(1)}, f32[2,128,128]{2,1,0:T(8,128)S(1)}, u32[]{:S(2)}, u32[]{:S(2)}) collective-permute-start(f32[2,128,128]{2,1,0:T(8,128)S(1)} %collective-permute-done.15.rest_16_), channel_id=1, source_target_pairs={{0,4},{4,0},{8,12},{12,8},{16,20},{20,16},{24,28},{28,24},{1,5},{5... | collective-permute-start | bytes 393224 | tf_op jit(solution)/shard_map/ppermute | solution.py:258
  41.6 1.5 %collective-permute-start.14 = (f32[2,128,128]{2,1,0:T(8,128)S(1)}, f32[2,128,128]{2,1,0:T(8,128)S(1)}, u32[]{:S(2)}, u32[]{:S(2)}) collective-permute-start(f32[2,128,128]{2,1,0:T(8,128)S(1)} %collective-permute-done.12.rest_14_), channel_id=1, source_target_pairs={{0,4},{4,0},{8,12},{12,8},{16,20},{20,16},{24,28},{28,24},{1,5},{5... | collective-permute-start | bytes 393224 | tf_op jit(solution)/shard_map/ppermute | solution.py:258
  (6 other events, 6.2 us)

commit v5 on v4

--- a/solution.py
+++ b/solution.py
@@ -76,9 +76,16 @@
     lax.fori_loop(0, vectors // (step * per_body), body, 0)
 
 
-def tile_kernel(pos_ref, lattice_ref, high_ref, low_ref, k_column, *, first):
+def lattice_rows(packed, channels, vectors):
+    share = packed.shape[1]
+    width = min(share, vectors)
+    chunks = [packed[channels + 3 * n : channels + 3 * n + 3, 0:width] for n in range(-(-vectors // share))]
+    return jnp.concatenate(chunks, axis=1)
+
+
+def tile_kernel(pos_ref, packed_ref, high_ref, low_ref, k_column, *, channels, vectors, first):
     rows = k_column.shape[0]
-    k_column[:, 0:3] = lattice_ref[:, first : first + rows].astype(F32).T
+    k_column[:, 0:3] = lattice_rows(packed_ref, channels, vectors)[:, first : first + rows].T
     cos, sin = pl.ds(0, rows), pl.ds(rows, rows)
     trig_blocks(k_column, pos_ref, None, (high_ref.at[cos], low_ref.at[cos], high_ref.at[sin], low_ref.at[sin]))
 
@@ -114,7 +121,7 @@
 def adjoint_of(cotangent_ref, offset, mask_ref, w_out_ref):
     share = cotangent_ref.shape[1]
     lanes = pl.ds(pl.multiple_of((lax.axis_index("kvec") ^ offset) * share, share), share)
-    return lanes, mask_ref[:, lanes] * dot3(w_out_ref[...], cotangent_ref[...], NN)
+    return lanes, mask_ref[:, lanes] * dot3(w_out_ref[...], cotangent_ref[0 : w_out_ref.shape[0], :], NN)
 
 
 def charge_kernel(pad_ref, feats_ref, species_ref, w_charge_ref, embed_ref, w_out_ref, *rest, groups):
@@ -159,12 +166,12 @@
     split_by_core(total, keep_ref, send_ref)
 
 
-def wave_kernel(pos_ref, lattice_ref, width_ref, after_ref, *rest, atom_total):
+def wave_kernel(pos_ref, packed_ref, width_ref, after_ref, *rest, atom_total):
     *gain_ref, cos, sin, cos_high, cos_low, sin_high, sin_low, k_ref, k_column = rest
     vectors = cos.shape[0]
     rows = vectors // 2
     core = lax.axis_index("atoms") % 2
-    k_column[:, 0:3] = lattice_ref[...].astype(F32).T
+    k_column[:, 0:3] = lattice_rows(packed_ref, width_ref.shape[1], vectors).T
     for flip in range(2):
         start = pl.multiple_of((core ^ flip) * rows, rows)
         k_ref[flip * rows : (flip + 1) * rows, :] = k_column[pl.ds(start, rows), :]
@@ -177,11 +184,11 @@
     trig_blocks(k_ref, pos_ref, first, (cos_high, cos_low, sin_high, sin_low), (cos, sin))
 
 
-def coefficient_stack(near_ref, far_ref, part):
-    channels = near_ref.shape[2] // 2
+def coefficient_stack(sides, part):
+    channels = sides[0].shape[2] // 2
     lanes = slice(part * channels, (part + 1) * channels)
-    sides = [jnp.concatenate([side[0, :, lanes], side[1, :, lanes]], axis=1) for side in (near_ref, far_ref)]
-    high, low = halves(jnp.concatenate(sides, axis=0))
+    rows = [jnp.concatenate([side[0, :, lanes], side[1, :, lanes]], axis=1) for side in sides]
+    high, low = halves(jnp.concatenate(rows, axis=0))
     return jnp.concatenate([high, low, high], axis=1)
 
 
@@ -196,11 +203,11 @@
     return wide[:width] + wide[width:] + dot16(stack[:, :width], tile_low, TN)
 
 
-def add_force(sums, wave, along, first):
+def add_force(sums, wave, along, rows, first):
     step = 16
     cos, sin, _, _, _, _, k_ref = wave
-    for start in range(0, cos.shape[0], step):
-        here = slice(start, start + step)
+    for start in range(0, rows.stop - rows.start, step):
+        here = slice(rows.start + start, rows.start + start + step)
         there = slice(first + start, first + start + step)
         slope = cos[here, :] * along[1, there, :] - sin[here, :] * along[0, there, :]
         for x in range(3):
@@ -209,43 +216,47 @@
     return sums
 
 
-def fields(own_ref, waves, coefs, channels, along, field, sums):
+def fields(own_ref, refs, layout, channels, along, field, sums):
+    entries = []
+    for count, first in layout:
+        wave, sides, refs = refs[:7], refs[7 : 7 + count], refs[7 + count :]
+        rows = sides[0].shape[1]
+        entries.append((wave, sides, slice(first * rows, (first + count) * rows)))
     other = own_stack(own_ref, channels)
-    coefs = [coefs[at : at + 2] for at in range(0, len(coefs), 2)]
-    parts = [[coefficient_stack(*pair, part) for pair in coefs] for part in range(2)]
+    stacks = [[coefficient_stack(sides, part) for _, sides, _ in entries] for part in range(2)]
     for part in range(2):
-        along[part] = dot16(jnp.concatenate(parts[part], axis=0), other, NN)
-    waves = [waves[at : at + 7] for at in range(0, len(waves), 7)]
-    for group, wave in enumerate(waves):
+        along[part] = dot16(jnp.concatenate(stacks[part], axis=0), other, NN)
+    for at, (wave, _, rows) in enumerate(entries):
         _, _, cos_high, cos_low, sin_high, sin_low, _ = wave
-        for part, high, low in ((parts[0], cos_high, cos_low), (parts[1], sin_high, sin_low)):
-            added = add_field(part[group], high[...], low[...])
+        for part, high, low in ((0, cos_high, cos_low), (1, sin_high, sin_low)):
+            added = add_field(stacks[part][at], high[rows, :], low[rows, :])
             field = added if field is None else field + added
-    for group, wave in enumerate(waves):
-        sums = add_force(sums, wave, along, group * wave[0].shape[0])
+    first = 0
+    for wave, _, rows in entries:
+        sums = add_force(sums, wave, along, rows, first)
+        first += rows.stop - rows.start
     return field, sums
 
 
-def partial_field_kernel(own_ref, *rest, groups, first):
-    waves, coefs, before = rest[: 7 * groups], rest[7 * groups : 9 * groups], rest[9 * groups : -3]
-    field_ref, sums_ref, along = rest[-3:]
+def partial_field_kernel(own_ref, *rest, layout, first):
+    refs, field_ref, sums_ref, along = rest[:-3], *rest[-3:]
     share = own_ref.shape[1]
     if first:
         field, sums = None, [jnp.zeros((8, share), F32)] * 3
     else:
+        refs, before = refs[:-2], refs[-2:]
         field, sums = before[0][...], [before[1][8 * x : 8 * x + 8, :] for x in range(3)]
-    field, sums = fields(own_ref, waves, coefs, coefs[0].shape[2] // 2, along, field, sums)
+    field, sums = fields(own_ref, refs, layout, field_ref.shape[0] // 2, along, field, sums)
     field_ref[...] = field
     for x in range(3):
         sums_ref[8 * x : 8 * x + 8, :] = sums[x]
 
 
-def field_kernel(own_ref, w_out_ref, w_charge_ref, *rest, groups):
-    waves, coefs = rest[: 7 * groups], rest[7 * groups : 9 * groups]
-    field_ref, sums_ref, message_ref, force_ref, grad_ref, along = rest[9 * groups :]
+def field_kernel(own_ref, w_out_ref, w_charge_ref, *rest, layout):
+    refs, field_ref, sums_ref, message_ref, force_ref, grad_ref, along = rest[:-6], *rest[-6:]
     channels = w_out_ref.shape[0]
     sums = [sums_ref[8 * x : 8 * x + 8, :] for x in range(3)]
-    field, sums = fields(own_ref, waves, coefs, channels, along, field_ref[...], sums)
+    field, sums = fields(own_ref, refs, layout, channels, along, field_ref[...], sums)
     field = own_ref[2 * channels : 2 * channels + 1, :] * field
     message_ref[...] = dot3(w_out_ref[...], field[:channels], TN)
     grad_ref[...] = dot3(w_charge_ref[...], field[channels:], NN)
@@ -282,12 +293,20 @@
     def planes(value):
         return [swap(value, "kvec", m) for m in range(group_count - 1, 0, -1)][::-1]
 
-    cotangents = [grad_out] + planes(grad_out)
+    chunks = -(-vectors // share)
+    below = -(-3 * chunks // 8) * 8
+    packed = jnp.pad(grad_out, ((0, below), (0, 0)))
+    for n in range(chunks):
+        chunk = k_lattice[:, n * share : (n + 1) * share]
+        first = channels + 3 * n
+        packed += jnp.pad(chunk, ((first, channels + below - first - 3), (0, share - chunk.shape[1]))).astype(F32)
+
+    packed = [packed] + planes(packed)
 
     tiles = []
     for part in range(2):
         tiles += pl.pallas_call(
-            functools.partial(tile_kernel, first=part * half),
+            functools.partial(tile_kernel, channels=channels, vectors=vectors, first=part * half),
             out_shape=[bf16(vectors, atoms)] * 2,
             in_specs=[VMEM] * 2,
             out_specs=[VMEM] * 2,
@@ -295,7 +314,7 @@
             compiler_params=PARAMS,
             cost_estimate=cost(9000 * half * atoms),
             name="waves_of_own_vectors",
-        )(positions, k_lattice)
+        )(positions, packed[0])
 
     middle = group_count // 2
     keep_h, send_h, own, mask, part = pl.pallas_call(
@@ -309,7 +328,7 @@
         name="charge_sums",
     )(
         pad_count.reshape(1, -1), feats, species.reshape(1, atoms), w_charge, species_embed.T, w_out,
-        *tiles, *cotangents[:middle],
+        *tiles, *packed[:middle],
     )
 
     wave_shapes = [f32(vectors, share)] * 2 + [bf16(vectors, share)] * 4 + [f32(vectors, 128)]
@@ -325,7 +344,7 @@
             compiler_params=PARAMS,
             cost_estimate=cost(20 * vectors * share),
             name="waves_of_own_atoms",
-        )(positions, lattices[group], filter_width.reshape(1, channels), after)
+        )(positions, packed[group], filter_width.reshape(1, channels), after)
         return list(made)
 
     arrived_h = swap(send_h, "atoms", 1)
@@ -338,7 +357,7 @@
         compiler_params=PARAMS,
         cost_estimate=cost(60 * vectors * atoms * channels),
         name="adjoint_sums",
-    )(mask, w_out, part, *tiles, *cotangents[middle:])
+    )(mask, w_out, part, *tiles, *packed[middle:])
 
     arrived_h, send_b = lax.optimization_barrier((arrived_h, send_b))
     arrived_b = swap(send_b, "atoms", 1)
@@ -349,62 +368,71 @@
     sum_b = keep_b + arrived_b
     next_b = swap_along_z(sum_b, steps[0], steps[-1])
 
-    next_h, next_b = lax.optimization_barrier((next_h, next_b))
+    def more_waves(count, after):
+        return [waves_of(group, after) for group in range(len(waves), min(len(waves) + count, group_count))]
+
+    waves = []
+    beside = more_waves(2, sum_b)
+    next_h, next_b, beside = lax.optimization_barrier((next_h, next_b, beside))
+    waves += beside
     total = jnp.stack([sum_h + next_h, sum_b + next_b])
-    lattices, waves = [k_lattice], []
-    for step in zip(steps[1:], steps[-2::-1]):
+    for at, step in enumerate(zip(steps[1:], steps[-2::-1])):
         arrived = swap_along_z(total, *step)
-        if not waves:
-            gain, *made = waves_of(0, total)
-            held, made = lax.optimization_barrier((k_lattice, made))
-            lattices += planes(held)
-            waves = [made, waves_of(1, total)]
-            arrived, gain, waves, lattices = lax.optimization_barrier((arrived, gain, waves, lattices))
+        beside = more_waves(group_count if at + 2 == len(steps) else 1, total)
+        arrived, beside = lax.optimization_barrier((arrived, beside))
+        waves += beside
         total = total + arrived
+    gain, *waves[0] = waves[0]
     near = gain[None] * total
     plane = {0: near}
     for group in range(group_count - 1, 0, -1):
         plane[group] = swap(near, "kvec", group)
-    waves += [waves_of(group, near) for group in range(2, group_count)]
     far = {0: swap(near, "atoms", 1)}
 
-    def partial_fields(groups, before):
-        count = len(groups)
-        coefs = [part[g] for g in groups for part in (plane, far)]
-        group_waves = [wave for g in groups for wave in waves[g]]
+    def operands_of(parts):
+        sides = [[plane[group], far.get(group)][first : first + count] for group, count, first in parts]
+        return [ref for part, side in zip(parts, sides) for ref in list(waves[part[0]]) + side]
+
+    def field_sizes(parts):
+        layout = tuple(part[1:] for part in parts)
+        return layout, pltpu.VMEM((2, sum(count for count, _ in layout) * half, share), F32)
+
+    def partial_fields(parts, before):
+        layout, scratch = field_sizes(parts)
+        operands = [own, *operands_of(parts), *before]
         return pl.pallas_call(
-            functools.partial(partial_field_kernel, groups=count, first=not before),
+            functools.partial(partial_field_kernel, layout=layout, first=not before),
             out_shape=[f32(both, share), f32(24, share)],
-            in_specs=[VMEM] * (1 + 9 * count + len(before)),
+            in_specs=[VMEM] * len(operands),
             out_specs=[VMEM] * 2,
-            scratch_shapes=[pltpu.VMEM((2, count * vectors, share), F32)],
+            scratch_shapes=[scratch],
             compiler_params=PARAMS,
-            cost_estimate=cost(count * vectors * share),
+            cost_estimate=cost(vectors * share),
             name="fields_of_some_groups",
-        )(own, *group_waves, *coefs, *before)
-
-    fields_so_far = partial_fields([0], [])
-    waves, fields_so_far = lax.optimization_barrier((waves, fields_so_far))
+        )(*operands)
+
+    fields_so_far = partial_fields([(0, 2, 0)], [])
     for group in range(group_count - 1, 0, -1):
         plane[group], fields_so_far = lax.optimization_barrier((plane[group], fields_so_far))
         far[group] = swap(plane[group], "atoms", 1)
     late = [2, 1] if group_count > 3 else [1]
-    fields_so_far = partial_fields(list(range(group_count - 1, len(late), -1)), fields_so_far)
-    late_operands = [wave for g in late for wave in waves[g]] + [part[g] for g in late for part in (plane, far)]
-
+    parts = [(group, 2, 0) for group in range(group_count - 1, len(late), -1)] + [(group, 1, 0) for group in late]
+    fields_so_far = partial_fields(parts, fields_so_far)
+
+    parts = [(group, 1, 1) for group in late]
+    layout, scratch = field_sizes(parts)
+    operands = [own, w_out, w_charge, *operands_of(parts), *fields_so_far]
     return tuple(
         pl.pallas_call(
-            functools.partial(field_kernel, groups=len(late)),
+            functools.partial(field_kernel, layout=layout),
             out_shape=[f32(channels, share), f32(3, share), f32(channels, share)],
-            in_specs=[VMEM] * (5 + 9 * len(late)),
+            in_specs=[VMEM] * len(operands),
             out_specs=[VMEM] * 3,
-            scratch_shapes=[pltpu.VMEM((2, len(late) * vectors, share), F32)],
+            scratch_shapes=[scratch],
             compiler_params=PARAMS,
             cost_estimate=cost(vectors * share),
             name="fields_and_forces",
-        )(
-            own, w_out, w_charge, *late_operands, *fields_so_far
-        )
+        )(*operands)
     )
 
 

time: 45.7 us -> 41.2 us (0.902)
  starting transfers between devices: 18.8 us -> 15 us
  local copies, waits for them, and re-layouts: 2.12 us -> 0.67 us
  other arithmetic: 0.07 us -> 1.01 us
    ppermute x15 -> x12, starting transfers between devices: 12.8 us -> 8.86 us  [swap(): lax.ppermute(value, axis, [(place, place ^ offset) for place in range(siz...]
    unnamed x24 -> x16, local copies, waits for them, and re-layouts: 2.12 us -> 0.67 us
    add x0 -> x1, other arithmetic: none -> 0.94 us  [on_device(): packed += jnp.pad(chunk, ((first, channels + below - first - 3), (0, shar...]
    ppermute x3, waiting for transfers between devices: 3.45 us -> 2.92 us  [swap_along_z(): return lax.ppermute(value, 'atoms', pairs)]
    ppermute x15 -> x12, waiting for transfers between devices: 6.12 us -> 6.22 us  [swap(): lax.ppermute(value, axis, [(place, place ^ offset) for place in range(siz...]
  transfers between devices with their start and end apart: 18 -> 15, of which waited for: 10 -> 7; matrix products, arithmetic and copies ran while one was open for 0% -> 0% of each run, Pallas kernels for 26% -> 31%
where the time goes in v5:
time: 41.2 us; the launch traced here: 41.1 us
  starting transfers between devices  15 us (36%)
  Pallas kernels  14.4 us (35%)
  waiting for transfers between devices  9.14 us (22%)
  other arithmetic  1.01 us (2%)
  between operations  0.88 us (2%)
  local copies, waits for them, and re-layouts  0.67 us (2%)
    ppermute x12, starting transfers between devices, swap(): lax.ppermute(value, axis, [(place, place ^ offset) for place in range(siz...  8.86 us
    ppermute x12, waiting for transfers between devices, swap(): lax.ppermute(value, axis, [(place, place ^ offset) for place in range(siz...  6.22 us
    ppermute x3, starting transfers between devices, swap_along_z(): return lax.ppermute(value, 'atoms', pairs)  6.13 us
    pallas_call x4, Pallas kernels, waves_of(): pl.pallas_call(functools.partial(wave_kernel, atom_total=atoms * atom_cou...  3.76 us
    pallas_call x2, Pallas kernels, on_device(): pl.pallas_call(functools.partial(tile_kernel, channels=channels, vectors=...  3.11 us
    ppermute x3, waiting for transfers between devices, swap_along_z(): return lax.ppermute(value, 'atoms', pairs)  2.92 us
    pallas_call x2, Pallas kernels, partial_fields(): pl.pallas_call(functools.partial(partial_field_kernel, layout=layout, fir...  2.45 us
    pallas_call x1, Pallas kernels, on_device(): pl.pallas_call(functools.partial(charge_kernel, groups=group_count), out_...  2.1 us
  transfers between devices with their start and end apart: 15, of which 7 were waited for; matrix products, arithmetic and copies ran while one was open for 0% of the time, Pallas kernels for 31%

profile of v5, /device:TPU:0, one launch (start us, length us, event | category | flops | bytes accessed | tf_op | source)
XLA Modules:
  0.0 41.1 jit_solution(3026639956224956938)
XLA Ops:
  0.6 0.9 %convert_add_fusion.packed_ref.rest_4_ = f32[72,512]{1,0:T(8,128)S(1)} fusion(s32[3,256]{1,0:T(4,128)} %param.14, f32[64,512]{1,0:T(8,128)} %param.19), kind=kLoop, calls=%fused_computation | loop fusion | flops 73728 | bytes 281600 | tf_op jit(solution)/shard_map/add | solution.py:302
  1.6 3.0 %collective-permute-start = (f32[72,512]{1,0:T(8,128)S(1)}, f32[72,512]{1,0:T(8,128)S(1)}, u32[]{:S(2)}, u32[]{:S(2)}) collective-permute-start(f32[72,512]{1,0:T(8,128)S(1)} %convert_add_fusion.packed_ref.rest_4_), channel_id=1, source_target_pairs={{0,1},{1,0},{2,3},{3,2},{4,5},{5,4},{6,7},{7,6},{8,9},{9,8},{10,11... | collective-permute-start | bytes 442376 | tf_op jit(solution)/shard_map/ppermute | solution.py:269
  4.6 1.5 %collective-permute-start.2 = (f32[72,512]{1,0:T(8,128)S(1)}, f32[72,512]{1,0:T(8,128)S(1)}, u32[]{:S(2)}, u32[]{:S(2)}) collective-permute-start(f32[72,512]{1,0:T(8,128)S(1)} %convert_add_fusion.packed_ref.rest_4_), channel_id=1, source_target_pairs={{0,2},{1,3},{2,0},{3,1},{4,6},{5,7},{6,4},{7,5},{8,10},{9,11},{10,... | collective-permute-start | bytes 442376 | tf_op jit(solution)/shard_map/ppermute | solution.py:269
  6.1 1.5 %waves_of_own_vectors.2 = (bf16[256,2048]{1,0:T(8,128)(2,1)S(1)}, bf16[256,2048]{1,0:T(8,128)(2,1)S(1)}) custom-call(f32[3,2048]{1,0:T(4,128)S(1)} %copy-done, f32[72,512]{1,0:T(8,128)S(1)} %convert_add_fusion.packed_ref.rest_4_), custom_call_target="tpu_custom_call" | custom-call | flops 2359296000 | tf_op jit(solution)/shard_map/waves_of_own_vectors/pallas_call | solution.py:308
  7.7 1.6 %waves_of_own_vectors.3 = (bf16[256,2048]{1,0:T(8,128)(2,1)S(1)}, bf16[256,2048]{1,0:T(8,128)(2,1)S(1)}) custom-call(f32[3,2048]{1,0:T(4,128)S(1)} %copy-done, f32[72,512]{1,0:T(8,128)S(1)} %convert_add_fusion.packed_ref.rest_4_), custom_call_target="tpu_custom_call" | custom-call | flops 2359296000 | tf_op jit(solution)/shard_map/waves_of_own_vectors/pallas_call | solution.py:308
  10.0 2.1 %charge_sums.1 = (f32[128,128]{1,0:T(8,128)S(1)}, f32[128,128]{1,0:T(8,128)S(1)}, f32[136,512]{1,0:T(8,128)S(1)}, f32[1,2048]{1,0:T(1,128)S(1)}, f32[256,128]{1,0:T(8,128)S(1)}) custom-call(s32[1,8]{1,0:T(1,128)S(1)} %bitcast.14, f32[64,2048]{1,0:T(8,128)S(1)} %copy-done.4, s32[1,2048]{1,0:T(1,128)S(1)} %bitcast.12, f32[64,64]{1,0:T(8,128)S(1)} %copy-done.1, ...), custom_call_target="tpu_custom_call" | custom-call | flops 2013265920 | tf_op jit(solution)/shard_map/charge_sums/pallas_call | solution.py:320
  12.2 0.9 %collective-permute-done.2.rest_4_.packed_ref = f32[72,512]{1,0:T(8,128)S(1)} collective-permute-done((f32[72,512]{1,0:T(8,128)S(1)}, f32[72,512]{1,0:T(8,128)S(1)}, u32[]{:S(2)}, u32[]{:S(2)}) %collective-permute-start.2) | collective-permute-done | bytes 147488 | tf_op jit(solution)/shard_map/ppermute | solution.py:269
  13.1 1.1 %adjoint_sums.1 = (f32[128,128]{1,0:T(8,128)S(1)}, f32[128,128]{1,0:T(8,128)S(1)}) custom-call(f32[1,2048]{1,0:T(1,128)S(1)} %get-tuple-element.98.mask_ref, f32[64,64]{1,0:T(8,128)S(1)} %copy-done.2, f32[256,128]{1,0:T(8,128)S(1)} %get-tuple-element.99.part_ref, bf16[256,2048]{1,0:T(8,128)(2,1)S(1)} %get-tuple-element.92.rest_0_, ...), custom_call_target="tpu_custom_call" | custom-call | flops 2013265920 | tf_op jit(solution)/shard_map/adjoint_sums/pallas_call | solution.py:351
  14.3 1.7 %collective-permute-start.5 = (f32[128,128]{1,0:T(8,128)S(1)}, f32[128,128]{1,0:T(8,128)S(1)}, u32[]{:S(2)}, u32[]{:S(2)}) collective-permute-start(f32[128,128]{1,0:T(8,128)S(1)} %add.23), channel_id=1, source_target_pairs={{0,8},{4,20},{8,0},{12,28},{16,24},{20,4},{24,16},{28,12},{1,9},{5... | collective-permute-start | bytes 196616 | tf_op jit(solution)/shard_map/ppermute | solution.py:274
  16.0 1.1 %collective-permute-start.6 = (f32[128,128]{1,0:T(8,128)S(1)}, f32[128,128]{1,0:T(8,128)S(1)}, u32[]{:S(2)}, u32[]{:S(2)}) collective-permute-start(f32[128,128]{1,0:T(8,128)S(1)} %add.24.after_ref), channel_id=1, source_target_pairs={{0,8},{4,20},{8,0},{12,28},{16,24},{20,4},{24,16},{28,12},{1,9},{5... | collective-permute-start | bytes 196616 | tf_op jit(solution)/shard_map/ppermute | solution.py:274
  17.2 1.1 %waves_of_own_atoms.4 = (f32[128,128]{1,0:T(8,128)S(1)}, f32[256,512]{1,0:T(8,128)S(1)}, f32[256,512]{1,0:T(8,128)S(1)}, bf16[256,512]{1,0:T(8,128)(2,1)S(1)}, b...) custom-call(f32[3,2048]{1,0:T(4,128)S(1)} %copy-done, ...), custom_call_target="tpu_custom_call" | custom-call | flops 2621440 | tf_op jit(solution)/shard_map/waves_of_own_atoms/pallas_call | solution.py:338
  18.3 0.9 %waves_of_own_atoms.5 = (f32[256,512]{1,0:T(8,128)S(1)}, f32[256,512]{1,0:T(8,128)S(1)}, bf16[256,512]{1,0:T(8,128)(2,1)S(1)}, bf16[256,512]{1,0:T(8,128)(2,1)S(...) custom-call(f32[3,2048]{1,0:T(4,128)S(1)} %copy-done, ...), custom_call_target="tpu_custom_call" | custom-call | flops 2621440 | tf_op jit(solution)/shard_map/waves_of_own_atoms/pallas_call | solution.py:338
  19.3 1.0 %collective-permute-done.6 = f32[128,128]{1,0:T(8,128)S(1)} collective-permute-done((f32[128,128]{1,0:T(8,128)S(1)}, f32[128,128]{1,0:T(8,128)S(1)}, u32[]{:S(2)}, u32[]{:S(2)}) %collective-permute-start.6) | collective-permute-done | bytes 65568 | tf_op jit(solution)/shard_map/ppermute | solution.py:274
  20.4 3.3 %collective-permute-start.7 = (f32[2,128,128]{2,1,0:T(8,128)S(1)}, f32[2,128,128]{2,1,0:T(8,128)S(1)}, u32[]{:S(2)}, u32[]{:S(2)}) collective-permute-start(f32[2,128,128]{2,1,0:T(8,128)S(1)} %pad_maximum_fusion.after_ref), channel_id=1, source_target_pairs={{0,16},{4,12},{8,24},{12,4},{16,0},{20,28},{24,8},{28,20},{1,17},{... | collective-permute-start | bytes 393224 | tf_op jit(solution)/shard_map/ppermute | solution.py:274
  23.7 0.9 %waves_of_own_atoms.7 = (f32[256,512]{1,0:T(8,128)S(1)}, f32[256,512]{1,0:T(8,128)S(1)}, bf16[256,512]{1,0:T(8,128)(2,1)S(1)}, bf16[256,512]{1,0:T(8,128)(2,1)S(...) custom-call(f32[3,2048]{1,0:T(4,128)S(1)} %copy-done, ...), custom_call_target="tpu_custom_call" | custom-call | flops 2621440 | tf_op jit(solution)/shard_map/waves_of_own_atoms/pallas_call | solution.py:338
  24.6 0.9 %waves_of_own_atoms.6 = (f32[256,512]{1,0:T(8,128)S(1)}, f32[256,512]{1,0:T(8,128)S(1)}, bf16[256,512]{1,0:T(8,128)(2,1)S(1)}, bf16[256,512]{1,0:T(8,128)(2,1)S(...) custom-call(f32[3,2048]{1,0:T(4,128)S(1)} %copy-done, ...), custom_call_target="tpu_custom_call" | custom-call | flops 2621440 | tf_op jit(solution)/shard_map/waves_of_own_atoms/pallas_call | solution.py:338
  25.4 1.8 %collective-permute-done.7 = f32[2,128,128]{2,1,0:T(8,128)S(1)} collective-permute-done((f32[2,128,128]{2,1,0:T(8,128)S(1)}, f32[2,128,128]{2,1,0:T(8,128)S(1)}, u32[]{:S(2)}, u32[]{:S(2)}) %collective-permute-start.7) | collective-permute-done | bytes 131104 | tf_op jit(solution)/shard_map/ppermute | solution.py:274
  27.4 1.9 %collective-permute-start.9 = (f32[2,128,128]{2,1,0:T(8,128)S(1)}, f32[2,128,128]{2,1,0:T(8,128)S(1)}, u32[]{:S(2)}, u32[]{:S(2)}) collective-permute-start(f32[2,128,128]{2,1,0:T(8,128)S(1)} %add_multiply_fusion.rest_7_), channel_id=1, source_target_pairs={{0,3},{1,2},{2,1},{3,0},{4,7},{5,6},{6,5},{7,4},{8,11},{9,10},{10,... | collective-permute-start | bytes 393224 | tf_op jit(solution)/shard_map/ppermute | solution.py:269
  30.0 0.9 %collective-permute-start.12 = (f32[2,128,128]{2,1,0:T(8,128)S(1)}, f32[2,128,128]{2,1,0:T(8,128)S(1)}, u32[]{:S(2)}, u32[]{:S(2)}) collective-permute-start(f32[2,128,128]{2,1,0:T(8,128)S(1)} %add_multiply_fusion.rest_7_), channel_id=1, source_target_pairs={{0,1},{1,0},{2,3},{3,2},{4,5},{5,4},{6,7},{7,6},{8,9},{9,8},{10,11... | collective-permute-start | bytes 393224 | tf_op jit(solution)/shard_map/ppermute | solution.py:269
  30.9 0.8 %fields_of_some_groups.2 = (f32[128,512]{1,0:T(8,128)S(1)}, f32[24,512]{1,0:T(8,128)S(1)}) custom-call(f32[136,512]{1,0:T(8,128)S(1)} %get-tuple-element.96.own_ref, f32[256,512]{1,0:T(8,128)S(1)} %get-tuple-element.147.rest_0_, f32[256,512]{1,0:T(8,128)S(1)} %get-tuple-element.148.rest_1_, bf16[256,512]{1,0:T(8,128)(2,1)S(1)} %get-tuple-element.149.rest_2_, ...), custom_call_target="tpu_custom_call" | custom-call | flops 131072 | tf_op jit(solution)/shard_map/fields_of_some_groups/pallas_call | solution.py:403
  31.7 2.9 %collective-permute-done.9.rest_7_ = f32[2,128,128]{2,1,0:T(8,128)S(1)} collective-permute-done((f32[2,128,128]{2,1,0:T(8,128)S(1)}, f32[2,128,128]{2,1,0:T(8,128)S(1)}, u32[]{:S(2)}, u32[]{:S(2)}) %collective-permute-start.9) | collective-permute-done | bytes 131104 | tf_op jit(solution)/shard_map/ppermute | solution.py:269
  34.6 2.3 %collective-permute-done.8.rest_16_ = f32[2,128,128]{2,1,0:T(8,128)S(1)} collective-permute-done((f32[2,128,128]{2,1,0:T(8,128)S(1)}, f32[2,128,128]{2,1,0:T(8,128)S(1)}, u32[]{:S(2)}, u32[]{:S(2)}) %collective-permute-start.8) | collective-permute-done | bytes 131104 | tf_op jit(solution)/shard_map/ppermute | solution.py:269
  37.6 1.6 %fields_of_some_groups.3 = (f32[128,512]{1,0:T(8,128)S(1)}, f32[24,512]{1,0:T(8,128)S(1)}) custom-call(f32[136,512]{1,0:T(8,128)S(1)} %get-tuple-element.96.own_ref, f32[256,512]{1,0:T(8,128)S(1)} %get-tuple-element.169.rest_0_, f32[256,512]{1,0:T(8,128)S(1)} %get-tuple-element.170.rest_1_, bf16[256,512]{1,0:T(8,128)(2,1)S(1)} %get-tuple-element.171.rest_2_, ...), custom_call_target="tpu_custom_call" | custom-call | flops 131072 | tf_op jit(solution)/shard_map/fields_of_some_groups/pallas_call | solution.py:403
  39.2 1.8 %fields_and_forces.1 = (f32[64,512]{1,0:T(8,128)}, f32[3,512]{1,0:T(4,128)}, f32[64,512]{1,0:T(8,128)}) custom-call(f32[136,512]{1,0:T(8,128)S(1)} %get-tuple-element.96.own_ref, f32[64,64]{1,0:T(8,128)S(1)} %copy-done.2, f32[64,64]{1,0:T(8,128)S(1)} %copy-done.1, f32[256,512]{1,0:T(8,128)S(1)} %get-tuple-element.138.rest_9_.rest_0_, ...), custom_call_target="tpu_custom_call" | custom-call | flops 131072 | tf_op jit(solution)/shard_map/fields_and_forces/pallas_call | solution.py:426
  (39 shorter events, 2.6 us)
Async XLA Ops:
  0.6 5.5 %copy-start = (f32[3,2048]{1,0:T(4,128)S(1)}, f32[3,2048]{1,0:T(4,128)}, u32[]{:S(2)}) copy-start(f32[3,2048]{1,0:T(4,128)} %pos_ref.11) | copy-start | bytes 73732
  1.6 7.7 %collective-permute-start = (f32[72,512]{1,0:T(8,128)S(1)}, f32[72,512]{1,0:T(8,128)S(1)}, u32[]{:S(2)}, u32[]{:S(2)}) collective-permute-start(f32[72,512]{1,0:T(8,128)S(1)} %convert_add_fusion.packed_ref.rest_4_), channel_id=1, source_target_pairs={{0,1},{1,0},{2,3},{3,2},{4,5},{5,4},{6,7},{7,6},{8,9},{9,8},{10,11... | collective-permute-start | bytes 442376 | tf_op jit(solution)/shard_map/ppermute | solution.py:269
  4.6 8.5 %collective-permute-start.2 = (f32[72,512]{1,0:T(8,128)S(1)}, f32[72,512]{1,0:T(8,128)S(1)}, u32[]{:S(2)}, u32[]{:S(2)}) collective-permute-start(f32[72,512]{1,0:T(8,128)S(1)} %convert_add_fusion.packed_ref.rest_4_), channel_id=1, source_target_pairs={{0,2},{1,3},{2,0},{3,1},{4,6},{5,7},{6,4},{7,5},{8,10},{9,11},{10,... | collective-permute-start | bytes 442376 | tf_op jit(solution)/shard_map/ppermute | solution.py:269
  6.1 7.0 %collective-permute-start.3 = (f32[72,512]{1,0:T(8,128)S(1)}, f32[72,512]{1,0:T(8,128)S(1)}, u32[]{:S(2)}, u32[]{:S(2)}) collective-permute-start(f32[72,512]{1,0:T(8,128)S(1)} %convert_add_fusion.packed_ref.rest_4_), channel_id=1, source_target_pairs={{0,3},{1,2},{2,1},{3,0},{4,7},{5,6},{6,5},{7,4},{8,11},{9,10},{10,... | collective-permute-start | bytes 442376 | tf_op jit(solution)/shard_map/ppermute | solution.py:269
  7.7 1.7 %copy-start.1 = (f32[64,64]{1,0:T(8,128)S(1)}, f32[64,64]{1,0:T(8,128)}, u32[]{:S(2)}) copy-start(f32[64,64]{1,0:T(8,128)} %w_charge_ref.3) | copy-start | bytes 49156
  7.7 1.7 %copy-start.2 = (f32[64,64]{1,0:T(8,128)S(1)}, f32[64,64]{1,0:T(8,128)}, u32[]{:S(2)}) copy-start(f32[64,64]{1,0:T(8,128)} %w_out_ref.5) | copy-start | bytes 49156
  7.7 1.7 %copy-start.4 = (f32[64,2048]{1,0:T(8,128)S(1)}, f32[64,2048]{1,0:T(8,128)}, u32[]{:S(2)}) copy-start(f32[64,2048]{1,0:T(8,128)} %feats_ref.1) | copy-start | bytes 1572868
  7.7 1.7 %copy-start.6 = (f32[64,16]{0,1:T(8,128)S(1)}, f32[64,16]{0,1:T(8,128)}, u32[]{:S(2)}) copy-start(f32[64,16]{0,1:T(8,128)} %param.17) | copy-start | bytes 12292
  9.3 0.7 %copy-start.5 = (s32[2048]{0:T(1024)S(1)}, s32[2048]{0:T(1024)}, u32[]{:S(2)}) copy-start(s32[2048]{0:T(1024)} %param.12) | copy-start | bytes 24580
  9.3 0.7 %copy-start.7 = (s32[8]{0:T(128)S(1)}, s32[8]{0:T(128)}, u32[]{:S(2)}) copy-start(s32[8]{0:T(128)} %param.13) | copy-start | bytes 100
  12.1 2.1 %collective-permute-start.1 = (f32[128,128]{1,0:T(8,128)S(1)}, f32[128,128]{1,0:T(8,128)S(1)}, u32[]{:S(2)}, u32[]{:S(2)}) collective-permute-start(f32[128,128]{1,0:T(8,128)S(1)} %get-tuple-element.97), channel_id=1, source_target_pairs={{0,4},{4,0},{8,12},{12,8},{16,20},{20,16},{24,28},{28,24},{1,5},{5... | collective-permute-start | bytes 196616 | tf_op jit(solution)/shard_map/ppermute | solution.py:269
  14.2 1.8 %collective-permute-start.4 = (f32[128,128]{1,0:T(8,128)S(1)}, f32[128,128]{1,0:T(8,128)S(1)}, u32[]{:S(2)}, u32[]{:S(2)}) collective-permute-start(f32[128,128]{1,0:T(8,128)S(1)} %get-tuple-element.101), channel_id=1, source_target_pairs={{0,4},{4,0},{8,12},{12,8},{16,20},{20,16},{24,28},{28,24},{1,5},{5... | collective-permute-start | bytes 196616 | tf_op jit(solution)/shard_map/ppermute | solution.py:269
  14.3 5.0 %collective-permute-start.5 = (f32[128,128]{1,0:T(8,128)S(1)}, f32[128,128]{1,0:T(8,128)S(1)}, u32[]{:S(2)}, u32[]{:S(2)}) collective-permute-start(f32[128,128]{1,0:T(8,128)S(1)} %add.23), channel_id=1, source_target_pairs={{0,8},{4,20},{8,0},{12,28},{16,24},{20,4},{24,16},{28,12},{1,9},{5... | collective-permute-start | bytes 196616 | tf_op jit(solution)/shard_map/ppermute | solution.py:274
  16.0 1.2 %copy-start.3 = (f32[64]{0:T(128)S(1)}, f32[64]{0:T(128)}, u32[]{:S(2)}) copy-start(f32[64]{0:T(128)} %param.15) | copy-start | bytes 772
  16.0 4.3 %collective-permute-start.6 = (f32[128,128]{1,0:T(8,128)S(1)}, f32[128,128]{1,0:T(8,128)S(1)}, u32[]{:S(2)}, u32[]{:S(2)}) collective-permute-start(f32[128,128]{1,0:T(8,128)S(1)} %add.24.after_ref), channel_id=1, source_target_pairs={{0,8},{4,20},{8,0},{12,28},{16,24},{20,4},{24,16},{28,12},{1,9},{5... | collective-permute-start | bytes 196616 | tf_op jit(solution)/shard_map/ppermute | solution.py:274
  20.4 6.8 %collective-permute-start.7 = (f32[2,128,128]{2,1,0:T(8,128)S(1)}, f32[2,128,128]{2,1,0:T(8,128)S(1)}, u32[]{:S(2)}, u32[]{:S(2)}) collective-permute-start(f32[2,128,128]{2,1,0:T(8,128)S(1)} %pad_maximum_fusion.after_ref), channel_id=1, source_target_pairs={{0,16},{4,12},{8,24},{12,4},{16,0},{20,28},{24,8},{28,20},{1,17},{... | collective-permute-start | bytes 393224 | tf_op jit(solution)/shard_map/ppermute | solution.py:274
  27.2 3.7 %collective-permute-start.10 = (f32[2,128,128]{2,1,0:T(8,128)S(1)}, f32[2,128,128]{2,1,0:T(8,128)S(1)}, u32[]{:S(2)}, u32[]{:S(2)}) collective-permute-start(f32[2,128,128]{2,1,0:T(8,128)S(1)} %add_multiply_fusion.rest_7_), channel_id=1, source_target_pairs={{0,4},{4,0},{8,12},{12,8},{16,20},{20,16},{24,28},{28,24},{1,5},{5... | collective-permute-start | bytes 393224 | tf_op jit(solution)/shard_map/ppermute | solution.py:269
  27.4 7.2 %collective-permute-start.9 = (f32[2,128,128]{2,1,0:T(8,128)S(1)}, f32[2,128,128]{2,1,0:T(8,128)S(1)}, u32[]{:S(2)}, u32[]{:S(2)}) collective-permute-start(f32[2,128,128]{2,1,0:T(8,128)S(1)} %add_multiply_fusion.rest_7_), channel_id=1, source_target_pairs={{0,3},{1,2},{2,1},{3,0},{4,7},{5,6},{6,5},{7,4},{8,11},{9,10},{10,... | collective-permute-start | bytes 393224 | tf_op jit(solution)/shard_map/ppermute | solution.py:269
  29.3 7.7 %collective-permute-start.8 = (f32[2,128,128]{2,1,0:T(8,128)S(1)}, f32[2,128,128]{2,1,0:T(8,128)S(1)}, u32[]{:S(2)}, u32[]{:S(2)}) collective-permute-start(f32[2,128,128]{2,1,0:T(8,128)S(1)} %add_multiply_fusion.rest_7_), channel_id=1, source_target_pairs={{0,2},{1,3},{2,0},{3,1},{4,6},{5,7},{6,4},{7,5},{8,10},{9,11},{10,... | collective-permute-start | bytes 393224 | tf_op jit(solution)/shard_map/ppermute | solution.py:269
  30.0 7.1 %collective-permute-start.12 = (f32[2,128,128]{2,1,0:T(8,128)S(1)}, f32[2,128,128]{2,1,0:T(8,128)S(1)}, u32[]{:S(2)}, u32[]{:S(2)}) collective-permute-start(f32[2,128,128]{2,1,0:T(8,128)S(1)} %add_multiply_fusion.rest_7_), channel_id=1, source_target_pairs={{0,1},{1,0},{2,3},{3,2},{4,5},{5,4},{6,7},{7,6},{8,9},{9,8},{10,11... | collective-permute-start | bytes 393224 | tf_op jit(solution)/shard_map/ppermute | solution.py:269
  34.6 2.9 %collective-permute-start.14 = (f32[2,128,128]{2,1,0:T(8,128)S(1)}, f32[2,128,128]{2,1,0:T(8,128)S(1)}, u32[]{:S(2)}, u32[]{:S(2)}) collective-permute-start(f32[2,128,128]{2,1,0:T(8,128)S(1)} %collective-permute-done.9.rest_7_), channel_id=1, source_target_pairs={{0,4},{4,0},{8,12},{12,8},{16,20},{20,16},{24,28},{28,24},{1,5},{5... | collective-permute-start | bytes 393224 | tf_op jit(solution)/shard_map/ppermute | solution.py:269
  37.1 2.2 %collective-permute-start.13 = (f32[2,128,128]{2,1,0:T(8,128)S(1)}, f32[2,128,128]{2,1,0:T(8,128)S(1)}, u32[]{:S(2)}, u32[]{:S(2)}) collective-permute-start(f32[2,128,128]{2,1,0:T(8,128)S(1)} %collective-permute-done.12.rest_24_), channel_id=1, source_target_pairs={{0,4},{4,0},{8,12},{12,8},{16,20},{20,16},{24,28},{28,24},{1,5},{5... | collective-permute-start | bytes 393224 | tf_op jit(solution)/shard_map/ppermute | solution.py:269
  37.1 2.2 %collective-permute-start.11 = (f32[2,128,128]{2,1,0:T(8,128)S(1)}, f32[2,128,128]{2,1,0:T(8,128)S(1)}, u32[]{:S(2)}, u32[]{:S(2)}) collective-permute-start(f32[2,128,128]{2,1,0:T(8,128)S(1)} %collective-permute-done.8.rest_16_), channel_id=1, source_target_pairs={{0,4},{4,0},{8,12},{12,8},{16,20},{20,16},{24,28},{28,24},{1,5},{5... | collective-permute-start | bytes 393224 | tf_op jit(solution)/shard_map/ppermute | solution.py:269

commit v6 on v5

--- a/solution.py
+++ b/solution.py
@@ -387,7 +387,7 @@
     plane = {0: near}
     for group in range(group_count - 1, 0, -1):
         plane[group] = swap(near, "kvec", group)
-    far = {0: swap(near, "atoms", 1)}
+    far = {}
 
     def operands_of(parts):
         sides = [[plane[group], far.get(group)][first : first + count] for group, count, first in parts]
@@ -411,12 +411,19 @@
             name="fields_of_some_groups",
         )(*operands)
 
-    fields_so_far = partial_fields([(0, 2, 0)], [])
-    for group in range(group_count - 1, 0, -1):
+    fields_so_far = partial_fields([(0, 1, 0)], [])
+    late = [2, 1] if group_count > 3 else [1]
+    early = [group for group in range(group_count - 1, 0, -1) if group not in late]
+    for group in early:
+        plane[group], near, fields_so_far = lax.optimization_barrier((plane[group], near, fields_so_far))
+        if not far:
+            far[0] = swap(near, "atoms", 1)
+        far[group] = swap(plane[group], "atoms", 1)
+    fields_so_far = partial_fields([(0, 1, 1)] + [(group, 1, 0) for group in early], fields_so_far)
+    for group in late:
         plane[group], fields_so_far = lax.optimization_barrier((plane[group], fields_so_far))
         far[group] = swap(plane[group], "atoms", 1)
-    late = [2, 1] if group_count > 3 else [1]
-    parts = [(group, 2, 0) for group in range(group_count - 1, len(late), -1)] + [(group, 1, 0) for group in late]
+    parts = [(group, 1, 1) for group in early] + [(group, 1, 0) for group in late]
     fields_so_far = partial_fields(parts, fields_so_far)
 
     parts = [(group, 1, 1) for group in late]

time: 41.2 us -> 44.8 us (1.087)
  waiting for transfers between devices: 9.14 us -> 11.5 us
  starting transfers between devices: 15 us -> 15.7 us
    ppermute x12, waiting for transfers between devices: 6.22 us -> 8.61 us  [swap(): lax.ppermute(value, axis, [(place, place ^ offset) for place in range(siz...]
    ppermute x12, starting transfers between devices: 8.86 us -> 9.57 us  [swap(): lax.ppermute(value, axis, [(place, place ^ offset) for place in range(siz...]
    pallas_call x2 -> x3, Pallas kernels: 2.45 us -> 2.89 us  [partial_fields(): pl.pallas_call(functools.partial(partial_field_kernel, layout=layout, fir...]
  transfers between devices with their start and end apart: 15 -> 15, of which waited for: 7 -> 7; matrix products, arithmetic and copies ran while one was open for 0% -> 0% of each run, Pallas kernels for 31% -> 29%
where the time goes in v6:
time: 44.8 us; the launch traced here: 44.6 us
  starting transfers between devices  15.7 us (35%)
  Pallas kernels  14.8 us (33%)
  waiting for transfers between devices  11.5 us (26%)
  other arithmetic  1.01 us (2%)
  between operations  0.9 us (2%)
  local copies, waits for them, and re-layouts  0.67 us (1%)
    ppermute x12, starting transfers between devices, swap(): lax.ppermute(value, axis, [(place, place ^ offset) for place in range(siz...  9.57 us
    ppermute x12, waiting for transfers between devices, swap(): lax.ppermute(value, axis, [(place, place ^ offset) for place in range(siz...  8.61 us
    ppermute x3, starting transfers between devices, swap_along_z(): return lax.ppermute(value, 'atoms', pairs)  6.15 us
    pallas_call x4, Pallas kernels, waves_of(): pl.pallas_call(functools.partial(wave_kernel, atom_total=atoms * atom_cou...  3.76 us
    pallas_call x2, Pallas kernels, on_device(): pl.pallas_call(functools.partial(tile_kernel, channels=channels, vectors=...  3.11 us
    ppermute x3, waiting for transfers between devices, swap_along_z(): return lax.ppermute(value, 'atoms', pairs)  2.9 us
    pallas_call x3, Pallas kernels, partial_fields(): pl.pallas_call(functools.partial(partial_field_kernel, layout=layout, fir...  2.89 us
    pallas_call x1, Pallas kernels, on_device(): pl.pallas_call(functools.partial(charge_kernel, groups=group_count), out_...  2.08 us
  transfers between devices with their start and end apart: 15, of which 7 were waited for; matrix products, arithmetic and copies ran while one was open for 0% of the time, Pallas kernels for 29%

profile of v6, /device:TPU:0, one launch (start us, length us, event | category | flops | bytes accessed | tf_op | source)
XLA Modules:
  0.0 44.6 jit_solution(12264470421892021623)
XLA Ops:
  0.6 0.9 %convert_add_fusion.packed_ref.rest_4_ = f32[72,512]{1,0:T(8,128)S(1)} fusion(s32[3,256]{1,0:T(4,128)} %param.14, f32[64,512]{1,0:T(8,128)} %param.19), kind=kLoop, calls=%fused_computation | loop fusion | flops 73728 | bytes 281600 | tf_op jit(solution)/shard_map/add | solution.py:302
  1.6 3.0 %collective-permute-start = (f32[72,512]{1,0:T(8,128)S(1)}, f32[72,512]{1,0:T(8,128)S(1)}, u32[]{:S(2)}, u32[]{:S(2)}) collective-permute-start(f32[72,512]{1,0:T(8,128)S(1)} %convert_add_fusion.packed_ref.rest_4_), channel_id=1, source_target_pairs={{0,1},{1,0},{2,3},{3,2},{4,5},{5,4},{6,7},{7,6},{8,9},{9,8},{10,11... | collective-permute-start | bytes 442376 | tf_op jit(solution)/shard_map/ppermute | solution.py:269
  4.6 1.5 %collective-permute-start.2 = (f32[72,512]{1,0:T(8,128)S(1)}, f32[72,512]{1,0:T(8,128)S(1)}, u32[]{:S(2)}, u32[]{:S(2)}) collective-permute-start(f32[72,512]{1,0:T(8,128)S(1)} %convert_add_fusion.packed_ref.rest_4_), channel_id=1, source_target_pairs={{0,2},{1,3},{2,0},{3,1},{4,6},{5,7},{6,4},{7,5},{8,10},{9,11},{10,... | collective-permute-start | bytes 442376 | tf_op jit(solution)/shard_map/ppermute | solution.py:269
  6.1 1.5 %waves_of_own_vectors.2 = (bf16[256,2048]{1,0:T(8,128)(2,1)S(1)}, bf16[256,2048]{1,0:T(8,128)(2,1)S(1)}) custom-call(f32[3,2048]{1,0:T(4,128)S(1)} %copy-done, f32[72,512]{1,0:T(8,128)S(1)} %convert_add_fusion.packed_ref.rest_4_), custom_call_target="tpu_custom_call" | custom-call | flops 2359296000 | tf_op jit(solution)/shard_map/waves_of_own_vectors/pallas_call | solution.py:308
  7.7 1.6 %waves_of_own_vectors.3 = (bf16[256,2048]{1,0:T(8,128)(2,1)S(1)}, bf16[256,2048]{1,0:T(8,128)(2,1)S(1)}) custom-call(f32[3,2048]{1,0:T(4,128)S(1)} %copy-done, f32[72,512]{1,0:T(8,128)S(1)} %convert_add_fusion.packed_ref.rest_4_), custom_call_target="tpu_custom_call" | custom-call | flops 2359296000 | tf_op jit(solution)/shard_map/waves_of_own_vectors/pallas_call | solution.py:308
  10.0 2.1 %charge_sums.1 = (f32[128,128]{1,0:T(8,128)S(1)}, f32[128,128]{1,0:T(8,128)S(1)}, f32[136,512]{1,0:T(8,128)S(1)}, f32[1,2048]{1,0:T(1,128)S(1)}, f32[256,128]{1,0:T(8,128)S(1)}) custom-call(s32[1,8]{1,0:T(1,128)S(1)} %bitcast.14, f32[64,2048]{1,0:T(8,128)S(1)} %copy-done.4, s32[1,2048]{1,0:T(1,128)S(1)} %bitcast.12, f32[64,64]{1,0:T(8,128)S(1)} %copy-done.1, ...), custom_call_target="tpu_custom_call" | custom-call | flops 2013265920 | tf_op jit(solution)/shard_map/charge_sums/pallas_call | solution.py:320
  12.2 0.9 %collective-permute-done.2.rest_4_.packed_ref = f32[72,512]{1,0:T(8,128)S(1)} collective-permute-done((f32[72,512]{1,0:T(8,128)S(1)}, f32[72,512]{1,0:T(8,128)S(1)}, u32[]{:S(2)}, u32[]{:S(2)}) %collective-permute-start.2) | collective-permute-done | bytes 147488 | tf_op jit(solution)/shard_map/ppermute | solution.py:269
  13.1 1.1 %adjoint_sums.1 = (f32[128,128]{1,0:T(8,128)S(1)}, f32[128,128]{1,0:T(8,128)S(1)}) custom-call(f32[1,2048]{1,0:T(1,128)S(1)} %get-tuple-element.101.mask_ref, f32[64,64]{1,0:T(8,128)S(1)} %copy-done.2, f32[256,128]{1,0:T(8,128)S(1)} %get-tuple-element.102.part_ref, bf16[256,2048]{1,0:T(8,128)(2,1)S(1)} %get-tuple-element.95.rest_0_, ...), custom_call_target="tpu_custom_call" | custom-call | flops 2013265920 | tf_op jit(solution)/shard_map/adjoint_sums/pallas_call | solution.py:351
  14.3 1.7 %collective-permute-start.5 = (f32[128,128]{1,0:T(8,128)S(1)}, f32[128,128]{1,0:T(8,128)S(1)}, u32[]{:S(2)}, u32[]{:S(2)}) collective-permute-start(f32[128,128]{1,0:T(8,128)S(1)} %add.23), channel_id=1, source_target_pairs={{0,8},{4,20},{8,0},{12,28},{16,24},{20,4},{24,16},{28,12},{1,9},{5... | collective-permute-start | bytes 196616 | tf_op jit(solution)/shard_map/ppermute | solution.py:274
  16.0 1.2 %collective-permute-start.6 = (f32[128,128]{1,0:T(8,128)S(1)}, f32[128,128]{1,0:T(8,128)S(1)}, u32[]{:S(2)}, u32[]{:S(2)}) collective-permute-start(f32[128,128]{1,0:T(8,128)S(1)} %add.24.after_ref), channel_id=1, source_target_pairs={{0,8},{4,20},{8,0},{12,28},{16,24},{20,4},{24,16},{28,12},{1,9},{5... | collective-permute-start | bytes 196616 | tf_op jit(solution)/shard_map/ppermute | solution.py:274
  17.2 1.1 %waves_of_own_atoms.4 = (f32[128,128]{1,0:T(8,128)S(1)}, f32[256,512]{1,0:T(8,128)S(1)}, f32[256,512]{1,0:T(8,128)S(1)}, bf16[256,512]{1,0:T(8,128)(2,1)S(1)}, b...) custom-call(f32[3,2048]{1,0:T(4,128)S(1)} %copy-done, ...), custom_call_target="tpu_custom_call" | custom-call | flops 2621440 | tf_op jit(solution)/shard_map/waves_of_own_atoms/pallas_call | solution.py:338
  18.3 0.9 %waves_of_own_atoms.5 = (f32[256,512]{1,0:T(8,128)S(1)}, f32[256,512]{1,0:T(8,128)S(1)}, bf16[256,512]{1,0:T(8,128)(2,1)S(1)}, bf16[256,512]{1,0:T(8,128)(2,1)S(...) custom-call(f32[3,2048]{1,0:T(4,128)S(1)} %copy-done, ...), custom_call_target="tpu_custom_call" | custom-call | flops 2621440 | tf_op jit(solution)/shard_map/waves_of_own_atoms/pallas_call | solution.py:338
  19.3 1.0 %collective-permute-done.6 = f32[128,128]{1,0:T(8,128)S(1)} collective-permute-done((f32[128,128]{1,0:T(8,128)S(1)}, f32[128,128]{1,0:T(8,128)S(1)}, u32[]{:S(2)}, u32[]{:S(2)}) %collective-permute-start.6) | collective-permute-done | bytes 65568 | tf_op jit(solution)/shard_map/ppermute | solution.py:274
  20.4 3.3 %collective-permute-start.7 = (f32[2,128,128]{2,1,0:T(8,128)S(1)}, f32[2,128,128]{2,1,0:T(8,128)S(1)}, u32[]{:S(2)}, u32[]{:S(2)}) collective-permute-start(f32[2,128,128]{2,1,0:T(8,128)S(1)} %pad_maximum_fusion.after_ref), channel_id=1, source_target_pairs={{0,16},{4,12},{8,24},{12,4},{16,0},{20,28},{24,8},{28,20},{1,17},{... | collective-permute-start | bytes 393224 | tf_op jit(solution)/shard_map/ppermute | solution.py:274
  25.4 1.8 %collective-permute-done.7 = f32[2,128,128]{2,1,0:T(8,128)S(1)} collective-permute-done((f32[2,128,128]{2,1,0:T(8,128)S(1)}, f32[2,128,128]{2,1,0:T(8,128)S(1)}, u32[]{:S(2)}, u32[]{:S(2)}) %collective-permute-start.7) | collective-permute-done | bytes 131104 | tf_op jit(solution)/shard_map/ppermute | solution.py:274
  27.2 1.9 %collective-permute-start.9 = (f32[2,128,128]{2,1,0:T(8,128)S(1)}, f32[2,128,128]{2,1,0:T(8,128)S(1)}, u32[]{:S(2)}, u32[]{:S(2)}) collective-permute-start(f32[2,128,128]{2,1,0:T(8,128)S(1)} %add_multiply_fusion.rest_7_), channel_id=1, source_target_pairs={{0,3},{1,2},{2,1},{3,0},{4,7},{5,6},{6,5},{7,4},{8,11},{9,10},{10,... | collective-permute-start | bytes 393224 | tf_op jit(solution)/shard_map/ppermute | solution.py:269
  29.7 4.0 %collective-permute-done.9.rest_15_ = f32[2,128,128]{2,1,0:T(8,128)S(1)} collective-permute-done((f32[2,128,128]{2,1,0:T(8,128)S(1)}, f32[2,128,128]{2,1,0:T(8,128)S(1)}, u32[]{:S(2)}, u32[]{:S(2)}) %collective-permute-start.9) | collective-permute-done | bytes 131104 | tf_op jit(solution)/shard_map/ppermute | solution.py:269
  33.7 1.5 %collective-permute-start.8 = (f32[2,128,128]{2,1,0:T(8,128)S(1)}, f32[2,128,128]{2,1,0:T(8,128)S(1)}, u32[]{:S(2)}, u32[]{:S(2)}) collective-permute-start(f32[2,128,128]{2,1,0:T(8,128)S(1)} %add_multiply_fusion.rest_7_), channel_id=1, source_target_pairs={{0,2},{1,3},{2,0},{3,1},{4,6},{5,7},{6,4},{7,5},{8,10},{9,11},{10,... | collective-permute-start | bytes 393224 | tf_op jit(solution)/shard_map/ppermute | solution.py:269
  35.2 0.9 %collective-permute-start.12 = (f32[2,128,128]{2,1,0:T(8,128)S(1)}, f32[2,128,128]{2,1,0:T(8,128)S(1)}, u32[]{:S(2)}, u32[]{:S(2)}) collective-permute-start(f32[2,128,128]{2,1,0:T(8,128)S(1)} %add_multiply_fusion.rest_7_), channel_id=1, source_target_pairs={{0,1},{1,0},{2,3},{3,2},{4,5},{5,4},{6,7},{7,6},{8,9},{9,8},{10,11... | collective-permute-start | bytes 393224 | tf_op jit(solution)/shard_map/ppermute | solution.py:269
  36.1 0.9 %fields_of_some_groups.4 = (f32[128,512]{1,0:T(8,128)S(1)}, f32[24,512]{1,0:T(8,128)S(1)}) custom-call(f32[136,512]{1,0:T(8,128)S(1)} %get-tuple-element.99.own_ref, f32[256,512]{1,0:T(8,128)S(1)} %get-tuple-element.150.rest_0_, f32[256,512]{1,0:T(8,128)S(1)} %get-tuple-element.151.rest_1_, bf16[256,512]{1,0:T(8,128)(2,1)S(1)} %get-tuple-element.152.rest_2_, ...), custom_call_target="tpu_custom_call" | custom-call | flops 131072 | tf_op jit(solution)/shard_map/fields_of_some_groups/pallas_call | solution.py:403
  37.1 2.5 %collective-permute-done.8.rest_15_ = f32[2,128,128]{2,1,0:T(8,128)S(1)} collective-permute-done((f32[2,128,128]{2,1,0:T(8,128)S(1)}, f32[2,128,128]{2,1,0:T(8,128)S(1)}, u32[]{:S(2)}, u32[]{:S(2)}) %collective-permute-start.8) | collective-permute-done | bytes 131104 | tf_op jit(solution)/shard_map/ppermute | solution.py:269
  39.6 1.2 %collective-permute-done.12.rest_23_ = f32[2,128,128]{2,1,0:T(8,128)S(1)} collective-permute-done((f32[2,128,128]{2,1,0:T(8,128)S(1)}, f32[2,128,128]{2,1,0:T(8,128)S(1)}, u32[]{:S(2)}, u32[]{:S(2)}) %collective-permute-start.12) | collective-permute-done | bytes 131104 | tf_op jit(solution)/shard_map/ppermute | solution.py:269
  41.3 1.4 %fields_of_some_groups.5 = (f32[128,512]{1,0:T(8,128)S(1)}, f32[24,512]{1,0:T(8,128)S(1)}) custom-call(f32[136,512]{1,0:T(8,128)S(1)} %get-tuple-element.99.own_ref, f32[256,512]{1,0:T(8,128)S(1)} %get-tuple-element.160.rest_8_.rest_0_, f32[256,512]{1,0:T(8,128)S(1)} %get-tuple-element.161.rest_9_.rest_1_, ...), custom_call_target="tpu_custom_call" | custom-call | flops 131072 | tf_op jit(solution)/shard_map/fields_of_some_groups/pallas_call | solution.py:403
  42.8 1.8 %fields_and_forces.1 = (f32[64,512]{1,0:T(8,128)}, f32[3,512]{1,0:T(4,128)}, f32[64,512]{1,0:T(8,128)}) custom-call(f32[136,512]{1,0:T(8,128)S(1)} %get-tuple-element.99.own_ref, f32[64,64]{1,0:T(8,128)S(1)} %copy-done.2, f32[64,64]{1,0:T(8,128)S(1)} %copy-done.1, f32[256,512]{1,0:T(8,128)S(1)} %get-tuple-element.141.rest_8_.rest_0_, ...), custom_call_target="tpu_custom_call" | custom-call | flops 131072 | tf_op jit(solution)/shard_map/fields_and_forces/pallas_call | solution.py:433
  (40 shorter events, 3.9 us)
Async XLA Ops:
  0.6 5.5 %copy-start = (f32[3,2048]{1,0:T(4,128)S(1)}, f32[3,2048]{1,0:T(4,128)}, u32[]{:S(2)}) copy-start(f32[3,2048]{1,0:T(4,128)} %pos_ref.11) | copy-start | bytes 73732
  1.6 7.7 %collective-permute-start = (f32[72,512]{1,0:T(8,128)S(1)}, f32[72,512]{1,0:T(8,128)S(1)}, u32[]{:S(2)}, u32[]{:S(2)}) collective-permute-start(f32[72,512]{1,0:T(8,128)S(1)} %convert_add_fusion.packed_ref.rest_4_), channel_id=1, source_target_pairs={{0,1},{1,0},{2,3},{3,2},{4,5},{5,4},{6,7},{7,6},{8,9},{9,8},{10,11... | collective-permute-start | bytes 442376 | tf_op jit(solution)/shard_map/ppermute | solution.py:269
  4.6 8.5 %collective-permute-start.2 = (f32[72,512]{1,0:T(8,128)S(1)}, f32[72,512]{1,0:T(8,128)S(1)}, u32[]{:S(2)}, u32[]{:S(2)}) collective-permute-start(f32[72,512]{1,0:T(8,128)S(1)} %convert_add_fusion.packed_ref.rest_4_), channel_id=1, source_target_pairs={{0,2},{1,3},{2,0},{3,1},{4,6},{5,7},{6,4},{7,5},{8,10},{9,11},{10,... | collective-permute-start | bytes 442376 | tf_op jit(solution)/shard_map/ppermute | solution.py:269
  6.1 7.0 %collective-permute-start.3 = (f32[72,512]{1,0:T(8,128)S(1)}, f32[72,512]{1,0:T(8,128)S(1)}, u32[]{:S(2)}, u32[]{:S(2)}) collective-permute-start(f32[72,512]{1,0:T(8,128)S(1)} %convert_add_fusion.packed_ref.rest_4_), channel_id=1, source_target_pairs={{0,3},{1,2},{2,1},{3,0},{4,7},{5,6},{6,5},{7,4},{8,11},{9,10},{10,... | collective-permute-start | bytes 442376 | tf_op jit(solution)/shard_map/ppermute | solution.py:269
  7.7 1.7 %copy-start.1 = (f32[64,64]{1,0:T(8,128)S(1)}, f32[64,64]{1,0:T(8,128)}, u32[]{:S(2)}) copy-start(f32[64,64]{1,0:T(8,128)} %w_charge_ref.3) | copy-start | bytes 49156
  7.7 1.7 %copy-start.2 = (f32[64,64]{1,0:T(8,128)S(1)}, f32[64,64]{1,0:T(8,128)}, u32[]{:S(2)}) copy-start(f32[64,64]{1,0:T(8,128)} %w_out_ref.5) | copy-start | bytes 49156
  7.7 1.7 %copy-start.4 = (f32[64,2048]{1,0:T(8,128)S(1)}, f32[64,2048]{1,0:T(8,128)}, u32[]{:S(2)}) copy-start(f32[64,2048]{1,0:T(8,128)} %feats_ref.1) | copy-start | bytes 1572868
  7.7 1.7 %copy-start.6 = (f32[64,16]{0,1:T(8,128)S(1)}, f32[64,16]{0,1:T(8,128)}, u32[]{:S(2)}) copy-start(f32[64,16]{0,1:T(8,128)} %param.17) | copy-start | bytes 12292
  9.3 0.7 %copy-start.5 = (s32[2048]{0:T(1024)S(1)}, s32[2048]{0:T(1024)}, u32[]{:S(2)}) copy-start(s32[2048]{0:T(1024)} %param.12) | copy-start | bytes 24580
  9.3 0.7 %copy-start.7 = (s32[8]{0:T(128)S(1)}, s32[8]{0:T(128)}, u32[]{:S(2)}) copy-start(s32[8]{0:T(128)} %param.13) | copy-start | bytes 100
  12.1 2.1 %collective-permute-start.1 = (f32[128,128]{1,0:T(8,128)S(1)}, f32[128,128]{1,0:T(8,128)S(1)}, u32[]{:S(2)}, u32[]{:S(2)}) collective-permute-start(f32[128,128]{1,0:T(8,128)S(1)} %get-tuple-element.100), channel_id=1, source_target_pairs={{0,4},{4,0},{8,12},{12,8},{16,20},{20,16},{24,28},{28,24},{1,5},{5... | collective-permute-start | bytes 196616 | tf_op jit(solution)/shard_map/ppermute | solution.py:269
  14.2 1.8 %collective-permute-start.4 = (f32[128,128]{1,0:T(8,128)S(1)}, f32[128,128]{1,0:T(8,128)S(1)}, u32[]{:S(2)}, u32[]{:S(2)}) collective-permute-start(f32[128,128]{1,0:T(8,128)S(1)} %get-tuple-element.104), channel_id=1, source_target_pairs={{0,4},{4,0},{8,12},{12,8},{16,20},{20,16},{24,28},{28,24},{1,5},{5... | collective-permute-start | bytes 196616 | tf_op jit(solution)/shard_map/ppermute | solution.py:269
  14.3 5.0 %collective-permute-start.5 = (f32[128,128]{1,0:T(8,128)S(1)}, f32[128,128]{1,0:T(8,128)S(1)}, u32[]{:S(2)}, u32[]{:S(2)}) collective-permute-start(f32[128,128]{1,0:T(8,128)S(1)} %add.23), channel_id=1, source_target_pairs={{0,8},{4,20},{8,0},{12,28},{16,24},{20,4},{24,16},{28,12},{1,9},{5... | collective-permute-start | bytes 196616 | tf_op jit(solution)/shard_map/ppermute | solution.py:274
  16.0 1.2 %copy-start.3 = (f32[64]{0:T(128)S(1)}, f32[64]{0:T(128)}, u32[]{:S(2)}) copy-start(f32[64]{0:T(128)} %param.15) | copy-start | bytes 772
  16.0 4.3 %collective-permute-start.6 = (f32[128,128]{1,0:T(8,128)S(1)}, f32[128,128]{1,0:T(8,128)S(1)}, u32[]{:S(2)}, u32[]{:S(2)}) collective-permute-start(f32[128,128]{1,0:T(8,128)S(1)} %add.24.after_ref), channel_id=1, source_target_pairs={{0,8},{4,20},{8,0},{12,28},{16,24},{20,4},{24,16},{28,12},{1,9},{5... | collective-permute-start | bytes 196616 | tf_op jit(solution)/shard_map/ppermute | solution.py:274
  20.4 6.8 %collective-permute-start.7 = (f32[2,128,128]{2,1,0:T(8,128)S(1)}, f32[2,128,128]{2,1,0:T(8,128)S(1)}, u32[]{:S(2)}, u32[]{:S(2)}) collective-permute-start(f32[2,128,128]{2,1,0:T(8,128)S(1)} %pad_maximum_fusion.after_ref), channel_id=1, source_target_pairs={{0,16},{4,12},{8,24},{12,4},{16,0},{20,28},{24,8},{28,20},{1,17},{... | collective-permute-start | bytes 393224 | tf_op jit(solution)/shard_map/ppermute | solution.py:274
  27.2 6.5 %collective-permute-start.9 = (f32[2,128,128]{2,1,0:T(8,128)S(1)}, f32[2,128,128]{2,1,0:T(8,128)S(1)}, u32[]{:S(2)}, u32[]{:S(2)}) collective-permute-start(f32[2,128,128]{2,1,0:T(8,128)S(1)} %add_multiply_fusion.rest_7_), channel_id=1, source_target_pairs={{0,3},{1,2},{2,1},{3,0},{4,7},{5,6},{6,5},{7,4},{8,11},{9,10},{10,... | collective-permute-start | bytes 393224 | tf_op jit(solution)/shard_map/ppermute | solution.py:269
  33.7 2.4 %collective-permute-start.10 = (f32[2,128,128]{2,1,0:T(8,128)S(1)}, f32[2,128,128]{2,1,0:T(8,128)S(1)}, u32[]{:S(2)}, u32[]{:S(2)}) collective-permute-start(f32[2,128,128]{2,1,0:T(8,128)S(1)} %add_multiply_fusion.rest_7_), channel_id=1, source_target_pairs={{0,4},{4,0},{8,12},{12,8},{16,20},{20,16},{24,28},{28,24},{1,5},{5... | collective-permute-start | bytes 393224 | tf_op jit(solution)/shard_map/ppermute | solution.py:269
  33.7 5.9 %collective-permute-start.8 = (f32[2,128,128]{2,1,0:T(8,128)S(1)}, f32[2,128,128]{2,1,0:T(8,128)S(1)}, u32[]{:S(2)}, u32[]{:S(2)}) collective-permute-start(f32[2,128,128]{2,1,0:T(8,128)S(1)} %add_multiply_fusion.rest_7_), channel_id=1, source_target_pairs={{0,2},{1,3},{2,0},{3,1},{4,6},{5,7},{6,4},{7,5},{8,10},{9,11},{10,... | collective-permute-start | bytes 393224 | tf_op jit(solution)/shard_map/ppermute | solution.py:269
  35.2 5.6 %collective-permute-start.12 = (f32[2,128,128]{2,1,0:T(8,128)S(1)}, f32[2,128,128]{2,1,0:T(8,128)S(1)}, u32[]{:S(2)}, u32[]{:S(2)}) collective-permute-start(f32[2,128,128]{2,1,0:T(8,128)S(1)} %add_multiply_fusion.rest_7_), channel_id=1, source_target_pairs={{0,1},{1,0},{2,3},{3,2},{4,5},{5,4},{6,7},{7,6},{8,9},{9,8},{10,11... | collective-permute-start | bytes 393224 | tf_op jit(solution)/shard_map/ppermute | solution.py:269
  36.1 5.2 %collective-permute-start.14 = (f32[2,128,128]{2,1,0:T(8,128)S(1)}, f32[2,128,128]{2,1,0:T(8,128)S(1)}, u32[]{:S(2)}, u32[]{:S(2)}) collective-permute-start(f32[2,128,128]{2,1,0:T(8,128)S(1)} %collective-permute-done.9.rest_15_), channel_id=1, source_target_pairs={{0,4},{4,0},{8,12},{12,8},{16,20},{20,16},{24,28},{28,24},{1,5},{5... | collective-permute-start | bytes 393224 | tf_op jit(solution)/shard_map/ppermute | solution.py:269
  40.8 1.9 %collective-permute-start.13 = (f32[2,128,128]{2,1,0:T(8,128)S(1)}, f32[2,128,128]{2,1,0:T(8,128)S(1)}, u32[]{:S(2)}, u32[]{:S(2)}) collective-permute-start(f32[2,128,128]{2,1,0:T(8,128)S(1)} %collective-permute-done.12.rest_23_), channel_id=1, source_target_pairs={{0,4},{4,0},{8,12},{12,8},{16,20},{20,16},{24,28},{28,24},{1,5},{5... | collective-permute-start | bytes 393224 | tf_op jit(solution)/shard_map/ppermute | solution.py:269
  40.8 1.9 %collective-permute-start.11 = (f32[2,128,128]{2,1,0:T(8,128)S(1)}, f32[2,128,128]{2,1,0:T(8,128)S(1)}, u32[]{:S(2)}, u32[]{:S(2)}) collective-permute-start(f32[2,128,128]{2,1,0:T(8,128)S(1)} %collective-permute-done.8.rest_15_), channel_id=1, source_target_pairs={{0,4},{4,0},{8,12},{12,8},{16,20},{20,16},{24,28},{28,24},{1,5},{5... | collective-permute-start | bytes 393224 | tf_op jit(solution)/shard_map/ppermute | solution.py:269

commit v7 on v6

--- a/solution.py
+++ b/solution.py
@@ -419,11 +419,11 @@
         if not far:
             far[0] = swap(near, "atoms", 1)
         far[group] = swap(plane[group], "atoms", 1)
-    fields_so_far = partial_fields([(0, 1, 1)] + [(group, 1, 0) for group in early], fields_so_far)
+    fields_so_far = partial_fields([(group, 1, 0) for group in early], fields_so_far)
     for group in late:
         plane[group], fields_so_far = lax.optimization_barrier((plane[group], fields_so_far))
         far[group] = swap(plane[group], "atoms", 1)
-    parts = [(group, 1, 1) for group in early] + [(group, 1, 0) for group in late]
+    parts = [(group, 1, 1) for group in [0] + early] + [(group, 1, 0) for group in late]
     fields_so_far = partial_fields(parts, fields_so_far)
 
     parts = [(group, 1, 1) for group in late]

time: 44.8 us -> 40.9 us (0.913)
  waiting for transfers between devices: 11.5 us -> 7.83 us
    ppermute x12, waiting for transfers between devices: 8.61 us -> 4.78 us  [swap(): lax.ppermute(value, axis, [(place, place ^ offset) for place in range(siz...]
  transfers between devices with their start and end apart: 15 -> 15, of which waited for: 7 -> 7; matrix products, arithmetic and copies ran while one was open for 0% -> 0% of each run, Pallas kernels for 29% -> 32%
where the time goes in v7:
time: 40.9 us; the launch traced here: 40.8 us
  starting transfers between devices  15.5 us (38%)
  Pallas kernels  14.9 us (36%)
  waiting for transfers between devices  7.83 us (19%)
  other arithmetic  1.01 us (2%)
  between operations  0.9 us (2%)
  local copies, waits for them, and re-layouts  0.67 us (2%)
    ppermute x12, starting transfers between devices, swap(): lax.ppermute(value, axis, [(place, place ^ offset) for place in range(siz...  9.26 us
    ppermute x3, starting transfers between devices, swap_along_z(): return lax.ppermute(value, 'atoms', pairs)  6.2 us
    ppermute x12, waiting for transfers between devices, swap(): lax.ppermute(value, axis, [(place, place ^ offset) for place in range(siz...  4.78 us
    pallas_call x4, Pallas kernels, waves_of(): pl.pallas_call(functools.partial(wave_kernel, atom_total=atoms * atom_cou...  3.76 us
    pallas_call x2, Pallas kernels, on_device(): pl.pallas_call(functools.partial(tile_kernel, channels=channels, vectors=...  3.16 us
    ppermute x3, waiting for transfers between devices, swap_along_z(): return lax.ppermute(value, 'atoms', pairs)  3.04 us
    pallas_call x3, Pallas kernels, partial_fields(): pl.pallas_call(functools.partial(partial_field_kernel, layout=layout, fir...  2.93 us
    pallas_call x1, Pallas kernels, on_device(): pl.pallas_call(functools.partial(charge_kernel, groups=group_count), out_...  2.08 us
  transfers between devices with their start and end apart: 15, of which 7 were waited for; matrix products, arithmetic and copies ran while one was open for 0% of the time, Pallas kernels for 32%

profile of v7, /device:TPU:0, one launch (start us, length us, event | category | flops | bytes accessed | tf_op | source)
XLA Modules:
  0.0 40.8 jit_solution(10791970386801885130)
XLA Ops:
  0.6 0.9 %convert_add_fusion.packed_ref.rest_4_ = f32[72,512]{1,0:T(8,128)S(1)} fusion(s32[3,256]{1,0:T(4,128)} %param.14, f32[64,512]{1,0:T(8,128)} %param.19), kind=kLoop, calls=%fused_computation | loop fusion | flops 73728 | bytes 281600 | tf_op jit(solution)/shard_map/add | solution.py:302
  1.6 3.0 %collective-permute-start = (f32[72,512]{1,0:T(8,128)S(1)}, f32[72,512]{1,0:T(8,128)S(1)}, u32[]{:S(2)}, u32[]{:S(2)}) collective-permute-start(f32[72,512]{1,0:T(8,128)S(1)} %convert_add_fusion.packed_ref.rest_4_), channel_id=1, source_target_pairs={{0,1},{1,0},{2,3},{3,2},{4,5},{5,4},{6,7},{7,6},{8,9},{9,8},{10,11... | collective-permute-start | bytes 442376 | tf_op jit(solution)/shard_map/ppermute | solution.py:269
  4.6 1.5 %collective-permute-start.2 = (f32[72,512]{1,0:T(8,128)S(1)}, f32[72,512]{1,0:T(8,128)S(1)}, u32[]{:S(2)}, u32[]{:S(2)}) collective-permute-start(f32[72,512]{1,0:T(8,128)S(1)} %convert_add_fusion.packed_ref.rest_4_), channel_id=1, source_target_pairs={{0,2},{1,3},{2,0},{3,1},{4,6},{5,7},{6,4},{7,5},{8,10},{9,11},{10,... | collective-permute-start | bytes 442376 | tf_op jit(solution)/shard_map/ppermute | solution.py:269
  6.1 1.6 %waves_of_own_vectors.2 = (bf16[256,2048]{1,0:T(8,128)(2,1)S(1)}, bf16[256,2048]{1,0:T(8,128)(2,1)S(1)}) custom-call(f32[3,2048]{1,0:T(4,128)S(1)} %copy-done, f32[72,512]{1,0:T(8,128)S(1)} %convert_add_fusion.packed_ref.rest_4_), custom_call_target="tpu_custom_call" | custom-call | flops 2359296000 | tf_op jit(solution)/shard_map/waves_of_own_vectors/pallas_call | solution.py:308
  7.8 1.6 %waves_of_own_vectors.3 = (bf16[256,2048]{1,0:T(8,128)(2,1)S(1)}, bf16[256,2048]{1,0:T(8,128)(2,1)S(1)}) custom-call(f32[3,2048]{1,0:T(4,128)S(1)} %copy-done, f32[72,512]{1,0:T(8,128)S(1)} %convert_add_fusion.packed_ref.rest_4_), custom_call_target="tpu_custom_call" | custom-call | flops 2359296000 | tf_op jit(solution)/shard_map/waves_of_own_vectors/pallas_call | solution.py:308
  10.1 2.1 %charge_sums.1 = (f32[128,128]{1,0:T(8,128)S(1)}, f32[128,128]{1,0:T(8,128)S(1)}, f32[136,512]{1,0:T(8,128)S(1)}, f32[1,2048]{1,0:T(1,128)S(1)}, f32[256,128]{1,0:T(8,128)S(1)}) custom-call(s32[1,8]{1,0:T(1,128)S(1)} %bitcast.14, f32[64,2048]{1,0:T(8,128)S(1)} %copy-done.4, s32[1,2048]{1,0:T(1,128)S(1)} %bitcast.12, f32[64,64]{1,0:T(8,128)S(1)} %copy-done.1, ...), custom_call_target="tpu_custom_call" | custom-call | flops 2013265920 | tf_op jit(solution)/shard_map/charge_sums/pallas_call | solution.py:320
  12.2 0.8 %collective-permute-done.2.rest_4_.packed_ref = f32[72,512]{1,0:T(8,128)S(1)} collective-permute-done((f32[72,512]{1,0:T(8,128)S(1)}, f32[72,512]{1,0:T(8,128)S(1)}, u32[]{:S(2)}, u32[]{:S(2)}) %collective-permute-start.2) | collective-permute-done | bytes 147488 | tf_op jit(solution)/shard_map/ppermute | solution.py:269
  13.1 1.1 %adjoint_sums.1 = (f32[128,128]{1,0:T(8,128)S(1)}, f32[128,128]{1,0:T(8,128)S(1)}) custom-call(f32[1,2048]{1,0:T(1,128)S(1)} %get-tuple-element.101.mask_ref, f32[64,64]{1,0:T(8,128)S(1)} %copy-done.2, f32[256,128]{1,0:T(8,128)S(1)} %get-tuple-element.102.part_ref, bf16[256,2048]{1,0:T(8,128)(2,1)S(1)} %get-tuple-element.95.rest_0_, ...), custom_call_target="tpu_custom_call" | custom-call | flops 2013265920 | tf_op jit(solution)/shard_map/adjoint_sums/pallas_call | solution.py:351
  14.3 1.8 %collective-permute-start.5 = (f32[128,128]{1,0:T(8,128)S(1)}, f32[128,128]{1,0:T(8,128)S(1)}, u32[]{:S(2)}, u32[]{:S(2)}) collective-permute-start(f32[128,128]{1,0:T(8,128)S(1)} %add.23), channel_id=1, source_target_pairs={{0,8},{4,20},{8,0},{12,28},{16,24},{20,4},{24,16},{28,12},{1,9},{5... | collective-permute-start | bytes 196616 | tf_op jit(solution)/shard_map/ppermute | solution.py:274
  16.1 1.1 %collective-permute-start.6 = (f32[128,128]{1,0:T(8,128)S(1)}, f32[128,128]{1,0:T(8,128)S(1)}, u32[]{:S(2)}, u32[]{:S(2)}) collective-permute-start(f32[128,128]{1,0:T(8,128)S(1)} %add.24.after_ref), channel_id=1, source_target_pairs={{0,8},{4,20},{8,0},{12,28},{16,24},{20,4},{24,16},{28,12},{1,9},{5... | collective-permute-start | bytes 196616 | tf_op jit(solution)/shard_map/ppermute | solution.py:274
  17.2 1.1 %waves_of_own_atoms.4 = (f32[128,128]{1,0:T(8,128)S(1)}, f32[256,512]{1,0:T(8,128)S(1)}, f32[256,512]{1,0:T(8,128)S(1)}, bf16[256,512]{1,0:T(8,128)(2,1)S(1)}, b...) custom-call(f32[3,2048]{1,0:T(4,128)S(1)} %copy-done, ...), custom_call_target="tpu_custom_call" | custom-call | flops 2621440 | tf_op jit(solution)/shard_map/waves_of_own_atoms/pallas_call | solution.py:338
  18.3 0.9 %waves_of_own_atoms.5 = (f32[256,512]{1,0:T(8,128)S(1)}, f32[256,512]{1,0:T(8,128)S(1)}, bf16[256,512]{1,0:T(8,128)(2,1)S(1)}, bf16[256,512]{1,0:T(8,128)(2,1)S(...) custom-call(f32[3,2048]{1,0:T(4,128)S(1)} %copy-done, ...), custom_call_target="tpu_custom_call" | custom-call | flops 2621440 | tf_op jit(solution)/shard_map/waves_of_own_atoms/pallas_call | solution.py:338
  19.3 1.1 %collective-permute-done.6 = f32[128,128]{1,0:T(8,128)S(1)} collective-permute-done((f32[128,128]{1,0:T(8,128)S(1)}, f32[128,128]{1,0:T(8,128)S(1)}, u32[]{:S(2)}, u32[]{:S(2)}) %collective-permute-start.6) | collective-permute-done | bytes 65568 | tf_op jit(solution)/shard_map/ppermute | solution.py:274
  20.4 3.3 %collective-permute-start.7 = (f32[2,128,128]{2,1,0:T(8,128)S(1)}, f32[2,128,128]{2,1,0:T(8,128)S(1)}, u32[]{:S(2)}, u32[]{:S(2)}) collective-permute-start(f32[2,128,128]{2,1,0:T(8,128)S(1)} %pad_maximum_fusion.after_ref), channel_id=1, source_target_pairs={{0,16},{4,12},{8,24},{12,4},{16,0},{20,28},{24,8},{28,20},{1,17},{... | collective-permute-start | bytes 393224 | tf_op jit(solution)/shard_map/ppermute | solution.py:274
  23.8 0.9 %waves_of_own_atoms.7 = (f32[256,512]{1,0:T(8,128)S(1)}, f32[256,512]{1,0:T(8,128)S(1)}, bf16[256,512]{1,0:T(8,128)(2,1)S(1)}, bf16[256,512]{1,0:T(8,128)(2,1)S(...) custom-call(f32[3,2048]{1,0:T(4,128)S(1)} %copy-done, ...), custom_call_target="tpu_custom_call" | custom-call | flops 2621440 | tf_op jit(solution)/shard_map/waves_of_own_atoms/pallas_call | solution.py:338
  24.7 0.9 %waves_of_own_atoms.6 = (f32[256,512]{1,0:T(8,128)S(1)}, f32[256,512]{1,0:T(8,128)S(1)}, bf16[256,512]{1,0:T(8,128)(2,1)S(1)}, bf16[256,512]{1,0:T(8,128)(2,1)S(...) custom-call(f32[3,2048]{1,0:T(4,128)S(1)} %copy-done, ...), custom_call_target="tpu_custom_call" | custom-call | flops 2621440 | tf_op jit(solution)/shard_map/waves_of_own_atoms/pallas_call | solution.py:338
  25.5 1.9 %collective-permute-done.7 = f32[2,128,128]{2,1,0:T(8,128)S(1)} collective-permute-done((f32[2,128,128]{2,1,0:T(8,128)S(1)}, f32[2,128,128]{2,1,0:T(8,128)S(1)}, u32[]{:S(2)}, u32[]{:S(2)}) %collective-permute-start.7) | collective-permute-done | bytes 131104 | tf_op jit(solution)/shard_map/ppermute | solution.py:274
  27.4 1.7 %collective-permute-start.9 = (f32[2,128,128]{2,1,0:T(8,128)S(1)}, f32[2,128,128]{2,1,0:T(8,128)S(1)}, u32[]{:S(2)}, u32[]{:S(2)}) collective-permute-start(f32[2,128,128]{2,1,0:T(8,128)S(1)} %add_multiply_fusion.rest_7_), channel_id=1, source_target_pairs={{0,3},{1,2},{2,1},{3,0},{4,7},{5,6},{6,5},{7,4},{8,11},{9,10},{10,... | collective-permute-start | bytes 393224 | tf_op jit(solution)/shard_map/ppermute | solution.py:269
  29.2 0.7 %collective-permute-start.8 = (f32[2,128,128]{2,1,0:T(8,128)S(1)}, f32[2,128,128]{2,1,0:T(8,128)S(1)}, u32[]{:S(2)}, u32[]{:S(2)}) collective-permute-start(f32[2,128,128]{2,1,0:T(8,128)S(1)} %add_multiply_fusion.rest_7_), channel_id=1, source_target_pairs={{0,2},{1,3},{2,0},{3,1},{4,6},{5,7},{6,4},{7,5},{8,10},{9,11},{10,... | collective-permute-start | bytes 393224 | tf_op jit(solution)/shard_map/ppermute | solution.py:269
  29.9 1.1 %collective-permute-start.11 = (f32[2,128,128]{2,1,0:T(8,128)S(1)}, f32[2,128,128]{2,1,0:T(8,128)S(1)}, u32[]{:S(2)}, u32[]{:S(2)}) collective-permute-start(f32[2,128,128]{2,1,0:T(8,128)S(1)} %add_multiply_fusion.rest_7_), channel_id=1, source_target_pairs={{0,1},{1,0},{2,3},{3,2},{4,5},{5,4},{6,7},{7,6},{8,9},{9,8},{10,11... | collective-permute-start | bytes 393224 | tf_op jit(solution)/shard_map/ppermute | solution.py:269
  31.6 3.0 %collective-permute-done.9.rest_7_ = f32[2,128,128]{2,1,0:T(8,128)S(1)} collective-permute-done((f32[2,128,128]{2,1,0:T(8,128)S(1)}, f32[2,128,128]{2,1,0:T(8,128)S(1)}, u32[]{:S(2)}, u32[]{:S(2)}) %collective-permute-start.9) | collective-permute-done | bytes 131104 | tf_op jit(solution)/shard_map/ppermute | solution.py:269
  35.7 0.8 %collective-permute-done.8.rest_23_ = f32[2,128,128]{2,1,0:T(8,128)S(1)} collective-permute-done((f32[2,128,128]{2,1,0:T(8,128)S(1)}, f32[2,128,128]{2,1,0:T(8,128)S(1)}, u32[]{:S(2)}, u32[]{:S(2)}) %collective-permute-start.8) | collective-permute-done | bytes 131104 | tf_op jit(solution)/shard_map/ppermute | solution.py:269
  37.1 1.8 %fields_of_some_groups.5 = (f32[128,512]{1,0:T(8,128)S(1)}, f32[24,512]{1,0:T(8,128)S(1)}) custom-call(f32[136,512]{1,0:T(8,128)S(1)} %get-tuple-element.99.own_ref, f32[256,512]{1,0:T(8,128)S(1)} %get-tuple-element.157.rest_0_, f32[256,512]{1,0:T(8,128)S(1)} %get-tuple-element.158.rest_1_, bf16[256,512]{1,0:T(8,128)(2,1)S(1)} %get-tuple-element.159.rest_2_, ...), custom_call_target="tpu_custom_call" | custom-call | flops 131072 | tf_op jit(solution)/shard_map/fields_of_some_groups/pallas_call | solution.py:403
  38.9 1.8 %fields_and_forces.1 = (f32[64,512]{1,0:T(8,128)}, f32[3,512]{1,0:T(4,128)}, f32[64,512]{1,0:T(8,128)}) custom-call(f32[136,512]{1,0:T(8,128)S(1)} %get-tuple-element.99.own_ref, f32[64,64]{1,0:T(8,128)S(1)} %copy-done.2, f32[64,64]{1,0:T(8,128)S(1)} %copy-done.1, f32[256,512]{1,0:T(8,128)S(1)} %get-tuple-element.141.rest_16_.rest_0_, ...), custom_call_target="tpu_custom_call" | custom-call | flops 131072 | tf_op jit(solution)/shard_map/fields_and_forces/pallas_call | solution.py:433
  (40 shorter events, 3.3 us)
Async XLA Ops:
  0.6 5.5 %copy-start = (f32[3,2048]{1,0:T(4,128)S(1)}, f32[3,2048]{1,0:T(4,128)}, u32[]{:S(2)}) copy-start(f32[3,2048]{1,0:T(4,128)} %pos_ref.11) | copy-start | bytes 73732
  1.6 7.8 %collective-permute-start = (f32[72,512]{1,0:T(8,128)S(1)}, f32[72,512]{1,0:T(8,128)S(1)}, u32[]{:S(2)}, u32[]{:S(2)}) collective-permute-start(f32[72,512]{1,0:T(8,128)S(1)} %convert_add_fusion.packed_ref.rest_4_), channel_id=1, source_target_pairs={{0,1},{1,0},{2,3},{3,2},{4,5},{5,4},{6,7},{7,6},{8,9},{9,8},{10,11... | collective-permute-start | bytes 442376 | tf_op jit(solution)/shard_map/ppermute | solution.py:269
  4.6 8.5 %collective-permute-start.2 = (f32[72,512]{1,0:T(8,128)S(1)}, f32[72,512]{1,0:T(8,128)S(1)}, u32[]{:S(2)}, u32[]{:S(2)}) collective-permute-start(f32[72,512]{1,0:T(8,128)S(1)} %convert_add_fusion.packed_ref.rest_4_), channel_id=1, source_target_pairs={{0,2},{1,3},{2,0},{3,1},{4,6},{5,7},{6,4},{7,5},{8,10},{9,11},{10,... | collective-permute-start | bytes 442376 | tf_op jit(solution)/shard_map/ppermute | solution.py:269
  6.1 7.0 %collective-permute-start.3 = (f32[72,512]{1,0:T(8,128)S(1)}, f32[72,512]{1,0:T(8,128)S(1)}, u32[]{:S(2)}, u32[]{:S(2)}) collective-permute-start(f32[72,512]{1,0:T(8,128)S(1)} %convert_add_fusion.packed_ref.rest_4_), channel_id=1, source_target_pairs={{0,3},{1,2},{2,1},{3,0},{4,7},{5,6},{6,5},{7,4},{8,11},{9,10},{10,... | collective-permute-start | bytes 442376 | tf_op jit(solution)/shard_map/ppermute | solution.py:269
  7.7 1.7 %copy-start.1 = (f32[64,64]{1,0:T(8,128)S(1)}, f32[64,64]{1,0:T(8,128)}, u32[]{:S(2)}) copy-start(f32[64,64]{1,0:T(8,128)} %w_charge_ref.3) | copy-start | bytes 49156
  7.7 1.7 %copy-start.2 = (f32[64,64]{1,0:T(8,128)S(1)}, f32[64,64]{1,0:T(8,128)}, u32[]{:S(2)}) copy-start(f32[64,64]{1,0:T(8,128)} %w_out_ref.5) | copy-start | bytes 49156
  7.7 1.7 %copy-start.4 = (f32[64,2048]{1,0:T(8,128)S(1)}, f32[64,2048]{1,0:T(8,128)}, u32[]{:S(2)}) copy-start(f32[64,2048]{1,0:T(8,128)} %feats_ref.1) | copy-start | bytes 1572868
  7.8 1.7 %copy-start.6 = (f32[64,16]{0,1:T(8,128)S(1)}, f32[64,16]{0,1:T(8,128)}, u32[]{:S(2)}) copy-start(f32[64,16]{0,1:T(8,128)} %param.17) | copy-start | bytes 12292
  9.4 0.7 %copy-start.5 = (s32[2048]{0:T(1024)S(1)}, s32[2048]{0:T(1024)}, u32[]{:S(2)}) copy-start(s32[2048]{0:T(1024)} %param.12) | copy-start | bytes 24580
  9.4 0.7 %copy-start.7 = (s32[8]{0:T(128)S(1)}, s32[8]{0:T(128)}, u32[]{:S(2)}) copy-start(s32[8]{0:T(128)} %param.13) | copy-start | bytes 100
  12.1 2.0 %collective-permute-start.1 = (f32[128,128]{1,0:T(8,128)S(1)}, f32[128,128]{1,0:T(8,128)S(1)}, u32[]{:S(2)}, u32[]{:S(2)}) collective-permute-start(f32[128,128]{1,0:T(8,128)S(1)} %get-tuple-element.100), channel_id=1, source_target_pairs={{0,4},{4,0},{8,12},{12,8},{16,20},{20,16},{24,28},{28,24},{1,5},{5... | collective-permute-start | bytes 196616 | tf_op jit(solution)/shard_map/ppermute | solution.py:269
  14.2 1.9 %collective-permute-start.4 = (f32[128,128]{1,0:T(8,128)S(1)}, f32[128,128]{1,0:T(8,128)S(1)}, u32[]{:S(2)}, u32[]{:S(2)}) collective-permute-start(f32[128,128]{1,0:T(8,128)S(1)} %get-tuple-element.104), channel_id=1, source_target_pairs={{0,4},{4,0},{8,12},{12,8},{16,20},{20,16},{24,28},{28,24},{1,5},{5... | collective-permute-start | bytes 196616 | tf_op jit(solution)/shard_map/ppermute | solution.py:269
  14.3 5.0 %collective-permute-start.5 = (f32[128,128]{1,0:T(8,128)S(1)}, f32[128,128]{1,0:T(8,128)S(1)}, u32[]{:S(2)}, u32[]{:S(2)}) collective-permute-start(f32[128,128]{1,0:T(8,128)S(1)} %add.23), channel_id=1, source_target_pairs={{0,8},{4,20},{8,0},{12,28},{16,24},{20,4},{24,16},{28,12},{1,9},{5... | collective-permute-start | bytes 196616 | tf_op jit(solution)/shard_map/ppermute | solution.py:274
  16.1 1.1 %copy-start.3 = (f32[64]{0:T(128)S(1)}, f32[64]{0:T(128)}, u32[]{:S(2)}) copy-start(f32[64]{0:T(128)} %param.15) | copy-start | bytes 772
  16.1 4.3 %collective-permute-start.6 = (f32[128,128]{1,0:T(8,128)S(1)}, f32[128,128]{1,0:T(8,128)S(1)}, u32[]{:S(2)}, u32[]{:S(2)}) collective-permute-start(f32[128,128]{1,0:T(8,128)S(1)} %add.24.after_ref), channel_id=1, source_target_pairs={{0,8},{4,20},{8,0},{12,28},{16,24},{20,4},{24,16},{28,12},{1,9},{5... | collective-permute-start | bytes 196616 | tf_op jit(solution)/shard_map/ppermute | solution.py:274
  20.4 7.0 %collective-permute-start.7 = (f32[2,128,128]{2,1,0:T(8,128)S(1)}, f32[2,128,128]{2,1,0:T(8,128)S(1)}, u32[]{:S(2)}, u32[]{:S(2)}) collective-permute-start(f32[2,128,128]{2,1,0:T(8,128)S(1)} %pad_maximum_fusion.after_ref), channel_id=1, source_target_pairs={{0,16},{4,12},{8,24},{12,4},{16,0},{20,28},{24,8},{28,20},{1,17},{... | collective-permute-start | bytes 393224 | tf_op jit(solution)/shard_map/ppermute | solution.py:274
  27.4 7.2 %collective-permute-start.9 = (f32[2,128,128]{2,1,0:T(8,128)S(1)}, f32[2,128,128]{2,1,0:T(8,128)S(1)}, u32[]{:S(2)}, u32[]{:S(2)}) collective-permute-start(f32[2,128,128]{2,1,0:T(8,128)S(1)} %add_multiply_fusion.rest_7_), channel_id=1, source_target_pairs={{0,3},{1,2},{2,1},{3,0},{4,7},{5,6},{6,5},{7,4},{8,11},{9,10},{10,... | collective-permute-start | bytes 393224 | tf_op jit(solution)/shard_map/ppermute | solution.py:269
  29.2 7.3 %collective-permute-start.8 = (f32[2,128,128]{2,1,0:T(8,128)S(1)}, f32[2,128,128]{2,1,0:T(8,128)S(1)}, u32[]{:S(2)}, u32[]{:S(2)}) collective-permute-start(f32[2,128,128]{2,1,0:T(8,128)S(1)} %add_multiply_fusion.rest_7_), channel_id=1, source_target_pairs={{0,2},{1,3},{2,0},{3,1},{4,6},{5,7},{6,4},{7,5},{8,10},{9,11},{10,... | collective-permute-start | bytes 393224 | tf_op jit(solution)/shard_map/ppermute | solution.py:269
  29.9 6.7 %collective-permute-start.11 = (f32[2,128,128]{2,1,0:T(8,128)S(1)}, f32[2,128,128]{2,1,0:T(8,128)S(1)}, u32[]{:S(2)}, u32[]{:S(2)}) collective-permute-start(f32[2,128,128]{2,1,0:T(8,128)S(1)} %add_multiply_fusion.rest_7_), channel_id=1, source_target_pairs={{0,1},{1,0},{2,3},{3,2},{4,5},{5,4},{6,7},{7,6},{8,9},{9,8},{10,11... | collective-permute-start | bytes 393224 | tf_op jit(solution)/shard_map/ppermute | solution.py:269
  34.6 2.5 %collective-permute-start.13 = (f32[2,128,128]{2,1,0:T(8,128)S(1)}, f32[2,128,128]{2,1,0:T(8,128)S(1)}, u32[]{:S(2)}, u32[]{:S(2)}) collective-permute-start(f32[2,128,128]{2,1,0:T(8,128)S(1)} %add_multiply_fusion.rest_7_), channel_id=1, source_target_pairs={{0,4},{4,0},{8,12},{12,8},{16,20},{20,16},{24,28},{28,24},{1,5},{5... | collective-permute-start | bytes 393224 | tf_op jit(solution)/shard_map/ppermute | solution.py:269
  34.6 2.5 %collective-permute-start.14 = (f32[2,128,128]{2,1,0:T(8,128)S(1)}, f32[2,128,128]{2,1,0:T(8,128)S(1)}, u32[]{:S(2)}, u32[]{:S(2)}) collective-permute-start(f32[2,128,128]{2,1,0:T(8,128)S(1)} %collective-permute-done.9.rest_7_), channel_id=1, source_target_pairs={{0,4},{4,0},{8,12},{12,8},{16,20},{20,16},{24,28},{28,24},{1,5},{5... | collective-permute-start | bytes 393224 | tf_op jit(solution)/shard_map/ppermute | solution.py:269
  36.6 2.3 %collective-permute-start.12 = (f32[2,128,128]{2,1,0:T(8,128)S(1)}, f32[2,128,128]{2,1,0:T(8,128)S(1)}, u32[]{:S(2)}, u32[]{:S(2)}) collective-permute-start(f32[2,128,128]{2,1,0:T(8,128)S(1)} %collective-permute-done.11.rest_31_), channel_id=1, source_target_pairs={{0,4},{4,0},{8,12},{12,8},{16,20},{20,16},{24,28},{28,24},{1,5},{5... | collective-permute-start | bytes 393224 | tf_op jit(solution)/shard_map/ppermute | solution.py:269
  36.6 2.3 %collective-permute-start.10 = (f32[2,128,128]{2,1,0:T(8,128)S(1)}, f32[2,128,128]{2,1,0:T(8,128)S(1)}, u32[]{:S(2)}, u32[]{:S(2)}) collective-permute-start(f32[2,128,128]{2,1,0:T(8,128)S(1)} %collective-permute-done.8.rest_23_), channel_id=1, source_target_pairs={{0,4},{4,0},{8,12},{12,8},{16,20},{20,16},{24,28},{28,24},{1,5},{5... | collective-permute-start | bytes 393224 | tf_op jit(solution)/shard_map/ppermute | solution.py:269

commit v8 on v7

--- a/solution.py
+++ b/solution.py
@@ -222,15 +222,17 @@
         wave, sides, refs = refs[:7], refs[7 : 7 + count], refs[7 + count :]
         rows = sides[0].shape[1]
         entries.append((wave, sides, slice(first * rows, (first + count) * rows)))
-    other = own_stack(own_ref, channels)
-    stacks = [[coefficient_stack(sides, part) for _, sides, _ in entries] for part in range(2)]
+    stack = jnp.concatenate([coefficient_stack(sides, part) for part in range(2) for _, sides, _ in entries], axis=0)
+    depth = stack.shape[0] // 2
+    slopes = dot16(stack, own_stack(own_ref, channels), NN)
     for part in range(2):
-        along[part] = dot16(jnp.concatenate(stacks[part], axis=0), other, NN)
-    for at, (wave, _, rows) in enumerate(entries):
-        _, _, cos_high, cos_low, sin_high, sin_low, _ = wave
-        for part, high, low in ((0, cos_high, cos_low), (1, sin_high, sin_low)):
-            added = add_field(stacks[part][at], high[rows, :], low[rows, :])
-            field = added if field is None else field + added
+        along[part] = slopes[part * depth : (part + 1) * depth]
+    tiles = [
+        jnp.concatenate([wave[at][rows, :] for at in kinds for wave, _, rows in entries], axis=0)
+        for kinds in ((2, 4), (3, 5))
+    ]
+    added = add_field(stack, *tiles)
+    field = added if field is None else field + added
     first = 0
     for wave, _, rows in entries:
         sums = add_force(sums, wave, along, rows, first)

time: 40.9 us -> 40.3 us (0.985)
  Pallas kernels: 14.9 us -> 14.1 us
    pallas_call x3, Pallas kernels: 2.93 us -> 2.27 us  [partial_fields(): pl.pallas_call(functools.partial(partial_field_kernel, layout=layout, fir...]
  transfers between devices with their start and end apart: 15 -> 15, of which waited for: 7 -> 7; matrix products, arithmetic and copies ran while one was open for 0% -> 0% of each run, Pallas kernels for 32% -> 31%
where the time goes in v8:
time: 40.3 us; the launch traced here: 40.2 us
  starting transfers between devices  15.5 us (38%)
  Pallas kernels  14.1 us (35%)
  waiting for transfers between devices  8.07 us (20%)
  other arithmetic  1.01 us (3%)
  between operations  0.89 us (2%)
  local copies, waits for them, and re-layouts  0.67 us (2%)
    ppermute x12, starting transfers between devices, swap(): lax.ppermute(value, axis, [(place, place ^ offset) for place in range(siz...  9.26 us
    ppermute x3, starting transfers between devices, swap_along_z(): return lax.ppermute(value, 'atoms', pairs)  6.2 us
    ppermute x12, waiting for transfers between devices, swap(): lax.ppermute(value, axis, [(place, place ^ offset) for place in range(siz...  5.02 us
    pallas_call x4, Pallas kernels, waves_of(): pl.pallas_call(functools.partial(wave_kernel, atom_total=atoms * atom_cou...  3.76 us
    pallas_call x2, Pallas kernels, on_device(): pl.pallas_call(functools.partial(tile_kernel, channels=channels, vectors=...  3.16 us
    ppermute x3, waiting for transfers between devices, swap_along_z(): return lax.ppermute(value, 'atoms', pairs)  3.04 us
    pallas_call x3, Pallas kernels, partial_fields(): pl.pallas_call(functools.partial(partial_field_kernel, layout=layout, fir...  2.27 us
    pallas_call x1, Pallas kernels, on_device(): pl.pallas_call(functools.partial(charge_kernel, groups=group_count), out_...  2.08 us
  transfers between devices with their start and end apart: 15, of which 7 were waited for; matrix products, arithmetic and copies ran while one was open for 0% of the time, Pallas kernels for 31%

profile of v8, /device:TPU:0, one launch (start us, length us, event | category | flops | bytes accessed | tf_op | source)
XLA Modules:
  0.0 40.2 jit_solution(7170813188736489628)
XLA Ops:
  0.6 0.9 %convert_add_fusion.packed_ref.rest_4_ = f32[72,512]{1,0:T(8,128)S(1)} fusion(s32[3,256]{1,0:T(4,128)} %param.14, f32[64,512]{1,0:T(8,128)} %param.19), kind=kLoop, calls=%fused_computation | loop fusion | flops 73728 | bytes 281600 | tf_op jit(solution)/shard_map/add | solution.py:304
  1.6 3.0 %collective-permute-start = (f32[72,512]{1,0:T(8,128)S(1)}, f32[72,512]{1,0:T(8,128)S(1)}, u32[]{:S(2)}, u32[]{:S(2)}) collective-permute-start(f32[72,512]{1,0:T(8,128)S(1)} %convert_add_fusion.packed_ref.rest_4_), channel_id=1, source_target_pairs={{0,1},{1,0},{2,3},{3,2},{4,5},{5,4},{6,7},{7,6},{8,9},{9,8},{10,11... | collective-permute-start | bytes 442376 | tf_op jit(solution)/shard_map/ppermute | solution.py:271
  4.6 1.5 %collective-permute-start.2 = (f32[72,512]{1,0:T(8,128)S(1)}, f32[72,512]{1,0:T(8,128)S(1)}, u32[]{:S(2)}, u32[]{:S(2)}) collective-permute-start(f32[72,512]{1,0:T(8,128)S(1)} %convert_add_fusion.packed_ref.rest_4_), channel_id=1, source_target_pairs={{0,2},{1,3},{2,0},{3,1},{4,6},{5,7},{6,4},{7,5},{8,10},{9,11},{10,... | collective-permute-start | bytes 442376 | tf_op jit(solution)/shard_map/ppermute | solution.py:271
  6.1 1.6 %waves_of_own_vectors.2 = (bf16[256,2048]{1,0:T(8,128)(2,1)S(1)}, bf16[256,2048]{1,0:T(8,128)(2,1)S(1)}) custom-call(f32[3,2048]{1,0:T(4,128)S(1)} %copy-done, f32[72,512]{1,0:T(8,128)S(1)} %convert_add_fusion.packed_ref.rest_4_), custom_call_target="tpu_custom_call" | custom-call | flops 2359296000 | tf_op jit(solution)/shard_map/waves_of_own_vectors/pallas_call | solution.py:310
  7.8 1.6 %waves_of_own_vectors.3 = (bf16[256,2048]{1,0:T(8,128)(2,1)S(1)}, bf16[256,2048]{1,0:T(8,128)(2,1)S(1)}) custom-call(f32[3,2048]{1,0:T(4,128)S(1)} %copy-done, f32[72,512]{1,0:T(8,128)S(1)} %convert_add_fusion.packed_ref.rest_4_), custom_call_target="tpu_custom_call" | custom-call | flops 2359296000 | tf_op jit(solution)/shard_map/waves_of_own_vectors/pallas_call | solution.py:310
  10.1 2.1 %charge_sums.1 = (f32[128,128]{1,0:T(8,128)S(1)}, f32[128,128]{1,0:T(8,128)S(1)}, f32[136,512]{1,0:T(8,128)S(1)}, f32[1,2048]{1,0:T(1,128)S(1)}, f32[256,128]{1,0:T(8,128)S(1)}) custom-call(s32[1,8]{1,0:T(1,128)S(1)} %bitcast.14, f32[64,2048]{1,0:T(8,128)S(1)} %copy-done.4, s32[1,2048]{1,0:T(1,128)S(1)} %bitcast.12, f32[64,64]{1,0:T(8,128)S(1)} %copy-done.1, ...), custom_call_target="tpu_custom_call" | custom-call | flops 2013265920 | tf_op jit(solution)/shard_map/charge_sums/pallas_call | solution.py:322
  12.2 0.8 %collective-permute-done.2.rest_4_.packed_ref = f32[72,512]{1,0:T(8,128)S(1)} collective-permute-done((f32[72,512]{1,0:T(8,128)S(1)}, f32[72,512]{1,0:T(8,128)S(1)}, u32[]{:S(2)}, u32[]{:S(2)}) %collective-permute-start.2) | collective-permute-done | bytes 147488 | tf_op jit(solution)/shard_map/ppermute | solution.py:271
  13.1 1.1 %adjoint_sums.1 = (f32[128,128]{1,0:T(8,128)S(1)}, f32[128,128]{1,0:T(8,128)S(1)}) custom-call(f32[1,2048]{1,0:T(1,128)S(1)} %get-tuple-element.101.mask_ref, f32[64,64]{1,0:T(8,128)S(1)} %copy-done.2, f32[256,128]{1,0:T(8,128)S(1)} %get-tuple-element.102.part_ref, bf16[256,2048]{1,0:T(8,128)(2,1)S(1)} %get-tuple-element.95.rest_0_, ...), custom_call_target="tpu_custom_call" | custom-call | flops 2013265920 | tf_op jit(solution)/shard_map/adjoint_sums/pallas_call | solution.py:353
  14.3 1.8 %collective-permute-start.5 = (f32[128,128]{1,0:T(8,128)S(1)}, f32[128,128]{1,0:T(8,128)S(1)}, u32[]{:S(2)}, u32[]{:S(2)}) collective-permute-start(f32[128,128]{1,0:T(8,128)S(1)} %add.23), channel_id=1, source_target_pairs={{0,8},{4,20},{8,0},{12,28},{16,24},{20,4},{24,16},{28,12},{1,9},{5... | collective-permute-start | bytes 196616 | tf_op jit(solution)/shard_map/ppermute | solution.py:276
  16.1 1.1 %collective-permute-start.6 = (f32[128,128]{1,0:T(8,128)S(1)}, f32[128,128]{1,0:T(8,128)S(1)}, u32[]{:S(2)}, u32[]{:S(2)}) collective-permute-start(f32[128,128]{1,0:T(8,128)S(1)} %add.24.after_ref), channel_id=1, source_target_pairs={{0,8},{4,20},{8,0},{12,28},{16,24},{20,4},{24,16},{28,12},{1,9},{5... | collective-permute-start | bytes 196616 | tf_op jit(solution)/shard_map/ppermute | solution.py:276
  17.2 1.1 %waves_of_own_atoms.4 = (f32[128,128]{1,0:T(8,128)S(1)}, f32[256,512]{1,0:T(8,128)S(1)}, f32[256,512]{1,0:T(8,128)S(1)}, bf16[256,512]{1,0:T(8,128)(2,1)S(1)}, b...) custom-call(f32[3,2048]{1,0:T(4,128)S(1)} %copy-done, ...), custom_call_target="tpu_custom_call" | custom-call | flops 2621440 | tf_op jit(solution)/shard_map/waves_of_own_atoms/pallas_call | solution.py:340
  18.3 0.9 %waves_of_own_atoms.5 = (f32[256,512]{1,0:T(8,128)S(1)}, f32[256,512]{1,0:T(8,128)S(1)}, bf16[256,512]{1,0:T(8,128)(2,1)S(1)}, bf16[256,512]{1,0:T(8,128)(2,1)S(...) custom-call(f32[3,2048]{1,0:T(4,128)S(1)} %copy-done, ...), custom_call_target="tpu_custom_call" | custom-call | flops 2621440 | tf_op jit(solution)/shard_map/waves_of_own_atoms/pallas_call | solution.py:340
  19.3 1.1 %collective-permute-done.6 = f32[128,128]{1,0:T(8,128)S(1)} collective-permute-done((f32[128,128]{1,0:T(8,128)S(1)}, f32[128,128]{1,0:T(8,128)S(1)}, u32[]{:S(2)}, u32[]{:S(2)}) %collective-permute-start.6) | collective-permute-done | bytes 65568 | tf_op jit(solution)/shard_map/ppermute | solution.py:276
  20.4 3.3 %collective-permute-start.7 = (f32[2,128,128]{2,1,0:T(8,128)S(1)}, f32[2,128,128]{2,1,0:T(8,128)S(1)}, u32[]{:S(2)}, u32[]{:S(2)}) collective-permute-start(f32[2,128,128]{2,1,0:T(8,128)S(1)} %pad_maximum_fusion.after_ref), channel_id=1, source_target_pairs={{0,16},{4,12},{8,24},{12,4},{16,0},{20,28},{24,8},{28,20},{1,17},{... | collective-permute-start | bytes 393224 | tf_op jit(solution)/shard_map/ppermute | solution.py:276
  23.8 0.9 %waves_of_own_atoms.7 = (f32[256,512]{1,0:T(8,128)S(1)}, f32[256,512]{1,0:T(8,128)S(1)}, bf16[256,512]{1,0:T(8,128)(2,1)S(1)}, bf16[256,512]{1,0:T(8,128)(2,1)S(...) custom-call(f32[3,2048]{1,0:T(4,128)S(1)} %copy-done, ...), custom_call_target="tpu_custom_call" | custom-call | flops 2621440 | tf_op jit(solution)/shard_map/waves_of_own_atoms/pallas_call | solution.py:340
  24.7 0.9 %waves_of_own_atoms.6 = (f32[256,512]{1,0:T(8,128)S(1)}, f32[256,512]{1,0:T(8,128)S(1)}, bf16[256,512]{1,0:T(8,128)(2,1)S(1)}, bf16[256,512]{1,0:T(8,128)(2,1)S(...) custom-call(f32[3,2048]{1,0:T(4,128)S(1)} %copy-done, ...), custom_call_target="tpu_custom_call" | custom-call | flops 2621440 | tf_op jit(solution)/shard_map/waves_of_own_atoms/pallas_call | solution.py:340
  25.5 1.9 %collective-permute-done.7 = f32[2,128,128]{2,1,0:T(8,128)S(1)} collective-permute-done((f32[2,128,128]{2,1,0:T(8,128)S(1)}, f32[2,128,128]{2,1,0:T(8,128)S(1)}, u32[]{:S(2)}, u32[]{:S(2)}) %collective-permute-start.7) | collective-permute-done | bytes 131104 | tf_op jit(solution)/shard_map/ppermute | solution.py:276
  27.4 1.7 %collective-permute-start.9 = (f32[2,128,128]{2,1,0:T(8,128)S(1)}, f32[2,128,128]{2,1,0:T(8,128)S(1)}, u32[]{:S(2)}, u32[]{:S(2)}) collective-permute-start(f32[2,128,128]{2,1,0:T(8,128)S(1)} %add_multiply_fusion.rest_7_), channel_id=1, source_target_pairs={{0,3},{1,2},{2,1},{3,0},{4,7},{5,6},{6,5},{7,4},{8,11},{9,10},{10,... | collective-permute-start | bytes 393224 | tf_op jit(solution)/shard_map/ppermute | solution.py:271
  29.2 0.7 %collective-permute-start.8 = (f32[2,128,128]{2,1,0:T(8,128)S(1)}, f32[2,128,128]{2,1,0:T(8,128)S(1)}, u32[]{:S(2)}, u32[]{:S(2)}) collective-permute-start(f32[2,128,128]{2,1,0:T(8,128)S(1)} %add_multiply_fusion.rest_7_), channel_id=1, source_target_pairs={{0,2},{1,3},{2,0},{3,1},{4,6},{5,7},{6,4},{7,5},{8,10},{9,11},{10,... | collective-permute-start | bytes 393224 | tf_op jit(solution)/shard_map/ppermute | solution.py:271
  29.9 1.1 %collective-permute-start.11 = (f32[2,128,128]{2,1,0:T(8,128)S(1)}, f32[2,128,128]{2,1,0:T(8,128)S(1)}, u32[]{:S(2)}, u32[]{:S(2)}) collective-permute-start(f32[2,128,128]{2,1,0:T(8,128)S(1)} %add_multiply_fusion.rest_7_), channel_id=1, source_target_pairs={{0,1},{1,0},{2,3},{3,2},{4,5},{5,4},{6,7},{7,6},{8,9},{9,8},{10,11... | collective-permute-start | bytes 393224 | tf_op jit(solution)/shard_map/ppermute | solution.py:271
  31.4 3.2 %collective-permute-done.9.rest_7_ = f32[2,128,128]{2,1,0:T(8,128)S(1)} collective-permute-done((f32[2,128,128]{2,1,0:T(8,128)S(1)}, f32[2,128,128]{2,1,0:T(8,128)S(1)}, u32[]{:S(2)}, u32[]{:S(2)}) %collective-permute-start.9) | collective-permute-done | bytes 131104 | tf_op jit(solution)/shard_map/ppermute | solution.py:271
  35.6 0.9 %collective-permute-done.8.rest_23_ = f32[2,128,128]{2,1,0:T(8,128)S(1)} collective-permute-done((f32[2,128,128]{2,1,0:T(8,128)S(1)}, f32[2,128,128]{2,1,0:T(8,128)S(1)}, u32[]{:S(2)}, u32[]{:S(2)}) %collective-permute-start.8) | collective-permute-done | bytes 131104 | tf_op jit(solution)/shard_map/ppermute | solution.py:271
  37.1 1.4 %fields_of_some_groups.5 = (f32[128,512]{1,0:T(8,128)S(1)}, f32[24,512]{1,0:T(8,128)S(1)}) custom-call(f32[136,512]{1,0:T(8,128)S(1)} %get-tuple-element.99.own_ref, f32[256,512]{1,0:T(8,128)S(1)} %get-tuple-element.157.rest_0_, f32[256,512]{1,0:T(8,128)S(1)} %get-tuple-element.158.rest_1_, bf16[256,512]{1,0:T(8,128)(2,1)S(1)} %get-tuple-element.159.rest_2_, ...), custom_call_target="tpu_custom_call" | custom-call | flops 131072 | tf_op jit(solution)/shard_map/fields_of_some_groups/pallas_call | solution.py:405
  38.5 1.7 %fields_and_forces.1 = (f32[64,512]{1,0:T(8,128)}, f32[3,512]{1,0:T(4,128)}, f32[64,512]{1,0:T(8,128)}) custom-call(f32[136,512]{1,0:T(8,128)S(1)} %get-tuple-element.99.own_ref, f32[64,64]{1,0:T(8,128)S(1)} %copy-done.2, f32[64,64]{1,0:T(8,128)S(1)} %copy-done.1, f32[256,512]{1,0:T(8,128)S(1)} %get-tuple-element.141.rest_16_.rest_0_, ...), custom_call_target="tpu_custom_call" | custom-call | flops 131072 | tf_op jit(solution)/shard_map/fields_and_forces/pallas_call | solution.py:435
  (40 shorter events, 3.1 us)
Async XLA Ops:
  0.6 5.5 %copy-start = (f32[3,2048]{1,0:T(4,128)S(1)}, f32[3,2048]{1,0:T(4,128)}, u32[]{:S(2)}) copy-start(f32[3,2048]{1,0:T(4,128)} %pos_ref.11) | copy-start | bytes 73732
  1.6 7.8 %collective-permute-start = (f32[72,512]{1,0:T(8,128)S(1)}, f32[72,512]{1,0:T(8,128)S(1)}, u32[]{:S(2)}, u32[]{:S(2)}) collective-permute-start(f32[72,512]{1,0:T(8,128)S(1)} %convert_add_fusion.packed_ref.rest_4_), channel_id=1, source_target_pairs={{0,1},{1,0},{2,3},{3,2},{4,5},{5,4},{6,7},{7,6},{8,9},{9,8},{10,11... | collective-permute-start | bytes 442376 | tf_op jit(solution)/shard_map/ppermute | solution.py:271
  4.6 8.5 %collective-permute-start.2 = (f32[72,512]{1,0:T(8,128)S(1)}, f32[72,512]{1,0:T(8,128)S(1)}, u32[]{:S(2)}, u32[]{:S(2)}) collective-permute-start(f32[72,512]{1,0:T(8,128)S(1)} %convert_add_fusion.packed_ref.rest_4_), channel_id=1, source_target_pairs={{0,2},{1,3},{2,0},{3,1},{4,6},{5,7},{6,4},{7,5},{8,10},{9,11},{10,... | collective-permute-start | bytes 442376 | tf_op jit(solution)/shard_map/ppermute | solution.py:271
  6.1 7.0 %collective-permute-start.3 = (f32[72,512]{1,0:T(8,128)S(1)}, f32[72,512]{1,0:T(8,128)S(1)}, u32[]{:S(2)}, u32[]{:S(2)}) collective-permute-start(f32[72,512]{1,0:T(8,128)S(1)} %convert_add_fusion.packed_ref.rest_4_), channel_id=1, source_target_pairs={{0,3},{1,2},{2,1},{3,0},{4,7},{5,6},{6,5},{7,4},{8,11},{9,10},{10,... | collective-permute-start | bytes 442376 | tf_op jit(solution)/shard_map/ppermute | solution.py:271
  7.7 1.7 %copy-start.1 = (f32[64,64]{1,0:T(8,128)S(1)}, f32[64,64]{1,0:T(8,128)}, u32[]{:S(2)}) copy-start(f32[64,64]{1,0:T(8,128)} %w_charge_ref.3) | copy-start | bytes 49156
  7.7 1.7 %copy-start.2 = (f32[64,64]{1,0:T(8,128)S(1)}, f32[64,64]{1,0:T(8,128)}, u32[]{:S(2)}) copy-start(f32[64,64]{1,0:T(8,128)} %w_out_ref.5) | copy-start | bytes 49156
  7.7 1.7 %copy-start.4 = (f32[64,2048]{1,0:T(8,128)S(1)}, f32[64,2048]{1,0:T(8,128)}, u32[]{:S(2)}) copy-start(f32[64,2048]{1,0:T(8,128)} %feats_ref.1) | copy-start | bytes 1572868
  7.8 1.7 %copy-start.6 = (f32[64,16]{0,1:T(8,128)S(1)}, f32[64,16]{0,1:T(8,128)}, u32[]{:S(2)}) copy-start(f32[64,16]{0,1:T(8,128)} %param.17) | copy-start | bytes 12292
  9.4 0.7 %copy-start.5 = (s32[2048]{0:T(1024)S(1)}, s32[2048]{0:T(1024)}, u32[]{:S(2)}) copy-start(s32[2048]{0:T(1024)} %param.12) | copy-start | bytes 24580
  9.4 0.7 %copy-start.7 = (s32[8]{0:T(128)S(1)}, s32[8]{0:T(128)}, u32[]{:S(2)}) copy-start(s32[8]{0:T(128)} %param.13) | copy-start | bytes 100
  12.1 2.0 %collective-permute-start.1 = (f32[128,128]{1,0:T(8,128)S(1)}, f32[128,128]{1,0:T(8,128)S(1)}, u32[]{:S(2)}, u32[]{:S(2)}) collective-permute-start(f32[128,128]{1,0:T(8,128)S(1)} %get-tuple-element.100), channel_id=1, source_target_pairs={{0,4},{4,0},{8,12},{12,8},{16,20},{20,16},{24,28},{28,24},{1,5},{5... | collective-permute-start | bytes 196616 | tf_op jit(solution)/shard_map/ppermute | solution.py:271
  14.2 1.9 %collective-permute-start.4 = (f32[128,128]{1,0:T(8,128)S(1)}, f32[128,128]{1,0:T(8,128)S(1)}, u32[]{:S(2)}, u32[]{:S(2)}) collective-permute-start(f32[128,128]{1,0:T(8,128)S(1)} %get-tuple-element.104), channel_id=1, source_target_pairs={{0,4},{4,0},{8,12},{12,8},{16,20},{20,16},{24,28},{28,24},{1,5},{5... | collective-permute-start | bytes 196616 | tf_op jit(solution)/shard_map/ppermute | solution.py:271
  14.3 5.0 %collective-permute-start.5 = (f32[128,128]{1,0:T(8,128)S(1)}, f32[128,128]{1,0:T(8,128)S(1)}, u32[]{:S(2)}, u32[]{:S(2)}) collective-permute-start(f32[128,128]{1,0:T(8,128)S(1)} %add.23), channel_id=1, source_target_pairs={{0,8},{4,20},{8,0},{12,28},{16,24},{20,4},{24,16},{28,12},{1,9},{5... | collective-permute-start | bytes 196616 | tf_op jit(solution)/shard_map/ppermute | solution.py:276
  16.1 1.1 %copy-start.3 = (f32[64]{0:T(128)S(1)}, f32[64]{0:T(128)}, u32[]{:S(2)}) copy-start(f32[64]{0:T(128)} %param.15) | copy-start | bytes 772
  16.1 4.3 %collective-permute-start.6 = (f32[128,128]{1,0:T(8,128)S(1)}, f32[128,128]{1,0:T(8,128)S(1)}, u32[]{:S(2)}, u32[]{:S(2)}) collective-permute-start(f32[128,128]{1,0:T(8,128)S(1)} %add.24.after_ref), channel_id=1, source_target_pairs={{0,8},{4,20},{8,0},{12,28},{16,24},{20,4},{24,16},{28,12},{1,9},{5... | collective-permute-start | bytes 196616 | tf_op jit(solution)/shard_map/ppermute | solution.py:276
  20.4 7.0 %collective-permute-start.7 = (f32[2,128,128]{2,1,0:T(8,128)S(1)}, f32[2,128,128]{2,1,0:T(8,128)S(1)}, u32[]{:S(2)}, u32[]{:S(2)}) collective-permute-start(f32[2,128,128]{2,1,0:T(8,128)S(1)} %pad_maximum_fusion.after_ref), channel_id=1, source_target_pairs={{0,16},{4,12},{8,24},{12,4},{16,0},{20,28},{24,8},{28,20},{1,17},{... | collective-permute-start | bytes 393224 | tf_op jit(solution)/shard_map/ppermute | solution.py:276
  27.4 7.2 %collective-permute-start.9 = (f32[2,128,128]{2,1,0:T(8,128)S(1)}, f32[2,128,128]{2,1,0:T(8,128)S(1)}, u32[]{:S(2)}, u32[]{:S(2)}) collective-permute-start(f32[2,128,128]{2,1,0:T(8,128)S(1)} %add_multiply_fusion.rest_7_), channel_id=1, source_target_pairs={{0,3},{1,2},{2,1},{3,0},{4,7},{5,6},{6,5},{7,4},{8,11},{9,10},{10,... | collective-permute-start | bytes 393224 | tf_op jit(solution)/shard_map/ppermute | solution.py:271
  29.2 7.3 %collective-permute-start.8 = (f32[2,128,128]{2,1,0:T(8,128)S(1)}, f32[2,128,128]{2,1,0:T(8,128)S(1)}, u32[]{:S(2)}, u32[]{:S(2)}) collective-permute-start(f32[2,128,128]{2,1,0:T(8,128)S(1)} %add_multiply_fusion.rest_7_), channel_id=1, source_target_pairs={{0,2},{1,3},{2,0},{3,1},{4,6},{5,7},{6,4},{7,5},{8,10},{9,11},{10,... | collective-permute-start | bytes 393224 | tf_op jit(solution)/shard_map/ppermute | solution.py:271
  29.9 6.7 %collective-permute-start.11 = (f32[2,128,128]{2,1,0:T(8,128)S(1)}, f32[2,128,128]{2,1,0:T(8,128)S(1)}, u32[]{:S(2)}, u32[]{:S(2)}) collective-permute-start(f32[2,128,128]{2,1,0:T(8,128)S(1)} %add_multiply_fusion.rest_7_), channel_id=1, source_target_pairs={{0,1},{1,0},{2,3},{3,2},{4,5},{5,4},{6,7},{7,6},{8,9},{9,8},{10,11... | collective-permute-start | bytes 393224 | tf_op jit(solution)/shard_map/ppermute | solution.py:271
  34.6 2.5 %collective-permute-start.13 = (f32[2,128,128]{2,1,0:T(8,128)S(1)}, f32[2,128,128]{2,1,0:T(8,128)S(1)}, u32[]{:S(2)}, u32[]{:S(2)}) collective-permute-start(f32[2,128,128]{2,1,0:T(8,128)S(1)} %add_multiply_fusion.rest_7_), channel_id=1, source_target_pairs={{0,4},{4,0},{8,12},{12,8},{16,20},{20,16},{24,28},{28,24},{1,5},{5... | collective-permute-start | bytes 393224 | tf_op jit(solution)/shard_map/ppermute | solution.py:271
  34.6 2.5 %collective-permute-start.14 = (f32[2,128,128]{2,1,0:T(8,128)S(1)}, f32[2,128,128]{2,1,0:T(8,128)S(1)}, u32[]{:S(2)}, u32[]{:S(2)}) collective-permute-start(f32[2,128,128]{2,1,0:T(8,128)S(1)} %collective-permute-done.9.rest_7_), channel_id=1, source_target_pairs={{0,4},{4,0},{8,12},{12,8},{16,20},{20,16},{24,28},{28,24},{1,5},{5... | collective-permute-start | bytes 393224 | tf_op jit(solution)/shard_map/ppermute | solution.py:271
  36.6 1.9 %collective-permute-start.12 = (f32[2,128,128]{2,1,0:T(8,128)S(1)}, f32[2,128,128]{2,1,0:T(8,128)S(1)}, u32[]{:S(2)}, u32[]{:S(2)}) collective-permute-start(f32[2,128,128]{2,1,0:T(8,128)S(1)} %collective-permute-done.11.rest_31_), channel_id=1, source_target_pairs={{0,4},{4,0},{8,12},{12,8},{16,20},{20,16},{24,28},{28,24},{1,5},{5... | collective-permute-start | bytes 393224 | tf_op jit(solution)/shard_map/ppermute | solution.py:271
  36.6 1.9 %collective-permute-start.10 = (f32[2,128,128]{2,1,0:T(8,128)S(1)}, f32[2,128,128]{2,1,0:T(8,128)S(1)}, u32[]{:S(2)}, u32[]{:S(2)}) collective-permute-start(f32[2,128,128]{2,1,0:T(8,128)S(1)} %collective-permute-done.8.rest_23_), channel_id=1, source_target_pairs={{0,4},{4,0},{8,12},{12,8},{16,20},{20,16},{24,28},{28,24},{1,5},{5... | collective-permute-start | bytes 393224 | tf_op jit(solution)/shard_map/ppermute | solution.py:271

commit v9 on v8

--- a/solution.py
+++ b/solution.py
@@ -29,11 +29,10 @@
 def dot3(left, right, dims):
     left_high, left_low = halves(left)
     right_high, right_low = halves(right)
-    return (
-        dot16(left_high, right_high, dims)
-        + dot16(left_low, right_high, dims)
-        + dot16(left_high, right_low, dims)
-    )
+    free = 1 - dims[0][0]
+    count = left.shape[free]
+    wide = dot16(jnp.concatenate([left_high, left_low], axis=free), right_high, dims)
+    return wide[:count] + wide[count:] + dot16(left_high, right_low, dims)
 
 
 def horner(terms, square):
@@ -166,8 +165,8 @@
     split_by_core(total, keep_ref, send_ref)
 
 
-def wave_kernel(pos_ref, packed_ref, width_ref, after_ref, *rest, atom_total):
-    *gain_ref, cos, sin, cos_high, cos_low, sin_high, sin_low, k_ref, k_column = rest
+def wave_kernel(pos_ref, packed_ref, width_ref, w_out_ref, w_charge_ref, after_ref, *rest, atom_total):
+    *first_refs, cos, sin, cos_high, cos_low, sin_high, sin_low, k_ref, k_column = rest
     vectors = cos.shape[0]
     rows = vectors // 2
     core = lax.axis_index("atoms") % 2
@@ -175,11 +174,18 @@
     for flip in range(2):
         start = pl.multiple_of((core ^ flip) * rows, rows)
         k_ref[flip * rows : (flip + 1) * rows, :] = k_column[pl.ds(start, rows), :]
-    if gain_ref:
+    if first_refs:
+        gain_ref, project_ref = first_refs
         waves = [2.0 * math.pi * k_ref[0:rows, x : x + 1] for x in range(3)]
         square = waves[0] * waves[0] + waves[1] * waves[1] + waves[2] * waves[2]
         gain = jnp.exp(-square * width_ref[...]) * 40.0 / (square + 40.0) / math.sqrt(atom_total)
-        gain_ref[0][...] = jnp.concatenate([gain, gain], axis=1)
+        gain_ref[...] = jnp.concatenate([gain, gain], axis=1)
+        empty = jnp.zeros_like(w_charge_ref[...])
+        blocks = (
+            jnp.concatenate([w_out_ref[...].T, empty], axis=1),
+            jnp.concatenate([empty, w_charge_ref[...]], axis=1),
+        )
+        project_ref[...] = jnp.concatenate(halves(jnp.concatenate(blocks, axis=0)), axis=0)
     first = lax.axis_index("kvec") * cos.shape[1]
     trig_blocks(k_ref, pos_ref, first, (cos_high, cos_low, sin_high, sin_low), (cos, sin))
 
@@ -254,14 +260,17 @@
         sums_ref[8 * x : 8 * x + 8, :] = sums[x]
 
 
-def field_kernel(own_ref, w_out_ref, w_charge_ref, *rest, layout):
+def field_kernel(own_ref, project_ref, *rest, layout):
     refs, field_ref, sums_ref, message_ref, force_ref, grad_ref, along = rest[:-6], *rest[-6:]
-    channels = w_out_ref.shape[0]
+    channels = message_ref.shape[0]
+    both = 2 * channels
     sums = [sums_ref[8 * x : 8 * x + 8, :] for x in range(3)]
     field, sums = fields(own_ref, refs, layout, channels, along, field_ref[...], sums)
-    field = own_ref[2 * channels : 2 * channels + 1, :] * field
-    message_ref[...] = dot3(w_out_ref[...], field[:channels], TN)
-    grad_ref[...] = dot3(w_charge_ref[...], field[channels:], NN)
+    high, low = halves(own_ref[both : both + 1, :] * field)
+    wide = dot16(project_ref[...], high, NN)
+    projected = wide[:both] + wide[both:] + dot16(project_ref[0:both, :], low, NN)
+    message_ref[...] = projected[:channels]
+    grad_ref[...] = projected[channels:]
     for x in range(3):
         force_ref[x : x + 1, :] = 2.0 * math.pi * jnp.sum(sums[x], axis=0, keepdims=True)
 
@@ -336,17 +345,17 @@
     wave_shapes = [f32(vectors, share)] * 2 + [bf16(vectors, share)] * 4 + [f32(vectors, 128)]
 
     def waves_of(group, after):
-        shapes = ([f32(half, both)] if group == 0 else []) + wave_shapes
+        shapes = ([f32(half, both), bf16(2 * both, both)] if group == 0 else []) + wave_shapes
         made = pl.pallas_call(
             functools.partial(wave_kernel, atom_total=atoms * atom_count),
             out_shape=shapes,
-            in_specs=[VMEM, VMEM, VMEM, ANY],
+            in_specs=[VMEM] * 5 + [ANY],
             out_specs=[VMEM] * len(shapes),
             scratch_shapes=[pltpu.VMEM((vectors, 128), F32)],
             compiler_params=PARAMS,
             cost_estimate=cost(20 * vectors * share),
             name="waves_of_own_atoms",
-        )(positions, packed[group], filter_width.reshape(1, channels), after)
+        )(positions, packed[group], filter_width.reshape(1, channels), w_out, w_charge, after)
         return list(made)
 
     arrived_h = swap(send_h, "atoms", 1)
@@ -384,7 +393,7 @@
         arrived, beside = lax.optimization_barrier((arrived, beside))
         waves += beside
         total = total + arrived
-    gain, *waves[0] = waves[0]
+    gain, project, *waves[0] = waves[0]
     near = gain[None] * total
     plane = {0: near}
     for group in range(group_count - 1, 0, -1):
@@ -430,7 +439,7 @@
 
     parts = [(group, 1, 1) for group in late]
     layout, scratch = field_sizes(parts)
-    operands = [own, w_out, w_charge, *operands_of(parts), *fields_so_far]
+    operands = [own, project, *operands_of(parts), *fields_so_far]
     return tuple(
         pl.pallas_call(
             functools.partial(field_kernel, layout=layout),

time: 40.3 us -> 40.3 us (level)
  no operation moved by 1% of the time
where the time goes in v9:
time: 40.3 us; the launch traced here: 40.2 us
  starting transfers between devices  15.4 us (38%)
  Pallas kernels  14.2 us (35%)
  waiting for transfers between devices  7.98 us (20%)
  other arithmetic  1.01 us (3%)
  between operations  0.89 us (2%)
  local copies, waits for them, and re-layouts  0.67 us (2%)
    ppermute x12, starting transfers between devices, swap(): lax.ppermute(value, axis, [(place, place ^ offset) for place in range(siz...  9.26 us
    ppermute x3, starting transfers between devices, swap_along_z(): return lax.ppermute(value, 'atoms', pairs)  6.18 us
    ppermute x12, waiting for transfers between devices, swap(): lax.ppermute(value, axis, [(place, place ^ offset) for place in range(siz...  5 us
    pallas_call x4, Pallas kernels, waves_of(): pl.pallas_call(functools.partial(wave_kernel, atom_total=atoms * atom_cou...  3.79 us
    pallas_call x2, Pallas kernels, on_device(): pl.pallas_call(functools.partial(tile_kernel, channels=channels, vectors=...  3.16 us
    ppermute x3, waiting for transfers between devices, swap_along_z(): return lax.ppermute(value, 'atoms', pairs)  2.98 us
    pallas_call x3, Pallas kernels, partial_fields(): pl.pallas_call(functools.partial(partial_field_kernel, layout=layout, fir...  2.28 us
    pallas_call x1, Pallas kernels, on_device(): pl.pallas_call(functools.partial(charge_kernel, groups=group_count), out_...  2.15 us
  transfers between devices with their start and end apart: 15, of which 7 were waited for; matrix products, arithmetic and copies ran while one was open for 0% of the time, Pallas kernels for 31%

profile of v9, /device:TPU:0, one launch (start us, length us, event | category | flops | bytes accessed | tf_op | source)
XLA Modules:
  0.0 40.2 jit_solution(9812024683919688725)
XLA Ops:
  0.6 0.9 %convert_add_fusion.packed_ref.rest_4_ = f32[72,512]{1,0:T(8,128)S(1)} fusion(s32[3,256]{1,0:T(4,128)} %param.14, f32[64,512]{1,0:T(8,128)} %param.19), kind=kLoop, calls=%fused_computation | loop fusion | flops 73728 | bytes 281600 | tf_op jit(solution)/shard_map/add | solution.py:313
  1.6 3.0 %collective-permute-start = (f32[72,512]{1,0:T(8,128)S(1)}, f32[72,512]{1,0:T(8,128)S(1)}, u32[]{:S(2)}, u32[]{:S(2)}) collective-permute-start(f32[72,512]{1,0:T(8,128)S(1)} %convert_add_fusion.packed_ref.rest_4_), channel_id=1, source_target_pairs={{0,1},{1,0},{2,3},{3,2},{4,5},{5,4},{6,7},{7,6},{8,9},{9,8},{10,11... | collective-permute-start | bytes 442376 | tf_op jit(solution)/shard_map/ppermute | solution.py:280
  4.6 1.5 %collective-permute-start.2 = (f32[72,512]{1,0:T(8,128)S(1)}, f32[72,512]{1,0:T(8,128)S(1)}, u32[]{:S(2)}, u32[]{:S(2)}) collective-permute-start(f32[72,512]{1,0:T(8,128)S(1)} %convert_add_fusion.packed_ref.rest_4_), channel_id=1, source_target_pairs={{0,2},{1,3},{2,0},{3,1},{4,6},{5,7},{6,4},{7,5},{8,10},{9,11},{10,... | collective-permute-start | bytes 442376 | tf_op jit(solution)/shard_map/ppermute | solution.py:280
  6.1 1.6 %waves_of_own_vectors.3 = (bf16[256,2048]{1,0:T(8,128)(2,1)S(1)}, bf16[256,2048]{1,0:T(8,128)(2,1)S(1)}) custom-call(f32[3,2048]{1,0:T(4,128)S(1)} %copy-done.2, f32[72,512]{1,0:T(8,128)S(1)} %convert_add_fusion.packed_ref.rest_4_), custom_call_target="tpu_custom_call" | custom-call | flops 2359296000 | tf_op jit(solution)/shard_map/waves_of_own_vectors/pallas_call | solution.py:319
  7.8 1.6 %waves_of_own_vectors.2 = (bf16[256,2048]{1,0:T(8,128)(2,1)S(1)}, bf16[256,2048]{1,0:T(8,128)(2,1)S(1)}) custom-call(f32[3,2048]{1,0:T(4,128)S(1)} %copy-done.2, f32[72,512]{1,0:T(8,128)S(1)} %convert_add_fusion.packed_ref.rest_4_), custom_call_target="tpu_custom_call" | custom-call | flops 2359296000 | tf_op jit(solution)/shard_map/waves_of_own_vectors/pallas_call | solution.py:319
  9.4 0.6 %copy-done.5 = s32[2048]{0:T(1024)S(1)} copy-done((s32[2048]{0:T(1024)S(1)}, s32[2048]{0:T(1024)}, u32[]{:S(2)}) %copy-start.5) | copy-done | bytes 8216
  10.1 2.2 %charge_sums.1 = (f32[128,128]{1,0:T(8,128)S(1)}, f32[128,128]{1,0:T(8,128)S(1)}, f32[136,512]{1,0:T(8,128)S(1)}, f32[1,2048]{1,0:T(1,128)S(1)}, f32[256,128]{1,0:T(8,128)S(1)}) custom-call(s32[1,8]{1,0:T(1,128)S(1)} %bitcast.14, f32[64,2048]{1,0:T(8,128)S(1)} %copy-done.4, s32[1,2048]{1,0:T(1,128)S(1)} %bitcast.12, f32[64,64]{1,0:T(8,128)S(1)} %copy-done, ...), custom_call_target="tpu_custom_call" | custom-call | flops 2013265920 | tf_op jit(solution)/shard_map/charge_sums/pallas_call | solution.py:331
  12.3 0.8 %collective-permute-done.2.rest_4_.packed_ref = f32[72,512]{1,0:T(8,128)S(1)} collective-permute-done((f32[72,512]{1,0:T(8,128)S(1)}, f32[72,512]{1,0:T(8,128)S(1)}, u32[]{:S(2)}, u32[]{:S(2)}) %collective-permute-start.2) | collective-permute-done | bytes 147488 | tf_op jit(solution)/shard_map/ppermute | solution.py:280
  13.1 1.1 %adjoint_sums.1 = (f32[128,128]{1,0:T(8,128)S(1)}, f32[128,128]{1,0:T(8,128)S(1)}) custom-call(f32[1,2048]{1,0:T(1,128)S(1)} %get-tuple-element.104.mask_ref, f32[64,64]{1,0:T(8,128)S(1)} %copy-done.1, f32[256,128]{1,0:T(8,128)S(1)} %get-tuple-element.105.part_ref, bf16[256,2048]{1,0:T(8,128)(2,1)S(1)} %get-tuple-element.97.rest_0_, ...), custom_call_target="tpu_custom_call" | custom-call | flops 2013265920 | tf_op jit(solution)/shard_map/adjoint_sums/pallas_call | solution.py:362
  14.3 1.8 %collective-permute-start.4 = (f32[128,128]{1,0:T(8,128)S(1)}, f32[128,128]{1,0:T(8,128)S(1)}, u32[]{:S(2)}, u32[]{:S(2)}) collective-permute-start(f32[128,128]{1,0:T(8,128)S(1)} %add.23), channel_id=1, source_target_pairs={{0,8},{4,20},{8,0},{12,28},{16,24},{20,4},{24,16},{28,12},{1,9},{5... | collective-permute-start | bytes 196616 | tf_op jit(solution)/shard_map/ppermute | solution.py:285
  16.1 1.0 %collective-permute-start.6 = (f32[128,128]{1,0:T(8,128)S(1)}, f32[128,128]{1,0:T(8,128)S(1)}, u32[]{:S(2)}, u32[]{:S(2)}) collective-permute-start(f32[128,128]{1,0:T(8,128)S(1)} %add.24.after_ref), channel_id=1, source_target_pairs={{0,8},{4,20},{8,0},{12,28},{16,24},{20,4},{24,16},{28,12},{1,9},{5... | collective-permute-start | bytes 196616 | tf_op jit(solution)/shard_map/ppermute | solution.py:285
  17.2 1.2 %waves_of_own_atoms.4 = (f32[128,128]{1,0:T(8,128)S(1)}, bf16[256,128]{1,0:T(8,128)(2,1)S(1)}, f32[256,512]{1,0:T(8,128)S(1)}, f32[256,512]{1,0:T(8,128)S(1)}, b...) custom-call(f32[3,2048]{1,0:T(4,128)S(1)} %copy-done.2, ...), custom_call_target="tpu_custom_call" | custom-call | flops 2621440 | tf_op jit(solution)/shard_map/waves_of_own_atoms/pallas_call | solution.py:349
  18.4 0.9 %waves_of_own_atoms.5 = (f32[256,512]{1,0:T(8,128)S(1)}, f32[256,512]{1,0:T(8,128)S(1)}, bf16[256,512]{1,0:T(8,128)(2,1)S(1)}, bf16[256,512]{1,0:T(8,128)(2,1)S(...) custom-call(f32[3,2048]{1,0:T(4,128)S(1)} %copy-done.2, ...), custom_call_target="tpu_custom_call" | custom-call | flops 2621440 | tf_op jit(solution)/shard_map/waves_of_own_atoms/pallas_call | solution.py:349
  19.3 1.2 %collective-permute-done.6 = f32[128,128]{1,0:T(8,128)S(1)} collective-permute-done((f32[128,128]{1,0:T(8,128)S(1)}, f32[128,128]{1,0:T(8,128)S(1)}, u32[]{:S(2)}, u32[]{:S(2)}) %collective-permute-start.6) | collective-permute-done | bytes 65568 | tf_op jit(solution)/shard_map/ppermute | solution.py:285
  20.5 3.3 %collective-permute-start.7 = (f32[2,128,128]{2,1,0:T(8,128)S(1)}, f32[2,128,128]{2,1,0:T(8,128)S(1)}, u32[]{:S(2)}, u32[]{:S(2)}) collective-permute-start(f32[2,128,128]{2,1,0:T(8,128)S(1)} %pad_maximum_fusion.after_ref), channel_id=1, source_target_pairs={{0,16},{4,12},{8,24},{12,4},{16,0},{20,28},{24,8},{28,20},{1,17},{... | collective-permute-start | bytes 393224 | tf_op jit(solution)/shard_map/ppermute | solution.py:285
  23.8 0.9 %waves_of_own_atoms.7 = (f32[256,512]{1,0:T(8,128)S(1)}, f32[256,512]{1,0:T(8,128)S(1)}, bf16[256,512]{1,0:T(8,128)(2,1)S(1)}, bf16[256,512]{1,0:T(8,128)(2,1)S(...) custom-call(f32[3,2048]{1,0:T(4,128)S(1)} %copy-done.2, ...), custom_call_target="tpu_custom_call" | custom-call | flops 2621440 | tf_op jit(solution)/shard_map/waves_of_own_atoms/pallas_call | solution.py:349
  24.7 0.9 %waves_of_own_atoms.6 = (f32[256,512]{1,0:T(8,128)S(1)}, f32[256,512]{1,0:T(8,128)S(1)}, bf16[256,512]{1,0:T(8,128)(2,1)S(1)}, bf16[256,512]{1,0:T(8,128)(2,1)S(...) custom-call(f32[3,2048]{1,0:T(4,128)S(1)} %copy-done.2, ...), custom_call_target="tpu_custom_call" | custom-call | flops 2621440 | tf_op jit(solution)/shard_map/waves_of_own_atoms/pallas_call | solution.py:349
  25.6 1.8 %collective-permute-done.7 = f32[2,128,128]{2,1,0:T(8,128)S(1)} collective-permute-done((f32[2,128,128]{2,1,0:T(8,128)S(1)}, f32[2,128,128]{2,1,0:T(8,128)S(1)}, u32[]{:S(2)}, u32[]{:S(2)}) %collective-permute-start.7) | collective-permute-done | bytes 131104 | tf_op jit(solution)/shard_map/ppermute | solution.py:285
  27.4 1.9 %collective-permute-start.9 = (f32[2,128,128]{2,1,0:T(8,128)S(1)}, f32[2,128,128]{2,1,0:T(8,128)S(1)}, u32[]{:S(2)}, u32[]{:S(2)}) collective-permute-start(f32[2,128,128]{2,1,0:T(8,128)S(1)} %add_multiply_fusion.rest_7_), channel_id=1, source_target_pairs={{0,3},{1,2},{2,1},{3,0},{4,7},{5,6},{6,5},{7,4},{8,11},{9,10},{10,... | collective-permute-start | bytes 393224 | tf_op jit(solution)/shard_map/ppermute | solution.py:280
  29.8 1.1 %collective-permute-start.11 = (f32[2,128,128]{2,1,0:T(8,128)S(1)}, f32[2,128,128]{2,1,0:T(8,128)S(1)}, u32[]{:S(2)}, u32[]{:S(2)}) collective-permute-start(f32[2,128,128]{2,1,0:T(8,128)S(1)} %add_multiply_fusion.rest_7_), channel_id=1, source_target_pairs={{0,1},{1,0},{2,3},{3,2},{4,5},{5,4},{6,7},{7,6},{8,9},{9,8},{10,11... | collective-permute-start | bytes 393224 | tf_op jit(solution)/shard_map/ppermute | solution.py:280
  31.4 3.1 %collective-permute-done.9.rest_7_ = f32[2,128,128]{2,1,0:T(8,128)S(1)} collective-permute-done((f32[2,128,128]{2,1,0:T(8,128)S(1)}, f32[2,128,128]{2,1,0:T(8,128)S(1)}, u32[]{:S(2)}, u32[]{:S(2)}) %collective-permute-start.9) | collective-permute-done | bytes 131104 | tf_op jit(solution)/shard_map/ppermute | solution.py:280
  35.4 1.0 %collective-permute-done.8.rest_23_ = f32[2,128,128]{2,1,0:T(8,128)S(1)} collective-permute-done((f32[2,128,128]{2,1,0:T(8,128)S(1)}, f32[2,128,128]{2,1,0:T(8,128)S(1)}, u32[]{:S(2)}, u32[]{:S(2)}) %collective-permute-start.8) | collective-permute-done | bytes 131104 | tf_op jit(solution)/shard_map/ppermute | solution.py:280
  37.1 1.4 %fields_of_some_groups.5 = (f32[128,512]{1,0:T(8,128)S(1)}, f32[24,512]{1,0:T(8,128)S(1)}) custom-call(f32[136,512]{1,0:T(8,128)S(1)} %get-tuple-element.101.own_ref, f32[256,512]{1,0:T(8,128)S(1)} %get-tuple-element.161.rest_0_, f32[256,512]{1,0:T(8,128)S(1)} %get-tuple-element.162.rest_1_, bf16[256,512]{1,0:T(8,128)(2,1)S(1)} %get-tuple-element.163.rest_2_, ...), custom_call_target="tpu_custom_call" | custom-call | flops 131072 | tf_op jit(solution)/shard_map/fields_of_some_groups/pallas_call | solution.py:414
  38.5 1.7 %fields_and_forces.1 = (f32[64,512]{1,0:T(8,128)}, f32[3,512]{1,0:T(4,128)}, f32[64,512]{1,0:T(8,128)}) custom-call(f32[136,512]{1,0:T(8,128)S(1)} %get-tuple-element.101.own_ref, bf16[256,128]{1,0:T(8,128)(2,1)S(1)} %get-tuple-element.127.project_ref, f32[256,512]{1,0:T(8,128)S(1)} %get-tuple-element.145.rest_16_.rest_0_, ...), custom_call_target="tpu_custom_call" | custom-call | flops 131072 | tf_op jit(solution)/shard_map/fields_and_forces/pallas_call | solution.py:444
  (40 shorter events, 2.9 us)
Async XLA Ops:
  0.6 5.5 %copy-start.2 = (f32[3,2048]{1,0:T(4,128)S(1)}, f32[3,2048]{1,0:T(4,128)}, u32[]{:S(2)}) copy-start(f32[3,2048]{1,0:T(4,128)} %pos_ref.11) | copy-start | bytes 73732
  1.6 7.8 %collective-permute-start = (f32[72,512]{1,0:T(8,128)S(1)}, f32[72,512]{1,0:T(8,128)S(1)}, u32[]{:S(2)}, u32[]{:S(2)}) collective-permute-start(f32[72,512]{1,0:T(8,128)S(1)} %convert_add_fusion.packed_ref.rest_4_), channel_id=1, source_target_pairs={{0,1},{1,0},{2,3},{3,2},{4,5},{5,4},{6,7},{7,6},{8,9},{9,8},{10,11... | collective-permute-start | bytes 442376 | tf_op jit(solution)/shard_map/ppermute | solution.py:280
  4.6 8.5 %collective-permute-start.2 = (f32[72,512]{1,0:T(8,128)S(1)}, f32[72,512]{1,0:T(8,128)S(1)}, u32[]{:S(2)}, u32[]{:S(2)}) collective-permute-start(f32[72,512]{1,0:T(8,128)S(1)} %convert_add_fusion.packed_ref.rest_4_), channel_id=1, source_target_pairs={{0,2},{1,3},{2,0},{3,1},{4,6},{5,7},{6,4},{7,5},{8,10},{9,11},{10,... | collective-permute-start | bytes 442376 | tf_op jit(solution)/shard_map/ppermute | solution.py:280
  6.1 7.0 %collective-permute-start.3 = (f32[72,512]{1,0:T(8,128)S(1)}, f32[72,512]{1,0:T(8,128)S(1)}, u32[]{:S(2)}, u32[]{:S(2)}) collective-permute-start(f32[72,512]{1,0:T(8,128)S(1)} %convert_add_fusion.packed_ref.rest_4_), channel_id=1, source_target_pairs={{0,3},{1,2},{2,1},{3,0},{4,7},{5,6},{6,5},{7,4},{8,11},{9,10},{10,... | collective-permute-start | bytes 442376 | tf_op jit(solution)/shard_map/ppermute | solution.py:280
  7.7 1.7 %copy-start = (f32[64,64]{1,0:T(8,128)S(1)}, f32[64,64]{1,0:T(8,128)}, u32[]{:S(2)}) copy-start(f32[64,64]{1,0:T(8,128)} %w_charge_ref.9) | copy-start | bytes 49156
  7.7 1.7 %copy-start.1 = (f32[64,64]{1,0:T(8,128)S(1)}, f32[64,64]{1,0:T(8,128)}, u32[]{:S(2)}) copy-start(f32[64,64]{1,0:T(8,128)} %w_out_ref.11) | copy-start | bytes 49156
  7.7 1.7 %copy-start.4 = (f32[64,2048]{1,0:T(8,128)S(1)}, f32[64,2048]{1,0:T(8,128)}, u32[]{:S(2)}) copy-start(f32[64,2048]{1,0:T(8,128)} %feats_ref.1) | copy-start | bytes 1572868
  7.8 1.7 %copy-start.6 = (f32[64,16]{0,1:T(8,128)S(1)}, f32[64,16]{0,1:T(8,128)}, u32[]{:S(2)}) copy-start(f32[64,16]{0,1:T(8,128)} %param.17) | copy-start | bytes 12292
  9.4 0.7 %copy-start.5 = (s32[2048]{0:T(1024)S(1)}, s32[2048]{0:T(1024)}, u32[]{:S(2)}) copy-start(s32[2048]{0:T(1024)} %param.12) | copy-start | bytes 24580
  9.4 0.7 %copy-start.7 = (s32[8]{0:T(128)S(1)}, s32[8]{0:T(128)}, u32[]{:S(2)}) copy-start(s32[8]{0:T(128)} %param.13) | copy-start | bytes 100
  12.2 2.0 %collective-permute-start.1 = (f32[128,128]{1,0:T(8,128)S(1)}, f32[128,128]{1,0:T(8,128)S(1)}, u32[]{:S(2)}, u32[]{:S(2)}) collective-permute-start(f32[128,128]{1,0:T(8,128)S(1)} %get-tuple-element.103), channel_id=1, source_target_pairs={{0,4},{4,0},{8,12},{12,8},{16,20},{20,16},{24,28},{28,24},{1,5},{5... | collective-permute-start | bytes 196616 | tf_op jit(solution)/shard_map/ppermute | solution.py:280
  14.2 1.9 %collective-permute-start.5 = (f32[128,128]{1,0:T(8,128)S(1)}, f32[128,128]{1,0:T(8,128)S(1)}, u32[]{:S(2)}, u32[]{:S(2)}) collective-permute-start(f32[128,128]{1,0:T(8,128)S(1)} %get-tuple-element.109), channel_id=1, source_target_pairs={{0,4},{4,0},{8,12},{12,8},{16,20},{20,16},{24,28},{28,24},{1,5},{5... | collective-permute-start | bytes 196616 | tf_op jit(solution)/shard_map/ppermute | solution.py:280
  14.3 5.0 %collective-permute-start.4 = (f32[128,128]{1,0:T(8,128)S(1)}, f32[128,128]{1,0:T(8,128)S(1)}, u32[]{:S(2)}, u32[]{:S(2)}) collective-permute-start(f32[128,128]{1,0:T(8,128)S(1)} %add.23), channel_id=1, source_target_pairs={{0,8},{4,20},{8,0},{12,28},{16,24},{20,4},{24,16},{28,12},{1,9},{5... | collective-permute-start | bytes 196616 | tf_op jit(solution)/shard_map/ppermute | solution.py:285
  16.1 1.1 %copy-start.3 = (f32[64]{0:T(128)S(1)}, f32[64]{0:T(128)}, u32[]{:S(2)}) copy-start(f32[64]{0:T(128)} %param.15) | copy-start | bytes 772
  16.1 4.3 %collective-permute-start.6 = (f32[128,128]{1,0:T(8,128)S(1)}, f32[128,128]{1,0:T(8,128)S(1)}, u32[]{:S(2)}, u32[]{:S(2)}) collective-permute-start(f32[128,128]{1,0:T(8,128)S(1)} %add.24.after_ref), channel_id=1, source_target_pairs={{0,8},{4,20},{8,0},{12,28},{16,24},{20,4},{24,16},{28,12},{1,9},{5... | collective-permute-start | bytes 196616 | tf_op jit(solution)/shard_map/ppermute | solution.py:285
  20.5 6.8 %collective-permute-start.7 = (f32[2,128,128]{2,1,0:T(8,128)S(1)}, f32[2,128,128]{2,1,0:T(8,128)S(1)}, u32[]{:S(2)}, u32[]{:S(2)}) collective-permute-start(f32[2,128,128]{2,1,0:T(8,128)S(1)} %pad_maximum_fusion.after_ref), channel_id=1, source_target_pairs={{0,16},{4,12},{8,24},{12,4},{16,0},{20,28},{24,8},{28,20},{1,17},{... | collective-permute-start | bytes 393224 | tf_op jit(solution)/shard_map/ppermute | solution.py:285
  27.4 7.1 %collective-permute-start.9 = (f32[2,128,128]{2,1,0:T(8,128)S(1)}, f32[2,128,128]{2,1,0:T(8,128)S(1)}, u32[]{:S(2)}, u32[]{:S(2)}) collective-permute-start(f32[2,128,128]{2,1,0:T(8,128)S(1)} %add_multiply_fusion.rest_7_), channel_id=1, source_target_pairs={{0,3},{1,2},{2,1},{3,0},{4,7},{5,6},{6,5},{7,4},{8,11},{9,10},{10,... | collective-permute-start | bytes 393224 | tf_op jit(solution)/shard_map/ppermute | solution.py:280
  29.3 7.2 %collective-permute-start.8 = (f32[2,128,128]{2,1,0:T(8,128)S(1)}, f32[2,128,128]{2,1,0:T(8,128)S(1)}, u32[]{:S(2)}, u32[]{:S(2)}) collective-permute-start(f32[2,128,128]{2,1,0:T(8,128)S(1)} %add_multiply_fusion.rest_7_), channel_id=1, source_target_pairs={{0,2},{1,3},{2,0},{3,1},{4,6},{5,7},{6,4},{7,5},{8,10},{9,11},{10,... | collective-permute-start | bytes 393224 | tf_op jit(solution)/shard_map/ppermute | solution.py:280
  29.8 6.8 %collective-permute-start.11 = (f32[2,128,128]{2,1,0:T(8,128)S(1)}, f32[2,128,128]{2,1,0:T(8,128)S(1)}, u32[]{:S(2)}, u32[]{:S(2)}) collective-permute-start(f32[2,128,128]{2,1,0:T(8,128)S(1)} %add_multiply_fusion.rest_7_), channel_id=1, source_target_pairs={{0,1},{1,0},{2,3},{3,2},{4,5},{5,4},{6,7},{7,6},{8,9},{9,8},{10,11... | collective-permute-start | bytes 393224 | tf_op jit(solution)/shard_map/ppermute | solution.py:280
  34.5 2.6 %collective-permute-start.13 = (f32[2,128,128]{2,1,0:T(8,128)S(1)}, f32[2,128,128]{2,1,0:T(8,128)S(1)}, u32[]{:S(2)}, u32[]{:S(2)}) collective-permute-start(f32[2,128,128]{2,1,0:T(8,128)S(1)} %add_multiply_fusion.rest_7_), channel_id=1, source_target_pairs={{0,4},{4,0},{8,12},{12,8},{16,20},{20,16},{24,28},{28,24},{1,5},{5... | collective-permute-start | bytes 393224 | tf_op jit(solution)/shard_map/ppermute | solution.py:280
  34.5 2.6 %collective-permute-start.14 = (f32[2,128,128]{2,1,0:T(8,128)S(1)}, f32[2,128,128]{2,1,0:T(8,128)S(1)}, u32[]{:S(2)}, u32[]{:S(2)}) collective-permute-start(f32[2,128,128]{2,1,0:T(8,128)S(1)} %collective-permute-done.9.rest_7_), channel_id=1, source_target_pairs={{0,4},{4,0},{8,12},{12,8},{16,20},{20,16},{24,28},{28,24},{1,5},{5... | collective-permute-start | bytes 393224 | tf_op jit(solution)/shard_map/ppermute | solution.py:280
  36.6 1.9 %collective-permute-start.12 = (f32[2,128,128]{2,1,0:T(8,128)S(1)}, f32[2,128,128]{2,1,0:T(8,128)S(1)}, u32[]{:S(2)}, u32[]{:S(2)}) collective-permute-start(f32[2,128,128]{2,1,0:T(8,128)S(1)} %collective-permute-done.11.rest_31_), channel_id=1, source_target_pairs={{0,4},{4,0},{8,12},{12,8},{16,20},{20,16},{24,28},{28,24},{1,5},{5... | collective-permute-start | bytes 393224 | tf_op jit(solution)/shard_map/ppermute | solution.py:280
  36.6 1.9 %collective-permute-start.10 = (f32[2,128,128]{2,1,0:T(8,128)S(1)}, f32[2,128,128]{2,1,0:T(8,128)S(1)}, u32[]{:S(2)}, u32[]{:S(2)}) collective-permute-start(f32[2,128,128]{2,1,0:T(8,128)S(1)} %collective-permute-done.8.rest_23_), channel_id=1, source_target_pairs={{0,4},{4,0},{8,12},{12,8},{16,20},{20,16},{24,28},{28,24},{1,5},{5... | collective-permute-start | bytes 393224 | tf_op jit(solution)/shard_map/ppermute | solution.py:280

commit v10 on v8

--- a/solution.py
+++ b/solution.py
@@ -55,7 +55,7 @@
     vectors, atoms = high_low[0].shape
     step = 32
     width = min(256, atoms)
-    per_body = max(1, 2048 // atoms)
+    per_body = max(1, 4096 // atoms)
     per_body = min(per_body, vectors // step)
 
     def body(block, _):

time: 40.3 us -> 40.2 us (level)
  Pallas kernels: 14.1 us -> 13.3 us
  waiting for transfers between devices: 8.07 us -> 8.8 us
    ppermute x12, waiting for transfers between devices: 5.02 us -> 5.55 us  [swap(): lax.ppermute(value, axis, [(place, place ^ offset) for place in range(siz...]
    pallas_call x4, Pallas kernels: 3.76 us -> 3.3 us  [waves_of(): pl.pallas_call(functools.partial(wave_kernel, atom_total=atoms * atom_cou...]
  transfers between devices with their start and end apart: 15 -> 15, of which waited for: 7 -> 7; matrix products, arithmetic and copies ran while one was open for 0% -> 0% of each run, Pallas kernels for 31% -> 29%
where the time goes in v10:
time: 40.2 us; the launch traced here: 40 us
  starting transfers between devices  15.3 us (38%)
  Pallas kernels  13.3 us (33%)
  waiting for transfers between devices  8.8 us (22%)
  other arithmetic  1.01 us (3%)
  between operations  0.89 us (2%)
  local copies, waits for them, and re-layouts  0.67 us (2%)
    ppermute x12, starting transfers between devices, swap(): lax.ppermute(value, axis, [(place, place ^ offset) for place in range(siz...  9.26 us
    ppermute x3, starting transfers between devices, swap_along_z(): return lax.ppermute(value, 'atoms', pairs)  6.08 us
    ppermute x12, waiting for transfers between devices, swap(): lax.ppermute(value, axis, [(place, place ^ offset) for place in range(siz...  5.55 us
    pallas_call x4, Pallas kernels, waves_of(): pl.pallas_call(functools.partial(wave_kernel, atom_total=atoms * atom_cou...  3.3 us
    ppermute x3, waiting for transfers between devices, swap_along_z(): return lax.ppermute(value, 'atoms', pairs)  3.25 us
    pallas_call x2, Pallas kernels, on_device(): pl.pallas_call(functools.partial(tile_kernel, channels=channels, vectors=...  2.87 us
    pallas_call x3, Pallas kernels, partial_fields(): pl.pallas_call(functools.partial(partial_field_kernel, layout=layout, fir...  2.27 us
    pallas_call x1, Pallas kernels, on_device(): pl.pallas_call(functools.partial(charge_kernel, groups=group_count), out_...  2.08 us
  transfers between devices with their start and end apart: 15, of which 7 were waited for; matrix products, arithmetic and copies ran while one was open for 0% of the time, Pallas kernels for 29%

profile of v10, /device:TPU:0, one launch (start us, length us, event | category | flops | bytes accessed | tf_op | source)
XLA Modules:
  0.0 40.0 jit_solution(12859799825041394446)
XLA Ops:
  0.6 0.9 %convert_add_fusion.packed_ref.rest_4_ = f32[72,512]{1,0:T(8,128)S(1)} fusion(s32[3,256]{1,0:T(4,128)} %param.14, f32[64,512]{1,0:T(8,128)} %param.19), kind=kLoop, calls=%fused_computation | loop fusion | flops 73728 | bytes 281600 | tf_op jit(solution)/shard_map/add | solution.py:304
  1.6 3.0 %collective-permute-start = (f32[72,512]{1,0:T(8,128)S(1)}, f32[72,512]{1,0:T(8,128)S(1)}, u32[]{:S(2)}, u32[]{:S(2)}) collective-permute-start(f32[72,512]{1,0:T(8,128)S(1)} %convert_add_fusion.packed_ref.rest_4_), channel_id=1, source_target_pairs={{0,1},{1,0},{2,3},{3,2},{4,5},{5,4},{6,7},{7,6},{8,9},{9,8},{10,11... | collective-permute-start | bytes 442376 | tf_op jit(solution)/shard_map/ppermute | solution.py:271
  4.6 1.5 %collective-permute-start.2 = (f32[72,512]{1,0:T(8,128)S(1)}, f32[72,512]{1,0:T(8,128)S(1)}, u32[]{:S(2)}, u32[]{:S(2)}) collective-permute-start(f32[72,512]{1,0:T(8,128)S(1)} %convert_add_fusion.packed_ref.rest_4_), channel_id=1, source_target_pairs={{0,2},{1,3},{2,0},{3,1},{4,6},{5,7},{6,4},{7,5},{8,10},{9,11},{10,... | collective-permute-start | bytes 442376 | tf_op jit(solution)/shard_map/ppermute | solution.py:271
  6.1 1.4 %waves_of_own_vectors.2 = (bf16[256,2048]{1,0:T(8,128)(2,1)S(1)}, bf16[256,2048]{1,0:T(8,128)(2,1)S(1)}) custom-call(f32[3,2048]{1,0:T(4,128)S(1)} %copy-done, f32[72,512]{1,0:T(8,128)S(1)} %convert_add_fusion.packed_ref.rest_4_), custom_call_target="tpu_custom_call" | custom-call | flops 2359296000 | tf_op jit(solution)/shard_map/waves_of_own_vectors/pallas_call | solution.py:310
  7.6 1.4 %waves_of_own_vectors.3 = (bf16[256,2048]{1,0:T(8,128)(2,1)S(1)}, bf16[256,2048]{1,0:T(8,128)(2,1)S(1)}) custom-call(f32[3,2048]{1,0:T(4,128)S(1)} %copy-done, f32[72,512]{1,0:T(8,128)S(1)} %convert_add_fusion.packed_ref.rest_4_), custom_call_target="tpu_custom_call" | custom-call | flops 2359296000 | tf_op jit(solution)/shard_map/waves_of_own_vectors/pallas_call | solution.py:310
  9.8 2.1 %charge_sums.1 = (f32[128,128]{1,0:T(8,128)S(1)}, f32[128,128]{1,0:T(8,128)S(1)}, f32[136,512]{1,0:T(8,128)S(1)}, f32[1,2048]{1,0:T(1,128)S(1)}, f32[256,128]{1,0:T(8,128)S(1)}) custom-call(s32[1,8]{1,0:T(1,128)S(1)} %bitcast.14, f32[64,2048]{1,0:T(8,128)S(1)} %copy-done.4, s32[1,2048]{1,0:T(1,128)S(1)} %bitcast.12, f32[64,64]{1,0:T(8,128)S(1)} %copy-done.1, ...), custom_call_target="tpu_custom_call" | custom-call | flops 2013265920 | tf_op jit(solution)/shard_map/charge_sums/pallas_call | solution.py:322
  11.9 1.1 %collective-permute-done.2.rest_4_.packed_ref = f32[72,512]{1,0:T(8,128)S(1)} collective-permute-done((f32[72,512]{1,0:T(8,128)S(1)}, f32[72,512]{1,0:T(8,128)S(1)}, u32[]{:S(2)}, u32[]{:S(2)}) %collective-permute-start.2) | collective-permute-done | bytes 147488 | tf_op jit(solution)/shard_map/ppermute | solution.py:271
  13.1 1.1 %adjoint_sums.1 = (f32[128,128]{1,0:T(8,128)S(1)}, f32[128,128]{1,0:T(8,128)S(1)}) custom-call(f32[1,2048]{1,0:T(1,128)S(1)} %get-tuple-element.101.mask_ref, f32[64,64]{1,0:T(8,128)S(1)} %copy-done.2, f32[256,128]{1,0:T(8,128)S(1)} %get-tuple-element.102.part_ref, bf16[256,2048]{1,0:T(8,128)(2,1)S(1)} %get-tuple-element.95.rest_0_, ...), custom_call_target="tpu_custom_call" | custom-call | flops 2013265920 | tf_op jit(solution)/shard_map/adjoint_sums/pallas_call | solution.py:353
  14.3 1.6 %collective-permute-start.5 = (f32[128,128]{1,0:T(8,128)S(1)}, f32[128,128]{1,0:T(8,128)S(1)}, u32[]{:S(2)}, u32[]{:S(2)}) collective-permute-start(f32[128,128]{1,0:T(8,128)S(1)} %add.23), channel_id=1, source_target_pairs={{0,8},{4,20},{8,0},{12,28},{16,24},{20,4},{24,16},{28,12},{1,9},{5... | collective-permute-start | bytes 196616 | tf_op jit(solution)/shard_map/ppermute | solution.py:276
  16.0 1.2 %collective-permute-start.6 = (f32[128,128]{1,0:T(8,128)S(1)}, f32[128,128]{1,0:T(8,128)S(1)}, u32[]{:S(2)}, u32[]{:S(2)}) collective-permute-start(f32[128,128]{1,0:T(8,128)S(1)} %add.24.after_ref), channel_id=1, source_target_pairs={{0,8},{4,20},{8,0},{12,28},{16,24},{20,4},{24,16},{28,12},{1,9},{5... | collective-permute-start | bytes 196616 | tf_op jit(solution)/shard_map/ppermute | solution.py:276
  17.2 0.9 %waves_of_own_atoms.4 = (f32[128,128]{1,0:T(8,128)S(1)}, f32[256,512]{1,0:T(8,128)S(1)}, f32[256,512]{1,0:T(8,128)S(1)}, bf16[256,512]{1,0:T(8,128)(2,1)S(1)}, b...) custom-call(f32[3,2048]{1,0:T(4,128)S(1)} %copy-done, ...), custom_call_target="tpu_custom_call" | custom-call | flops 2621440 | tf_op jit(solution)/shard_map/waves_of_own_atoms/pallas_call | solution.py:340
  18.1 0.8 %waves_of_own_atoms.5 = (f32[256,512]{1,0:T(8,128)S(1)}, f32[256,512]{1,0:T(8,128)S(1)}, bf16[256,512]{1,0:T(8,128)(2,1)S(1)}, bf16[256,512]{1,0:T(8,128)(2,1)S(...) custom-call(f32[3,2048]{1,0:T(4,128)S(1)} %copy-done, ...), custom_call_target="tpu_custom_call" | custom-call | flops 2621440 | tf_op jit(solution)/shard_map/waves_of_own_atoms/pallas_call | solution.py:340
  19.3 1.0 %collective-permute-done.6 = f32[128,128]{1,0:T(8,128)S(1)} collective-permute-done((f32[128,128]{1,0:T(8,128)S(1)}, f32[128,128]{1,0:T(8,128)S(1)}, u32[]{:S(2)}, u32[]{:S(2)}) %collective-permute-start.6) | collective-permute-done | bytes 65568 | tf_op jit(solution)/shard_map/ppermute | solution.py:276
  20.3 3.2 %collective-permute-start.7 = (f32[2,128,128]{2,1,0:T(8,128)S(1)}, f32[2,128,128]{2,1,0:T(8,128)S(1)}, u32[]{:S(2)}, u32[]{:S(2)}) collective-permute-start(f32[2,128,128]{2,1,0:T(8,128)S(1)} %pad_maximum_fusion.after_ref), channel_id=1, source_target_pairs={{0,16},{4,12},{8,24},{12,4},{16,0},{20,28},{24,8},{28,20},{1,17},{... | collective-permute-start | bytes 393224 | tf_op jit(solution)/shard_map/ppermute | solution.py:276
  23.5 0.8 %waves_of_own_atoms.7 = (f32[256,512]{1,0:T(8,128)S(1)}, f32[256,512]{1,0:T(8,128)S(1)}, bf16[256,512]{1,0:T(8,128)(2,1)S(1)}, bf16[256,512]{1,0:T(8,128)(2,1)S(...) custom-call(f32[3,2048]{1,0:T(4,128)S(1)} %copy-done, ...), custom_call_target="tpu_custom_call" | custom-call | flops 2621440 | tf_op jit(solution)/shard_map/waves_of_own_atoms/pallas_call | solution.py:340
  24.3 0.8 %waves_of_own_atoms.6 = (f32[256,512]{1,0:T(8,128)S(1)}, f32[256,512]{1,0:T(8,128)S(1)}, bf16[256,512]{1,0:T(8,128)(2,1)S(1)}, bf16[256,512]{1,0:T(8,128)(2,1)S(...) custom-call(f32[3,2048]{1,0:T(4,128)S(1)} %copy-done, ...), custom_call_target="tpu_custom_call" | custom-call | flops 2621440 | tf_op jit(solution)/shard_map/waves_of_own_atoms/pallas_call | solution.py:340
  25.2 1.9 %collective-permute-done.7 = f32[2,128,128]{2,1,0:T(8,128)S(1)} collective-permute-done((f32[2,128,128]{2,1,0:T(8,128)S(1)}, f32[2,128,128]{2,1,0:T(8,128)S(1)}, u32[]{:S(2)}, u32[]{:S(2)}) %collective-permute-start.7) | collective-permute-done | bytes 131104 | tf_op jit(solution)/shard_map/ppermute | solution.py:276
  27.0 2.1 %collective-permute-start.9 = (f32[2,128,128]{2,1,0:T(8,128)S(1)}, f32[2,128,128]{2,1,0:T(8,128)S(1)}, u32[]{:S(2)}, u32[]{:S(2)}) collective-permute-start(f32[2,128,128]{2,1,0:T(8,128)S(1)} %add_multiply_fusion.rest_7_), channel_id=1, source_target_pairs={{0,3},{1,2},{2,1},{3,0},{4,7},{5,6},{6,5},{7,4},{8,11},{9,10},{10,... | collective-permute-start | bytes 393224 | tf_op jit(solution)/shard_map/ppermute | solution.py:271
  29.2 0.8 %collective-permute-start.8 = (f32[2,128,128]{2,1,0:T(8,128)S(1)}, f32[2,128,128]{2,1,0:T(8,128)S(1)}, u32[]{:S(2)}, u32[]{:S(2)}) collective-permute-start(f32[2,128,128]{2,1,0:T(8,128)S(1)} %add_multiply_fusion.rest_7_), channel_id=1, source_target_pairs={{0,2},{1,3},{2,0},{3,1},{4,6},{5,7},{6,4},{7,5},{8,10},{9,11},{10,... | collective-permute-start | bytes 393224 | tf_op jit(solution)/shard_map/ppermute | solution.py:271
  29.9 0.7 %collective-permute-start.11 = (f32[2,128,128]{2,1,0:T(8,128)S(1)}, f32[2,128,128]{2,1,0:T(8,128)S(1)}, u32[]{:S(2)}, u32[]{:S(2)}) collective-permute-start(f32[2,128,128]{2,1,0:T(8,128)S(1)} %add_multiply_fusion.rest_7_), channel_id=1, source_target_pairs={{0,1},{1,0},{2,3},{3,2},{4,5},{5,4},{6,7},{7,6},{8,9},{9,8},{10,11... | collective-permute-start | bytes 393224 | tf_op jit(solution)/shard_map/ppermute | solution.py:271
  31.1 3.2 %collective-permute-done.9.rest_7_ = f32[2,128,128]{2,1,0:T(8,128)S(1)} collective-permute-done((f32[2,128,128]{2,1,0:T(8,128)S(1)}, f32[2,128,128]{2,1,0:T(8,128)S(1)}, u32[]{:S(2)}, u32[]{:S(2)}) %collective-permute-start.9) | collective-permute-done | bytes 131104 | tf_op jit(solution)/shard_map/ppermute | solution.py:271
  35.2 1.1 %collective-permute-done.8.rest_23_ = f32[2,128,128]{2,1,0:T(8,128)S(1)} collective-permute-done((f32[2,128,128]{2,1,0:T(8,128)S(1)}, f32[2,128,128]{2,1,0:T(8,128)S(1)}, u32[]{:S(2)}, u32[]{:S(2)}) %collective-permute-start.8) | collective-permute-done | bytes 131104 | tf_op jit(solution)/shard_map/ppermute | solution.py:271
  36.9 1.4 %fields_of_some_groups.5 = (f32[128,512]{1,0:T(8,128)S(1)}, f32[24,512]{1,0:T(8,128)S(1)}) custom-call(f32[136,512]{1,0:T(8,128)S(1)} %get-tuple-element.99.own_ref, f32[256,512]{1,0:T(8,128)S(1)} %get-tuple-element.157.rest_0_, f32[256,512]{1,0:T(8,128)S(1)} %get-tuple-element.158.rest_1_, bf16[256,512]{1,0:T(8,128)(2,1)S(1)} %get-tuple-element.159.rest_2_, ...), custom_call_target="tpu_custom_call" | custom-call | flops 131072 | tf_op jit(solution)/shard_map/fields_of_some_groups/pallas_call | solution.py:405
  38.3 1.7 %fields_and_forces.1 = (f32[64,512]{1,0:T(8,128)}, f32[3,512]{1,0:T(4,128)}, f32[64,512]{1,0:T(8,128)}) custom-call(f32[136,512]{1,0:T(8,128)S(1)} %get-tuple-element.99.own_ref, f32[64,64]{1,0:T(8,128)S(1)} %copy-done.2, f32[64,64]{1,0:T(8,128)S(1)} %copy-done.1, f32[256,512]{1,0:T(8,128)S(1)} %get-tuple-element.141.rest_16_.rest_0_, ...), custom_call_target="tpu_custom_call" | custom-call | flops 131072 | tf_op jit(solution)/shard_map/fields_and_forces/pallas_call | solution.py:435
  (40 shorter events, 3.4 us)
Async XLA Ops:
  0.6 5.5 %copy-start = (f32[3,2048]{1,0:T(4,128)S(1)}, f32[3,2048]{1,0:T(4,128)}, u32[]{:S(2)}) copy-start(f32[3,2048]{1,0:T(4,128)} %pos_ref.11) | copy-start | bytes 73732
  1.6 7.5 %collective-permute-start = (f32[72,512]{1,0:T(8,128)S(1)}, f32[72,512]{1,0:T(8,128)S(1)}, u32[]{:S(2)}, u32[]{:S(2)}) collective-permute-start(f32[72,512]{1,0:T(8,128)S(1)} %convert_add_fusion.packed_ref.rest_4_), channel_id=1, source_target_pairs={{0,1},{1,0},{2,3},{3,2},{4,5},{5,4},{6,7},{7,6},{8,9},{9,8},{10,11... | collective-permute-start | bytes 442376 | tf_op jit(solution)/shard_map/ppermute | solution.py:271
  4.6 8.5 %collective-permute-start.2 = (f32[72,512]{1,0:T(8,128)S(1)}, f32[72,512]{1,0:T(8,128)S(1)}, u32[]{:S(2)}, u32[]{:S(2)}) collective-permute-start(f32[72,512]{1,0:T(8,128)S(1)} %convert_add_fusion.packed_ref.rest_4_), channel_id=1, source_target_pairs={{0,2},{1,3},{2,0},{3,1},{4,6},{5,7},{6,4},{7,5},{8,10},{9,11},{10,... | collective-permute-start | bytes 442376 | tf_op jit(solution)/shard_map/ppermute | solution.py:271
  6.1 7.0 %collective-permute-start.3 = (f32[72,512]{1,0:T(8,128)S(1)}, f32[72,512]{1,0:T(8,128)S(1)}, u32[]{:S(2)}, u32[]{:S(2)}) collective-permute-start(f32[72,512]{1,0:T(8,128)S(1)} %convert_add_fusion.packed_ref.rest_4_), channel_id=1, source_target_pairs={{0,3},{1,2},{2,1},{3,0},{4,7},{5,6},{6,5},{7,4},{8,11},{9,10},{10,... | collective-permute-start | bytes 442376 | tf_op jit(solution)/shard_map/ppermute | solution.py:271
  7.6 1.5 %copy-start.1 = (f32[64,64]{1,0:T(8,128)S(1)}, f32[64,64]{1,0:T(8,128)}, u32[]{:S(2)}) copy-start(f32[64,64]{1,0:T(8,128)} %w_charge_ref.3) | copy-start | bytes 49156
  7.6 1.5 %copy-start.2 = (f32[64,64]{1,0:T(8,128)S(1)}, f32[64,64]{1,0:T(8,128)}, u32[]{:S(2)}) copy-start(f32[64,64]{1,0:T(8,128)} %w_out_ref.5) | copy-start | bytes 49156
  7.6 1.5 %copy-start.4 = (f32[64,2048]{1,0:T(8,128)S(1)}, f32[64,2048]{1,0:T(8,128)}, u32[]{:S(2)}) copy-start(f32[64,2048]{1,0:T(8,128)} %feats_ref.1) | copy-start | bytes 1572868
  7.6 1.5 %copy-start.6 = (f32[64,16]{0,1:T(8,128)S(1)}, f32[64,16]{0,1:T(8,128)}, u32[]{:S(2)}) copy-start(f32[64,16]{0,1:T(8,128)} %param.17) | copy-start | bytes 12292
  9.1 0.7 %copy-start.5 = (s32[2048]{0:T(1024)S(1)}, s32[2048]{0:T(1024)}, u32[]{:S(2)}) copy-start(s32[2048]{0:T(1024)} %param.12) | copy-start | bytes 24580
  9.1 0.7 %copy-start.7 = (s32[8]{0:T(128)S(1)}, s32[8]{0:T(128)}, u32[]{:S(2)}) copy-start(s32[8]{0:T(128)} %param.13) | copy-start | bytes 100
  11.9 2.3 %collective-permute-start.1 = (f32[128,128]{1,0:T(8,128)S(1)}, f32[128,128]{1,0:T(8,128)S(1)}, u32[]{:S(2)}, u32[]{:S(2)}) collective-permute-start(f32[128,128]{1,0:T(8,128)S(1)} %get-tuple-element.100), channel_id=1, source_target_pairs={{0,4},{4,0},{8,12},{12,8},{16,20},{20,16},{24,28},{28,24},{1,5},{5... | collective-permute-start | bytes 196616 | tf_op jit(solution)/shard_map/ppermute | solution.py:271
  14.2 1.7 %collective-permute-start.4 = (f32[128,128]{1,0:T(8,128)S(1)}, f32[128,128]{1,0:T(8,128)S(1)}, u32[]{:S(2)}, u32[]{:S(2)}) collective-permute-start(f32[128,128]{1,0:T(8,128)S(1)} %get-tuple-element.104), channel_id=1, source_target_pairs={{0,4},{4,0},{8,12},{12,8},{16,20},{20,16},{24,28},{28,24},{1,5},{5... | collective-permute-start | bytes 196616 | tf_op jit(solution)/shard_map/ppermute | solution.py:271
  14.3 5.0 %collective-permute-start.5 = (f32[128,128]{1,0:T(8,128)S(1)}, f32[128,128]{1,0:T(8,128)S(1)}, u32[]{:S(2)}, u32[]{:S(2)}) collective-permute-start(f32[128,128]{1,0:T(8,128)S(1)} %add.23), channel_id=1, source_target_pairs={{0,8},{4,20},{8,0},{12,28},{16,24},{20,4},{24,16},{28,12},{1,9},{5... | collective-permute-start | bytes 196616 | tf_op jit(solution)/shard_map/ppermute | solution.py:276
  15.9 1.2 %copy-start.3 = (f32[64]{0:T(128)S(1)}, f32[64]{0:T(128)}, u32[]{:S(2)}) copy-start(f32[64]{0:T(128)} %param.15) | copy-start | bytes 772
  16.0 4.3 %collective-permute-start.6 = (f32[128,128]{1,0:T(8,128)S(1)}, f32[128,128]{1,0:T(8,128)S(1)}, u32[]{:S(2)}, u32[]{:S(2)}) collective-permute-start(f32[128,128]{1,0:T(8,128)S(1)} %add.24.after_ref), channel_id=1, source_target_pairs={{0,8},{4,20},{8,0},{12,28},{16,24},{20,4},{24,16},{28,12},{1,9},{5... | collective-permute-start | bytes 196616 | tf_op jit(solution)/shard_map/ppermute | solution.py:276
  20.3 6.7 %collective-permute-start.7 = (f32[2,128,128]{2,1,0:T(8,128)S(1)}, f32[2,128,128]{2,1,0:T(8,128)S(1)}, u32[]{:S(2)}, u32[]{:S(2)}) collective-permute-start(f32[2,128,128]{2,1,0:T(8,128)S(1)} %pad_maximum_fusion.after_ref), channel_id=1, source_target_pairs={{0,16},{4,12},{8,24},{12,4},{16,0},{20,28},{24,8},{28,20},{1,17},{... | collective-permute-start | bytes 393224 | tf_op jit(solution)/shard_map/ppermute | solution.py:276
  27.0 7.2 %collective-permute-start.9 = (f32[2,128,128]{2,1,0:T(8,128)S(1)}, f32[2,128,128]{2,1,0:T(8,128)S(1)}, u32[]{:S(2)}, u32[]{:S(2)}) collective-permute-start(f32[2,128,128]{2,1,0:T(8,128)S(1)} %add_multiply_fusion.rest_7_), channel_id=1, source_target_pairs={{0,3},{1,2},{2,1},{3,0},{4,7},{5,6},{6,5},{7,4},{8,11},{9,10},{10,... | collective-permute-start | bytes 393224 | tf_op jit(solution)/shard_map/ppermute | solution.py:271
  29.2 7.2 %collective-permute-start.8 = (f32[2,128,128]{2,1,0:T(8,128)S(1)}, f32[2,128,128]{2,1,0:T(8,128)S(1)}, u32[]{:S(2)}, u32[]{:S(2)}) collective-permute-start(f32[2,128,128]{2,1,0:T(8,128)S(1)} %add_multiply_fusion.rest_7_), channel_id=1, source_target_pairs={{0,2},{1,3},{2,0},{3,1},{4,6},{5,7},{6,4},{7,5},{8,10},{9,11},{10,... | collective-permute-start | bytes 393224 | tf_op jit(solution)/shard_map/ppermute | solution.py:271
  29.9 6.5 %collective-permute-start.11 = (f32[2,128,128]{2,1,0:T(8,128)S(1)}, f32[2,128,128]{2,1,0:T(8,128)S(1)}, u32[]{:S(2)}, u32[]{:S(2)}) collective-permute-start(f32[2,128,128]{2,1,0:T(8,128)S(1)} %add_multiply_fusion.rest_7_), channel_id=1, source_target_pairs={{0,1},{1,0},{2,3},{3,2},{4,5},{5,4},{6,7},{7,6},{8,9},{9,8},{10,11... | collective-permute-start | bytes 393224 | tf_op jit(solution)/shard_map/ppermute | solution.py:271
  34.2 2.7 %collective-permute-start.13 = (f32[2,128,128]{2,1,0:T(8,128)S(1)}, f32[2,128,128]{2,1,0:T(8,128)S(1)}, u32[]{:S(2)}, u32[]{:S(2)}) collective-permute-start(f32[2,128,128]{2,1,0:T(8,128)S(1)} %add_multiply_fusion.rest_7_), channel_id=1, source_target_pairs={{0,4},{4,0},{8,12},{12,8},{16,20},{20,16},{24,28},{28,24},{1,5},{5... | collective-permute-start | bytes 393224 | tf_op jit(solution)/shard_map/ppermute | solution.py:271
  34.2 2.7 %collective-permute-start.14 = (f32[2,128,128]{2,1,0:T(8,128)S(1)}, f32[2,128,128]{2,1,0:T(8,128)S(1)}, u32[]{:S(2)}, u32[]{:S(2)}) collective-permute-start(f32[2,128,128]{2,1,0:T(8,128)S(1)} %collective-permute-done.9.rest_7_), channel_id=1, source_target_pairs={{0,4},{4,0},{8,12},{12,8},{16,20},{20,16},{24,28},{28,24},{1,5},{5... | collective-permute-start | bytes 393224 | tf_op jit(solution)/shard_map/ppermute | solution.py:271
  36.4 1.9 %collective-permute-start.12 = (f32[2,128,128]{2,1,0:T(8,128)S(1)}, f32[2,128,128]{2,1,0:T(8,128)S(1)}, u32[]{:S(2)}, u32[]{:S(2)}) collective-permute-start(f32[2,128,128]{2,1,0:T(8,128)S(1)} %collective-permute-done.11.rest_31_), channel_id=1, source_target_pairs={{0,4},{4,0},{8,12},{12,8},{16,20},{20,16},{24,28},{28,24},{1,5},{5... | collective-permute-start | bytes 393224 | tf_op jit(solution)/shard_map/ppermute | solution.py:271
  36.4 1.9 %collective-permute-start.10 = (f32[2,128,128]{2,1,0:T(8,128)S(1)}, f32[2,128,128]{2,1,0:T(8,128)S(1)}, u32[]{:S(2)}, u32[]{:S(2)}) collective-permute-start(f32[2,128,128]{2,1,0:T(8,128)S(1)} %collective-permute-done.8.rest_23_), channel_id=1, source_target_pairs={{0,4},{4,0},{8,12},{12,8},{16,20},{20,16},{24,28},{28,24},{1,5},{5... | collective-permute-start | bytes 393224 | tf_op jit(solution)/shard_map/ppermute | solution.py:271
